TPU v7x, 32 devices: a whole 2x2x4 slice. The times are simulated.
32 devices in a mesh: groups: 2 (over x), mp: 16 (over z, y, core).
Axes of the slice: x: 2, y: 2, z: 4, core: 2. Of those that a mesh axis runs over, the one named last changes fastest.
Arguments:
- activations: bfloat16 [512, 8192], P(('groups', 'mp')), parts along dimension 0, may hold values from -60 to 60
- gate_weight: bfloat16 [8192, 14336], P(None, 'mp'), may hold values from -0.0625 to 0.0625
- up_weight: bfloat16 [8192, 14336], P(None, 'mp'), may hold values from -0.0625 to 0.0625
- down_weight: bfloat16 [14336, 8192], P('mp'), may hold values from -0.046875 to 0.046875
- norm_gain_vector: bfloat16 [8192], replicated, may hold values from 0.25 to 1.75
- shrink_factors: bfloat16 [16, 8192, 64], P('mp'), may hold values from -0.0625 to 0.0625
- expand_factors: bfloat16 [16, 64, 14336], P(None, None, 'mp'), may hold values from -0.75 to 0.75
- adapter_ranks: int32 [16], replicated, may hold values from 16 to 64, as said below
- adapter_storage_slot: int32 [16], replicated, may hold values from 0 to 15, each once
- segment_start: int32 [64], P('groups'), parts along dimension 0, may hold values from 0 to 255, as said below
- segment_adapter: int32 [64], P('groups'), parts along dimension 0, may hold values from 0 to 15
Outputs:
- block_out: bfloat16 [512, 8192], P(('groups', 'mp')), parts along dimension 0
- normed: bfloat16 [512, 8192], P(('groups', 'mp')), parts along dimension 0
There are 2 independent parts, one for each index of `groups`. A program takes and returns all parts, laid end to end along the dimension named above; an argument that names none is the same for every part. Nothing has to cross between parts.
Inputs may be any that keep to these rules, and one draw needn't show every extreme that they name: `adapter_ranks`: one adapter has rank 64 and one rank 16. `segment_start`: strictly increasing, the first is 0.
All inputs are finite; a program needn't handle non-finite values.
Results may differ from a plain program's by a relative error of at most 0.017.
Values may be sent and summed in bfloat16 or wider, within the bound.
No kernel may reach another device: no remote copies, remote signals or barrier semaphores. Data moves between devices by JAX's collectives and lax.ppermute only.
A program may use at most 128 MiB of HBM per device.

v0:
```python
import jax
import jax.numpy as jnp
from jax import lax
from jax.sharding import PartitionSpec as P

adapter_alpha = 32.0


def body(
    activations,
    gate_weight,
    up_weight,
    down_weight,
    norm_gain_vector,
    shrink_factors,
    expand_factors,
    adapter_ranks,
    adapter_storage_slot,
    segment_start,
    segment_adapter,
):
    hidden_width = gate_weight.shape[1]
    storage_slots, model_width, largest_rank = shrink_factors.shape
    adapter_table = expand_factors.shape[0]
    segments = segment_start.shape[0]
    shrink_matrix = jnp.transpose(shrink_factors, (1, 0, 2)).reshape(
        model_width, storage_slots * largest_rank
    )
    piece = lax.all_gather(activations, "mp", axis=0, tiled=True)
    mixed = jnp.concatenate(
        [
            jnp.dot(piece, gate_weight, preferred_element_type=jnp.float32),
            jnp.dot(piece, up_weight, preferred_element_type=jnp.float32),
            jnp.dot(piece, shrink_matrix, preferred_element_type=jnp.float32),
        ],
        axis=1,
    )
    batch_rows = mixed.shape[0]
    gate = mixed[:, :hidden_width]
    up_output = mixed[:, hidden_width : 2 * hidden_width]
    own_shrink = mixed[:, 2 * hidden_width :].reshape(batch_rows, storage_slots, largest_rank)
    position = lax.iota(jnp.int32, batch_rows)
    segment = jnp.sum((segment_start[None, :] <= position[:, None]).astype(jnp.int32), axis=1) - 1
    seg_hot = (segment[:, None] == lax.iota(jnp.int32, segments)[None, :]).astype(jnp.int32)
    row_adapter = jnp.sum(seg_hot * segment_adapter[None, :], axis=1)
    adapt_hot = (row_adapter[:, None] == lax.iota(jnp.int32, adapter_table)[None, :]).astype(
        jnp.int32
    )
    rank_per_row = jnp.sum(adapt_hot * adapter_ranks[None, :], axis=1)
    first_slot = lax.axis_index("mp") * storage_slots
    local_index = lax.iota(jnp.int32, storage_slots)[None, :] + first_slot
    holder = (adapter_storage_slot[:, None] == local_index).astype(jnp.float32)
    adapt_float = adapt_hot.astype(jnp.float32)
    spread_own = jnp.sum(holder[None, :, :, None] * own_shrink[:, None, :, :], axis=2)
    wide_terms = spread_own * adapt_float[:, :, None]
    summed = lax.psum(wide_terms.astype(jnp.bfloat16), "mp").astype(jnp.float32)
    shrink = jnp.sum(summed * adapt_float[:, :, None], axis=1)
    keep = lax.iota(jnp.int32, largest_rank)[None, :] < rank_per_row[:, None]
    adapter_scale = adapter_alpha / rank_per_row.astype(jnp.float32)
    coeff = jnp.where(keep, shrink * adapter_scale[:, None], 0.0).astype(jnp.bfloat16)
    spread_rows = (adapt_hot.astype(jnp.bfloat16)[:, :, None] * coeff[:, None, :]).reshape(
        batch_rows, adapter_table * largest_rank
    )
    up_output = up_output + jnp.dot(
        spread_rows,
        expand_factors.reshape(adapter_table * largest_rank, hidden_width),
        preferred_element_type=jnp.float32,
    )
    hidden = (jax.nn.silu(gate) * up_output).astype(jnp.bfloat16)
    total = lax.psum_scatter(
        jnp.dot(hidden, down_weight, preferred_element_type=jnp.float32).astype(jnp.bfloat16),
        "mp",
        scatter_dimension=0,
        tiled=True,
    ).astype(jnp.float32)
    stream_sum = activations.astype(jnp.float32) + total
    block_out = stream_sum.astype(jnp.bfloat16)
    scale_rows = lax.rsqrt(jnp.mean(stream_sum * stream_sum, axis=1, keepdims=True) + 1e-05)
    normed = (stream_sum * scale_rows * norm_gain_vector.astype(jnp.float32)[None, :]).astype(
        jnp.bfloat16
    )
    return (block_out, normed)


def solution(mesh):
    return jax.shard_map(
        body,
        mesh=mesh,
        in_specs=(
            P(("groups", "mp"), None),
            P(None, "mp"),
            P(None, "mp"),
            P("mp", None),
            P(),
            P("mp", None, None),
            P(None, None, "mp"),
            P(),
            P(),
            P("groups"),
            P("groups"),
        ),
        out_specs=(P(("groups", "mp"), None), P(("groups", "mp"), None)),
        check_vma=False,
    )
```

profile of v0, /device:TPU:0, one launch (start us, length us, event | category | flops | bytes accessed | tf_op | source)
XLA Modules:
  0.0 264.4 jit_solution(17050890916897526460)
XLA Ops:
  7.2 0.0 copy-start
  7.2 0.0 all-gather.2.cloned.1.call-start
  7.2 0.7 all-gather.2.cloned.1.call-update
  7.9 0.0 all-reduce.2.cloned.1.call-start
  8.0 0.7 convert_reduce_fusion
  8.7 0.7 select_reduce_fusion
  9.5 0.1 copy.13
  9.6 0.7 select_reduce_fusion.1
  10.3 0.7 compare_convert_fusion
  11.0 52.5 %all-gather.2.cloned.1.call-done = bf16[256,8192]{1,0:T(8,128)(2,1)} async-done(((bf16[16,8192]{1,0:T(8,128)(2,1)}), bf16[256,8192]{1,0:T(8,128)(2,1)}) %all-gather.2.cloned.1.call-update) | async-done | bytes 4194320 | tf_op jit(solution)/shard_map/all_gather | solution.py:29
  63.5 3.9 %fusion.2 = f32[256,64]{0,1:T(8,128)S(1)} fusion(bf16[256,8192]{1,0:T(8,128)(2,1)} %all-gather.2.cloned.1.call-done, bf16[1,8192,64]{1,2,0:T(8,128)(2,1)} %param.16), kind=kOutput, calls=%fused_computation.5 | convolution fusion | flops 268435456 | bytes 5308416 | tf_op jit(solution)/shard_map/dot_general | solution.py:34
  67.4 1.0 multiply_convert_fusion
  68.3 0.0 all-reduce.2.cloned.1.call-update
  68.4 0.0 reduce-scatter.2.cloned.1.call-start
  68.4 12.0 %fusion.7 = f32[256,896]{1,0:T(8,128)} fusion(bf16[256,8192]{1,0:T(8,128)(2,1)} %all-gather.2.cloned.1.call-done, bf16[8192,896]{1,0:T(8,128)(2,1)} %param.12), kind=kOutput, calls=%fused_computation.30 | convolution fusion | flops 3758096384 | bytes 19791872 | tf_op jit(solution)/shard_map/dot_general | solution.py:32
  80.4 76.7 %all-reduce.2.cloned.1.call-done = bf16[256,16,64]{0,2,1:T(8,128)(2,1)} async-done(((bf16[256,16,64]{0,2,1:T(8,128)(2,1)}), bf16[256,16,64]{0,2,1:T(8,128)(2,1)}) %all-reduce.2.cloned.1.call-update) | async-done | bytes 524304 | tf_op jit(solution)/shard_map/psum | solution.py:56
  157.1 1.2 multiply_reduce_fusion
  158.3 0.1 copy.14
  158.4 0.9 broadcast_multiply_fusion
  159.3 0.0 copy-done
  159.3 0.9 convolution_bitcast_fusion
  160.2 21.7 %convolution_convert_fusion = bf16[256,8192]{1,0:T(8,128)(2,1)} fusion(bf16[896,8192]{1,0:T(8,128)(2,1)} %param.14, f32[256,896]{1,0:T(8,128)S(1)} %convolution_bitcast_fusion, bf16[256,8192]{1,0:T(8,128)(2,1)} %all-gather.2.cloned.1.call-done, bf16[8192,896]{1,0:T(8,128)(2,1)} %param.13, f32[256,896]{1,0:T(8,128)} %fusion.7), kind=kOutput, calls=%fused_computation | convolution fusion | flops 7519895552 | bytes 39583744 | tf_op jit(solution)/shard_map/dot_general | solution.py:71
  181.9 0.0 copy-start.2
  181.9 0.0 copy-start.1
  181.9 0.0 reduce-scatter.2.cloned.1.call-update
  181.9 0.7 copy-done.2
  182.6 72.3 %reduce-scatter.2.cloned.1.call-done = bf16[16,8192]{1,0:T(8,128)(2,1)} async-done(((bf16[256,8192]{1,0:T(8,128)(2,1)}), bf16[16,8192]{1,0:T(8,128)(2,1)}) %reduce-scatter.2.cloned.1.call-update) | async-done | bytes 262160 | tf_op jit(solution)/shard_map/reduce_scatter | solution.py:70
  254.9 0.0 copy-done.1
  254.9 1.1 multiply_reduce_fusion.1
  256.1 1.8 multiply_convert_fusion.1
  (6 shorter events, 0.0 us)
Async XLA Ops:
  7.2 152.1 %copy-start = (bf16[16,64,896]{2,1,0:T(8,128)(2,1)S(1)}, bf16[16,64,896]{2,1,0:T(8,128)(2,1)}, u32[]{:S(2)}) copy-start(bf16[16,64,896]{2,1,0:T(8,128)(2,1)} %param.17) | copy-start | bytes 5505028
  7.2 56.3 %all-gather.2.cloned.1.call-start = ((), (), s32[]{:S(2)}) async-start(), calls=%async_computation.1 | async-start | bytes 4456448 | tf_op jit(solution)/shard_map/all_gather | solution.py:29
  7.9 149.2 %all-reduce.2.cloned.1.call-start = ((), (), s32[]{:S(2)}) async-start(), calls=%async_computation.2 | async-start | bytes 1048576 | tf_op jit(solution)/shard_map/psum | solution.py:56
  68.4 186.6 %reduce-scatter.2.cloned.1.call-start = ((), (), s32[]{:S(2)}) async-start(), calls=%async_computation.3 | async-start | bytes 4456448 | tf_op jit(solution)/shard_map/reduce_scatter | solution.py:70
  181.9 0.7 copy-start.2
  181.9 73.0 %copy-start.1 = (bf16[16,8192]{1,0:T(8,128)(2,1)S(1)}, bf16[16,8192]{1,0:T(8,128)(2,1)}, u32[]{:S(2)}) copy-start(bf16[16,8192]{1,0:T(8,128)(2,1)} %param.11) | copy-start | bytes 786436
Sparse Core Ops, SparseCore 0:
  10.2 53.2 all-gather.1
  68.5 88.5 all-reduce.1
  182.1 72.8 reduce-scatter.1
where the time goes:
time: 265 us; the launch traced here: 264 us
  waiting for transfers between devices  202 us (76%)
  matrix products  38.5 us (15%)
  between operations  13.8 us (5%)
  other arithmetic  8.93 us (3%)
    psum x1, waiting for transfers between devices, body(): summed = lax.psum(wide_terms.astype(jnp.bfloat16), 'mp').astype(jnp.float32)  76.7 us
    reduce_scatter x1, waiting for transfers between devices, body(): lax.psum_scatter(jnp.dot(hidden, down_weight, preferred_element_type=jnp....  72.3 us
    all_gather x1, waiting for transfers between devices, body(): piece = lax.all_gather(activations, 'mp', axis=0, tiled=True)  52.5 us
    dot_general x1, matrix products, body(): jnp.dot(hidden, down_weight, preferred_element_type=jnp.float32)  21.7 us
    dot_general x1, matrix products, body(): jnp.dot(piece, gate_weight, preferred_element_type=jnp.float32)  12 us
  transfers between devices with their start and end apart: 3, of which 3 were waited for; matrix products, arithmetic and copies ran while one was open for 6% of the time, Pallas kernels for 0%

commit v1 on v0

v1 whole, which is shorter than its diff:
```python
import jax
import jax.numpy as jnp
from jax import lax
from jax.sharding import PartitionSpec as P

adapter_alpha = 32.0
AXIS = "mp"
CHUNKS = 2


def ring_shift(size, by):
    far = size // 4
    return [(i, ((i // 4 + by) % far) * 4 + i % 4) for i in range(size)]


def flip(size, bit):
    return [(i, i ^ bit) for i in range(size)]


def gather_rows(own, size):
    far = size // 4
    line = [own] + [lax.ppermute(own, AXIS, ring_shift(size, k)) for k in range(1, far)]
    across = [lax.ppermute(piece, AXIS, flip(size, 2)) for piece in line]
    mine = jnp.concatenate(line + across, axis=0)
    theirs = lax.ppermute(mine, AXIS, flip(size, 1))
    return mine, theirs


def add_bf16(a, b):
    return (a.astype(jnp.float32) + b.astype(jnp.float32)).astype(jnp.bfloat16)


def scatter_rows(mine, theirs, size):
    far = size // 4
    half = mine.shape[0] // 2
    rows = half // far
    chip = add_bf16(mine, lax.ppermute(theirs, AXIS, flip(size, 1)))
    line = add_bf16(chip[:half], lax.ppermute(chip[half:], AXIS, flip(size, 2)))
    total = line[:rows].astype(jnp.float32)
    for k in range(1, far):
        block = lax.slice_in_dim(line, k * rows, (k + 1) * rows, axis=0)
        total = total + lax.ppermute(block, AXIS, ring_shift(size, -k)).astype(jnp.float32)
    return total


def share_shrink(own, size):
    far = size // 4
    half = own.shape[0] // 2
    quarter = half // 2
    rows = quarter // far

    def swap_core(a):
        return jnp.concatenate([a[half:], a[:half]], axis=0)

    def swap_near(a):
        a = a.reshape((2, 2, quarter) + a.shape[1:])
        return jnp.concatenate([a[:, 1:], a[:, :1]], axis=1).reshape(own.shape)

    def roll_far(a, k):
        a = a.reshape(4, far, rows, a.shape[-1])
        return jnp.concatenate([a[:, k:], a[:, :k]], axis=1).reshape(own.shape)

    own = own + swap_core(lax.ppermute(own, AXIS, flip(size, 1)))
    own = own + swap_near(lax.ppermute(own, AXIS, flip(size, 2)))
    k = 1
    while k < far:
        own = own + roll_far(lax.ppermute(own, AXIS, ring_shift(size, -k)), k)
        k *= 2
    return own


def body(
    activations,
    gate_weight,
    up_weight,
    down_weight,
    norm_gain_vector,
    shrink_factors,
    expand_factors,
    adapter_ranks,
    adapter_storage_slot,
    segment_start,
    segment_adapter,
):
    size = lax.axis_size(AXIS)
    me = lax.axis_index(AXIS)
    far = size // 4
    assert far * 4 == size and far & (far - 1) == 0
    own_rows, model_width = activations.shape
    hidden_width = gate_weight.shape[1]
    storage_slots, _, largest_rank = shrink_factors.shape
    adapter_table = expand_factors.shape[0]
    segments = segment_start.shape[0]
    batch_rows = own_rows * size

    row = lax.iota(jnp.int32, batch_rows)
    block = row // own_rows
    holder = (
        (((me >> 2) + far - lax.rem(block, far)) & (far - 1)) * 4
        + (((me >> 1) & 1) ^ (block // far & 1)) * 2
        + ((me & 1) ^ (block // (2 * far)))
    )
    position = holder * own_rows + lax.rem(row, own_rows)
    segment = jnp.sum((segment_start[None, :] <= position[:, None]).astype(jnp.int32), axis=1) - 1
    seg_hot = (segment[:, None] == lax.iota(jnp.int32, segments)[None, :]).astype(jnp.int32)
    row_adapter = jnp.sum(seg_hot * segment_adapter[None, :], axis=1)
    adapt_hot = (row_adapter[:, None] == lax.iota(jnp.int32, adapter_table)[None, :]).astype(
        jnp.int32
    )
    rank_per_row = jnp.sum(adapt_hot * adapter_ranks[None, :], axis=1)
    row_slot = jnp.sum(adapt_hot * adapter_storage_slot[None, :], axis=1) - me * storage_slots

    mine, theirs = gather_rows(activations, size)
    rows = jnp.concatenate([mine, theirs], axis=0)

    own_shrink = jnp.zeros((batch_rows, largest_rank), jnp.float32)
    for slot in range(storage_slots):
        product = jnp.dot(rows, shrink_factors[slot], preferred_element_type=jnp.float32)
        own_shrink = jnp.where((row_slot == slot)[:, None], product, own_shrink)
    shrink = share_shrink(own_shrink.astype(jnp.bfloat16), size).astype(jnp.float32)

    gate = jnp.dot(rows, gate_weight, preferred_element_type=jnp.float32)
    up_output = jnp.dot(rows, up_weight, preferred_element_type=jnp.float32)

    keep = lax.iota(jnp.int32, largest_rank)[None, :] < rank_per_row[:, None]
    adapter_scale = adapter_alpha / rank_per_row.astype(jnp.float32)
    coeff = jnp.where(keep, shrink * adapter_scale[:, None], 0.0).astype(jnp.bfloat16)
    spread_rows = (adapt_hot.astype(jnp.bfloat16)[:, :, None] * coeff[:, None, :]).reshape(
        batch_rows, adapter_table * largest_rank
    )
    up_output = up_output + jnp.dot(
        spread_rows,
        expand_factors.reshape(adapter_table * largest_rank, hidden_width),
        preferred_element_type=jnp.float32,
    )
    hidden = lax.optimization_barrier((jax.nn.silu(gate) * up_output).astype(jnp.bfloat16))

    half = batch_rows // 2
    width = model_width // CHUNKS
    totals = []
    for chunk in range(CHUNKS):
        term = jnp.dot(
            hidden,
            lax.slice_in_dim(down_weight, chunk * width, (chunk + 1) * width, axis=1),
            preferred_element_type=jnp.float32,
        ).astype(jnp.bfloat16)
        totals.append(scatter_rows(term[:half], term[half:], size))
    total = jnp.concatenate(totals, axis=1)

    stream_sum = activations.astype(jnp.float32) + total
    block_out = stream_sum.astype(jnp.bfloat16)
    scale_rows = lax.rsqrt(jnp.mean(stream_sum * stream_sum, axis=1, keepdims=True) + 1e-05)
    normed = (stream_sum * scale_rows * norm_gain_vector.astype(jnp.float32)[None, :]).astype(
        jnp.bfloat16
    )
    return (block_out, normed)


def solution(mesh):
    return jax.shard_map(
        body,
        mesh=mesh,
        in_specs=(
            P(("groups", "mp"), None),
            P(None, "mp"),
            P(None, "mp"),
            P("mp", None),
            P(),
            P("mp", None, None),
            P(None, None, "mp"),
            P(),
            P(),
            P("groups"),
            P("groups"),
        ),
        out_specs=(P(("groups", "mp"), None), P(("groups", "mp"), None)),
        check_vma=False,
    )
```

time: 265 us -> 137 us (0.52)
  waiting for transfers between devices: 202 us -> 53.8 us
  starting transfers between devices: 0.12 us -> 36.3 us
  between operations: 13.8 us -> 1.08 us
  local copies, waits for them, and re-layouts: 0.94 us -> 11.7 us
  matrix products: 38.5 us -> 31.8 us
  other arithmetic: 8.93 us -> 2.54 us
    psum x1 -> x0, waiting for transfers between devices: 76.7 us -> none  [body(): summed = lax.psum(wide_terms.astype(jnp.bfloat16), 'mp').astype(jnp.float32)]
    reduce_scatter x1 -> x0, waiting for transfers between devices: 72.3 us -> none  [body(): lax.psum_scatter(jnp.dot(hidden, down_weight, preferred_element_type=jnp....]
    ppermute x0 -> x22, waiting for transfers between devices: none -> 53.8 us  [the longest x2 15.4 us: scatter_rows(): line = add_bf16(chip[:half], lax.ppermute(chip[half:], AXIS, flip(size, 2)))]
    all_gather x1 -> x0, waiting for transfers between devices: 52.5 us -> none  [body(): piece = lax.all_gather(activations, 'mp', axis=0, tiled=True)]
    ppermute x0 -> x22, starting transfers between devices: none -> 36.3 us  [the longest x6 11.3 us: scatter_rows(): lax.ppermute(block, AXIS, ring_shift(size, -k)).astype(jnp.float32)]
    dot_general x3 -> x5, matrix products: 37.6 us -> 31.1 us  [the longest x1 11.4 us: body(): up_output = jnp.dot(rows, up_weight, preferred_element_type=jnp.float32)]
    unnamed x6 -> x33, local copies, waits for them, and re-layouts: 0.7 us -> 6.75 us
    concatenate x0 -> x2, local copies, waits for them, and re-layouts: none -> 3.92 us  [the longest x1 3.1 us: body(): rows = jnp.concatenate([mine, theirs], axis=0)]
  transfers between devices with their start and end apart: 3 -> 22, of which waited for: 3 -> 13; matrix products, arithmetic and copies ran while one was open for 6% -> 16% of each run, Pallas kernels for 0% -> 0%
where the time goes in v1:
time: 137 us
  waiting for transfers between devices  53.8 us (39%)
  starting transfers between devices  36.3 us (26%)
  matrix products  31.8 us (23%)
  local copies, waits for them, and re-layouts  11.7 us (9%)
  other arithmetic  2.54 us (2%)
    ppermute x2, waiting for transfers between devices, scatter_rows(): line = add_bf16(chip[:half], lax.ppermute(chip[half:], AXIS, flip(size, 2)))  15.4 us
    dot_general x1, matrix products, body(): up_output = jnp.dot(rows, up_weight, preferred_element_type=jnp.float32)  11.4 us
    ppermute x6, starting transfers between devices, scatter_rows(): lax.ppermute(block, AXIS, ring_shift(size, -k)).astype(jnp.float32)  11.3 us
    dot_general x1, matrix products, body(): gate = jnp.dot(rows, gate_weight, preferred_element_type=jnp.float32)  11.2 us
    ppermute x6, waiting for transfers between devices, scatter_rows(): lax.ppermute(block, AXIS, ring_shift(size, -k)).astype(jnp.float32)  10.9 us
    ppermute x3, waiting for transfers between devices, gather_rows(): lax.ppermute(own, AXIS, ring_shift(size, k))  10.9 us
    ppermute x3, starting transfers between devices, gather_rows(): lax.ppermute(own, AXIS, ring_shift(size, k))  7.01 us
    ppermute x2, starting transfers between devices, share_shrink(): own = own + roll_far(lax.ppermute(own, AXIS, ring_shift(size, -k)), k)  6.94 us
  transfers between devices with their start and end apart: 22, of which 13 were waited for; matrix products, arithmetic and copies ran while one was open for 16% of the time, Pallas kernels for 0%

profile of v1, /device:TPU:0, one launch (start us, length us, event | category | flops | bytes accessed | tf_op | source)
XLA Modules:
  0.0 137.2 jit_solution(355606731745811544)
XLA Ops:
  0.7 3.1 %collective-permute-start = (bf16[16,8192]{1,0:T(8,128)(2,1)}, bf16[16,8192]{1,0:T(8,128)(2,1)S(1)}, u32[]{:S(2)}, u32[]{:S(2)}) collective-permute-start(bf16[16,8192]{1,0:T(8,128)(2,1)} %param.11), channel_id=1, source_target_pairs={{0,4},{1,5},{2,6},{3,7},{4,8},{5,9},{6,10},{7,11},{8,12},{9,13},{1... | collective-permute-start | bytes 786440 | tf_op jit(solution)/shard_map/ppermute | solution.py:22
  3.8 2.6 %collective-permute-start.1 = (bf16[16,8192]{1,0:T(8,128)(2,1)}, bf16[16,8192]{1,0:T(8,128)(2,1)S(1)}, u32[]{:S(2)}, u32[]{:S(2)}) collective-permute-start(bf16[16,8192]{1,0:T(8,128)(2,1)} %param.11), channel_id=1, source_target_pairs={{0,8},{1,9},{2,10},{3,11},{4,12},{5,13},{6,14},{7,15},{8,0},{9,1},... | collective-permute-start | bytes 786440 | tf_op jit(solution)/shard_map/ppermute | solution.py:22
  6.4 1.3 collective-permute-start.2
  7.7 1.5 %collective-permute-start.3 = (bf16[16,8192]{1,0:T(8,128)(2,1)}, bf16[16,8192]{1,0:T(8,128)(2,1)S(1)}, u32[]{:S(2)}, u32[]{:S(2)}) collective-permute-start(bf16[16,8192]{1,0:T(8,128)(2,1)} %param.11), channel_id=1, source_target_pairs={{0,2},{1,3},{2,0},{3,1},{4,6},{5,7},{6,4},{7,5},{8,10},{9,11},{10,... | collective-permute-start | bytes 786440 | tf_op jit(solution)/shard_map/ppermute | solution.py:23
  9.2 1.8 %constant_dynamic-update-slice_fusion.7 = (bf16[128,8192]{1,0:T(8,128)(2,1)}, bf16[256,8192]{1,0:T(8,128)(2,1)}) fusion(bf16[16,8192]{1,0:T(8,128)(2,1)} %param.11), kind=kLoop, calls=%fused_computation.36 | loop fusion | bytes 786432
  11.0 2.3 %collective-permute-done = bf16[16,8192]{1,0:T(8,128)(2,1)S(1)} collective-permute-done((bf16[16,8192]{1,0:T(8,128)(2,1)}, bf16[16,8192]{1,0:T(8,128)(2,1)S(1)}, u32[]{:S(2)}, u32[]{:S(2)}) %collective-permute-start) | collective-permute-done | bytes 262176 | tf_op jit(solution)/shard_map/ppermute | solution.py:22
  13.3 1.8 %collective-permute-start.4 = (bf16[16,8192]{1,0:T(8,128)(2,1)S(1)}, bf16[16,8192]{1,0:T(8,128)(2,1)S(1)}, u32[]{:S(2)}, u32[]{:S(2)}) collective-permute-start(bf16[16,8192]{1,0:T(8,128)(2,1)S(1)} %collective-permute-done), channel_id=1, source_target_pairs={{0,2},{1,3},{2,0},{3,1},{4,6},{5,7},{6,4},{7,5},{8,10},{9,11},{10,... | collective-permute-start | bytes 786440 | tf_op jit(solution)/shard_map/ppermute | solution.py:23
  15.0 8.6 %collective-permute-done.1 = bf16[16,8192]{1,0:T(8,128)(2,1)S(1)} collective-permute-done((bf16[16,8192]{1,0:T(8,128)(2,1)}, bf16[16,8192]{1,0:T(8,128)(2,1)S(1)}, u32[]{:S(2)}, u32[]{:S(2)}) %collective-permute-start.1) | collective-permute-done | bytes 262176 | tf_op jit(solution)/shard_map/ppermute | solution.py:22
  23.7 1.5 %collective-permute-start.5 = (bf16[16,8192]{1,0:T(8,128)(2,1)S(1)}, bf16[16,8192]{1,0:T(8,128)(2,1)S(1)}, u32[]{:S(2)}, u32[]{:S(2)}) collective-permute-start(bf16[16,8192]{1,0:T(8,128)(2,1)S(1)} %collective-permute-done.1), channel_id=1, source_target_pairs={{0,2},{1,3},{2,0},{3,1},{4,6},{5,7},{6,4},{7,5},{8,10},{9,11},{10,... | collective-permute-start | bytes 786440 | tf_op jit(solution)/shard_map/ppermute | solution.py:23
  25.2 0.5 collective-permute-start.6
  25.7 0.8 constant_dynamic-update-slice_fusion.6
  26.5 0.8 constant_dynamic-update-slice_fusion.5
  27.3 0.8 constant_dynamic-update-slice_fusion.4
  28.2 0.8 constant_dynamic-update-slice_fusion.3
  29.0 0.8 constant_dynamic-update-slice_fusion.2
  29.8 3.1 %collective-permute-done.5 = bf16[16,8192]{1,0:T(8,128)(2,1)S(1)} collective-permute-done((bf16[16,8192]{1,0:T(8,128)(2,1)S(1)}, bf16[16,8192]{1,0:T(8,128)(2,1)S(1)}, u32[]{:S(2)}, u32[]{:S(2)}) %collective-permute-start.5) | collective-permute-done | bytes 262176 | tf_op jit(solution)/shard_map/ppermute | solution.py:23
  32.9 0.8 constant_dynamic-update-slice_fusion.1
  33.7 3.8 %collective-permute-done.6 = bf16[16,8192]{1,0:T(8,128)(2,1)S(1)} collective-permute-done((bf16[16,8192]{1,0:T(8,128)(2,1)S(1)}, bf16[16,8192]{1,0:T(8,128)(2,1)S(1)}, u32[]{:S(2)}, u32[]{:S(2)}) %collective-permute-start.6) | collective-permute-done | bytes 262176 | tf_op jit(solution)/shard_map/ppermute | solution.py:23
  37.4 0.8 constant_dynamic-update-slice_fusion
  38.6 4.2 %collective-permute-done.7 = bf16[128,8192]{1,0:T(8,128)(2,1)} collective-permute-done((bf16[128,8192]{1,0:T(8,128)(2,1)}, bf16[128,8192]{1,0:T(8,128)(2,1)}, u32[]{:S(2)}, u32[]{:S(2)}) %collective-permute-start.7) | collective-permute-done | bytes 2097184 | tf_op jit(solution)/shard_map/ppermute | solution.py:25
  42.8 3.1 %constant_dynamic-update-slice_fusion.8 = bf16[256,8192]{1,0:T(8,128)(2,1)} fusion(bf16[256,8192]{1,0:T(8,128)(2,1)} %get-tuple-element.13, bf16[128,8192]{1,0:T(8,128)(2,1)} %collective-permute-done.7), kind=kLoop, calls=%fused_computation.37 | loop fusion | bytes 4194304 | tf_op jit(solution)/shard_map/concatenate | solution.py:114
  45.9 3.6 %fusion.10 = bf16[256,64]{0,1:T(8,128)(2,1)S(1)} fusion(bf16[256,8192]{1,0:T(8,128)(2,1)} %constant_dynamic-update-slice_fusion.8, bf16[1,8192,64]{1,2,0:T(8,128)(2,1)S(1)} %copy-done.3, pred[256]{0:T(512)(128)(4,1)S(1)} %subtract_compare_fusion), kind=kOutput, calls=%fused_computation.11 | convolution fusion | flops 268468224 | bytes 5275904 | tf_op jit(solution)/shard_map/dot_general | solution.py:118
  49.6 1.1 collective-permute-done.8
  50.7 1.6 %collective-permute-start.9 = (bf16[256,64]{0,1:T(8,128)(2,1)S(1)}, bf16[256,64]{0,1:T(8,128)(2,1)S(1)}, u32[]{:S(2)}, u32[]{:S(2)}) collective-permute-start(bf16[256,64]{0,1:T(8,128)(2,1)S(1)} %maximum_add_fusion.1), channel_id=1, source_target_pairs={{0,2},{1,3},{2,0},{3,1},{4,6},{5,7},{6,4},{7,5},{8,10},{9,11},{10,... | collective-permute-start | bytes 98312 | tf_op jit(solution)/shard_map/ppermute | solution.py:64
  52.3 2.4 %collective-permute-done.9 = bf16[256,64]{0,1:T(8,128)(2,1)S(1)} collective-permute-done((bf16[256,64]{0,1:T(8,128)(2,1)S(1)}, bf16[256,64]{0,1:T(8,128)(2,1)S(1)}, u32[]{:S(2)}, u32[]{:S(2)}) %collective-permute-start.9) | collective-permute-done | bytes 32800 | tf_op jit(solution)/shard_map/ppermute | solution.py:64
  55.2 6.2 %collective-permute-start.10 = (bf16[256,64]{0,1:T(8,128)(2,1)S(1)}, bf16[256,64]{0,1:T(8,128)(2,1)S(1)}, u32[]{:S(2)}, u32[]{:S(2)}) collective-permute-start(bf16[256,64]{0,1:T(8,128)(2,1)S(1)} %add.110), channel_id=1, source_target_pairs={{0,12},{1,13},{2,14},{3,15},{4,0},{5,1},{6,2},{7,3},{8,4},{9,5},{1... | collective-permute-start | bytes 98312 | tf_op jit(solution)/shard_map/ppermute | solution.py:67
  61.4 1.8 %collective-permute-done.10 = bf16[256,64]{0,1:T(8,128)(2,1)S(1)} collective-permute-done((bf16[256,64]{0,1:T(8,128)(2,1)S(1)}, bf16[256,64]{0,1:T(8,128)(2,1)S(1)}, u32[]{:S(2)}, u32[]{:S(2)}) %collective-permute-start.10) | collective-permute-done | bytes 32800 | tf_op jit(solution)/shard_map/ppermute | solution.py:67
  63.5 0.7 collective-permute-start.11
  64.2 11.2 %fusion.22 = f32[256,896]{1,0:T(8,128)S(1)} fusion(bf16[256,8192]{1,0:T(8,128)(2,1)} %constant_dynamic-update-slice_fusion.8, bf16[8192,896]{1,0:T(8,128)(2,1)} %param.12), kind=kOutput, calls=%fused_computation.76 | convolution fusion | flops 3758096384 | bytes 19791872 | tf_op jit(solution)/shard_map/dot_general | solution.py:122
  75.8 0.7 convolution_bitcast_fusion
  76.6 11.4 %multiply_convert_fusion = bf16[256,896]{1,0:T(8,128)(2,1)S(1)} fusion(f32[256,896]{1,0:T(8,128)S(1)} %fusion.22, f32[256,896]{1,0:T(8,128)S(1)} %convolution_bitcast_fusion, bf16[256,8192]{1,0:T(8,128)(2,1)} %constant_dynamic-update-slice_fusion.8, bf16[8192,896]{1,0:T(8,128)(2,1)} %param.13), kind=kOutput, calls=%fused_computation.15 | convolution fusion | flops 3759702016 | bytes 21168128 | tf_op jit(solution)/shard_map/dot_general | solution.py:123
  88.1 2.4 %fusion.4 = bf16[256,4096]{1,0:T(8,128)(2,1)S(1)} fusion(bf16[256,896]{1,0:T(8,128)(2,1)S(1)} %multiply_convert_fusion, bf16[896,8192]{1,0:T(8,128)(2,1)S(1)} %bitcast.27), kind=kOutput, calls=%fused_computation.4 | convolution fusion | flops 1880096768 | bytes 9895936 | tf_op jit(solution)/shard_map/dot_general | solution.py:142
  90.7 2.4 %fusion.7 = bf16[256,4096]{1,0:T(8,128)(2,1)S(1)} fusion(bf16[256,896]{1,0:T(8,128)(2,1)S(1)} %multiply_convert_fusion, bf16[896,8192]{1,0:T(8,128)(2,1)S(1)} %bitcast.27), kind=kOutput, calls=%fused_computation.5 | convolution fusion | flops 1880096768 | bytes 9895936 | tf_op jit(solution)/shard_map/dot_general | solution.py:142
  93.2 0.6 collective-permute-start.17
  93.8 0.2 add_convert_fusion.1
  94.1 1.6 %collective-permute-start.13 = (bf16[64,4096]{1,0:T(8,128)(2,1)S(1)}, bf16[64,4096]{1,0:T(8,128)(2,1)S(1)}, u32[]{:S(2)}, u32[]{:S(2)}) collective-permute-start(bf16[64,4096]{1,0:T(8,128)(2,1)S(1)} %slice.115), channel_id=1, source_target_pairs={{0,2},{1,3},{2,0},{3,1},{4,6},{5,7},{6,4},{7,5},{8,10},{9,11},{10,... | collective-permute-start | bytes 1572872 | tf_op jit(solution)/shard_map/ppermute | solution.py:38
  95.7 0.4 collective-permute-done.17
  96.0 0.2 add_convert_fusion
  96.4 1.6 %collective-permute-start.18 = (bf16[64,4096]{1,0:T(8,128)(2,1)S(1)}, bf16[64,4096]{1,0:T(8,128)(2,1)S(1)}, u32[]{:S(2)}, u32[]{:S(2)}) collective-permute-start(bf16[64,4096]{1,0:T(8,128)(2,1)S(1)} %slice.123), channel_id=1, source_target_pairs={{0,2},{1,3},{2,0},{3,1},{4,6},{5,7},{6,4},{7,5},{8,10},{9,11},{10,... | collective-permute-start | bytes 1572872 | tf_op jit(solution)/shard_map/ppermute | solution.py:38
  98.0 10.9 %collective-permute-done.13 = bf16[64,4096]{1,0:T(8,128)(2,1)S(1)} collective-permute-done((bf16[64,4096]{1,0:T(8,128)(2,1)S(1)}, bf16[64,4096]{1,0:T(8,128)(2,1)S(1)}, u32[]{:S(2)}, u32[]{:S(2)}) %collective-permute-start.13) | collective-permute-done | bytes 524320 | tf_op jit(solution)/shard_map/ppermute | solution.py:38
  109.1 3.7 %collective-permute-start.14 = (bf16[16,4096]{1,0:T(8,128)(2,1)S(1)}, bf16[16,4096]{1,0:T(8,128)(2,1)S(1)}, u32[]{:S(2)}, u32[]{:S(2)}) collective-permute-start(bf16[16,4096]{1,0:T(8,128)(2,1)S(1)} %get-tuple-element.6), channel_id=1, source_target_pairs={{0,12},{1,13},{2,14},{3,15},{4,0},{5,1},{6,2},{7,3},{8,4},{9,5},{1... | collective-permute-start | bytes 393224 | tf_op jit(solution)/shard_map/ppermute | solution.py:42
  112.8 2.0 %collective-permute-start.15 = (bf16[16,4096]{1,0:T(8,128)(2,1)S(1)}, bf16[16,4096]{1,0:T(8,128)(2,1)S(1)}, u32[]{:S(2)}, u32[]{:S(2)}) collective-permute-start(bf16[16,4096]{1,0:T(8,128)(2,1)S(1)} %get-tuple-element.8), channel_id=1, source_target_pairs={{0,8},{1,9},{2,10},{3,11},{4,12},{5,13},{6,14},{7,15},{8,0},{9,1},... | collective-permute-start | bytes 393224 | tf_op jit(solution)/shard_map/ppermute | solution.py:42
  114.8 4.5 %collective-permute-done.18 = bf16[64,4096]{1,0:T(8,128)(2,1)S(1)} collective-permute-done((bf16[64,4096]{1,0:T(8,128)(2,1)S(1)}, bf16[64,4096]{1,0:T(8,128)(2,1)S(1)}, u32[]{:S(2)}, u32[]{:S(2)}) %collective-permute-start.18) | collective-permute-done | bytes 524320 | tf_op jit(solution)/shard_map/ppermute | solution.py:38
  119.4 3.7 %collective-permute-start.19 = (bf16[16,4096]{1,0:T(8,128)(2,1)S(1)}, bf16[16,4096]{1,0:T(8,128)(2,1)S(1)}, u32[]{:S(2)}, u32[]{:S(2)}) collective-permute-start(bf16[16,4096]{1,0:T(8,128)(2,1)S(1)} %get-tuple-element.9), channel_id=1, source_target_pairs={{0,12},{1,13},{2,14},{3,15},{4,0},{5,1},{6,2},{7,3},{8,4},{9,5},{1... | collective-permute-start | bytes 393224 | tf_op jit(solution)/shard_map/ppermute | solution.py:42
  123.1 2.0 %collective-permute-start.20 = (bf16[16,4096]{1,0:T(8,128)(2,1)S(1)}, bf16[16,4096]{1,0:T(8,128)(2,1)S(1)}, u32[]{:S(2)}, u32[]{:S(2)}) collective-permute-start(bf16[16,4096]{1,0:T(8,128)(2,1)S(1)} %get-tuple-element.11), channel_id=1, source_target_pairs={{0,8},{1,9},{2,10},{3,11},{4,12},{5,13},{6,14},{7,15},{8,0},{9,1},... | collective-permute-start | bytes 393224 | tf_op jit(solution)/shard_map/ppermute | solution.py:42
  125.2 2.5 %collective-permute-done.19 = bf16[16,4096]{1,0:T(8,128)(2,1)S(1)} collective-permute-done((bf16[16,4096]{1,0:T(8,128)(2,1)S(1)}, bf16[16,4096]{1,0:T(8,128)(2,1)S(1)}, u32[]{:S(2)}, u32[]{:S(2)}) %collective-permute-start.19) | collective-permute-done | bytes 131104 | tf_op jit(solution)/shard_map/ppermute | solution.py:42
  127.6 8.4 %collective-permute-done.20 = bf16[16,4096]{1,0:T(8,128)(2,1)S(1)} collective-permute-done((bf16[16,4096]{1,0:T(8,128)(2,1)S(1)}, bf16[16,4096]{1,0:T(8,128)(2,1)S(1)}, u32[]{:S(2)}, u32[]{:S(2)}) %collective-permute-start.20) | collective-permute-done | bytes 131104 | tf_op jit(solution)/shard_map/ppermute | solution.py:42
  136.4 0.9 multiply_convert_fusion.1
  (80 shorter events, 2.6 us)
Async XLA Ops:
  0.6 75.2 %copy-start = (bf16[16,64,896]{2,1,0:T(8,128)(2,1)S(1)}, bf16[16,64,896]{2,1,0:T(8,128)(2,1)}, u32[]{:S(2)}) copy-start(bf16[16,64,896]{2,1,0:T(8,128)(2,1)} %param.17) | copy-start | bytes 5505028
  0.6 37.6 %copy-start.5 = (s32[32]{0:T(128)S(1)}, s32[32]{0:T(128)}, u32[]{:S(2)}) copy-start(s32[32]{0:T(128)} %param.20) | copy-start | bytes 388
  0.7 37.7 %copy-start.6 = (s32[32]{0:T(128)S(1)}, s32[32]{0:T(128)}, u32[]{:S(2)}) copy-start(s32[32]{0:T(128)} %param.21) | copy-start | bytes 388
  0.7 37.8 %copy-start.8 = (s32[16]{0:T(128)S(1)}, s32[16]{0:T(128)}, u32[]{:S(2)}) copy-start(s32[16]{0:T(128)} %param.18) | copy-start | bytes 196
  0.7 37.8 %copy-start.7 = (s32[16]{0:T(128)S(1)}, s32[16]{0:T(128)}, u32[]{:S(2)}) copy-start(s32[16]{0:T(128)} %param.19) | copy-start | bytes 196
  0.7 12.6 %collective-permute-start = (bf16[16,8192]{1,0:T(8,128)(2,1)}, bf16[16,8192]{1,0:T(8,128)(2,1)S(1)}, u32[]{:S(2)}, u32[]{:S(2)}) collective-permute-start(bf16[16,8192]{1,0:T(8,128)(2,1)} %param.11), channel_id=1, source_target_pairs={{0,4},{1,5},{2,6},{3,7},{4,8},{5,9},{6,10},{7,11},{8,12},{9,13},{1... | collective-permute-start | bytes 786440 | tf_op jit(solution)/shard_map/ppermute | solution.py:22
  3.8 19.9 %collective-permute-start.1 = (bf16[16,8192]{1,0:T(8,128)(2,1)}, bf16[16,8192]{1,0:T(8,128)(2,1)S(1)}, u32[]{:S(2)}, u32[]{:S(2)}) collective-permute-start(bf16[16,8192]{1,0:T(8,128)(2,1)} %param.11), channel_id=1, source_target_pairs={{0,8},{1,9},{2,10},{3,11},{4,12},{5,13},{6,14},{7,15},{8,0},{9,1},... | collective-permute-start | bytes 786440 | tf_op jit(solution)/shard_map/ppermute | solution.py:22
  6.4 18.8 %collective-permute-start.2 = (bf16[16,8192]{1,0:T(8,128)(2,1)}, bf16[16,8192]{1,0:T(8,128)(2,1)S(1)}, u32[]{:S(2)}, u32[]{:S(2)}) collective-permute-start(bf16[16,8192]{1,0:T(8,128)(2,1)} %param.11), channel_id=1, source_target_pairs={{0,12},{1,13},{2,14},{3,15},{4,0},{5,1},{6,2},{7,3},{8,4},{9,5},{1... | collective-permute-start | bytes 786440 | tf_op jit(solution)/shard_map/ppermute | solution.py:22
  7.7 20.5 %collective-permute-start.3 = (bf16[16,8192]{1,0:T(8,128)(2,1)}, bf16[16,8192]{1,0:T(8,128)(2,1)S(1)}, u32[]{:S(2)}, u32[]{:S(2)}) collective-permute-start(bf16[16,8192]{1,0:T(8,128)(2,1)} %param.11), channel_id=1, source_target_pairs={{0,2},{1,3},{2,0},{3,1},{4,6},{5,7},{6,4},{7,5},{8,10},{9,11},{10,... | collective-permute-start | bytes 786440 | tf_op jit(solution)/shard_map/ppermute | solution.py:23
  13.3 15.7 %collective-permute-start.4 = (bf16[16,8192]{1,0:T(8,128)(2,1)S(1)}, bf16[16,8192]{1,0:T(8,128)(2,1)S(1)}, u32[]{:S(2)}, u32[]{:S(2)}) collective-permute-start(bf16[16,8192]{1,0:T(8,128)(2,1)S(1)} %collective-permute-done), channel_id=1, source_target_pairs={{0,2},{1,3},{2,0},{3,1},{4,6},{5,7},{6,4},{7,5},{8,10},{9,11},{10,... | collective-permute-start | bytes 786440 | tf_op jit(solution)/shard_map/ppermute | solution.py:23
  23.7 9.2 %collective-permute-start.5 = (bf16[16,8192]{1,0:T(8,128)(2,1)S(1)}, bf16[16,8192]{1,0:T(8,128)(2,1)S(1)}, u32[]{:S(2)}, u32[]{:S(2)}) collective-permute-start(bf16[16,8192]{1,0:T(8,128)(2,1)S(1)} %collective-permute-done.1), channel_id=1, source_target_pairs={{0,2},{1,3},{2,0},{3,1},{4,6},{5,7},{6,4},{7,5},{8,10},{9,11},{10,... | collective-permute-start | bytes 786440 | tf_op jit(solution)/shard_map/ppermute | solution.py:23
  25.2 12.2 %collective-permute-start.6 = (bf16[16,8192]{1,0:T(8,128)(2,1)S(1)}, bf16[16,8192]{1,0:T(8,128)(2,1)S(1)}, u32[]{:S(2)}, u32[]{:S(2)}) collective-permute-start(bf16[16,8192]{1,0:T(8,128)(2,1)S(1)} %collective-permute-done.2), channel_id=1, source_target_pairs={{0,2},{1,3},{2,0},{3,1},{4,6},{5,7},{6,4},{7,5},{8,10},{9,11},{10,... | collective-permute-start | bytes 786440 | tf_op jit(solution)/shard_map/ppermute | solution.py:23
  27.3 18.5 %copy-start.3 = (bf16[1,8192,64]{1,2,0:T(8,128)(2,1)S(1)}, bf16[1,8192,64]{1,2,0:T(8,128)(2,1)}, u32[]{:S(2)}) copy-start(bf16[1,8192,64]{1,2,0:T(8,128)(2,1)} %param.16) | copy-start | bytes 3145732
  38.3 4.5 %collective-permute-start.7 = (bf16[128,8192]{1,0:T(8,128)(2,1)}, bf16[128,8192]{1,0:T(8,128)(2,1)}, u32[]{:S(2)}, u32[]{:S(2)}) collective-permute-start(bf16[128,8192]{1,0:T(8,128)(2,1)} %get-tuple-element.12), channel_id=1, source_target_pairs={{0,1},{1,0},{2,3},{3,2},{4,5},{5,4},{6,7},{7,6},{8,9},{9,8},{10,11... | collective-permute-start | bytes 6291464 | tf_op jit(solution)/shard_map/ppermute | solution.py:25
  49.4 1.3 collective-permute-start.8
  50.7 4.0 %collective-permute-start.9 = (bf16[256,64]{0,1:T(8,128)(2,1)S(1)}, bf16[256,64]{0,1:T(8,128)(2,1)S(1)}, u32[]{:S(2)}, u32[]{:S(2)}) collective-permute-start(bf16[256,64]{0,1:T(8,128)(2,1)S(1)} %maximum_add_fusion.1), channel_id=1, source_target_pairs={{0,2},{1,3},{2,0},{3,1},{4,6},{5,7},{6,4},{7,5},{8,10},{9,11},{10,... | collective-permute-start | bytes 98312 | tf_op jit(solution)/shard_map/ppermute | solution.py:64
  55.2 8.0 %collective-permute-start.10 = (bf16[256,64]{0,1:T(8,128)(2,1)S(1)}, bf16[256,64]{0,1:T(8,128)(2,1)S(1)}, u32[]{:S(2)}, u32[]{:S(2)}) collective-permute-start(bf16[256,64]{0,1:T(8,128)(2,1)S(1)} %add.110), channel_id=1, source_target_pairs={{0,12},{1,13},{2,14},{3,15},{4,0},{5,1},{6,2},{7,3},{8,4},{9,5},{1... | collective-permute-start | bytes 98312 | tf_op jit(solution)/shard_map/ppermute | solution.py:67
  63.5 12.0 %collective-permute-start.11 = (bf16[256,64]{0,1:T(8,128)(2,1)S(1)}, bf16[256,64]{0,1:T(8,128)(2,1)S(1)}, u32[]{:S(2)}, u32[]{:S(2)}) collective-permute-start(bf16[256,64]{0,1:T(8,128)(2,1)S(1)} %add.111), channel_id=1, source_target_pairs={{0,8},{1,9},{2,10},{3,11},{4,12},{5,13},{6,14},{7,15},{8,0},{9,1},... | collective-permute-start | bytes 98312 | tf_op jit(solution)/shard_map/ppermute | solution.py:67
  75.8 12.2 %slice-start = ((s8[14680064]{0:T(1024)(128)(4,1)}), s8[4194304]{0:T(1024)(128)(4,1)S(1)}, s32[]{:S(2)}) async-start(s8[14680064]{0:T(1024)(128)(4,1)} %bitcast.26), calls=%async_computation | async-start | bytes 8388608
  76.6 11.5 %slice-start.1 = ((s8[14680064]{0:T(1024)(128)(4,1)}), s8[4194304]{0:T(1024)(128)(4,1)S(1)}, s32[]{:S(2)}) async-start(s8[14680064]{0:T(1024)(128)(4,1)} %bitcast.26), calls=%async_computation.1 | async-start | bytes 8388608
  76.6 11.5 %slice-start.2 = ((s8[14680064]{0:T(1024)(128)(4,1)}), s8[4194304]{0:T(1024)(128)(4,1)S(1)}, s32[]{:S(2)}) async-start(s8[14680064]{0:T(1024)(128)(4,1)} %bitcast.26), calls=%async_computation.2 | async-start | bytes 8388608
  76.6 11.5 %slice-start.3 = ((s8[14680064]{0:T(1024)(128)(4,1)}), s8[2097152]{0:T(1024)(128)(4,1)S(1)}, s32[]{:S(2)}) async-start(s8[14680064]{0:T(1024)(128)(4,1)} %bitcast.26), calls=%async_computation.3 | async-start | bytes 4194304
  90.6 3.2 %copy-start.4 = (bf16[8192]{0:T(1024)(128)(2,1)S(1)}, bf16[8192]{0:T(1024)(128)(2,1)}, u32[]{:S(2)}) copy-start(bf16[8192]{0:T(1024)(128)(2,1)} %param.15) | copy-start | bytes 49156
  90.6 3.2 %collective-permute-start.12 = (bf16[128,4096]{1,0:T(8,128)(2,1)S(1)}, bf16[128,4096]{1,0:T(8,128)(2,1)S(1)}, u32[]{:S(2)}, u32[]{:S(2)}) collective-permute-start(bf16[128,4096]{1,0:T(8,128)(2,1)S(1)} %slice.113), channel_id=1, source_target_pairs={{0,1},{1,0},{2,3},{3,2},{4,5},{5,4},{6,7},{7,6},{8,9},{9,8},{10,11... | collective-permute-start | bytes 3145736 | tf_op jit(solution)/shard_map/ppermute | solution.py:37
  93.2 2.8 %collective-permute-start.17 = (bf16[128,4096]{1,0:T(8,128)(2,1)S(1)}, bf16[128,4096]{1,0:T(8,128)(2,1)S(1)}, u32[]{:S(2)}, u32[]{:S(2)}) collective-permute-start(bf16[128,4096]{1,0:T(8,128)(2,1)S(1)} %slice.121), channel_id=1, source_target_pairs={{0,1},{1,0},{2,3},{3,2},{4,5},{5,4},{6,7},{7,6},{8,9},{9,8},{10,11... | collective-permute-start | bytes 3145736 | tf_op jit(solution)/shard_map/ppermute | solution.py:37
  94.1 14.8 %collective-permute-start.13 = (bf16[64,4096]{1,0:T(8,128)(2,1)S(1)}, bf16[64,4096]{1,0:T(8,128)(2,1)S(1)}, u32[]{:S(2)}, u32[]{:S(2)}) collective-permute-start(bf16[64,4096]{1,0:T(8,128)(2,1)S(1)} %slice.115), channel_id=1, source_target_pairs={{0,2},{1,3},{2,0},{3,1},{4,6},{5,7},{6,4},{7,5},{8,10},{9,11},{10,... | collective-permute-start | bytes 1572872 | tf_op jit(solution)/shard_map/ppermute | solution.py:38
  96.3 39.8 %copy-start.2 = (bf16[16,8192]{1,0:T(8,128)(2,1)S(1)}, bf16[16,8192]{1,0:T(8,128)(2,1)}, u32[]{:S(2)}) copy-start(bf16[16,8192]{1,0:T(8,128)(2,1)} %param.11) | copy-start | bytes 786436
  96.3 40.9 %copy-start.1 = (bf16[16,64,896]{2,1,0:T(8,128)(2,1)S(1)}, bf16[16,64,896]{2,1,0:T(8,128)(2,1)}, u32[]{:S(2)}) copy-start(bf16[16,64,896]{2,1,0:T(8,128)(2,1)} %param.17) | copy-start | bytes 5505028
  96.4 22.9 %collective-permute-start.18 = (bf16[64,4096]{1,0:T(8,128)(2,1)S(1)}, bf16[64,4096]{1,0:T(8,128)(2,1)S(1)}, u32[]{:S(2)}, u32[]{:S(2)}) collective-permute-start(bf16[64,4096]{1,0:T(8,128)(2,1)S(1)} %slice.123), channel_id=1, source_target_pairs={{0,2},{1,3},{2,0},{3,1},{4,6},{5,7},{6,4},{7,5},{8,10},{9,11},{10,... | collective-permute-start | bytes 1572872 | tf_op jit(solution)/shard_map/ppermute | solution.py:38
  109.1 16.0 %collective-permute-start.14 = (bf16[16,4096]{1,0:T(8,128)(2,1)S(1)}, bf16[16,4096]{1,0:T(8,128)(2,1)S(1)}, u32[]{:S(2)}, u32[]{:S(2)}) collective-permute-start(bf16[16,4096]{1,0:T(8,128)(2,1)S(1)} %get-tuple-element.6), channel_id=1, source_target_pairs={{0,12},{1,13},{2,14},{3,15},{4,0},{5,1},{6,2},{7,3},{8,4},{9,5},{1... | collective-permute-start | bytes 393224 | tf_op jit(solution)/shard_map/ppermute | solution.py:42
  112.8 12.3 %collective-permute-start.15 = (bf16[16,4096]{1,0:T(8,128)(2,1)S(1)}, bf16[16,4096]{1,0:T(8,128)(2,1)S(1)}, u32[]{:S(2)}, u32[]{:S(2)}) collective-permute-start(bf16[16,4096]{1,0:T(8,128)(2,1)S(1)} %get-tuple-element.8), channel_id=1, source_target_pairs={{0,8},{1,9},{2,10},{3,11},{4,12},{5,13},{6,14},{7,15},{8,0},{9,1},... | collective-permute-start | bytes 393224 | tf_op jit(solution)/shard_map/ppermute | solution.py:42
  114.8 10.3 %collective-permute-start.16 = (bf16[16,4096]{1,0:T(8,128)(2,1)S(1)}, bf16[16,4096]{1,0:T(8,128)(2,1)S(1)}, u32[]{:S(2)}, u32[]{:S(2)}) collective-permute-start(bf16[16,4096]{1,0:T(8,128)(2,1)S(1)} %get-tuple-element.7), channel_id=1, source_target_pairs={{0,4},{1,5},{2,6},{3,7},{4,8},{5,9},{6,10},{7,11},{8,12},{9,13},{1... | collective-permute-start | bytes 393224 | tf_op jit(solution)/shard_map/ppermute | solution.py:42
  119.4 8.2 %collective-permute-start.19 = (bf16[16,4096]{1,0:T(8,128)(2,1)S(1)}, bf16[16,4096]{1,0:T(8,128)(2,1)S(1)}, u32[]{:S(2)}, u32[]{:S(2)}) collective-permute-start(bf16[16,4096]{1,0:T(8,128)(2,1)S(1)} %get-tuple-element.9), channel_id=1, source_target_pairs={{0,12},{1,13},{2,14},{3,15},{4,0},{5,1},{6,2},{7,3},{8,4},{9,5},{1... | collective-permute-start | bytes 393224 | tf_op jit(solution)/shard_map/ppermute | solution.py:42
  123.1 13.0 %collective-permute-start.20 = (bf16[16,4096]{1,0:T(8,128)(2,1)S(1)}, bf16[16,4096]{1,0:T(8,128)(2,1)S(1)}, u32[]{:S(2)}, u32[]{:S(2)}) collective-permute-start(bf16[16,4096]{1,0:T(8,128)(2,1)S(1)} %get-tuple-element.11), channel_id=1, source_target_pairs={{0,8},{1,9},{2,10},{3,11},{4,12},{5,13},{6,14},{7,15},{8,0},{9,1},... | collective-permute-start | bytes 393224 | tf_op jit(solution)/shard_map/ppermute | solution.py:42
  125.1 11.0 %collective-permute-start.21 = (bf16[16,4096]{1,0:T(8,128)(2,1)S(1)}, bf16[16,4096]{1,0:T(8,128)(2,1)S(1)}, u32[]{:S(2)}, u32[]{:S(2)}) collective-permute-start(bf16[16,4096]{1,0:T(8,128)(2,1)S(1)} %get-tuple-element.10), channel_id=1, source_target_pairs={{0,4},{1,5},{2,6},{3,7},{4,8},{5,9},{6,10},{7,11},{8,12},{9,13},{1... | collective-permute-start | bytes 393224 | tf_op jit(solution)/shard_map/ppermute | solution.py:42

commit v2 on v0

v2 whole, which is shorter than its diff:
```python
import functools

import jax
import jax.numpy as jnp
from jax import lax
from jax.experimental import pallas as pl
from jax.experimental.pallas import tpu as pltpu
from jax.sharding import PartitionSpec as P

adapter_alpha = 32.0
AXIS = "mp"
HALVES = 2
VMEM_LIMIT = 32 * 1024 * 1024


def chip_at(place, chips):
    if chips == 8:
        return jnp.where(place < 4, 2 * place, 2 * (7 - place) + 1)
    return place


def place_of(chip, chips):
    if chips == 8:
        return jnp.where((chip & 1) == 0, chip >> 1, 7 - (chip >> 1))
    return chip


def ring(size, by):
    chips = size // 2
    order = [0, 2, 4, 6, 7, 5, 3, 1] if chips == 8 else list(range(chips))
    pairs = []
    for place, chip in enumerate(order):
        to = order[(place + by) % chips]
        pairs += [(2 * chip + core, 2 * to + core) for core in range(2)]
    return pairs


def flip(size, bit):
    return [(i, i ^ bit) for i in range(size)]


def row_positions(me, row, own_rows, size):
    chips = size // 2
    block = row // own_rows
    index = block & (chips - 1)
    step = (index + 1) >> 1
    delta = jnp.where((index & 1) == 1, step, -step)
    place = (place_of(me >> 1, chips) - delta + chips) & (chips - 1)
    core = (me & 1) ^ (block // chips)
    return (2 * chip_at(place, chips) + core) * own_rows + (row & (own_rows - 1))


def pick(index, table):
    hot = index == lax.broadcasted_iota(jnp.int32, (1, table.shape[1]), 1)
    return jnp.sum(jnp.where(hot, table, 0), axis=1, keepdims=True)


def row_adapters(position, start, adapters):
    segment = jnp.sum((start <= position).astype(jnp.int32), axis=1, keepdims=True) - 1
    return pick(segment, adapters)


def whole(space=pltpu.VMEM):
    return pl.BlockSpec(memory_space=space)


def join(right, left):
    rows, width = right[0].shape
    pieces = right + left
    out_rows = rows * len(pieces) // HALVES

    def kernel(*refs):
        out = refs[-1]
        for i, ref in enumerate(refs[:-1]):
            at = (i // HALVES * rows, i % HALVES * width)
            out[at[0] : at[0] + rows, at[1] : at[1] + width] = ref[...]

    return pl.pallas_call(
        kernel,
        out_shape=jax.ShapeDtypeStruct((out_rows, HALVES * width), right[0].dtype),
        in_specs=[whole()] * len(pieces),
        out_specs=whole(),
        compiler_params=pltpu.CompilerParams(vmem_limit_bytes=VMEM_LIMIT),
        name="join_pieces",
    )(*pieces)


def gather_rows(own, size):
    chips = size // 2
    width = own.shape[1] // HALVES
    halves = [own[:, h * width : (h + 1) * width] for h in range(HALVES)]
    right, left = list(halves), list(halves)
    mine = [own]
    theirs = [lax.ppermute(own, AXIS, flip(size, 1))]
    for step in range(1, chips // 2 + 1):
        if step < chips // 2:
            for h in range(HALVES):
                right[h] = lax.ppermute(right[h], AXIS, ring(size, 1))
                left[h] = lax.ppermute(left[h], AXIS, ring(size, -1))
            part = join(right, left)
        else:
            part = join(
                [
                    lax.ppermute(right[0], AXIS, ring(size, 1)),
                    lax.ppermute(left[1], AXIS, ring(size, -1)),
                ],
                [],
            )
        mine.append(part)
        theirs.append(lax.ppermute(part, AXIS, flip(size, 1)))
    return mine + theirs


def shrink_kernel(own_rows, size, steps, count, *refs):
    me_ref, start, adapters, ranks, slots = refs[:5]
    parts = refs[5 : 5 + count]
    factor, rows_out, coeff_out, total = refs[5 + count :]
    k = pl.program_id(0)
    at = 0
    for part in parts:
        rows_out[at : at + part.shape[0], :] = part[...]
        at += part.shape[0]

    @pl.when(k == 0)
    def _():
        total[...] = jnp.zeros_like(total)

    total[...] += lax.dot_general(
        rows_out[...], factor[...], (((1,), (1,)), ((), ())), preferred_element_type=jnp.float32
    )

    @pl.when(k == steps - 1)
    def _():
        me = me_ref[0]
        batch_rows = total.shape[0]
        rank_limit = coeff_out.shape[1]
        held = total.shape[1] // rank_limit
        row = lax.broadcasted_iota(jnp.int32, (batch_rows, 1), 0)
        adapter = row_adapters(row_positions(me, row, own_rows, size), start[...], adapters[...])
        rank = pick(adapter, ranks[...])
        slot = pick(adapter, slots[...]) - me * held
        shrink = jnp.zeros((batch_rows, rank_limit), jnp.float32)
        for s in range(held):
            shrink = jnp.where(
                slot == s, total[:, s * rank_limit : (s + 1) * rank_limit], shrink
            )
        keep = lax.broadcasted_iota(jnp.int32, (1, rank_limit), 1) < rank
        coeff = jnp.where(keep, shrink * (adapter_alpha / rank.astype(jnp.float32)), 0.0)
        column = lax.broadcasted_iota(jnp.int32, (1, batch_rows), 1)
        place = row_positions(me, column, own_rows, size)
        to_place = (place == row).astype(jnp.bfloat16)
        coeff_out[...] = jnp.dot(
            to_place, coeff.astype(jnp.bfloat16), preferred_element_type=jnp.float32
        ).astype(jnp.bfloat16)


def shrink_rows(parts, shrink_factors, tables, me, own_rows, size):
    slots, model_width, rank_limit = shrink_factors.shape
    factor = jnp.swapaxes(shrink_factors, 1, 2).reshape(slots * rank_limit, model_width)
    steps = 8
    width = model_width // steps
    batch_rows = own_rows * size

    def columns(rows):
        return pl.BlockSpec((rows, width), lambda k: (0, k))

    return pl.pallas_call(
        functools.partial(shrink_kernel, own_rows, size, steps, len(parts)),
        out_shape=(
            jax.ShapeDtypeStruct((batch_rows, model_width), jnp.bfloat16),
            jax.ShapeDtypeStruct((batch_rows, rank_limit), jnp.bfloat16),
        ),
        grid=(steps,),
        in_specs=[whole(pltpu.SMEM)]
        + [pl.BlockSpec(table.shape, lambda k: (0, 0)) for table in tables]
        + [columns(part.shape[0]) for part in parts]
        + [columns(slots * rank_limit)],
        out_specs=(columns(batch_rows), pl.BlockSpec((batch_rows, rank_limit), lambda k: (0, 0))),
        scratch_shapes=[pltpu.VMEM((batch_rows, slots * rank_limit), jnp.float32)],
        compiler_params=pltpu.CompilerParams(vmem_limit_bytes=VMEM_LIMIT),
        cost_estimate=pl.CostEstimate(
            flops=2 * batch_rows * model_width * slots * rank_limit,
            bytes_accessed=4 * batch_rows * model_width,
            transcendentals=0,
        ),
        name="shrink_rows",
    )(me, *tables, *parts, factor)


def matmul_kernel(rows, weight, out):
    @pl.when(pl.program_id(0) == 0)
    def _():
        out[...] = jnp.zeros_like(out)

    out[...] += jnp.dot(rows[...], weight[...], preferred_element_type=jnp.float32)


def matmul(rows, weight, name):
    batch_rows, depth = rows.shape
    width = weight.shape[1]
    steps = 8
    return pl.pallas_call(
        matmul_kernel,
        out_shape=jax.ShapeDtypeStruct((batch_rows, width), jnp.float32),
        grid=(steps,),
        in_specs=[
            pl.BlockSpec((batch_rows, depth // steps), lambda k: (0, k)),
            pl.BlockSpec((depth // steps, width), lambda k: (k, 0)),
        ],
        out_specs=pl.BlockSpec((batch_rows, width), lambda k: (0, 0)),
        compiler_params=pltpu.CompilerParams(vmem_limit_bytes=VMEM_LIMIT),
        cost_estimate=pl.CostEstimate(
            flops=2 * batch_rows * depth * width,
            bytes_accessed=2 * depth * width,
            transcendentals=0,
        ),
        name=name,
    )(rows, weight)


def hidden_kernel(
    own_rows, size, me_ref, start, adapters, coeff, expand, gate, up, out, spread
):
    me = me_ref[0]
    batch_rows, rank_limit = coeff.shape
    row = lax.broadcasted_iota(jnp.int32, (batch_rows, 1), 0)
    position = row_positions(me, row, own_rows, size)
    adapter = row_adapters(position, start[...], adapters[...])
    from_place = position == lax.broadcasted_iota(jnp.int32, (1, batch_rows), 1)
    own = jnp.dot(
        from_place.astype(jnp.bfloat16), coeff[...], preferred_element_type=jnp.float32
    )
    pair = jnp.concatenate([own, own], axis=1)
    second = lax.broadcasted_iota(jnp.int32, (1, 2 * rank_limit), 1) // rank_limit
    for p in range(spread.shape[1] // (2 * rank_limit)):
        spread[:, p * 2 * rank_limit : (p + 1) * 2 * rank_limit] = jnp.where(
            adapter == second + 2 * p, pair, 0.0
        ).astype(jnp.bfloat16)
    lora = jnp.dot(spread[...], expand[...], preferred_element_type=jnp.float32)
    value = gate[...]
    out[...] = (value / (1.0 + jnp.exp(-value)) * (up[...] + lora)).astype(jnp.bfloat16)


def hidden_rows(gate, up, coeff, expand_factors, tables, me, own_rows, size):
    adapters, rank_limit, width = expand_factors.shape
    batch_rows = gate.shape[0]
    return pl.pallas_call(
        functools.partial(hidden_kernel, own_rows, size),
        out_shape=jax.ShapeDtypeStruct((batch_rows, width), jnp.bfloat16),
        in_specs=[whole(pltpu.SMEM)] + [whole()] * 6,
        out_specs=whole(),
        scratch_shapes=[pltpu.VMEM((batch_rows, adapters * rank_limit), jnp.bfloat16)],
        compiler_params=pltpu.CompilerParams(vmem_limit_bytes=VMEM_LIMIT),
        cost_estimate=pl.CostEstimate(
            flops=2 * batch_rows * adapters * rank_limit * width,
            bytes_accessed=2 * adapters * rank_limit * width,
            transcendentals=batch_rows * width,
        ),
        name="hidden_rows",
    )(
        me,
        *tables,
        coeff,
        expand_factors.reshape(adapters * rank_limit, width),
        gate,
        up,
    )


def scatter_rows(terms, own_rows, size):
    chips = size // 2
    core_rows = own_rows * chips
    received = [lax.ppermute(term[core_rows:], AXIS, flip(size, 1)) for term in terms]

    def block(h, index):
        rows = slice(index * own_rows, (index + 1) * own_rows)
        return terms[h][rows].astype(jnp.float32) + received[h][rows].astype(jnp.float32)

    def send(value, by):
        return lax.ppermute(value.astype(jnp.bfloat16), AXIS, ring(size, by)).astype(jnp.float32)

    right, left = [None] * HALVES, [None] * HALVES
    opposite = chips - 1
    right[0] = send(block(0, opposite), 1)
    left[1] = send(block(1, opposite), -1)
    for step in range(chips // 2 - 1, 0, -1):
        for h in range(HALVES):
            value = block(h, 2 * step)
            right[h] = send(value if right[h] is None else value + right[h], 1)
            value = block(h, 2 * step - 1)
            left[h] = send(value if left[h] is None else value + left[h], -1)
    return [block(h, 0) + right[h] + left[h] for h in range(HALVES)]


def body(
    activations,
    gate_weight,
    up_weight,
    down_weight,
    norm_gain_vector,
    shrink_factors,
    expand_factors,
    adapter_ranks,
    adapter_storage_slot,
    segment_start,
    segment_adapter,
):
    size = lax.axis_size(AXIS)
    me = lax.axis_index(AXIS).astype(jnp.int32).reshape(1)
    own_rows, model_width = activations.shape
    assert size & (size - 1) == 0 and own_rows & (own_rows - 1) == 0
    rows_tables = (segment_start[None], segment_adapter[None])
    all_tables = rows_tables + (adapter_ranks[None], adapter_storage_slot[None])

    parts = gather_rows(activations, size)
    rows, coeff = shrink_rows(parts, shrink_factors, all_tables, me, own_rows, size)

    bit = 1
    while bit < size:
        coeff = coeff + lax.ppermute(coeff, AXIS, flip(size, bit))
        bit *= 2
    gate = matmul(rows, gate_weight, "gate_rows")
    up = matmul(rows, up_weight, "up_rows")
    hidden = hidden_rows(gate, up, coeff, expand_factors, rows_tables, me, own_rows, size)

    width = model_width // HALVES
    terms = [
        jnp.dot(
            hidden,
            down_weight[:, h * width : (h + 1) * width],
            preferred_element_type=jnp.float32,
        ).astype(jnp.bfloat16)
        for h in range(HALVES)
    ]
    total = jnp.concatenate(scatter_rows(terms, own_rows, size), axis=1)

    stream_sum = activations.astype(jnp.float32) + total
    block_out = stream_sum.astype(jnp.bfloat16)
    scale_rows = lax.rsqrt(jnp.mean(stream_sum * stream_sum, axis=1, keepdims=True) + 1e-05)
    normed = (stream_sum * scale_rows * norm_gain_vector.astype(jnp.float32)[None, :]).astype(
        jnp.bfloat16
    )
    return (block_out, normed)


def solution(mesh):
    return jax.shard_map(
        body,
        mesh=mesh,
        in_specs=(
            P(("groups", "mp"), None),
            P(None, "mp"),
            P(None, "mp"),
            P("mp", None),
            P(),
            P("mp", None, None),
            P(None, None, "mp"),
            P(),
            P(),
            P("groups"),
            P("groups"),
        ),
        out_specs=(P(("groups", "mp"), None), P(("groups", "mp"), None)),
        check_vma=False,
    )
```

time: 265 us -> 124 us (0.47)
  waiting for transfers between devices: 202 us -> 42.8 us
  starting transfers between devices: 0.12 us -> 37.6 us
  matrix products: 38.5 us -> 7.97 us
  Pallas kernels: 0 us -> 20.3 us
  between operations: 13.8 us -> 1.03 us
  local copies, waits for them, and re-layouts: 0.94 us -> 11.7 us
  other arithmetic: 8.93 us -> 1.96 us
    psum x1 -> x0, waiting for transfers between devices: 76.7 us -> none  [body(): summed = lax.psum(wide_terms.astype(jnp.bfloat16), 'mp').astype(jnp.float32)]
    reduce_scatter x1 -> x0, waiting for transfers between devices: 72.3 us -> none  [body(): lax.psum_scatter(jnp.dot(hidden, down_weight, preferred_element_type=jnp....]
    all_gather x1 -> x0, waiting for transfers between devices: 52.5 us -> none  [body(): piece = lax.all_gather(activations, 'mp', axis=0, tiled=True)]
    ppermute x0 -> x39, waiting for transfers between devices: none -> 42.8 us  [the longest x14 22.5 us: send(): lax.ppermute(value.astype(jnp.bfloat16), AXIS, ring(size, by))]
    ppermute x0 -> x39, starting transfers between devices: none -> 37.6 us  [the longest x14 14.4 us: send(): lax.ppermute(value.astype(jnp.bfloat16), AXIS, ring(size, by))]
    dot_general x4 -> x2, matrix products: 38.5 us -> 7.97 us  [body(): jnp.dot(hidden, down_weight[:, h * width:(h + 1) * width], preferred_elem...]
    pallas_call x0 -> x8, Pallas kernels: none -> 20.3 us  [the longest x2 12.4 us: matmul(): pl.pallas_call(matmul_kernel, out_shape=jax.ShapeDtypeStruct((batch_rows,...]
    unnamed x6 -> x28, local copies, waits for them, and re-layouts: 0.7 us -> 10.5 us
  transfers between devices with their start and end apart: 3 -> 39, of which waited for: 3 -> 26; matrix products, arithmetic and copies ran while one was open for 6% -> 3% of each run, Pallas kernels for 0% -> 10%
where the time goes in v2:
time: 124 us; the launch traced here: 123 us
  waiting for transfers between devices  42.8 us (35%)
  starting transfers between devices  37.6 us (30%)
  Pallas kernels  20.3 us (16%)
  local copies, waits for them, and re-layouts  11.7 us (9%)
  matrix products  7.97 us (6%)
  other arithmetic  1.96 us (2%)
    ppermute x14, waiting for transfers between devices, send(): lax.ppermute(value.astype(jnp.bfloat16), AXIS, ring(size, by))  22.5 us
    ppermute x14, starting transfers between devices, send(): lax.ppermute(value.astype(jnp.bfloat16), AXIS, ring(size, by))  14.4 us
    ppermute x6, starting transfers between devices, gather_rows(): left[h] = lax.ppermute(left[h], AXIS, ring(size, -1))  12.9 us
    pallas_call x2, Pallas kernels, matmul(): pl.pallas_call(matmul_kernel, out_shape=jax.ShapeDtypeStruct((batch_rows,...  12.4 us
    unnamed x28, local copies, waits for them, and re-layouts  10.5 us
    dot_general x2, matrix products, body(): jnp.dot(hidden, down_weight[:, h * width:(h + 1) * width], preferred_elem...  7.97 us
    pallas_call x1, Pallas kernels, shrink_rows(): pl.pallas_call(functools.partial(shrink_kernel, own_rows, size, steps, le...  6.48 us
    ppermute x6, waiting for transfers between devices, gather_rows(): left[h] = lax.ppermute(left[h], AXIS, ring(size, -1))  6.4 us
  transfers between devices with their start and end apart: 39, of which 26 were waited for; matrix products, arithmetic and copies ran while one was open for 3% of the time, Pallas kernels for 10%

profile of v2, /device:TPU:0, one launch (start us, length us, event | category | flops | bytes accessed | tf_op | source)
XLA Modules:
  0.0 123.5 jit_solution(6904386996909910757)
XLA Ops:
  0.7 1.1 fusion.11
  1.8 3.0 %collective-permute-start.3 = (bf16[16,4096]{1,0:T(8,128)(2,1)S(1)}, bf16[16,4096]{1,0:T(8,128)(2,1)S(1)}, u32[]{:S(2)}, u32[]{:S(2)}) collective-permute-start(bf16[16,4096]{1,0:T(8,128)(2,1)S(1)} %get-tuple-element.12), channel_id=1, source_target_pairs={{0,2},{1,3},{4,0},{5,1},{8,4},{9,5},{12,8},{13,9},{14,12},{15,13},... | collective-permute-start | bytes 393224 | tf_op jit(solution)/shard_map/ppermute | solution.py:99
  4.9 1.9 %collective-permute-start.2 = (bf16[16,4096]{1,0:T(8,128)(2,1)S(1)}, bf16[16,4096]{1,0:T(8,128)(2,1)S(1)}, u32[]{:S(2)}, u32[]{:S(2)}) collective-permute-start(bf16[16,4096]{1,0:T(8,128)(2,1)S(1)} %get-tuple-element.13), channel_id=1, source_target_pairs={{0,2},{1,3},{4,0},{5,1},{8,4},{9,5},{12,8},{13,9},{14,12},{15,13},... | collective-permute-start | bytes 393224 | tf_op jit(solution)/shard_map/ppermute | solution.py:99
  6.9 2.2 %collective-permute-done.3.refs_3_ = bf16[16,4096]{1,0:T(8,128)(2,1)S(1)} collective-permute-done((bf16[16,4096]{1,0:T(8,128)(2,1)S(1)}, bf16[16,4096]{1,0:T(8,128)(2,1)S(1)}, u32[]{:S(2)}, u32[]{:S(2)}) %collective-permute-start.3) | collective-permute-done | bytes 131104 | tf_op jit(solution)/shard_map/ppermute | solution.py:99
  9.2 2.0 %collective-permute-start.7 = (bf16[16,4096]{1,0:T(8,128)(2,1)S(1)}, bf16[16,4096]{1,0:T(8,128)(2,1)S(1)}, u32[]{:S(2)}, u32[]{:S(2)}) collective-permute-start(bf16[16,4096]{1,0:T(8,128)(2,1)S(1)} %collective-permute-done.3.refs_3_), channel_id=1, source_target_pairs={{0,2},{1,3},{4,0},{5,1},{8,4},{9,5},{12,8},{13,9},{14,12},{15,13},... | collective-permute-start | bytes 393224 | tf_op jit(solution)/shard_map/ppermute | solution.py:99
  12.0 2.0 %collective-permute-start.6 = (bf16[16,4096]{1,0:T(8,128)(2,1)S(1)}, bf16[16,4096]{1,0:T(8,128)(2,1)S(1)}, u32[]{:S(2)}, u32[]{:S(2)}) collective-permute-start(bf16[16,4096]{1,0:T(8,128)(2,1)S(1)} %collective-permute-done.2.refs_2_), channel_id=1, source_target_pairs={{0,2},{1,3},{4,0},{5,1},{8,4},{9,5},{12,8},{13,9},{14,12},{15,13},... | collective-permute-start | bytes 393224 | tf_op jit(solution)/shard_map/ppermute | solution.py:99
  14.1 1.3 %collective-permute-done.7.refs_3_ = bf16[16,4096]{1,0:T(8,128)(2,1)S(1)} collective-permute-done((bf16[16,4096]{1,0:T(8,128)(2,1)S(1)}, bf16[16,4096]{1,0:T(8,128)(2,1)S(1)}, u32[]{:S(2)}, u32[]{:S(2)}) %collective-permute-start.7) | collective-permute-done | bytes 131104 | tf_op jit(solution)/shard_map/ppermute | solution.py:99
  15.3 2.1 %collective-permute-start.11 = (bf16[16,4096]{1,0:T(8,128)(2,1)S(1)}, bf16[16,4096]{1,0:T(8,128)(2,1)S(1)}, u32[]{:S(2)}, u32[]{:S(2)}) collective-permute-start(bf16[16,4096]{1,0:T(8,128)(2,1)S(1)} %collective-permute-done.7.refs_3_), channel_id=1, source_target_pairs={{0,2},{1,3},{4,0},{5,1},{8,4},{9,5},{12,8},{13,9},{14,12},{15,13},... | collective-permute-start | bytes 393224 | tf_op jit(solution)/shard_map/ppermute | solution.py:99
  17.7 0.8 collective-permute-done.6.refs_2_
  18.5 1.9 %collective-permute-start.10 = (bf16[16,4096]{1,0:T(8,128)(2,1)S(1)}, bf16[16,4096]{1,0:T(8,128)(2,1)S(1)}, u32[]{:S(2)}, u32[]{:S(2)}) collective-permute-start(bf16[16,4096]{1,0:T(8,128)(2,1)S(1)} %collective-permute-done.6.refs_2_), channel_id=1, source_target_pairs={{0,2},{1,3},{4,0},{5,1},{8,4},{9,5},{12,8},{13,9},{14,12},{15,13},... | collective-permute-start | bytes 393224 | tf_op jit(solution)/shard_map/ppermute | solution.py:99
  21.2 1.3 %collective-permute-done.8.refs_0_ = bf16[16,4096]{1,0:T(8,128)(2,1)S(1)} collective-permute-done((bf16[16,4096]{1,0:T(8,128)(2,1)S(1)}, bf16[16,4096]{1,0:T(8,128)(2,1)S(1)}, u32[]{:S(2)}, u32[]{:S(2)}) %collective-permute-start.8) | collective-permute-done | bytes 131104 | tf_op jit(solution)/shard_map/ppermute | solution.py:98
  22.5 0.9 collective-permute-done.10.refs_2_
  23.4 1.9 %collective-permute-done.9.refs_1_ = bf16[16,4096]{1,0:T(8,128)(2,1)S(1)} collective-permute-done((bf16[16,4096]{1,0:T(8,128)(2,1)S(1)}, bf16[16,4096]{1,0:T(8,128)(2,1)S(1)}, u32[]{:S(2)}, u32[]{:S(2)}) %collective-permute-start.9) | collective-permute-done | bytes 131104 | tf_op jit(solution)/shard_map/ppermute | solution.py:98
  25.6 1.9 %collective-permute-start.13 = (bf16[16,4096]{1,0:T(8,128)(2,1)S(1)}, bf16[16,4096]{1,0:T(8,128)(2,1)S(1)}, u32[]{:S(2)}, u32[]{:S(2)}) collective-permute-start(bf16[16,4096]{1,0:T(8,128)(2,1)S(1)} %collective-permute-done.11.refs_3_), channel_id=1, source_target_pairs={{0,2},{1,3},{4,0},{5,1},{8,4},{9,5},{12,8},{13,9},{14,12},{15,13},... | collective-permute-start | bytes 393224 | tf_op jit(solution)/shard_map/ppermute | solution.py:105
  27.5 3.8 %collective-permute-done.12.refs_0_ = bf16[16,4096]{1,0:T(8,128)(2,1)S(1)} collective-permute-done((bf16[16,4096]{1,0:T(8,128)(2,1)S(1)}, bf16[16,4096]{1,0:T(8,128)(2,1)S(1)}, u32[]{:S(2)}, u32[]{:S(2)}) %collective-permute-start.12) | collective-permute-done | bytes 131104 | tf_op jit(solution)/shard_map/ppermute | solution.py:104
  31.9 0.9 collective-permute-done.14.refs_10_
  33.4 6.5 %shrink_rows.1 = (bf16[256,8192]{1,0:T(8,128)(2,1)S(1)}, bf16[256,64]{1,0:T(8,128)(2,1)S(1)}) custom-call(s32[1]{0:T(128)} %bitcast.refs_0_.me_ref, s32[1,32]{1,0:T(1,128)S(1)} %bitcast.13, s32[1,32]{1,0:T(1,128)S(1)} %bitcast.15, s32[1,16]{1,0:T(1,128)S(1)} %bitcast.17, s32[1,16]{1,0:T(1,128)S(1)} %bitcast.18, bf16[16,8192]{1,0:T(8,128)(2,1)S(1)} %copy-done.2, ...), custom_call_target="tpu_custom_call" | custom-call | flops 268435456 | bytes 8388608 | tf_op jit(solution)/shard_map/shrink_rows/pallas_call | solution.py:167
  40.2 1.0 collective-permute-done.19
  41.2 1.7 %collective-permute-start.20 = (bf16[256,64]{1,0:T(8,128)(2,1)S(1)}, bf16[256,64]{1,0:T(8,128)(2,1)S(1)}, u32[]{:S(2)}, u32[]{:S(2)}) collective-permute-start(bf16[256,64]{1,0:T(8,128)(2,1)S(1)} %add.113), channel_id=1, source_target_pairs={{0,2},{1,3},{2,0},{3,1},{4,6},{5,7},{6,4},{7,5},{8,10},{9,11},{10,... | collective-permute-start | bytes 98312 | tf_op jit(solution)/shard_map/ppermute | solution.py:320
  42.9 2.7 %collective-permute-done.20 = bf16[256,64]{1,0:T(8,128)(2,1)S(1)} collective-permute-done((bf16[256,64]{1,0:T(8,128)(2,1)S(1)}, bf16[256,64]{1,0:T(8,128)(2,1)S(1)}, u32[]{:S(2)}, u32[]{:S(2)}) %collective-permute-start.20) | collective-permute-done | bytes 32800 | tf_op jit(solution)/shard_map/ppermute | solution.py:320
  45.6 1.7 %collective-permute-start.21 = (bf16[256,64]{1,0:T(8,128)(2,1)S(1)}, bf16[256,64]{1,0:T(8,128)(2,1)S(1)}, u32[]{:S(2)}, u32[]{:S(2)}) collective-permute-start(bf16[256,64]{1,0:T(8,128)(2,1)S(1)} %add.114), channel_id=1, source_target_pairs={{0,4},{1,5},{2,6},{3,7},{4,0},{5,1},{6,2},{7,3},{8,12},{9,13},{10,... | collective-permute-start | bytes 98312 | tf_op jit(solution)/shard_map/ppermute | solution.py:320
  47.3 5.2 %copy-done = bf16[8192,896]{1,0:T(8,128)(2,1)S(1)} copy-done((bf16[8192,896]{1,0:T(8,128)(2,1)S(1)}, bf16[8192,896]{1,0:T(8,128)(2,1)}, u32[]{:S(2)}) %copy-start) | copy-done | bytes 14680088
  52.4 6.2 %gate_rows.1.gate = f32[256,896]{1,0:T(8,128)S(1)} custom-call(bf16[256,8192]{1,0:T(8,128)(2,1)S(1)} %get-tuple-element.5.rows, bf16[8192,896]{1,0:T(8,128)(2,1)S(1)} %copy-done), custom_call_target="tpu_custom_call" | custom-call | flops 3758096384 | bytes 14680064 | tf_op jit(solution)/shard_map/gate_rows/pallas_call | solution.py:202
  58.7 2.6 %collective-permute-start.22 = (bf16[256,64]{1,0:T(8,128)(2,1)S(1)}, bf16[256,64]{1,0:T(8,128)(2,1)S(1)}, u32[]{:S(2)}, u32[]{:S(2)}) collective-permute-start(bf16[256,64]{1,0:T(8,128)(2,1)S(1)} %add.115), channel_id=1, source_target_pairs={{0,8},{1,9},{2,10},{3,11},{4,12},{5,13},{6,14},{7,15},{8,0},{9,1},... | collective-permute-start | bytes 98312 | tf_op jit(solution)/shard_map/ppermute | solution.py:320
  61.3 5.2 %copy-done.1 = bf16[8192,896]{1,0:T(8,128)(2,1)S(1)} copy-done((bf16[8192,896]{1,0:T(8,128)(2,1)S(1)}, bf16[8192,896]{1,0:T(8,128)(2,1)}, u32[]{:S(2)}) %copy-start.1) | copy-done | bytes 14680088
  66.5 6.2 %up_rows.1.up = f32[256,896]{1,0:T(8,128)S(1)} custom-call(bf16[256,8192]{1,0:T(8,128)(2,1)S(1)} %get-tuple-element.5.rows, bf16[8192,896]{1,0:T(8,128)(2,1)S(1)} %copy-done.1), custom_call_target="tpu_custom_call" | custom-call | flops 3758096384 | bytes 14680064 | tf_op jit(solution)/shard_map/up_rows/pallas_call | solution.py:202
  72.8 1.2 %hidden_rows.1 = bf16[256,896]{1,0:T(8,128)(2,1)S(1)} custom-call(s32[1]{0:T(128)} %bitcast.refs_0_.me_ref, s32[1,32]{1,0:T(1,128)S(1)} %bitcast.14, s32[1,32]{1,0:T(1,128)S(1)} %bitcast.16, bf16[256,64]{1,0:T(8,128)(2,1)S(1)} %add.116.coeff, bf16[1024,896]{1,0:T(8,128)(2,1)S(1)} %bitcast.11, f32[256,896]{1,0:T(8,128)S(1)} %gate_rows.1.gate, ...), custom_call_target="tpu_custom_call" | custom-call | flops 469762048 | bytes 1835008 | tf_op jit(solution)/shard_map/hidden_rows/pallas_call | solution.py:247
  74.0 5.6 %fusion.4 = bf16[256,4096]{1,0:T(8,128)(2,1)S(1)} fusion(bf16[256,896]{1,0:T(8,128)(2,1)S(1)} %hidden_rows.1, bf16[896,8192]{1,0:T(8,128)(2,1)} %param.14), kind=kOutput, calls=%fused_computation.4 | convolution fusion | flops 1880096768 | bytes 9895936 | tf_op jit(solution)/shard_map/dot_general | solution.py:328
  79.9 2.3 %fusion.7 = bf16[256,4096]{1,0:T(8,128)(2,1)S(1)} fusion(bf16[256,896]{1,0:T(8,128)(2,1)S(1)} %hidden_rows.1, bf16[896,8192]{1,0:T(8,128)(2,1)S(1)} %bitcast.20), kind=kOutput, calls=%fused_computation.5 | convolution fusion | flops 1880096768 | bytes 9895936 | tf_op jit(solution)/shard_map/dot_general | solution.py:328
  83.5 1.6 %collective-permute-done.31 = bf16[128,4096]{1,0:T(8,128)(2,1)S(1)} collective-permute-done((bf16[128,4096]{1,0:T(8,128)(2,1)S(1)}, bf16[128,4096]{1,0:T(8,128)(2,1)S(1)}, u32[]{:S(2)}, u32[]{:S(2)}) %collective-permute-start.31) | collective-permute-done | bytes 1048608 | tf_op jit(solution)/shard_map/ppermute | solution.py:273
  85.7 3.6 %collective-permute-done.24 = bf16[16,4096]{1,0:T(8,128)(2,1)S(1)} collective-permute-done((bf16[16,4096]{1,0:T(8,128)(2,1)S(1)}, bf16[16,4096]{1,0:T(8,128)(2,1)S(1)}, u32[]{:S(2)}, u32[]{:S(2)}) %collective-permute-start.24) | collective-permute-done | bytes 131104 | tf_op jit(solution)/shard_map/ppermute | solution.py:280
  89.9 2.2 %collective-permute-done.32 = bf16[16,4096]{1,0:T(8,128)(2,1)S(1)} collective-permute-done((bf16[16,4096]{1,0:T(8,128)(2,1)S(1)}, bf16[16,4096]{1,0:T(8,128)(2,1)S(1)}, u32[]{:S(2)}, u32[]{:S(2)}) %collective-permute-start.32) | collective-permute-done | bytes 131104 | tf_op jit(solution)/shard_map/ppermute | solution.py:280
  92.7 2.3 %collective-permute-done.25 = bf16[16,4096]{1,0:T(8,128)(2,1)S(1)} collective-permute-done((bf16[16,4096]{1,0:T(8,128)(2,1)S(1)}, bf16[16,4096]{1,0:T(8,128)(2,1)S(1)}, u32[]{:S(2)}, u32[]{:S(2)}) %collective-permute-start.25) | collective-permute-done | bytes 131104 | tf_op jit(solution)/shard_map/ppermute | solution.py:280
  95.5 3.1 %collective-permute-done.33 = bf16[16,4096]{1,0:T(8,128)(2,1)S(1)} collective-permute-done((bf16[16,4096]{1,0:T(8,128)(2,1)S(1)}, bf16[16,4096]{1,0:T(8,128)(2,1)S(1)}, u32[]{:S(2)}, u32[]{:S(2)}) %collective-permute-start.33) | collective-permute-done | bytes 131104 | tf_op jit(solution)/shard_map/ppermute | solution.py:280
  98.7 1.5 %collective-permute-start.35 = (bf16[16,4096]{1,0:T(8,128)(2,1)S(1)}, bf16[16,4096]{1,0:T(8,128)(2,1)S(1)}, u32[]{:S(2)}, u32[]{:S(2)}) collective-permute-start(bf16[16,4096]{1,0:T(8,128)(2,1)S(1)} %get-tuple-element.9), channel_id=1, source_target_pairs={{0,2},{1,3},{4,0},{5,1},{8,4},{9,5},{12,8},{13,9},{14,12},{15,13},... | collective-permute-start | bytes 393224 | tf_op jit(solution)/shard_map/ppermute | solution.py:280
  100.9 1.8 %collective-permute-start.28 = (bf16[16,4096]{1,0:T(8,128)(2,1)S(1)}, bf16[16,4096]{1,0:T(8,128)(2,1)S(1)}, u32[]{:S(2)}, u32[]{:S(2)}) collective-permute-start(bf16[16,4096]{1,0:T(8,128)(2,1)S(1)} %get-tuple-element.7), channel_id=1, source_target_pairs={{0,2},{1,3},{4,0},{5,1},{8,4},{9,5},{12,8},{13,9},{14,12},{15,13},... | collective-permute-start | bytes 393224 | tf_op jit(solution)/shard_map/ppermute | solution.py:280
  103.0 2.1 %collective-permute-done.35 = bf16[16,4096]{1,0:T(8,128)(2,1)S(1)} collective-permute-done((bf16[16,4096]{1,0:T(8,128)(2,1)S(1)}, bf16[16,4096]{1,0:T(8,128)(2,1)S(1)}, u32[]{:S(2)}, u32[]{:S(2)}) %collective-permute-start.35) | collective-permute-done | bytes 131104 | tf_op jit(solution)/shard_map/ppermute | solution.py:280
  105.2 1.5 %collective-permute-start.36 = (bf16[16,4096]{1,0:T(8,128)(2,1)S(1)}, bf16[16,4096]{1,0:T(8,128)(2,1)S(1)}, u32[]{:S(2)}, u32[]{:S(2)}) collective-permute-start(bf16[16,4096]{1,0:T(8,128)(2,1)S(1)} %add_convert_fusion.2), channel_id=1, source_target_pairs={{0,2},{1,3},{4,0},{5,1},{8,4},{9,5},{12,8},{13,9},{14,12},{15,13},... | collective-permute-start | bytes 393224 | tf_op jit(solution)/shard_map/ppermute | solution.py:280
  106.7 1.1 collective-permute-done.28
  107.9 1.5 %collective-permute-start.29 = (bf16[16,4096]{1,0:T(8,128)(2,1)S(1)}, bf16[16,4096]{1,0:T(8,128)(2,1)S(1)}, u32[]{:S(2)}, u32[]{:S(2)}) collective-permute-start(bf16[16,4096]{1,0:T(8,128)(2,1)S(1)} %add_convert_fusion.8), channel_id=1, source_target_pairs={{0,2},{1,3},{4,0},{5,1},{8,4},{9,5},{12,8},{13,9},{14,12},{15,13},... | collective-permute-start | bytes 393224 | tf_op jit(solution)/shard_map/ppermute | solution.py:280
  109.4 1.3 %collective-permute-done.36 = bf16[16,4096]{1,0:T(8,128)(2,1)S(1)} collective-permute-done((bf16[16,4096]{1,0:T(8,128)(2,1)S(1)}, bf16[16,4096]{1,0:T(8,128)(2,1)S(1)}, u32[]{:S(2)}, u32[]{:S(2)}) %collective-permute-start.36) | collective-permute-done | bytes 131104 | tf_op jit(solution)/shard_map/ppermute | solution.py:280
  110.8 1.5 %collective-permute-start.37 = (bf16[16,4096]{1,0:T(8,128)(2,1)S(1)}, bf16[16,4096]{1,0:T(8,128)(2,1)S(1)}, u32[]{:S(2)}, u32[]{:S(2)}) collective-permute-start(bf16[16,4096]{1,0:T(8,128)(2,1)S(1)} %add_convert_fusion.1), channel_id=1, source_target_pairs={{0,2},{1,3},{4,0},{5,1},{8,4},{9,5},{12,8},{13,9},{14,12},{15,13},... | collective-permute-start | bytes 393224 | tf_op jit(solution)/shard_map/ppermute | solution.py:280
  112.4 2.0 %collective-permute-done.29 = bf16[16,4096]{1,0:T(8,128)(2,1)S(1)} collective-permute-done((bf16[16,4096]{1,0:T(8,128)(2,1)S(1)}, bf16[16,4096]{1,0:T(8,128)(2,1)S(1)}, u32[]{:S(2)}, u32[]{:S(2)}) %collective-permute-start.29) | collective-permute-done | bytes 131104 | tf_op jit(solution)/shard_map/ppermute | solution.py:280
  114.4 1.5 %collective-permute-start.30 = (bf16[16,4096]{1,0:T(8,128)(2,1)S(1)}, bf16[16,4096]{1,0:T(8,128)(2,1)S(1)}, u32[]{:S(2)}, u32[]{:S(2)}) collective-permute-start(bf16[16,4096]{1,0:T(8,128)(2,1)S(1)} %add_convert_fusion.7), channel_id=1, source_target_pairs={{0,2},{1,3},{4,0},{5,1},{8,4},{9,5},{12,8},{13,9},{14,12},{15,13},... | collective-permute-start | bytes 393224 | tf_op jit(solution)/shard_map/ppermute | solution.py:280
  116.0 1.2 %collective-permute-done.37 = bf16[16,4096]{1,0:T(8,128)(2,1)S(1)} collective-permute-done((bf16[16,4096]{1,0:T(8,128)(2,1)S(1)}, bf16[16,4096]{1,0:T(8,128)(2,1)S(1)}, u32[]{:S(2)}, u32[]{:S(2)}) %collective-permute-start.37) | collective-permute-done | bytes 131104 | tf_op jit(solution)/shard_map/ppermute | solution.py:280
  117.3 1.5 %collective-permute-start.38 = (bf16[16,4096]{1,0:T(8,128)(2,1)S(1)}, bf16[16,4096]{1,0:T(8,128)(2,1)S(1)}, u32[]{:S(2)}, u32[]{:S(2)}) collective-permute-start(bf16[16,4096]{1,0:T(8,128)(2,1)S(1)} %add_convert_fusion), channel_id=1, source_target_pairs={{0,2},{1,3},{4,0},{5,1},{8,4},{9,5},{12,8},{13,9},{14,12},{15,13},... | collective-permute-start | bytes 393224 | tf_op jit(solution)/shard_map/ppermute | solution.py:280
  119.5 2.8 %collective-permute-done.38 = bf16[16,4096]{1,0:T(8,128)(2,1)S(1)} collective-permute-done((bf16[16,4096]{1,0:T(8,128)(2,1)S(1)}, bf16[16,4096]{1,0:T(8,128)(2,1)S(1)}, u32[]{:S(2)}, u32[]{:S(2)}) %collective-permute-start.38) | collective-permute-done | bytes 131104 | tf_op jit(solution)/shard_map/ppermute | solution.py:280
  122.6 0.9 multiply_convert_fusion
  (94 shorter events, 10.1 us)
Async XLA Ops:
  0.6 30.7 %copy-start.2 = (bf16[16,8192]{1,0:T(8,128)(2,1)S(1)}, bf16[16,8192]{1,0:T(8,128)(2,1)}, u32[]{:S(2)}) copy-start(bf16[16,8192]{1,0:T(8,128)(2,1)} %refs_5_.1) | copy-start | bytes 786436
  0.6 32.7 %copy-start.5 = (s32[32]{0:T(128)S(1)}, s32[32]{0:T(128)}, u32[]{:S(2)}) copy-start(s32[32]{0:T(128)} %param.20) | copy-start | bytes 388
  0.7 32.7 %copy-start.6 = (s32[32]{0:T(128)S(1)}, s32[32]{0:T(128)}, u32[]{:S(2)}) copy-start(s32[32]{0:T(128)} %param.21) | copy-start | bytes 388
  0.7 32.7 %copy-start.7 = (s32[16]{0:T(128)S(1)}, s32[16]{0:T(128)}, u32[]{:S(2)}) copy-start(s32[16]{0:T(128)} %param.18) | copy-start | bytes 196
  0.7 32.7 %copy-start.8 = (s32[16]{0:T(128)S(1)}, s32[16]{0:T(128)}, u32[]{:S(2)}) copy-start(s32[16]{0:T(128)} %param.19) | copy-start | bytes 196
  0.7 32.7 %copy-start.4 = (bf16[1,8192,64]{1,2,0:T(8,128)(2,1)S(1)}, bf16[1,8192,64]{1,2,0:T(8,128)(2,1)}, u32[]{:S(2)}) copy-start(bf16[1,8192,64]{1,2,0:T(8,128)(2,1)} %param.16) | copy-start | bytes 3145732
  1.8 7.4 %collective-permute-start.3 = (bf16[16,4096]{1,0:T(8,128)(2,1)S(1)}, bf16[16,4096]{1,0:T(8,128)(2,1)S(1)}, u32[]{:S(2)}, u32[]{:S(2)}) collective-permute-start(bf16[16,4096]{1,0:T(8,128)(2,1)S(1)} %get-tuple-element.12), channel_id=1, source_target_pairs={{0,2},{1,3},{4,0},{5,1},{8,4},{9,5},{12,8},{13,9},{14,12},{15,13},... | collective-permute-start | bytes 393224 | tf_op jit(solution)/shard_map/ppermute | solution.py:99
  4.8 6.4 %collective-permute-start = (bf16[16,4096]{1,0:T(8,128)(2,1)S(1)}, bf16[16,4096]{1,0:T(8,128)(2,1)S(1)}, u32[]{:S(2)}, u32[]{:S(2)}) collective-permute-start(bf16[16,4096]{1,0:T(8,128)(2,1)S(1)} %get-tuple-element.13), channel_id=1, source_target_pairs={{0,4},{1,5},{4,8},{5,9},{8,12},{9,13},{12,14},{13,15},{14,10},{15,... | collective-permute-start | bytes 393224 | tf_op jit(solution)/shard_map/ppermute | solution.py:98
  4.9 7.1 %collective-permute-start.2 = (bf16[16,4096]{1,0:T(8,128)(2,1)S(1)}, bf16[16,4096]{1,0:T(8,128)(2,1)S(1)}, u32[]{:S(2)}, u32[]{:S(2)}) collective-permute-start(bf16[16,4096]{1,0:T(8,128)(2,1)S(1)} %get-tuple-element.13), channel_id=1, source_target_pairs={{0,2},{1,3},{4,0},{5,1},{8,4},{9,5},{12,8},{13,9},{14,12},{15,13},... | collective-permute-start | bytes 393224 | tf_op jit(solution)/shard_map/ppermute | solution.py:99
  6.8 7.2 %collective-permute-start.1 = (bf16[16,4096]{1,0:T(8,128)(2,1)S(1)}, bf16[16,4096]{1,0:T(8,128)(2,1)S(1)}, u32[]{:S(2)}, u32[]{:S(2)}) collective-permute-start(bf16[16,4096]{1,0:T(8,128)(2,1)S(1)} %get-tuple-element.12), channel_id=1, source_target_pairs={{0,4},{1,5},{4,8},{5,9},{8,12},{9,13},{12,14},{13,15},{14,10},{15,... | collective-permute-start | bytes 393224 | tf_op jit(solution)/shard_map/ppermute | solution.py:98
  9.2 6.2 %collective-permute-start.7 = (bf16[16,4096]{1,0:T(8,128)(2,1)S(1)}, bf16[16,4096]{1,0:T(8,128)(2,1)S(1)}, u32[]{:S(2)}, u32[]{:S(2)}) collective-permute-start(bf16[16,4096]{1,0:T(8,128)(2,1)S(1)} %collective-permute-done.3.refs_3_), channel_id=1, source_target_pairs={{0,2},{1,3},{4,0},{5,1},{8,4},{9,5},{12,8},{13,9},{14,12},{15,13},... | collective-permute-start | bytes 393224 | tf_op jit(solution)/shard_map/ppermute | solution.py:99
  11.2 6.2 %collective-permute-start.4 = (bf16[16,4096]{1,0:T(8,128)(2,1)S(1)}, bf16[16,4096]{1,0:T(8,128)(2,1)S(1)}, u32[]{:S(2)}, u32[]{:S(2)}) collective-permute-start(bf16[16,4096]{1,0:T(8,128)(2,1)S(1)} %collective-permute-done.refs_0_), channel_id=1, source_target_pairs={{0,4},{1,5},{4,8},{5,9},{8,12},{9,13},{12,14},{13,15},{14,10},{15,... | collective-permute-start | bytes 393224 | tf_op jit(solution)/shard_map/ppermute | solution.py:98
  12.0 6.5 %collective-permute-start.6 = (bf16[16,4096]{1,0:T(8,128)(2,1)S(1)}, bf16[16,4096]{1,0:T(8,128)(2,1)S(1)}, u32[]{:S(2)}, u32[]{:S(2)}) collective-permute-start(bf16[16,4096]{1,0:T(8,128)(2,1)S(1)} %collective-permute-done.2.refs_2_), channel_id=1, source_target_pairs={{0,2},{1,3},{4,0},{5,1},{8,4},{9,5},{12,8},{13,9},{14,12},{15,13},... | collective-permute-start | bytes 393224 | tf_op jit(solution)/shard_map/ppermute | solution.py:99
  14.0 6.3 %collective-permute-start.5 = (bf16[16,4096]{1,0:T(8,128)(2,1)S(1)}, bf16[16,4096]{1,0:T(8,128)(2,1)S(1)}, u32[]{:S(2)}, u32[]{:S(2)}) collective-permute-start(bf16[16,4096]{1,0:T(8,128)(2,1)S(1)} %collective-permute-done.1.refs_1_), channel_id=1, source_target_pairs={{0,4},{1,5},{4,8},{5,9},{8,12},{9,13},{12,14},{13,15},{14,10},{15,... | collective-permute-start | bytes 393224 | tf_op jit(solution)/shard_map/ppermute | solution.py:98
  15.3 5.9 %collective-permute-start.11 = (bf16[16,4096]{1,0:T(8,128)(2,1)S(1)}, bf16[16,4096]{1,0:T(8,128)(2,1)S(1)}, u32[]{:S(2)}, u32[]{:S(2)}) collective-permute-start(bf16[16,4096]{1,0:T(8,128)(2,1)S(1)} %collective-permute-done.7.refs_3_), channel_id=1, source_target_pairs={{0,2},{1,3},{4,0},{5,1},{8,4},{9,5},{12,8},{13,9},{14,12},{15,13},... | collective-permute-start | bytes 393224 | tf_op jit(solution)/shard_map/ppermute | solution.py:99
  17.4 5.2 %collective-permute-start.8 = (bf16[16,4096]{1,0:T(8,128)(2,1)S(1)}, bf16[16,4096]{1,0:T(8,128)(2,1)S(1)}, u32[]{:S(2)}, u32[]{:S(2)}) collective-permute-start(bf16[16,4096]{1,0:T(8,128)(2,1)S(1)} %collective-permute-done.4.refs_0_), channel_id=1, source_target_pairs={{0,4},{1,5},{4,8},{5,9},{8,12},{9,13},{12,14},{13,15},{14,10},{15,... | collective-permute-start | bytes 393224 | tf_op jit(solution)/shard_map/ppermute | solution.py:98
  18.5 5.0 %collective-permute-start.10 = (bf16[16,4096]{1,0:T(8,128)(2,1)S(1)}, bf16[16,4096]{1,0:T(8,128)(2,1)S(1)}, u32[]{:S(2)}, u32[]{:S(2)}) collective-permute-start(bf16[16,4096]{1,0:T(8,128)(2,1)S(1)} %collective-permute-done.6.refs_2_), channel_id=1, source_target_pairs={{0,2},{1,3},{4,0},{5,1},{8,4},{9,5},{12,8},{13,9},{14,12},{15,13},... | collective-permute-start | bytes 393224 | tf_op jit(solution)/shard_map/ppermute | solution.py:99
  20.3 5.0 %collective-permute-start.9 = (bf16[16,4096]{1,0:T(8,128)(2,1)S(1)}, bf16[16,4096]{1,0:T(8,128)(2,1)S(1)}, u32[]{:S(2)}, u32[]{:S(2)}) collective-permute-start(bf16[16,4096]{1,0:T(8,128)(2,1)S(1)} %collective-permute-done.5.refs_1_), channel_id=1, source_target_pairs={{0,4},{1,5},{4,8},{5,9},{8,12},{9,13},{12,14},{13,15},{14,10},{15,... | collective-permute-start | bytes 393224 | tf_op jit(solution)/shard_map/ppermute | solution.py:98
  20.5 12.3 %collective-permute-start.15 = (bf16[32,8192]{1,0:T(8,128)(2,1)S(1)}, bf16[32,8192]{1,0:T(8,128)(2,1)}, u32[]{:S(2)}, u32[]{:S(2)}) collective-permute-start(bf16[32,8192]{1,0:T(8,128)(2,1)S(1)} %join_pieces.4.refs_6_), channel_id=1, source_target_pairs={{0,1},{1,0},{2,3},{3,2},{4,5},{5,4},{6,7},{7,6},{8,9},{9,8},{10,11... | collective-permute-start | bytes 1572872 | tf_op jit(solution)/shard_map/ppermute | solution.py:110
  21.2 11.6 %collective-permute-start.16 = (bf16[32,8192]{1,0:T(8,128)(2,1)S(1)}, bf16[32,8192]{1,0:T(8,128)(2,1)}, u32[]{:S(2)}, u32[]{:S(2)}) collective-permute-start(bf16[32,8192]{1,0:T(8,128)(2,1)S(1)} %join_pieces.5.refs_7_), channel_id=1, source_target_pairs={{0,1},{1,0},{2,3},{3,2},{4,5},{5,4},{6,7},{7,6},{8,9},{9,8},{10,11... | collective-permute-start | bytes 1572872 | tf_op jit(solution)/shard_map/ppermute | solution.py:110
  25.3 8.0 %collective-permute-start.17 = (bf16[32,8192]{1,0:T(8,128)(2,1)S(1)}, bf16[32,8192]{1,0:T(8,128)(2,1)}, u32[]{:S(2)}, u32[]{:S(2)}) collective-permute-start(bf16[32,8192]{1,0:T(8,128)(2,1)S(1)} %join_pieces.6.refs_8_), channel_id=1, source_target_pairs={{0,1},{1,0},{2,3},{3,2},{4,5},{5,4},{6,7},{7,6},{8,9},{9,8},{10,11... | collective-permute-start | bytes 1572872 | tf_op jit(solution)/shard_map/ppermute | solution.py:110
  25.4 5.9 %collective-permute-start.12 = (bf16[16,4096]{1,0:T(8,128)(2,1)S(1)}, bf16[16,4096]{1,0:T(8,128)(2,1)S(1)}, u32[]{:S(2)}, u32[]{:S(2)}) collective-permute-start(bf16[16,4096]{1,0:T(8,128)(2,1)S(1)} %collective-permute-done.8.refs_0_), channel_id=1, source_target_pairs={{0,4},{1,5},{4,8},{5,9},{8,12},{9,13},{12,14},{13,15},{14,10},{15,... | collective-permute-start | bytes 393224 | tf_op jit(solution)/shard_map/ppermute | solution.py:104
  25.6 5.8 %collective-permute-start.13 = (bf16[16,4096]{1,0:T(8,128)(2,1)S(1)}, bf16[16,4096]{1,0:T(8,128)(2,1)S(1)}, u32[]{:S(2)}, u32[]{:S(2)}) collective-permute-start(bf16[16,4096]{1,0:T(8,128)(2,1)S(1)} %collective-permute-done.11.refs_3_), channel_id=1, source_target_pairs={{0,2},{1,3},{4,0},{5,1},{8,4},{9,5},{12,8},{13,9},{14,12},{15,13},... | collective-permute-start | bytes 393224 | tf_op jit(solution)/shard_map/ppermute | solution.py:105
  31.3 1.5 %collective-permute-start.14 = (bf16[16,8192]{1,0:T(8,128)(2,1)S(1)}, bf16[16,8192]{1,0:T(8,128)(2,1)S(1)}, u32[]{:S(2)}, u32[]{:S(2)}) collective-permute-start(bf16[16,8192]{1,0:T(8,128)(2,1)S(1)} %copy-done.2), channel_id=1, source_target_pairs={{0,1},{1,0},{2,3},{3,2},{4,5},{5,4},{6,7},{7,6},{8,9},{9,8},{10,11... | collective-permute-start | bytes 786440 | tf_op jit(solution)/shard_map/ppermute | solution.py:94
  31.5 1.9 %collective-permute-start.18 = (bf16[16,8192]{1,0:T(8,128)(2,1)S(1)}, bf16[16,8192]{1,0:T(8,128)(2,1)}, u32[]{:S(2)}, u32[]{:S(2)}) collective-permute-start(bf16[16,8192]{1,0:T(8,128)(2,1)S(1)} %join_pieces.7.refs_9_), channel_id=1, source_target_pairs={{0,1},{1,0},{2,3},{3,2},{4,5},{5,4},{6,7},{7,6},{8,9},{9,8},{10,11... | collective-permute-start | bytes 786440 | tf_op jit(solution)/shard_map/ppermute | solution.py:110
  39.9 1.3 %collective-permute-start.19 = (bf16[256,64]{1,0:T(8,128)(2,1)S(1)}, bf16[256,64]{1,0:T(8,128)(2,1)S(1)}, u32[]{:S(2)}, u32[]{:S(2)}) collective-permute-start(bf16[256,64]{1,0:T(8,128)(2,1)S(1)} %get-tuple-element.4), channel_id=1, source_target_pairs={{0,1},{1,0},{2,3},{3,2},{4,5},{5,4},{6,7},{7,6},{8,9},{9,8},{10,11... | collective-permute-start | bytes 98312 | tf_op jit(solution)/shard_map/ppermute | solution.py:320
  41.2 4.3 %collective-permute-start.20 = (bf16[256,64]{1,0:T(8,128)(2,1)S(1)}, bf16[256,64]{1,0:T(8,128)(2,1)S(1)}, u32[]{:S(2)}, u32[]{:S(2)}) collective-permute-start(bf16[256,64]{1,0:T(8,128)(2,1)S(1)} %add.113), channel_id=1, source_target_pairs={{0,2},{1,3},{2,0},{3,1},{4,6},{5,7},{6,4},{7,5},{8,10},{9,11},{10,... | collective-permute-start | bytes 98312 | tf_op jit(solution)/shard_map/ppermute | solution.py:320
  45.6 13.1 %collective-permute-start.21 = (bf16[256,64]{1,0:T(8,128)(2,1)S(1)}, bf16[256,64]{1,0:T(8,128)(2,1)S(1)}, u32[]{:S(2)}, u32[]{:S(2)}) collective-permute-start(bf16[256,64]{1,0:T(8,128)(2,1)S(1)} %add.114), channel_id=1, source_target_pairs={{0,4},{1,5},{2,6},{3,7},{4,0},{5,1},{6,2},{7,3},{8,12},{9,13},{10,... | collective-permute-start | bytes 98312 | tf_op jit(solution)/shard_map/ppermute | solution.py:320
  58.7 14.0 %collective-permute-start.22 = (bf16[256,64]{1,0:T(8,128)(2,1)S(1)}, bf16[256,64]{1,0:T(8,128)(2,1)S(1)}, u32[]{:S(2)}, u32[]{:S(2)}) collective-permute-start(bf16[256,64]{1,0:T(8,128)(2,1)S(1)} %add.115), channel_id=1, source_target_pairs={{0,8},{1,9},{2,10},{3,11},{4,12},{5,13},{6,14},{7,15},{8,0},{9,1},... | collective-permute-start | bytes 98312 | tf_op jit(solution)/shard_map/ppermute | solution.py:320
  66.5 13.4 %slice-start = ((s8[14680064]{0:T(1024)(128)(4,1)}), s8[2097152]{0:T(1024)(128)(4,1)S(1)}, s32[]{:S(2)}) async-start(s8[14680064]{0:T(1024)(128)(4,1)} %bitcast.19), calls=%async_computation | async-start | bytes 4194304
  66.5 13.4 %slice-start.1 = ((s8[14680064]{0:T(1024)(128)(4,1)}), s8[4194304]{0:T(1024)(128)(4,1)S(1)}, s32[]{:S(2)}) async-start(s8[14680064]{0:T(1024)(128)(4,1)} %bitcast.19), calls=%async_computation.1 | async-start | bytes 8388608
  72.8 7.1 %slice-start.2 = ((s8[14680064]{0:T(1024)(128)(4,1)}), s8[4194304]{0:T(1024)(128)(4,1)S(1)}, s32[]{:S(2)}) async-start(s8[14680064]{0:T(1024)(128)(4,1)} %bitcast.19), calls=%async_computation.2 | async-start | bytes 8388608
  79.8 3.2 %collective-permute-start.23 = (bf16[128,4096]{1,0:T(8,128)(2,1)S(1)}, bf16[128,4096]{1,0:T(8,128)(2,1)S(1)}, u32[]{:S(2)}, u32[]{:S(2)}) collective-permute-start(bf16[128,4096]{1,0:T(8,128)(2,1)S(1)} %slice.153), channel_id=1, source_target_pairs={{0,1},{1,0},{2,3},{3,2},{4,5},{5,4},{6,7},{7,6},{8,9},{9,8},{10,11... | collective-permute-start | bytes 3145736 | tf_op jit(solution)/shard_map/ppermute | solution.py:273
  82.3 2.8 %collective-permute-start.31 = (bf16[128,4096]{1,0:T(8,128)(2,1)S(1)}, bf16[128,4096]{1,0:T(8,128)(2,1)S(1)}, u32[]{:S(2)}, u32[]{:S(2)}) collective-permute-start(bf16[128,4096]{1,0:T(8,128)(2,1)S(1)} %slice.170), channel_id=1, source_target_pairs={{0,1},{1,0},{2,3},{3,2},{4,5},{5,4},{6,7},{7,6},{8,9},{9,8},{10,11... | collective-permute-start | bytes 3145736 | tf_op jit(solution)/shard_map/ppermute | solution.py:273
  83.0 6.4 %collective-permute-start.24 = (bf16[16,4096]{1,0:T(8,128)(2,1)S(1)}, bf16[16,4096]{1,0:T(8,128)(2,1)S(1)}, u32[]{:S(2)}, u32[]{:S(2)}) collective-permute-start(bf16[16,4096]{1,0:T(8,128)(2,1)S(1)} %add_convert_fusion.13), channel_id=1, source_target_pairs={{0,4},{1,5},{4,8},{5,9},{8,12},{9,13},{12,14},{13,15},{14,10},{15,... | collective-permute-start | bytes 393224 | tf_op jit(solution)/shard_map/ppermute | solution.py:280
  85.2 6.9 %collective-permute-start.32 = (bf16[16,4096]{1,0:T(8,128)(2,1)S(1)}, bf16[16,4096]{1,0:T(8,128)(2,1)S(1)}, u32[]{:S(2)}, u32[]{:S(2)}) collective-permute-start(bf16[16,4096]{1,0:T(8,128)(2,1)S(1)} %add_convert_fusion.6), channel_id=1, source_target_pairs={{0,4},{1,5},{4,8},{5,9},{8,12},{9,13},{12,14},{13,15},{14,10},{15,... | collective-permute-start | bytes 393224 | tf_op jit(solution)/shard_map/ppermute | solution.py:280
  89.4 5.5 %collective-permute-start.25 = (bf16[16,4096]{1,0:T(8,128)(2,1)S(1)}, bf16[16,4096]{1,0:T(8,128)(2,1)S(1)}, u32[]{:S(2)}, u32[]{:S(2)}) collective-permute-start(bf16[16,4096]{1,0:T(8,128)(2,1)S(1)} %add_convert_fusion.12), channel_id=1, source_target_pairs={{0,4},{1,5},{4,8},{5,9},{8,12},{9,13},{12,14},{13,15},{14,10},{15,... | collective-permute-start | bytes 393224 | tf_op jit(solution)/shard_map/ppermute | solution.py:280
  92.2 6.5 %collective-permute-start.33 = (bf16[16,4096]{1,0:T(8,128)(2,1)S(1)}, bf16[16,4096]{1,0:T(8,128)(2,1)S(1)}, u32[]{:S(2)}, u32[]{:S(2)}) collective-permute-start(bf16[16,4096]{1,0:T(8,128)(2,1)S(1)} %add_convert_fusion.5), channel_id=1, source_target_pairs={{0,4},{1,5},{4,8},{5,9},{8,12},{9,13},{12,14},{13,15},{14,10},{15,... | collective-permute-start | bytes 393224 | tf_op jit(solution)/shard_map/ppermute | solution.py:280
  95.0 5.8 %collective-permute-start.26 = (bf16[16,4096]{1,0:T(8,128)(2,1)S(1)}, bf16[16,4096]{1,0:T(8,128)(2,1)S(1)}, u32[]{:S(2)}, u32[]{:S(2)}) collective-permute-start(bf16[16,4096]{1,0:T(8,128)(2,1)S(1)} %add_convert_fusion.11), channel_id=1, source_target_pairs={{0,4},{1,5},{4,8},{5,9},{8,12},{9,13},{12,14},{13,15},{14,10},{15,... | collective-permute-start | bytes 393224 | tf_op jit(solution)/shard_map/ppermute | solution.py:280
  98.7 6.4 %collective-permute-start.35 = (bf16[16,4096]{1,0:T(8,128)(2,1)S(1)}, bf16[16,4096]{1,0:T(8,128)(2,1)S(1)}, u32[]{:S(2)}, u32[]{:S(2)}) collective-permute-start(bf16[16,4096]{1,0:T(8,128)(2,1)S(1)} %get-tuple-element.9), channel_id=1, source_target_pairs={{0,2},{1,3},{4,0},{5,1},{8,4},{9,5},{12,8},{13,9},{14,12},{15,13},... | collective-permute-start | bytes 393224 | tf_op jit(solution)/shard_map/ppermute | solution.py:280
  100.3 19.3 %collective-permute-start.34 = (bf16[16,4096]{1,0:T(8,128)(2,1)S(1)}, bf16[16,4096]{1,0:T(8,128)(2,1)S(1)}, u32[]{:S(2)}, u32[]{:S(2)}) collective-permute-start(bf16[16,4096]{1,0:T(8,128)(2,1)S(1)} %get-tuple-element.8), channel_id=1, source_target_pairs={{0,4},{1,5},{4,8},{5,9},{8,12},{9,13},{12,14},{13,15},{14,10},{15,... | collective-permute-start | bytes 393224 | tf_op jit(solution)/shard_map/ppermute | solution.py:280
  100.9 6.9 %collective-permute-start.28 = (bf16[16,4096]{1,0:T(8,128)(2,1)S(1)}, bf16[16,4096]{1,0:T(8,128)(2,1)S(1)}, u32[]{:S(2)}, u32[]{:S(2)}) collective-permute-start(bf16[16,4096]{1,0:T(8,128)(2,1)S(1)} %get-tuple-element.7), channel_id=1, source_target_pairs={{0,2},{1,3},{4,0},{5,1},{8,4},{9,5},{12,8},{13,9},{14,12},{15,13},... | collective-permute-start | bytes 393224 | tf_op jit(solution)/shard_map/ppermute | solution.py:280
  102.7 16.1 %collective-permute-start.27 = (bf16[16,4096]{1,0:T(8,128)(2,1)S(1)}, bf16[16,4096]{1,0:T(8,128)(2,1)S(1)}, u32[]{:S(2)}, u32[]{:S(2)}) collective-permute-start(bf16[16,4096]{1,0:T(8,128)(2,1)S(1)} %get-tuple-element.6), channel_id=1, source_target_pairs={{0,4},{1,5},{4,8},{5,9},{8,12},{9,13},{12,14},{13,15},{14,10},{15,... | collective-permute-start | bytes 393224 | tf_op jit(solution)/shard_map/ppermute | solution.py:280
  105.2 5.6 %collective-permute-start.36 = (bf16[16,4096]{1,0:T(8,128)(2,1)S(1)}, bf16[16,4096]{1,0:T(8,128)(2,1)S(1)}, u32[]{:S(2)}, u32[]{:S(2)}) collective-permute-start(bf16[16,4096]{1,0:T(8,128)(2,1)S(1)} %add_convert_fusion.2), channel_id=1, source_target_pairs={{0,2},{1,3},{4,0},{5,1},{8,4},{9,5},{12,8},{13,9},{14,12},{15,13},... | collective-permute-start | bytes 393224 | tf_op jit(solution)/shard_map/ppermute | solution.py:280
  107.9 6.5 %collective-permute-start.29 = (bf16[16,4096]{1,0:T(8,128)(2,1)S(1)}, bf16[16,4096]{1,0:T(8,128)(2,1)S(1)}, u32[]{:S(2)}, u32[]{:S(2)}) collective-permute-start(bf16[16,4096]{1,0:T(8,128)(2,1)S(1)} %add_convert_fusion.8), channel_id=1, source_target_pairs={{0,2},{1,3},{4,0},{5,1},{8,4},{9,5},{12,8},{13,9},{14,12},{15,13},... | collective-permute-start | bytes 393224 | tf_op jit(solution)/shard_map/ppermute | solution.py:280
  110.8 6.4 %collective-permute-start.37 = (bf16[16,4096]{1,0:T(8,128)(2,1)S(1)}, bf16[16,4096]{1,0:T(8,128)(2,1)S(1)}, u32[]{:S(2)}, u32[]{:S(2)}) collective-permute-start(bf16[16,4096]{1,0:T(8,128)(2,1)S(1)} %add_convert_fusion.1), channel_id=1, source_target_pairs={{0,2},{1,3},{4,0},{5,1},{8,4},{9,5},{12,8},{13,9},{14,12},{15,13},... | collective-permute-start | bytes 393224 | tf_op jit(solution)/shard_map/ppermute | solution.py:280
  114.4 5.0 %collective-permute-start.30 = (bf16[16,4096]{1,0:T(8,128)(2,1)S(1)}, bf16[16,4096]{1,0:T(8,128)(2,1)S(1)}, u32[]{:S(2)}, u32[]{:S(2)}) collective-permute-start(bf16[16,4096]{1,0:T(8,128)(2,1)S(1)} %add_convert_fusion.7), channel_id=1, source_target_pairs={{0,2},{1,3},{4,0},{5,1},{8,4},{9,5},{12,8},{13,9},{14,12},{15,13},... | collective-permute-start | bytes 393224 | tf_op jit(solution)/shard_map/ppermute | solution.py:280
  117.3 5.0 %collective-permute-start.38 = (bf16[16,4096]{1,0:T(8,128)(2,1)S(1)}, bf16[16,4096]{1,0:T(8,128)(2,1)S(1)}, u32[]{:S(2)}, u32[]{:S(2)}) collective-permute-start(bf16[16,4096]{1,0:T(8,128)(2,1)S(1)} %add_convert_fusion), channel_id=1, source_target_pairs={{0,2},{1,3},{4,0},{5,1},{8,4},{9,5},{12,8},{13,9},{14,12},{15,13},... | collective-permute-start | bytes 393224 | tf_op jit(solution)/shard_map/ppermute | solution.py:280
  (5 other events, 23.2 us)

commit v3 on v2

v3 whole, which is shorter than its diff:
```python
import functools

import jax
import jax.numpy as jnp
from jax import lax
from jax.experimental import pallas as pl
from jax.experimental.pallas import tpu as pltpu
from jax.sharding import PartitionSpec as P

adapter_alpha = 32.0
AXIS = "mp"
HALVES = 2
DEPTH_BLOCKS = 8
VMEM_LIMIT = 16 * 1024 * 1024
STREAM_LIMIT = 48 * 1024 * 1024


def chip_at(place, chips):
    if chips == 8:
        return jnp.where(place < 4, 2 * place, 2 * (7 - place) + 1)
    return place


def place_of(chip, chips):
    if chips == 8:
        return jnp.where((chip & 1) == 0, chip >> 1, 7 - (chip >> 1))
    return chip


def ring(size, by):
    chips = size // 2
    order = [0, 2, 4, 6, 7, 5, 3, 1] if chips == 8 else list(range(chips))
    pairs = []
    for place, chip in enumerate(order):
        to = order[(place + by) % chips]
        pairs += [(2 * chip + core, 2 * to + core) for core in range(2)]
    return pairs


def flip(size, bit):
    return [(i, i ^ bit) for i in range(size)]


def row_positions(me, row, own_rows, size):
    chips = size // 2
    block = row // own_rows
    index = block & (chips - 1)
    step = (index + 1) >> 1
    delta = jnp.where((index & 1) == 1, step, -step)
    place = (place_of(me >> 1, chips) - delta + chips) & (chips - 1)
    core = (me & 1) ^ (block // chips)
    return (2 * chip_at(place, chips) + core) * own_rows + (row & (own_rows - 1))


def pick(index, table):
    hot = index == lax.broadcasted_iota(jnp.int32, (1, table.shape[1]), 1)
    return jnp.sum(jnp.where(hot, table, 0), axis=1, keepdims=True)


def row_adapters(position, start, adapters):
    segment = jnp.sum((start <= position).astype(jnp.int32), axis=1, keepdims=True) - 1
    return pick(segment, adapters)


def whole(space=pltpu.VMEM):
    return pl.BlockSpec(memory_space=space)


def call(kernel, out_shape, operands, name, ordered=(), limit=VMEM_LIMIT, **options):
    count = len(operands)

    def run(*refs):
        kernel(*refs[:count], *refs[count + len(ordered) :])

    return pl.pallas_call(
        run,
        out_shape=out_shape,
        in_specs=[
            whole(pltpu.SMEM if operand.ndim == 1 else pltpu.VMEM) for operand in operands
        ]
        + [whole(pl.ANY)] * len(ordered),
        out_specs=jax.tree.map(lambda _: whole(), out_shape),
        compiler_params=pltpu.CompilerParams(vmem_limit_bytes=limit),
        name=name,
        **options,
    )(*operands, *ordered)


def split_columns(array):
    rows, columns = array.shape
    width = columns // HALVES
    half = jax.ShapeDtypeStruct((rows, width), array.dtype)

    def kernel(ref, *outs):
        for h, out in enumerate(outs):
            out[...] = ref[:, h * width : (h + 1) * width]

    return call(kernel, (half,) * HALVES, [array], "split_columns")


def join(pieces, ordered=()):
    rows, width = pieces[0].shape

    def kernel(*refs):
        out = refs[-1]
        for i, ref in enumerate(refs[:-1]):
            top, left = i // HALVES * rows, i % HALVES * width
            out[top : top + rows, left : left + width] = ref[...]

    shape = (rows * len(pieces) // HALVES, HALVES * width)
    return call(
        kernel, jax.ShapeDtypeStruct(shape, pieces[0].dtype), pieces, "join_pieces", ordered
    )


def gather_rows(own, size):
    chips = size // 2
    last = chips // 2
    other = lax.ppermute(own, AXIS, flip(size, 1))
    halves = split_columns(own)
    right, left = list(halves), list(halves)
    pieces = []
    mine, theirs = [own], [other]
    for step in range(1, last + 1):
        if step < last:
            right[0] = lax.ppermute(right[0], AXIS, ring(size, 1))
            left[1] = lax.ppermute(left[1], AXIS, ring(size, -1))
            right[1] = lax.ppermute(right[1], AXIS, ring(size, 1))
            left[0] = lax.ppermute(left[0], AXIS, ring(size, -1))
            pieces += right + left
        else:
            pieces.append(lax.ppermute(right[0], AXIS, ring(size, 1)))
            pieces.append(lax.ppermute(left[1], AXIS, ring(size, -1)))
        if step == last - 2 or step == last:
            part = join(pieces, [other] if step < last else [])
            pieces = []
            mine.append(part)
            theirs.append(lax.ppermute(part, AXIS, flip(size, 1)))
    return mine + theirs


def shrink_kernel(own_rows, size, count, *refs):
    me_ref, start, adapters, ranks, slots = refs[:5]
    parts = refs[5 : 5 + count]
    factor, rows_out, coeff_out, total = refs[5 + count :]
    batch_rows, model_width = rows_out.shape
    width = model_width // 8

    def columns(k, _):
        at = pl.ds(pl.multiple_of(k * width, width), width)
        top = 0
        for part in parts:
            rows_out[top : top + part.shape[0], at] = part[:, at]
            top += part.shape[0]
        product = lax.dot_general(
            rows_out[:, at],
            factor[:, at],
            (((1,), (1,)), ((), ())),
            preferred_element_type=jnp.float32,
        )
        total[...] = jnp.where(k == 0, product, total[...] + product)
        return 0

    lax.fori_loop(0, model_width // width, columns, 0)

    me = me_ref[0]
    rank_limit = coeff_out.shape[1]
    held = total.shape[1] // rank_limit
    row = lax.broadcasted_iota(jnp.int32, (batch_rows, 1), 0)
    adapter = row_adapters(row_positions(me, row, own_rows, size), start[...], adapters[...])
    rank = pick(adapter, ranks[...])
    slot = pick(adapter, slots[...]) - me * held
    shrink = jnp.zeros((batch_rows, rank_limit), jnp.float32)
    for s in range(held):
        shrink = jnp.where(slot == s, total[:, s * rank_limit : (s + 1) * rank_limit], shrink)
    keep = lax.broadcasted_iota(jnp.int32, (1, rank_limit), 1) < rank
    coeff = jnp.where(keep, shrink * (adapter_alpha / rank.astype(jnp.float32)), 0.0)
    column = lax.broadcasted_iota(jnp.int32, (1, batch_rows), 1)
    place = row_positions(me, column, own_rows, size)
    to_place = (place == row).astype(jnp.bfloat16)
    coeff_out[...] = jnp.dot(
        to_place, coeff.astype(jnp.bfloat16), preferred_element_type=jnp.float32
    ).astype(jnp.bfloat16)


def shrink_rows(parts, shrink_factors, tables, me, own_rows, size):
    slots, model_width, rank_limit = shrink_factors.shape
    factor = jnp.swapaxes(shrink_factors, 1, 2).reshape(slots * rank_limit, model_width)
    batch_rows = own_rows * size
    return call(
        functools.partial(shrink_kernel, own_rows, size, len(parts)),
        (
            jax.ShapeDtypeStruct((batch_rows, model_width), jnp.bfloat16),
            jax.ShapeDtypeStruct((batch_rows, rank_limit), jnp.bfloat16),
        ),
        [me, *tables, *parts, factor],
        "shrink_rows",
        scratch_shapes=[pltpu.VMEM((batch_rows, slots * rank_limit), jnp.float32)],
        cost_estimate=pl.CostEstimate(
            flops=2 * batch_rows * model_width * slots * rank_limit,
            bytes_accessed=4 * batch_rows * model_width,
            transcendentals=0,
        ),
    )


def add_coefficients(a, b, ordered):
    def kernel(a_ref, b_ref, out):
        out[...] = a_ref[...] + b_ref[...]

    return call(
        kernel, jax.ShapeDtypeStruct(a.shape, a.dtype), [a, b], "add_coefficients", ordered
    )


def matmul(rows, weight, name, first, last, ordered=()):
    batch_rows, depth = rows.shape
    width = weight.shape[1]
    block = depth // DEPTH_BLOCKS

    def kernel(rows_ref, weight_ref, *rest):
        out = rest[-1]
        k = pl.program_id(0)
        at = pl.ds(pl.multiple_of((k + first) * block, block), block)
        product = jnp.dot(rows_ref[:, at], weight_ref[...], preferred_element_type=jnp.float32)

        @pl.when(k == 0)
        def _():
            out[...] = product

        @pl.when(k > 0)
        def _():
            out[...] += product

    return pl.pallas_call(
        kernel,
        out_shape=jax.ShapeDtypeStruct((batch_rows, width), jnp.float32),
        grid=(last - first,),
        in_specs=[whole(), pl.BlockSpec((block, width), lambda k: (k + first, 0))]
        + [whole(pl.ANY)] * len(ordered),
        out_specs=pl.BlockSpec((batch_rows, width), lambda k: (0, 0)),
        compiler_params=pltpu.CompilerParams(vmem_limit_bytes=STREAM_LIMIT),
        cost_estimate=pl.CostEstimate(
            flops=2 * batch_rows * (last - first) * block * width,
            bytes_accessed=2 * (last - first) * block * width,
            transcendentals=0,
        ),
        name=name,
    )(rows, weight, *ordered)


def hidden_kernel(
    own_rows, size, me_ref, start, adapters, coeff, recv, expand, gate, up, more, out, spread
):
    me = me_ref[0]
    batch_rows, rank_limit = coeff.shape
    row = lax.broadcasted_iota(jnp.int32, (batch_rows, 1), 0)
    position = row_positions(me, row, own_rows, size)
    adapter = row_adapters(position, start[...], adapters[...])
    from_place = position == lax.broadcasted_iota(jnp.int32, (1, batch_rows), 1)
    own = jnp.dot(
        from_place.astype(jnp.bfloat16),
        coeff[...] + recv[...],
        preferred_element_type=jnp.float32,
    )
    pair = jnp.concatenate([own, own], axis=1)
    second = lax.broadcasted_iota(jnp.int32, (1, 2 * rank_limit), 1) // rank_limit
    for p in range(spread.shape[1] // (2 * rank_limit)):
        spread[:, p * 2 * rank_limit : (p + 1) * 2 * rank_limit] = jnp.where(
            adapter == second + 2 * p, pair, 0.0
        ).astype(jnp.bfloat16)
    lora = jnp.dot(spread[...], expand[...], preferred_element_type=jnp.float32)
    value = gate[...]
    total = up[...] + more[...] + lora
    out[...] = (value / (1.0 + jnp.exp(-value)) * total).astype(jnp.bfloat16)


def hidden_rows(gate, up, more, coeff, recv, expand_factors, tables, me, own_rows, size):
    adapters, rank_limit, width = expand_factors.shape
    batch_rows = gate.shape[0]
    return call(
        functools.partial(hidden_kernel, own_rows, size),
        jax.ShapeDtypeStruct((batch_rows, width), jnp.bfloat16),
        [
            me,
            *tables,
            coeff,
            recv,
            expand_factors.reshape(adapters * rank_limit, width),
            gate,
            up,
            more,
        ],
        "hidden_rows",
        scratch_shapes=[pltpu.VMEM((batch_rows, adapters * rank_limit), jnp.bfloat16)],
        cost_estimate=pl.CostEstimate(
            flops=2 * batch_rows * adapters * rank_limit * width,
            bytes_accessed=2 * adapters * rank_limit * width,
            transcendentals=batch_rows * width,
        ),
    )


def down_rows(hidden, down_weight, half, ordered=()):
    batch_rows, hidden_width = hidden.shape
    width = down_weight.shape[1] // HALVES
    steps = 8
    block = width // steps
    core_rows = batch_rows // 2

    def kernel(hidden_ref, weight, *rest):
        mine, theirs = rest[-2:]
        product = jnp.dot(
            hidden_ref[...], weight[...], preferred_element_type=jnp.float32
        ).astype(jnp.bfloat16)
        theirs[...] = product[core_rows:]
        mine[...] = product[:core_rows]

    part = jax.ShapeDtypeStruct((core_rows, width), jnp.bfloat16)
    return pl.pallas_call(
        kernel,
        out_shape=(part, part),
        grid=(steps,),
        in_specs=[
            whole(),
            pl.BlockSpec((hidden_width, block), lambda n: (0, n + half * steps)),
        ]
        + [whole(pl.ANY)] * len(ordered),
        out_specs=[pl.BlockSpec((core_rows, block), lambda n: (0, n))] * 2,
        compiler_params=pltpu.CompilerParams(vmem_limit_bytes=STREAM_LIMIT),
        cost_estimate=pl.CostEstimate(
            flops=2 * batch_rows * hidden_width * width,
            bytes_accessed=2 * hidden_width * width,
            transcendentals=0,
        ),
        name="down_rows",
    )(hidden, down_weight, *ordered)


def add_blocks(sides, own_rows, ordered):
    operands, shapes = [], []
    for mine, theirs, _, arrived in sides:
        operands += [mine, theirs] + ([] if arrived is None else [arrived])
        shapes.append(jax.ShapeDtypeStruct((own_rows, mine.shape[1]), jnp.bfloat16))

    def kernel(*refs):
        refs = list(refs)
        outs = refs[-len(sides) :]
        for (_, _, index, arrived), out in zip(sides, outs):
            at = slice(index * own_rows, (index + 1) * own_rows)
            total = refs.pop(0)[at, :].astype(jnp.float32)
            total = total + refs.pop(0)[at, :].astype(jnp.float32)
            if arrived is not None:
                total = total + refs.pop(0)[...].astype(jnp.float32)
            out[...] = total.astype(jnp.bfloat16)

    return call(kernel, tuple(shapes), operands, "add_blocks", ordered)


def scatter_rows(mine, theirs, own_rows, size):
    chips = size // 2
    last = chips // 2
    right, left = [None] * HALVES, [None] * HALVES
    ordered = []
    for step in range(last, 0, -1):
        for r in range(HALVES):
            if step == last and r == 1:
                continue
            l = 1 - r
            if step == last:
                at_right = at_left = chips - 1
            else:
                at_right, at_left = 2 * step, 2 * step - 1
            sums = add_blocks(
                [
                    (mine[r], theirs[r], at_right, right[r]),
                    (mine[l], theirs[l], at_left, left[l]),
                ],
                own_rows,
                ordered,
            )
            ordered = [sums[0]]
            right[r] = lax.ppermute(sums[0], AXIS, ring(size, 1))
            left[l] = lax.ppermute(sums[1], AXIS, ring(size, -1))
    return list(zip(mine, theirs, right, left))


def finish_rows(halves, activations, gain, own_rows):
    width = activations.shape[1] // HALVES

    def kernel(*refs):
        refs, (act, gain_ref, block_out, normed, stream) = refs[:-5], refs[-5:]
        square = jnp.zeros((own_rows, 1), jnp.float32)
        for h in range(HALVES):
            mine, theirs, right, left = refs[4 * h : 4 * h + 4]
            at = slice(h * width, (h + 1) * width)
            total = act[:, at].astype(jnp.float32)
            for ref in (mine, theirs):
                total = total + ref[:own_rows, :].astype(jnp.float32)
            for ref in (right, left):
                total = total + ref[...].astype(jnp.float32)
            stream[:, at] = total
            block_out[:, at] = total.astype(jnp.bfloat16)
            square = square + jnp.sum(total * total, axis=1, keepdims=True)
        scale = lax.rsqrt(square * (1.0 / act.shape[1]) + 1e-05)
        normed[...] = (stream[...] * scale * gain_ref[...].astype(jnp.float32)).astype(
            jnp.bfloat16
        )

    out = jax.ShapeDtypeStruct(activations.shape, jnp.bfloat16)
    return call(
        kernel,
        (out, out),
        [array for half in halves for array in half] + [activations, gain],
        "finish_rows",
        scratch_shapes=[pltpu.VMEM(activations.shape, jnp.float32)],
    )


def body(
    activations,
    gate_weight,
    up_weight,
    down_weight,
    norm_gain_vector,
    shrink_factors,
    expand_factors,
    adapter_ranks,
    adapter_storage_slot,
    segment_start,
    segment_adapter,
):
    size = lax.axis_size(AXIS)
    me = lax.axis_index(AXIS).astype(jnp.int32).reshape(1)
    own_rows, model_width = activations.shape
    assert size & (size - 1) == 0 and own_rows & (own_rows - 1) == 0
    rows_tables = (segment_start[None], segment_adapter[None])
    all_tables = rows_tables + (adapter_ranks[None], adapter_storage_slot[None])

    parts = gather_rows(activations, size)
    rows, coeff = shrink_rows(parts, shrink_factors, all_tables, me, own_rows, size)

    bits = [1 << b for b in range(size.bit_length() - 1)]
    work = []
    for bit in bits[:-1]:
        received = lax.ppermute(coeff, AXIS, flip(size, bit))
        if bit == bits[1]:
            work = [matmul(rows, gate_weight, "gate_rows", 0, DEPTH_BLOCKS, [coeff])]
            gate = work[0]
        if bit == bits[2]:
            work = [matmul(rows, up_weight, "up_rows", 0, DEPTH_BLOCKS // 2, [coeff])]
            up = work[0]
        coeff = add_coefficients(coeff, received, work)
    received = lax.ppermute(coeff, AXIS, flip(size, bits[-1]))
    more = matmul(rows, up_weight, "up_rows", DEPTH_BLOCKS // 2, DEPTH_BLOCKS, [coeff])
    hidden = hidden_rows(
        gate, up, more, coeff, received, expand_factors, rows_tables, me, own_rows, size
    )

    mine, theirs = [None] * HALVES, [None] * HALVES
    ordered = []
    for h in range(HALVES):
        mine[h], part = down_rows(hidden, down_weight, h, ordered)
        ordered = [part]
        theirs[h] = lax.ppermute(part, AXIS, flip(size, 1))
    halves = scatter_rows(mine, theirs, own_rows, size)
    return finish_rows(halves, activations, norm_gain_vector[None], own_rows)


def solution(mesh):
    return jax.shard_map(
        body,
        mesh=mesh,
        in_specs=(
            P(("groups", "mp"), None),
            P(None, "mp"),
            P(None, "mp"),
            P("mp", None),
            P(),
            P("mp", None, None),
            P(None, None, "mp"),
            P(),
            P(),
            P("groups"),
            P("groups"),
        ),
        out_specs=(P(("groups", "mp"), None), P(("groups", "mp"), None)),
        check_vma=False,
    )
```

time: 124 us -> 119 us (0.960)
  Pallas kernels: 20.3 us -> 43 us
  waiting for transfers between devices: 42.8 us -> 32.4 us
  matrix products: 7.97 us -> 0 us
  local copies, waits for them, and re-layouts: 11.7 us -> 5.79 us
  other arithmetic: 1.96 us -> 0 us
  starting transfers between devices: 37.6 us -> 36 us
    pallas_call x8 -> x21, Pallas kernels: 20.3 us -> 43 us  [the longest x3 21.4 us: matmul(): pl.pallas_call(kernel, out_shape=jax.ShapeDtypeStruct((batch_rows, width)...]
    ppermute x35, waiting for transfers between devices: 42.3 us -> 30 us  [the longest x7 8.4 us: scatter_rows(): right[r] = lax.ppermute(sums[0], AXIS, ring(size, 1))]
    dot_general x2 -> x0, matrix products: 7.97 us -> none  [body(): jnp.dot(hidden, down_weight[:, h * width:(h + 1) * width], preferred_elem...]
    unnamed x28 -> x24, local copies, waits for them, and re-layouts: 10.5 us -> 5.77 us
    ppermute x4 -> x2, waiting for transfers between devices: 0.51 us -> 2.39 us  [gather_rows(): theirs.append(lax.ppermute(part, AXIS, flip(size, 1)))]
    convert_element_type x14 -> x0, other arithmetic: 1.52 us -> none  [the longest x1 0.87 us: body(): (stream_sum * scale_rows * norm_gain_vector.astype(jnp.float32)[None, :])...]
  transfers between devices with their start and end apart: 39 -> 37, of which waited for: 26 -> 25; matrix products, arithmetic and copies ran while one was open for 3% -> 0% of each run, Pallas kernels for 10% -> 19%
where the time goes in v3:
time: 119 us; the launch traced here: 118 us
  Pallas kernels  43 us (36%)
  starting transfers between devices  36 us (30%)
  waiting for transfers between devices  32.4 us (27%)
  local copies, waits for them, and re-layouts  5.79 us (5%)
    pallas_call x3, Pallas kernels, matmul(): pl.pallas_call(kernel, out_shape=jax.ShapeDtypeStruct((batch_rows, width)...  21.4 us
    pallas_call x2, Pallas kernels, down_rows(): pl.pallas_call(kernel, out_shape=(part, part), grid=(steps,), in_specs=[w...  14.5 us
    ppermute x7, starting transfers between devices, scatter_rows(): left[l] = lax.ppermute(sums[1], AXIS, ring(size, -1))  9.99 us
    ppermute x7, waiting for transfers between devices, scatter_rows(): right[r] = lax.ppermute(sums[0], AXIS, ring(size, 1))  8.4 us
    ppermute x3, starting transfers between devices, gather_rows(): right[0] = lax.ppermute(right[0], AXIS, ring(size, 1))  7.36 us
    pallas_call x16, Pallas kernels, call(): pl.pallas_call(run, out_shape=out_shape, in_specs=[whole(pltpu.SMEM if op...  7.14 us
    ppermute x7, starting transfers between devices, scatter_rows(): right[r] = lax.ppermute(sums[0], AXIS, ring(size, 1))  5.77 us
    unnamed x24, local copies, waits for them, and re-layouts  5.77 us
  transfers between devices with their start and end apart: 37, of which 25 were waited for; matrix products, arithmetic and copies ran while one was open for 0% of the time, Pallas kernels for 19%

profile of v3, /device:TPU:0, one launch (start us, length us, event | category | flops | bytes accessed | tf_op | source)
XLA Modules:
  0.0 118.1 jit_solution(16745976598637069749)
XLA Ops:
  0.6 0.9 copy-done
  1.6 3.1 %collective-permute-start = (bf16[16,4096]{1,0:T(8,128)(2,1)S(1)}, bf16[16,4096]{1,0:T(8,128)(2,1)S(1)}, u32[]{:S(2)}, u32[]{:S(2)}) collective-permute-start(bf16[16,4096]{1,0:T(8,128)(2,1)S(1)} %get-tuple-element.24), channel_id=1, source_target_pairs={{0,4},{1,5},{4,8},{5,9},{8,12},{9,13},{12,14},{13,15},{14,10},{15,... | collective-permute-start | bytes 393224 | tf_op jit(solution)/shard_map/ppermute | solution.py:126
  4.7 2.0 %collective-permute-start.1 = (bf16[16,4096]{1,0:T(8,128)(2,1)S(1)}, bf16[16,4096]{1,0:T(8,128)(2,1)S(1)}, u32[]{:S(2)}, u32[]{:S(2)}) collective-permute-start(bf16[16,4096]{1,0:T(8,128)(2,1)S(1)} %get-tuple-element.25), channel_id=1, source_target_pairs={{0,4},{1,5},{4,8},{5,9},{8,12},{9,13},{12,14},{13,15},{14,10},{15,... | collective-permute-start | bytes 393224 | tf_op jit(solution)/shard_map/ppermute | solution.py:128
  6.7 2.2 %collective-permute-done.refs_0_ = bf16[16,4096]{1,0:T(8,128)(2,1)S(1)} collective-permute-done((bf16[16,4096]{1,0:T(8,128)(2,1)S(1)}, bf16[16,4096]{1,0:T(8,128)(2,1)S(1)}, u32[]{:S(2)}, u32[]{:S(2)}) %collective-permute-start) | collective-permute-done | bytes 131104 | tf_op jit(solution)/shard_map/ppermute | solution.py:126
  8.9 2.1 %collective-permute-start.4 = (bf16[16,4096]{1,0:T(8,128)(2,1)S(1)}, bf16[16,4096]{1,0:T(8,128)(2,1)S(1)}, u32[]{:S(2)}, u32[]{:S(2)}) collective-permute-start(bf16[16,4096]{1,0:T(8,128)(2,1)S(1)} %collective-permute-done.refs_0_), channel_id=1, source_target_pairs={{0,4},{1,5},{4,8},{5,9},{8,12},{9,13},{12,14},{13,15},{14,10},{15,... | collective-permute-start | bytes 393224 | tf_op jit(solution)/shard_map/ppermute | solution.py:126
  11.8 1.8 %collective-permute-start.5 = (bf16[16,4096]{1,0:T(8,128)(2,1)S(1)}, bf16[16,4096]{1,0:T(8,128)(2,1)S(1)}, u32[]{:S(2)}, u32[]{:S(2)}) collective-permute-start(bf16[16,4096]{1,0:T(8,128)(2,1)S(1)} %collective-permute-done.1.refs_1_), channel_id=1, source_target_pairs={{0,4},{1,5},{4,8},{5,9},{8,12},{9,13},{12,14},{13,15},{14,10},{15,... | collective-permute-start | bytes 393224 | tf_op jit(solution)/shard_map/ppermute | solution.py:128
  13.8 1.3 %collective-permute-done.4.refs_4_ = bf16[16,4096]{1,0:T(8,128)(2,1)S(1)} collective-permute-done((bf16[16,4096]{1,0:T(8,128)(2,1)S(1)}, bf16[16,4096]{1,0:T(8,128)(2,1)S(1)}, u32[]{:S(2)}, u32[]{:S(2)}) %collective-permute-start.4) | collective-permute-done | bytes 131104 | tf_op jit(solution)/shard_map/ppermute | solution.py:126
  15.1 2.2 %collective-permute-start.9 = (bf16[16,4096]{1,0:T(8,128)(2,1)S(1)}, bf16[16,4096]{1,0:T(8,128)(2,1)S(1)}, u32[]{:S(2)}, u32[]{:S(2)}) collective-permute-start(bf16[16,4096]{1,0:T(8,128)(2,1)S(1)} %collective-permute-done.4.refs_4_), channel_id=1, source_target_pairs={{0,4},{1,5},{4,8},{5,9},{8,12},{9,13},{12,14},{13,15},{14,10},{15,... | collective-permute-start | bytes 393224 | tf_op jit(solution)/shard_map/ppermute | solution.py:126
  17.4 0.7 collective-permute-done.5.refs_5_
  18.2 1.5 %collective-permute-done.6.refs_6_ = bf16[16,4096]{1,0:T(8,128)(2,1)S(1)} collective-permute-done((bf16[16,4096]{1,0:T(8,128)(2,1)S(1)}, bf16[16,4096]{1,0:T(8,128)(2,1)S(1)}, u32[]{:S(2)}, u32[]{:S(2)}) %collective-permute-start.6) | collective-permute-done | bytes 131104 | tf_op jit(solution)/shard_map/ppermute | solution.py:129
  19.8 1.6 %collective-permute-start.10 = (bf16[16,4096]{1,0:T(8,128)(2,1)S(1)}, bf16[16,4096]{1,0:T(8,128)(2,1)S(1)}, u32[]{:S(2)}, u32[]{:S(2)}) collective-permute-start(bf16[16,4096]{1,0:T(8,128)(2,1)S(1)} %collective-permute-done.5.refs_5_), channel_id=1, source_target_pairs={{0,4},{1,5},{4,8},{5,9},{8,12},{9,13},{12,14},{13,15},{14,10},{15,... | collective-permute-start | bytes 393224 | tf_op jit(solution)/shard_map/ppermute | solution.py:128
  21.9 1.6 %collective-permute-start.13 = (bf16[16,4096]{1,0:T(8,128)(2,1)S(1)}, bf16[16,4096]{1,0:T(8,128)(2,1)S(1)}, u32[]{:S(2)}, u32[]{:S(2)}) collective-permute-start(bf16[16,4096]{1,0:T(8,128)(2,1)S(1)} %collective-permute-done.9.refs_0_), channel_id=1, source_target_pairs={{0,4},{1,5},{4,8},{5,9},{8,12},{9,13},{12,14},{13,15},{14,10},{15,... | collective-permute-start | bytes 393224 | tf_op jit(solution)/shard_map/ppermute | solution.py:132
  23.9 2.2 %collective-permute-done.10.refs_1_ = bf16[16,4096]{1,0:T(8,128)(2,1)S(1)} collective-permute-done((bf16[16,4096]{1,0:T(8,128)(2,1)S(1)}, bf16[16,4096]{1,0:T(8,128)(2,1)S(1)}, u32[]{:S(2)}, u32[]{:S(2)}) %collective-permute-start.10) | collective-permute-done | bytes 131104 | tf_op jit(solution)/shard_map/ppermute | solution.py:128
  26.1 1.6 %collective-permute-done.11.refs_2_ = bf16[16,4096]{1,0:T(8,128)(2,1)S(1)} collective-permute-done((bf16[16,4096]{1,0:T(8,128)(2,1)S(1)}, bf16[16,4096]{1,0:T(8,128)(2,1)S(1)}, u32[]{:S(2)}, u32[]{:S(2)}) %collective-permute-start.11) | collective-permute-done | bytes 131104 | tf_op jit(solution)/shard_map/ppermute | solution.py:129
  27.8 0.7 collective-permute-done.13.refs_4_
  28.5 1.3 %collective-permute-done.14.refs_5_ = bf16[16,4096]{1,0:T(8,128)(2,1)S(1)} collective-permute-done((bf16[16,4096]{1,0:T(8,128)(2,1)S(1)}, bf16[16,4096]{1,0:T(8,128)(2,1)S(1)}, u32[]{:S(2)}, u32[]{:S(2)}) %collective-permute-start.14) | collective-permute-done | bytes 131104 | tf_op jit(solution)/shard_map/ppermute | solution.py:133
  29.9 2.4 %collective-permute-done.16.refs_10_ = bf16[48,8192]{1,0:T(8,128)(2,1)} collective-permute-done((bf16[48,8192]{1,0:T(8,128)(2,1)S(1)}, bf16[48,8192]{1,0:T(8,128)(2,1)}, u32[]{:S(2)}, u32[]{:S(2)}) %collective-permute-start.16) | collective-permute-done | bytes 786464 | tf_op jit(solution)/shard_map/ppermute | solution.py:138
  32.3 0.9 copy-done.1
  33.3 1.2 %copy-done.4 = bf16[1,8192,64]{1,2,0:T(8,128)(2,1)S(1)} copy-done((bf16[1,8192,64]{1,2,0:T(8,128)(2,1)S(1)}, bf16[1,8192,64]{1,2,0:T(8,128)(2,1)}, u32[]{:S(2)}) %copy-start.4) | copy-done | bytes 1048600
  37.1 4.1 %shrink_rows.1 = (bf16[256,8192]{1,0:T(8,128)(2,1)S(1)}, bf16[256,64]{1,0:T(8,128)(2,1)S(1)}) custom-call(s32[1]{0:T(128)} %bitcast.refs_0_, s32[1,32]{1,0:T(1,128)S(1)} %bitcast.11, s32[1,32]{1,0:T(1,128)S(1)} %bitcast.13, s32[1,16]{1,0:T(1,128)S(1)} %bitcast.15, s32[1,16]{1,0:T(1,128)S(1)} %bitcast.16, bf16[16,8192]{1,0:T(8,128)(2,1)S(1)} %copy-done.1, ...), custom_call_target="tpu_custom_call" | custom-call | flops 268435456 | bytes 8388608 | tf_op jit(solution)/shard_map/shrink_rows/pallas_call | solution.py:75
  41.4 1.1 collective-permute-done.17.refs_1_
  43.1 10.4 %gate_rows.1.refs_2_.refs_6_ = f32[256,896]{1,0:T(8,128)S(1)} custom-call(bf16[256,8192]{1,0:T(8,128)(2,1)S(1)} %get-tuple-element.27.rows_ref, bf16[8192,896]{1,0:T(8,128)(2,1)} %weight_ref.3, bf16[256,64]{1,0:T(8,128)(2,1)S(1)} %add_coefficients.3.rest_0_.refs_0_), custom_call_target="tpu_custom_call" | custom-call | flops 3758096384 | bytes 14680064 | tf_op jit(solution)/shard_map/gate_rows/pallas_call | solution.py:235
  53.5 1.2 %collective-permute-start.19 = (bf16[256,64]{1,0:T(8,128)(2,1)S(1)}, bf16[256,64]{1,0:T(8,128)(2,1)S(1)}, u32[]{:S(2)}, u32[]{:S(2)}) collective-permute-start(bf16[256,64]{1,0:T(8,128)(2,1)S(1)} %add_coefficients.4.rest_0_.refs_0_), channel_id=1, source_target_pairs={{0,4},{1,5},{2,6},{3,7},{4,0},{5,1},{6,2},{7,3},{8,12},{9,13},{10,... | collective-permute-start | bytes 98312 | tf_op jit(solution)/shard_map/ppermute | solution.py:446
  54.7 5.5 %up_rows.2.refs_2_.refs_7_ = f32[256,896]{1,0:T(8,128)S(1)} custom-call(bf16[256,8192]{1,0:T(8,128)(2,1)S(1)} %get-tuple-element.27.rows_ref, bf16[8192,896]{1,0:T(8,128)(2,1)} %weight_ref.5, bf16[256,64]{1,0:T(8,128)(2,1)S(1)} %add_coefficients.4.rest_0_.refs_0_), custom_call_target="tpu_custom_call" | custom-call | flops 1879048192 | bytes 7340032 | tf_op jit(solution)/shard_map/up_rows/pallas_call | solution.py:235
  60.3 1.9 %collective-permute-start.20 = (bf16[256,64]{1,0:T(8,128)(2,1)S(1)}, bf16[256,64]{1,0:T(8,128)(2,1)S(1)}, u32[]{:S(2)}, u32[]{:S(2)}) collective-permute-start(bf16[256,64]{1,0:T(8,128)(2,1)S(1)} %add_coefficients.5.rest_0_.refs_3_), channel_id=1, source_target_pairs={{0,8},{1,9},{2,10},{3,11},{4,12},{5,13},{6,14},{7,15},{8,0},{9,1},... | collective-permute-start | bytes 98312 | tf_op jit(solution)/shard_map/ppermute | solution.py:454
  62.2 5.5 %up_rows.3.refs_8_ = f32[256,896]{1,0:T(8,128)S(1)} custom-call(bf16[256,8192]{1,0:T(8,128)(2,1)S(1)} %get-tuple-element.27.rows_ref, bf16[8192,896]{1,0:T(8,128)(2,1)} %weight_ref.5, bf16[256,64]{1,0:T(8,128)(2,1)S(1)} %add_coefficients.5.rest_0_.refs_3_), custom_call_target="tpu_custom_call" | custom-call | flops 1879048192 | bytes 7340032 | tf_op jit(solution)/shard_map/up_rows/pallas_call | solution.py:235
  67.8 1.2 %hidden_rows.1.hidden_ref = bf16[256,896]{1,0:T(8,128)(2,1)S(1)} custom-call(s32[1]{0:T(128)} %bitcast.refs_0_, s32[1,32]{1,0:T(1,128)S(1)} %bitcast.12, s32[1,32]{1,0:T(1,128)S(1)} %bitcast.14, bf16[256,64]{1,0:T(8,128)(2,1)S(1)} %add_coefficients.5.rest_0_.refs_3_, bf16[256,64]{1,0:T(8,128)(2,1)S(1)} %collective-permute-done.20.refs_4_, ...), custom_call_target="tpu_custom_call" | custom-call | flops 469762048 | bytes 1835008 | tf_op jit(solution)/shard_map/hidden_rows/pallas_call | solution.py:75
  69.0 7.2 %down_rows.2 = (bf16[128,4096]{1,0:T(8,128)(2,1)S(1)}, bf16[128,4096]{1,0:T(8,128)(2,1)S(1)}) custom-call(bf16[256,896]{1,0:T(8,128)(2,1)S(1)} %hidden_rows.1.hidden_ref, bf16[896,8192]{1,0:T(8,128)(2,1)} %weight.3), custom_call_target="tpu_custom_call" | custom-call | flops 1879048192 | bytes 7340032 | tf_op jit(solution)/shard_map/down_rows/pallas_call | solution.py:320
  76.2 7.2 %down_rows.3 = (bf16[128,4096]{1,0:T(8,128)(2,1)S(1)}, bf16[128,4096]{1,0:T(8,128)(2,1)S(1)}) custom-call(bf16[256,896]{1,0:T(8,128)(2,1)S(1)} %hidden_rows.1.hidden_ref, bf16[896,8192]{1,0:T(8,128)(2,1)} %weight.3, bf16[128,4096]{1,0:T(8,128)(2,1)S(1)} %get-tuple-element.29.rest_0_), custom_call_target="tpu_custom_call" | custom-call | flops 1879048192 | bytes 7340032 | tf_op jit(solution)/shard_map/down_rows/pallas_call | solution.py:320
  84.1 2.1 %collective-permute-done.22.refs_3_.refs_4_.refs_1_.refs_5_ = bf16[128,4096]{1,0:T(8,128)(2,1)S(1)} collective-permute-done((bf16[128,4096]{1,0:T(8,128)(2,1)S(1)}, bf16[128,4096]{1,0:T(8,128)(2,1)S(1)}, u32[]{:S(2)}, u32[]{:S(2)}) %collective-permute-start.22) | collective-permute-done | bytes 1048608 | tf_op jit(solution)/shard_map/ppermute | solution.py:465
  86.2 1.5 %collective-permute-done.21.refs_1_.refs_3_.refs_4_ = bf16[128,4096]{1,0:T(8,128)(2,1)S(1)} collective-permute-done((bf16[128,4096]{1,0:T(8,128)(2,1)S(1)}, bf16[128,4096]{1,0:T(8,128)(2,1)S(1)}, u32[]{:S(2)}, u32[]{:S(2)}) %collective-permute-start.21) | collective-permute-done | bytes 1048608 | tf_op jit(solution)/shard_map/ppermute | solution.py:465
  87.8 1.2 %collective-permute-start.23 = (bf16[16,4096]{1,0:T(8,128)(2,1)S(1)}, bf16[16,4096]{1,0:T(8,128)(2,1)S(1)}, u32[]{:S(2)}, u32[]{:S(2)}) collective-permute-start(bf16[16,4096]{1,0:T(8,128)(2,1)S(1)} %get-tuple-element.32.refs_6_), channel_id=1, source_target_pairs={{0,4},{1,5},{4,8},{5,9},{8,12},{9,13},{12,14},{13,15},{14,10},{15,... | collective-permute-start | bytes 393224 | tf_op jit(solution)/shard_map/ppermute | solution.py:383
  89.0 0.9 collective-permute-start.24
  89.9 3.5 %collective-permute-done.23.refs_2_ = bf16[16,4096]{1,0:T(8,128)(2,1)S(1)} collective-permute-done((bf16[16,4096]{1,0:T(8,128)(2,1)S(1)}, bf16[16,4096]{1,0:T(8,128)(2,1)S(1)}, u32[]{:S(2)}, u32[]{:S(2)}) %collective-permute-start.23) | collective-permute-done | bytes 131104 | tf_op jit(solution)/shard_map/ppermute | solution.py:383
  93.4 0.9 collective-permute-done.24.refs_5_
  94.9 1.5 %collective-permute-start.26 = (bf16[16,4096]{1,0:T(8,128)(2,1)S(1)}, bf16[16,4096]{1,0:T(8,128)(2,1)S(1)}, u32[]{:S(2)}, u32[]{:S(2)}) collective-permute-start(bf16[16,4096]{1,0:T(8,128)(2,1)S(1)} %get-tuple-element.35), channel_id=1, source_target_pairs={{0,2},{1,3},{4,0},{5,1},{8,4},{9,5},{12,8},{13,9},{14,12},{15,13},... | collective-permute-start | bytes 393224 | tf_op jit(solution)/shard_map/ppermute | solution.py:384
  97.1 1.5 %collective-permute-start.30 = (bf16[16,4096]{1,0:T(8,128)(2,1)S(1)}, bf16[16,4096]{1,0:T(8,128)(2,1)S(1)}, u32[]{:S(2)}, u32[]{:S(2)}) collective-permute-start(bf16[16,4096]{1,0:T(8,128)(2,1)S(1)} %get-tuple-element.39), channel_id=1, source_target_pairs={{0,2},{1,3},{4,0},{5,1},{8,4},{9,5},{12,8},{13,9},{14,12},{15,13},... | collective-permute-start | bytes 393224 | tf_op jit(solution)/shard_map/ppermute | solution.py:384
  98.6 1.8 %collective-permute-done.25.refs_2_ = bf16[16,4096]{1,0:T(8,128)(2,1)S(1)} collective-permute-done((bf16[16,4096]{1,0:T(8,128)(2,1)S(1)}, bf16[16,4096]{1,0:T(8,128)(2,1)S(1)}, u32[]{:S(2)}, u32[]{:S(2)}) %collective-permute-start.25) | collective-permute-done | bytes 131104 | tf_op jit(solution)/shard_map/ppermute | solution.py:383
  100.8 0.8 collective-permute-start.27
  101.6 1.2 %collective-permute-start.28 = (bf16[16,4096]{1,0:T(8,128)(2,1)S(1)}, bf16[16,4096]{1,0:T(8,128)(2,1)S(1)}, u32[]{:S(2)}, u32[]{:S(2)}) collective-permute-start(bf16[16,4096]{1,0:T(8,128)(2,1)S(1)} %get-tuple-element.38), channel_id=1, source_target_pairs={{0,2},{1,3},{4,0},{5,1},{8,4},{9,5},{12,8},{13,9},{14,12},{15,13},... | collective-permute-start | bytes 393224 | tf_op jit(solution)/shard_map/ppermute | solution.py:384
  103.8 1.6 %collective-permute-start.33 = (bf16[16,4096]{1,0:T(8,128)(2,1)S(1)}, bf16[16,4096]{1,0:T(8,128)(2,1)S(1)}, u32[]{:S(2)}, u32[]{:S(2)}) collective-permute-start(bf16[16,4096]{1,0:T(8,128)(2,1)S(1)} %get-tuple-element.42), channel_id=1, source_target_pairs={{0,2},{1,3},{4,0},{5,1},{8,4},{9,5},{12,8},{13,9},{14,12},{15,13},... | collective-permute-start | bytes 393224 | tf_op jit(solution)/shard_map/ppermute | solution.py:384
  106.7 1.7 %collective-permute-start.31 = (bf16[16,4096]{1,0:T(8,128)(2,1)S(1)}, bf16[16,4096]{1,0:T(8,128)(2,1)S(1)}, u32[]{:S(2)}, u32[]{:S(2)}) collective-permute-start(bf16[16,4096]{1,0:T(8,128)(2,1)S(1)} %get-tuple-element.41.refs_6_), channel_id=1, source_target_pairs={{0,4},{1,5},{4,8},{5,9},{8,12},{9,13},{12,14},{13,15},{14,10},{15,... | collective-permute-start | bytes 393224 | tf_op jit(solution)/shard_map/ppermute | solution.py:383
  108.9 1.0 collective-permute-done.33.refs_5_
  110.0 1.7 %collective-permute-start.34 = (bf16[16,4096]{1,0:T(8,128)(2,1)S(1)}, bf16[16,4096]{1,0:T(8,128)(2,1)S(1)}, u32[]{:S(2)}, u32[]{:S(2)}) collective-permute-start(bf16[16,4096]{1,0:T(8,128)(2,1)S(1)} %get-tuple-element.43), channel_id=1, source_target_pairs={{0,2},{1,3},{4,0},{5,1},{8,4},{9,5},{12,8},{13,9},{14,12},{15,13},... | collective-permute-start | bytes 393224 | tf_op jit(solution)/shard_map/ppermute | solution.py:384
  112.1 1.6 %collective-permute-start.36 = (bf16[16,4096]{1,0:T(8,128)(2,1)S(1)}, bf16[16,4096]{1,0:T(8,128)(2,1)S(1)}, u32[]{:S(2)}, u32[]{:S(2)}) collective-permute-start(bf16[16,4096]{1,0:T(8,128)(2,1)S(1)} %get-tuple-element.45), channel_id=1, source_target_pairs={{0,2},{1,3},{4,0},{5,1},{8,4},{9,5},{12,8},{13,9},{14,12},{15,13},... | collective-permute-start | bytes 393224 | tf_op jit(solution)/shard_map/ppermute | solution.py:384
  113.7 1.3 %collective-permute-done.34.refs_3_ = bf16[16,4096]{1,0:T(8,128)(2,1)S(1)} collective-permute-done((bf16[16,4096]{1,0:T(8,128)(2,1)S(1)}, bf16[16,4096]{1,0:T(8,128)(2,1)S(1)}, u32[]{:S(2)}, u32[]{:S(2)}) %collective-permute-start.34) | collective-permute-done | bytes 131104 | tf_op jit(solution)/shard_map/ppermute | solution.py:384
  115.0 1.6 %collective-permute-done.35.refs_6_ = bf16[16,4096]{1,0:T(8,128)(2,1)S(1)} collective-permute-done((bf16[16,4096]{1,0:T(8,128)(2,1)S(1)}, bf16[16,4096]{1,0:T(8,128)(2,1)S(1)}, u32[]{:S(2)}, u32[]{:S(2)}) %collective-permute-start.35) | collective-permute-done | bytes 131104 | tf_op jit(solution)/shard_map/ppermute | solution.py:383
  117.1 1.0 finish_rows.1
  (72 shorter events, 11.8 us)
Async XLA Ops:
  0.6 1.0 copy-start
  1.6 7.3 %collective-permute-start = (bf16[16,4096]{1,0:T(8,128)(2,1)S(1)}, bf16[16,4096]{1,0:T(8,128)(2,1)S(1)}, u32[]{:S(2)}, u32[]{:S(2)}) collective-permute-start(bf16[16,4096]{1,0:T(8,128)(2,1)S(1)} %get-tuple-element.24), channel_id=1, source_target_pairs={{0,4},{1,5},{4,8},{5,9},{8,12},{9,13},{12,14},{13,15},{14,10},{15,... | collective-permute-start | bytes 393224 | tf_op jit(solution)/shard_map/ppermute | solution.py:126
  4.7 6.4 %collective-permute-start.3 = (bf16[16,4096]{1,0:T(8,128)(2,1)S(1)}, bf16[16,4096]{1,0:T(8,128)(2,1)S(1)}, u32[]{:S(2)}, u32[]{:S(2)}) collective-permute-start(bf16[16,4096]{1,0:T(8,128)(2,1)S(1)} %get-tuple-element.25), channel_id=1, source_target_pairs={{0,2},{1,3},{4,0},{5,1},{8,4},{9,5},{12,8},{13,9},{14,12},{15,13},... | collective-permute-start | bytes 393224 | tf_op jit(solution)/shard_map/ppermute | solution.py:127
  4.7 7.1 %collective-permute-start.1 = (bf16[16,4096]{1,0:T(8,128)(2,1)S(1)}, bf16[16,4096]{1,0:T(8,128)(2,1)S(1)}, u32[]{:S(2)}, u32[]{:S(2)}) collective-permute-start(bf16[16,4096]{1,0:T(8,128)(2,1)S(1)} %get-tuple-element.25), channel_id=1, source_target_pairs={{0,4},{1,5},{4,8},{5,9},{8,12},{9,13},{12,14},{13,15},{14,10},{15,... | collective-permute-start | bytes 393224 | tf_op jit(solution)/shard_map/ppermute | solution.py:128
  6.7 6.8 %collective-permute-start.2 = (bf16[16,4096]{1,0:T(8,128)(2,1)S(1)}, bf16[16,4096]{1,0:T(8,128)(2,1)S(1)}, u32[]{:S(2)}, u32[]{:S(2)}) collective-permute-start(bf16[16,4096]{1,0:T(8,128)(2,1)S(1)} %get-tuple-element.24), channel_id=1, source_target_pairs={{0,2},{1,3},{4,0},{5,1},{8,4},{9,5},{12,8},{13,9},{14,12},{15,13},... | collective-permute-start | bytes 393224 | tf_op jit(solution)/shard_map/ppermute | solution.py:129
  6.7 12.9 %collective-permute-start.8 = (bf16[16,8192]{1,0:T(8,128)(2,1)S(1)}, bf16[16,8192]{1,0:T(8,128)(2,1)S(1)}, u32[]{:S(2)}, u32[]{:S(2)}) collective-permute-start(bf16[16,8192]{1,0:T(8,128)(2,1)S(1)} %copy-done), channel_id=1, source_target_pairs={{0,1},{1,0},{2,3},{3,2},{4,5},{5,4},{6,7},{7,6},{8,9},{9,8},{10,11... | collective-permute-start | bytes 786440 | tf_op jit(solution)/shard_map/ppermute | solution.py:119
  8.9 6.2 %collective-permute-start.4 = (bf16[16,4096]{1,0:T(8,128)(2,1)S(1)}, bf16[16,4096]{1,0:T(8,128)(2,1)S(1)}, u32[]{:S(2)}, u32[]{:S(2)}) collective-permute-start(bf16[16,4096]{1,0:T(8,128)(2,1)S(1)} %collective-permute-done.refs_0_), channel_id=1, source_target_pairs={{0,4},{1,5},{4,8},{5,9},{8,12},{9,13},{12,14},{13,15},{14,10},{15,... | collective-permute-start | bytes 393224 | tf_op jit(solution)/shard_map/ppermute | solution.py:126
  11.1 6.2 %collective-permute-start.7 = (bf16[16,4096]{1,0:T(8,128)(2,1)S(1)}, bf16[16,4096]{1,0:T(8,128)(2,1)S(1)}, u32[]{:S(2)}, u32[]{:S(2)}) collective-permute-start(bf16[16,4096]{1,0:T(8,128)(2,1)S(1)} %collective-permute-done.3.refs_3_), channel_id=1, source_target_pairs={{0,2},{1,3},{4,0},{5,1},{8,4},{9,5},{12,8},{13,9},{14,12},{15,13},... | collective-permute-start | bytes 393224 | tf_op jit(solution)/shard_map/ppermute | solution.py:127
  11.8 6.4 %collective-permute-start.5 = (bf16[16,4096]{1,0:T(8,128)(2,1)S(1)}, bf16[16,4096]{1,0:T(8,128)(2,1)S(1)}, u32[]{:S(2)}, u32[]{:S(2)}) collective-permute-start(bf16[16,4096]{1,0:T(8,128)(2,1)S(1)} %collective-permute-done.1.refs_1_), channel_id=1, source_target_pairs={{0,4},{1,5},{4,8},{5,9},{8,12},{9,13},{12,14},{13,15},{14,10},{15,... | collective-permute-start | bytes 393224 | tf_op jit(solution)/shard_map/ppermute | solution.py:128
  13.5 6.1 %collective-permute-start.6 = (bf16[16,4096]{1,0:T(8,128)(2,1)S(1)}, bf16[16,4096]{1,0:T(8,128)(2,1)S(1)}, u32[]{:S(2)}, u32[]{:S(2)}) collective-permute-start(bf16[16,4096]{1,0:T(8,128)(2,1)S(1)} %collective-permute-done.2.refs_2_), channel_id=1, source_target_pairs={{0,2},{1,3},{4,0},{5,1},{8,4},{9,5},{12,8},{13,9},{14,12},{15,13},... | collective-permute-start | bytes 393224 | tf_op jit(solution)/shard_map/ppermute | solution.py:129
  15.1 6.8 %collective-permute-start.9 = (bf16[16,4096]{1,0:T(8,128)(2,1)S(1)}, bf16[16,4096]{1,0:T(8,128)(2,1)S(1)}, u32[]{:S(2)}, u32[]{:S(2)}) collective-permute-start(bf16[16,4096]{1,0:T(8,128)(2,1)S(1)} %collective-permute-done.4.refs_4_), channel_id=1, source_target_pairs={{0,4},{1,5},{4,8},{5,9},{8,12},{9,13},{12,14},{13,15},{14,10},{15,... | collective-permute-start | bytes 393224 | tf_op jit(solution)/shard_map/ppermute | solution.py:126
  17.3 6.2 %collective-permute-start.12 = (bf16[16,4096]{1,0:T(8,128)(2,1)S(1)}, bf16[16,4096]{1,0:T(8,128)(2,1)S(1)}, u32[]{:S(2)}, u32[]{:S(2)}) collective-permute-start(bf16[16,4096]{1,0:T(8,128)(2,1)S(1)} %collective-permute-done.7.refs_7_), channel_id=1, source_target_pairs={{0,2},{1,3},{4,0},{5,1},{8,4},{9,5},{12,8},{13,9},{14,12},{15,13},... | collective-permute-start | bytes 393224 | tf_op jit(solution)/shard_map/ppermute | solution.py:127
  19.7 10.2 %collective-permute-start.15 = (bf16[64,8192]{1,0:T(8,128)(2,1)S(1)}, bf16[64,8192]{1,0:T(8,128)(2,1)S(1)}, u32[]{:S(2)}, u32[]{:S(2)}) collective-permute-start(bf16[64,8192]{1,0:T(8,128)(2,1)S(1)} %join_pieces.2.refs_6_), channel_id=1, source_target_pairs={{0,1},{1,0},{2,3},{3,2},{4,5},{5,4},{6,7},{7,6},{8,9},{9,8},{10,11... | collective-permute-start | bytes 3145736 | tf_op jit(solution)/shard_map/ppermute | solution.py:138
  19.8 6.3 %collective-permute-start.10 = (bf16[16,4096]{1,0:T(8,128)(2,1)S(1)}, bf16[16,4096]{1,0:T(8,128)(2,1)S(1)}, u32[]{:S(2)}, u32[]{:S(2)}) collective-permute-start(bf16[16,4096]{1,0:T(8,128)(2,1)S(1)} %collective-permute-done.5.refs_5_), channel_id=1, source_target_pairs={{0,4},{1,5},{4,8},{5,9},{8,12},{9,13},{12,14},{13,15},{14,10},{15,... | collective-permute-start | bytes 393224 | tf_op jit(solution)/shard_map/ppermute | solution.py:128
  21.4 6.3 %collective-permute-start.11 = (bf16[16,4096]{1,0:T(8,128)(2,1)S(1)}, bf16[16,4096]{1,0:T(8,128)(2,1)S(1)}, u32[]{:S(2)}, u32[]{:S(2)}) collective-permute-start(bf16[16,4096]{1,0:T(8,128)(2,1)S(1)} %collective-permute-done.6.refs_6_), channel_id=1, source_target_pairs={{0,2},{1,3},{4,0},{5,1},{8,4},{9,5},{12,8},{13,9},{14,12},{15,13},... | collective-permute-start | bytes 393224 | tf_op jit(solution)/shard_map/ppermute | solution.py:129
  21.9 6.6 %collective-permute-start.13 = (bf16[16,4096]{1,0:T(8,128)(2,1)S(1)}, bf16[16,4096]{1,0:T(8,128)(2,1)S(1)}, u32[]{:S(2)}, u32[]{:S(2)}) collective-permute-start(bf16[16,4096]{1,0:T(8,128)(2,1)S(1)} %collective-permute-done.9.refs_0_), channel_id=1, source_target_pairs={{0,4},{1,5},{4,8},{5,9},{8,12},{9,13},{12,14},{13,15},{14,10},{15,... | collective-permute-start | bytes 393224 | tf_op jit(solution)/shard_map/ppermute | solution.py:132
  23.4 6.3 %collective-permute-start.14 = (bf16[16,4096]{1,0:T(8,128)(2,1)S(1)}, bf16[16,4096]{1,0:T(8,128)(2,1)S(1)}, u32[]{:S(2)}, u32[]{:S(2)}) collective-permute-start(bf16[16,4096]{1,0:T(8,128)(2,1)S(1)} %collective-permute-done.12.refs_3_), channel_id=1, source_target_pairs={{0,2},{1,3},{4,0},{5,1},{8,4},{9,5},{12,8},{13,9},{14,12},{15,13},... | collective-permute-start | bytes 393224 | tf_op jit(solution)/shard_map/ppermute | solution.py:133
  29.8 2.5 %collective-permute-start.16 = (bf16[48,8192]{1,0:T(8,128)(2,1)S(1)}, bf16[48,8192]{1,0:T(8,128)(2,1)}, u32[]{:S(2)}, u32[]{:S(2)}) collective-permute-start(bf16[48,8192]{1,0:T(8,128)(2,1)S(1)} %join_pieces.3.refs_7_), channel_id=1, source_target_pairs={{0,1},{1,0},{2,3},{3,2},{4,5},{5,4},{6,7},{7,6},{8,9},{9,8},{10,11... | collective-permute-start | bytes 2359304 | tf_op jit(solution)/shard_map/ppermute | solution.py:138
  32.3 1.0 copy-start.1
  33.3 1.2 %copy-start.4 = (bf16[1,8192,64]{1,2,0:T(8,128)(2,1)S(1)}, bf16[1,8192,64]{1,2,0:T(8,128)(2,1)}, u32[]{:S(2)}) copy-start(bf16[1,8192,64]{1,2,0:T(8,128)(2,1)} %param.16) | copy-start | bytes 3145732
  34.5 0.7 copy-start.5
  35.2 0.7 copy-start.7
  35.8 0.7 copy-start.9
  41.2 1.3 %collective-permute-start.17 = (bf16[256,64]{1,0:T(8,128)(2,1)S(1)}, bf16[256,64]{1,0:T(8,128)(2,1)S(1)}, u32[]{:S(2)}, u32[]{:S(2)}) collective-permute-start(bf16[256,64]{1,0:T(8,128)(2,1)S(1)} %get-tuple-element.26.refs_0_), channel_id=1, source_target_pairs={{0,1},{1,0},{2,3},{3,2},{4,5},{5,4},{6,7},{7,6},{8,9},{9,8},{10,11... | collective-permute-start | bytes 98312 | tf_op jit(solution)/shard_map/ppermute | solution.py:446
  42.6 10.9 %collective-permute-start.18 = (bf16[256,64]{1,0:T(8,128)(2,1)S(1)}, bf16[256,64]{1,0:T(8,128)(2,1)S(1)}, u32[]{:S(2)}, u32[]{:S(2)}) collective-permute-start(bf16[256,64]{1,0:T(8,128)(2,1)S(1)} %add_coefficients.3.rest_0_.refs_0_), channel_id=1, source_target_pairs={{0,2},{1,3},{2,0},{3,1},{4,6},{5,7},{6,4},{7,5},{8,10},{9,11},{10,... | collective-permute-start | bytes 98312 | tf_op jit(solution)/shard_map/ppermute | solution.py:446
  53.5 6.8 %collective-permute-start.19 = (bf16[256,64]{1,0:T(8,128)(2,1)S(1)}, bf16[256,64]{1,0:T(8,128)(2,1)S(1)}, u32[]{:S(2)}, u32[]{:S(2)}) collective-permute-start(bf16[256,64]{1,0:T(8,128)(2,1)S(1)} %add_coefficients.4.rest_0_.refs_0_), channel_id=1, source_target_pairs={{0,4},{1,5},{2,6},{3,7},{4,0},{5,1},{6,2},{7,3},{8,12},{9,13},{10,... | collective-permute-start | bytes 98312 | tf_op jit(solution)/shard_map/ppermute | solution.py:446
  60.2 7.5 %copy-start.3 = (bf16[16,64,896]{2,1,0:T(8,128)(2,1)S(1)}, bf16[16,64,896]{2,1,0:T(8,128)(2,1)}, u32[]{:S(2)}) copy-start(bf16[16,64,896]{2,1,0:T(8,128)(2,1)} %param.17) | copy-start | bytes 5505028
  60.3 7.5 %copy-start.6 = (s32[32]{0:T(128)S(1)}, s32[32]{0:T(128)}, u32[]{:S(2)}) copy-start(s32[32]{0:T(128)} %param.20) | copy-start | bytes 388
  60.3 7.5 %copy-start.8 = (s32[32]{0:T(128)S(1)}, s32[32]{0:T(128)}, u32[]{:S(2)}) copy-start(s32[32]{0:T(128)} %param.21) | copy-start | bytes 388
  60.3 7.4 %collective-permute-start.20 = (bf16[256,64]{1,0:T(8,128)(2,1)S(1)}, bf16[256,64]{1,0:T(8,128)(2,1)S(1)}, u32[]{:S(2)}, u32[]{:S(2)}) collective-permute-start(bf16[256,64]{1,0:T(8,128)(2,1)S(1)} %add_coefficients.5.rest_0_.refs_3_), channel_id=1, source_target_pairs={{0,8},{1,9},{2,10},{3,11},{4,12},{5,13},{6,14},{7,15},{8,0},{9,1},... | collective-permute-start | bytes 98312 | tf_op jit(solution)/shard_map/ppermute | solution.py:454
  83.5 2.7 %collective-permute-start.22 = (bf16[128,4096]{1,0:T(8,128)(2,1)S(1)}, bf16[128,4096]{1,0:T(8,128)(2,1)S(1)}, u32[]{:S(2)}, u32[]{:S(2)}) collective-permute-start(bf16[128,4096]{1,0:T(8,128)(2,1)S(1)} %get-tuple-element.31), channel_id=1, source_target_pairs={{0,1},{1,0},{2,3},{3,2},{4,5},{5,4},{6,7},{7,6},{8,9},{9,8},{10,11... | collective-permute-start | bytes 3145736 | tf_op jit(solution)/shard_map/ppermute | solution.py:465
  83.6 4.1 %collective-permute-start.21 = (bf16[128,4096]{1,0:T(8,128)(2,1)S(1)}, bf16[128,4096]{1,0:T(8,128)(2,1)S(1)}, u32[]{:S(2)}, u32[]{:S(2)}) collective-permute-start(bf16[128,4096]{1,0:T(8,128)(2,1)S(1)} %get-tuple-element.29.rest_0_), channel_id=1, source_target_pairs={{0,1},{1,0},{2,3},{3,2},{4,5},{5,4},{6,7},{7,6},{8,9},{9,8},{10,11... | collective-permute-start | bytes 3145736 | tf_op jit(solution)/shard_map/ppermute | solution.py:465
  87.8 25.9 %copy-start.11 = (bf16[8192]{0:T(1024)(128)(2,1)S(1)}, bf16[8192]{0:T(1024)(128)(2,1)}, u32[]{:S(2)}) copy-start(bf16[8192]{0:T(1024)(128)(2,1)} %param.15) | copy-start | bytes 49156
  87.8 29.3 %copy-start.2 = (bf16[16,8192]{1,0:T(8,128)(2,1)S(1)}, bf16[16,8192]{1,0:T(8,128)(2,1)}, u32[]{:S(2)}) copy-start(bf16[16,8192]{1,0:T(8,128)(2,1)} %refs_8_.1) | copy-start | bytes 786436
  87.8 5.6 %collective-permute-start.23 = (bf16[16,4096]{1,0:T(8,128)(2,1)S(1)}, bf16[16,4096]{1,0:T(8,128)(2,1)S(1)}, u32[]{:S(2)}, u32[]{:S(2)}) collective-permute-start(bf16[16,4096]{1,0:T(8,128)(2,1)S(1)} %get-tuple-element.32.refs_6_), channel_id=1, source_target_pairs={{0,4},{1,5},{4,8},{5,9},{8,12},{9,13},{12,14},{13,15},{14,10},{15,... | collective-permute-start | bytes 393224 | tf_op jit(solution)/shard_map/ppermute | solution.py:383
  89.0 5.3 %collective-permute-start.24 = (bf16[16,4096]{1,0:T(8,128)(2,1)S(1)}, bf16[16,4096]{1,0:T(8,128)(2,1)S(1)}, u32[]{:S(2)}, u32[]{:S(2)}) collective-permute-start(bf16[16,4096]{1,0:T(8,128)(2,1)S(1)} %get-tuple-element.33), channel_id=1, source_target_pairs={{0,2},{1,3},{4,0},{5,1},{8,4},{9,5},{12,8},{13,9},{14,12},{15,13},... | collective-permute-start | bytes 393224 | tf_op jit(solution)/shard_map/ppermute | solution.py:384
  94.4 6.1 %collective-permute-start.25 = (bf16[16,4096]{1,0:T(8,128)(2,1)S(1)}, bf16[16,4096]{1,0:T(8,128)(2,1)S(1)}, u32[]{:S(2)}, u32[]{:S(2)}) collective-permute-start(bf16[16,4096]{1,0:T(8,128)(2,1)S(1)} %get-tuple-element.34.refs_4_), channel_id=1, source_target_pairs={{0,4},{1,5},{4,8},{5,9},{8,12},{9,13},{12,14},{13,15},{14,10},{15,... | collective-permute-start | bytes 393224 | tf_op jit(solution)/shard_map/ppermute | solution.py:383
  94.9 5.8 %collective-permute-start.26 = (bf16[16,4096]{1,0:T(8,128)(2,1)S(1)}, bf16[16,4096]{1,0:T(8,128)(2,1)S(1)}, u32[]{:S(2)}, u32[]{:S(2)}) collective-permute-start(bf16[16,4096]{1,0:T(8,128)(2,1)S(1)} %get-tuple-element.35), channel_id=1, source_target_pairs={{0,2},{1,3},{4,0},{5,1},{8,4},{9,5},{12,8},{13,9},{14,12},{15,13},... | collective-permute-start | bytes 393224 | tf_op jit(solution)/shard_map/ppermute | solution.py:384
  96.5 6.7 %collective-permute-start.29 = (bf16[16,4096]{1,0:T(8,128)(2,1)S(1)}, bf16[16,4096]{1,0:T(8,128)(2,1)S(1)}, u32[]{:S(2)}, u32[]{:S(2)}) collective-permute-start(bf16[16,4096]{1,0:T(8,128)(2,1)S(1)} %get-tuple-element.36.refs_6_), channel_id=1, source_target_pairs={{0,4},{1,5},{4,8},{5,9},{8,12},{9,13},{12,14},{13,15},{14,10},{15,... | collective-permute-start | bytes 393224 | tf_op jit(solution)/shard_map/ppermute | solution.py:383
  97.1 6.1 %collective-permute-start.30 = (bf16[16,4096]{1,0:T(8,128)(2,1)S(1)}, bf16[16,4096]{1,0:T(8,128)(2,1)S(1)}, u32[]{:S(2)}, u32[]{:S(2)}) collective-permute-start(bf16[16,4096]{1,0:T(8,128)(2,1)S(1)} %get-tuple-element.39), channel_id=1, source_target_pairs={{0,2},{1,3},{4,0},{5,1},{8,4},{9,5},{12,8},{13,9},{14,12},{15,13},... | collective-permute-start | bytes 393224 | tf_op jit(solution)/shard_map/ppermute | solution.py:384
  100.8 5.2 %collective-permute-start.27 = (bf16[16,4096]{1,0:T(8,128)(2,1)S(1)}, bf16[16,4096]{1,0:T(8,128)(2,1)S(1)}, u32[]{:S(2)}, u32[]{:S(2)}) collective-permute-start(bf16[16,4096]{1,0:T(8,128)(2,1)S(1)} %get-tuple-element.37.refs_6_), channel_id=1, source_target_pairs={{0,4},{1,5},{4,8},{5,9},{8,12},{9,13},{12,14},{13,15},{14,10},{15,... | collective-permute-start | bytes 393224 | tf_op jit(solution)/shard_map/ppermute | solution.py:383
  101.6 5.0 %collective-permute-start.28 = (bf16[16,4096]{1,0:T(8,128)(2,1)S(1)}, bf16[16,4096]{1,0:T(8,128)(2,1)S(1)}, u32[]{:S(2)}, u32[]{:S(2)}) collective-permute-start(bf16[16,4096]{1,0:T(8,128)(2,1)S(1)} %get-tuple-element.38), channel_id=1, source_target_pairs={{0,2},{1,3},{4,0},{5,1},{8,4},{9,5},{12,8},{13,9},{14,12},{15,13},... | collective-permute-start | bytes 393224 | tf_op jit(solution)/shard_map/ppermute | solution.py:384
  103.3 5.6 %collective-permute-start.32 = (bf16[16,4096]{1,0:T(8,128)(2,1)S(1)}, bf16[16,4096]{1,0:T(8,128)(2,1)S(1)}, u32[]{:S(2)}, u32[]{:S(2)}) collective-permute-start(bf16[16,4096]{1,0:T(8,128)(2,1)S(1)} %get-tuple-element.40.refs_6_), channel_id=1, source_target_pairs={{0,4},{1,5},{4,8},{5,9},{8,12},{9,13},{12,14},{13,15},{14,10},{15,... | collective-permute-start | bytes 393224 | tf_op jit(solution)/shard_map/ppermute | solution.py:383
  103.8 6.1 %collective-permute-start.33 = (bf16[16,4096]{1,0:T(8,128)(2,1)S(1)}, bf16[16,4096]{1,0:T(8,128)(2,1)S(1)}, u32[]{:S(2)}, u32[]{:S(2)}) collective-permute-start(bf16[16,4096]{1,0:T(8,128)(2,1)S(1)} %get-tuple-element.42), channel_id=1, source_target_pairs={{0,2},{1,3},{4,0},{5,1},{8,4},{9,5},{12,8},{13,9},{14,12},{15,13},... | collective-permute-start | bytes 393224 | tf_op jit(solution)/shard_map/ppermute | solution.py:384
  106.7 9.9 %collective-permute-start.31 = (bf16[16,4096]{1,0:T(8,128)(2,1)S(1)}, bf16[16,4096]{1,0:T(8,128)(2,1)S(1)}, u32[]{:S(2)}, u32[]{:S(2)}) collective-permute-start(bf16[16,4096]{1,0:T(8,128)(2,1)S(1)} %get-tuple-element.41.refs_6_), channel_id=1, source_target_pairs={{0,4},{1,5},{4,8},{5,9},{8,12},{9,13},{12,14},{13,15},{14,10},{15,... | collective-permute-start | bytes 393224 | tf_op jit(solution)/shard_map/ppermute | solution.py:383
  110.0 5.0 %collective-permute-start.34 = (bf16[16,4096]{1,0:T(8,128)(2,1)S(1)}, bf16[16,4096]{1,0:T(8,128)(2,1)S(1)}, u32[]{:S(2)}, u32[]{:S(2)}) collective-permute-start(bf16[16,4096]{1,0:T(8,128)(2,1)S(1)} %get-tuple-element.43), channel_id=1, source_target_pairs={{0,2},{1,3},{4,0},{5,1},{8,4},{9,5},{12,8},{13,9},{14,12},{15,13},... | collective-permute-start | bytes 393224 | tf_op jit(solution)/shard_map/ppermute | solution.py:384
  111.7 5.0 %collective-permute-start.35 = (bf16[16,4096]{1,0:T(8,128)(2,1)S(1)}, bf16[16,4096]{1,0:T(8,128)(2,1)S(1)}, u32[]{:S(2)}, u32[]{:S(2)}) collective-permute-start(bf16[16,4096]{1,0:T(8,128)(2,1)S(1)} %get-tuple-element.44), channel_id=1, source_target_pairs={{0,4},{1,5},{4,8},{5,9},{8,12},{9,13},{12,14},{13,15},{14,10},{15,... | collective-permute-start | bytes 393224 | tf_op jit(solution)/shard_map/ppermute | solution.py:383
  112.1 5.0 %collective-permute-start.36 = (bf16[16,4096]{1,0:T(8,128)(2,1)S(1)}, bf16[16,4096]{1,0:T(8,128)(2,1)S(1)}, u32[]{:S(2)}, u32[]{:S(2)}) collective-permute-start(bf16[16,4096]{1,0:T(8,128)(2,1)S(1)} %get-tuple-element.45), channel_id=1, source_target_pairs={{0,2},{1,3},{4,0},{5,1},{8,4},{9,5},{12,8},{13,9},{14,12},{15,13},... | collective-permute-start | bytes 393224 | tf_op jit(solution)/shard_map/ppermute | solution.py:384
  (1 other events, 0.7 us)

commit v4 on v3

--- a/solution.py
+++ b/solution.py
@@ -10,9 +10,11 @@
 adapter_alpha = 32.0
 AXIS = "mp"
 HALVES = 2
-DEPTH_BLOCKS = 8
+DEPTH_BLOCK = 512
+WIDTH_BLOCK = 512
+IN_FLIGHT = 4
 VMEM_LIMIT = 16 * 1024 * 1024
-STREAM_LIMIT = 48 * 1024 * 1024
+STREAM_LIMIT = 46 * 1024 * 1024
 
 
 def chip_at(place, chips):
@@ -113,7 +115,7 @@
     )
 
 
-def gather_rows(own, size):
+def gather_rows(own, size, ordered):
     chips = size // 2
     last = chips // 2
     other = lax.ppermute(own, AXIS, flip(size, 1))
@@ -131,69 +133,91 @@
         else:
             pieces.append(lax.ppermute(right[0], AXIS, ring(size, 1)))
             pieces.append(lax.ppermute(left[1], AXIS, ring(size, -1)))
-        if step == last - 2 or step == last:
-            part = join(pieces, [other] if step < last else [])
+        if step >= last - 1:
+            part = join(pieces, ordered if step < last else [])
             pieces = []
             mine.append(part)
             theirs.append(lax.ppermute(part, AXIS, flip(size, 1)))
     return mine + theirs
 
 
-def shrink_kernel(own_rows, size, count, *refs):
-    me_ref, start, adapters, ranks, slots = refs[:5]
-    parts = refs[5 : 5 + count]
-    factor, rows_out, coeff_out, total = refs[5 + count :]
-    batch_rows, model_width = rows_out.shape
-    width = model_width // 8
-
-    def columns(k, _):
-        at = pl.ds(pl.multiple_of(k * width, width), width)
-        top = 0
-        for part in parts:
-            rows_out[top : top + part.shape[0], at] = part[:, at]
-            top += part.shape[0]
-        product = lax.dot_general(
-            rows_out[:, at],
-            factor[:, at],
-            (((1,), (1,)), ((), ())),
-            preferred_element_type=jnp.float32,
-        )
-        total[...] = jnp.where(k == 0, product, total[...] + product)
-        return 0
-
-    lax.fori_loop(0, model_width // width, columns, 0)
-
-    me = me_ref[0]
-    rank_limit = coeff_out.shape[1]
-    held = total.shape[1] // rank_limit
-    row = lax.broadcasted_iota(jnp.int32, (batch_rows, 1), 0)
-    adapter = row_adapters(row_positions(me, row, own_rows, size), start[...], adapters[...])
-    rank = pick(adapter, ranks[...])
-    slot = pick(adapter, slots[...]) - me * held
-    shrink = jnp.zeros((batch_rows, rank_limit), jnp.float32)
-    for s in range(held):
-        shrink = jnp.where(slot == s, total[:, s * rank_limit : (s + 1) * rank_limit], shrink)
-    keep = lax.broadcasted_iota(jnp.int32, (1, rank_limit), 1) < rank
-    coeff = jnp.where(keep, shrink * (adapter_alpha / rank.astype(jnp.float32)), 0.0)
-    column = lax.broadcasted_iota(jnp.int32, (1, batch_rows), 1)
-    place = row_positions(me, column, own_rows, size)
-    to_place = (place == row).astype(jnp.bfloat16)
-    coeff_out[...] = jnp.dot(
-        to_place, coeff.astype(jnp.bfloat16), preferred_element_type=jnp.float32
-    ).astype(jnp.bfloat16)
-
-
-def shrink_rows(parts, shrink_factors, tables, me, own_rows, size):
+def row_masks(me, tables, own_rows, size, slots, rank_limit):
+    batch_rows = own_rows * size
+    adapters = tables[2].shape[1]
+
+    def kernel(me_ref, start, segment_adapter, ranks, slot_of, scale, to_place, from_place, hot):
+        me = me_ref[0]
+        row = lax.broadcasted_iota(jnp.int32, (batch_rows, 1), 0)
+        column = lax.broadcasted_iota(jnp.int32, (1, batch_rows), 1)
+        position = row_positions(me, row, own_rows, size)
+        adapter = row_adapters(position, start[...], segment_adapter[...])
+        rank = pick(adapter, ranks[...])
+        slot = pick(adapter, slot_of[...]) - me * slots
+        at = lax.broadcasted_iota(jnp.int32, (1, slots * rank_limit), 1)
+        keep = (at // rank_limit == slot) & (at % rank_limit < rank)
+        scale[...] = jnp.where(keep, adapter_alpha / rank.astype(jnp.float32), 0.0)
+        to_place[...] = (row_positions(me, column, own_rows, size) == row).astype(jnp.bfloat16)
+        from_place[...] = (position == column).astype(jnp.bfloat16)
+        depth = lax.broadcasted_iota(jnp.int32, (1, adapters * rank_limit), 1)
+        hot[...] = (depth // rank_limit == adapter).astype(jnp.bfloat16)
+
+    shapes = (
+        jax.ShapeDtypeStruct((batch_rows, slots * rank_limit), jnp.float32),
+        jax.ShapeDtypeStruct((batch_rows, batch_rows), jnp.bfloat16),
+        jax.ShapeDtypeStruct((batch_rows, batch_rows), jnp.bfloat16),
+        jax.ShapeDtypeStruct((batch_rows, adapters * rank_limit), jnp.bfloat16),
+    )
+    return pl.pallas_call(
+        kernel,
+        out_shape=shapes,
+        grid=(1,),
+        in_specs=[whole(pltpu.SMEM)] + [pl.BlockSpec(t.shape, lambda i: (0, 0)) for t in tables],
+        out_specs=[pl.BlockSpec(shape.shape, lambda i: (0, 0)) for shape in shapes],
+        compiler_params=pltpu.CompilerParams(vmem_limit_bytes=VMEM_LIMIT),
+        name="row_masks",
+    )(me, *tables)
+
+
+def shrink_rows(parts, shrink_factors, scale, to_place):
     slots, model_width, rank_limit = shrink_factors.shape
     factor = jnp.swapaxes(shrink_factors, 1, 2).reshape(slots * rank_limit, model_width)
-    batch_rows = own_rows * size
+    batch_rows = to_place.shape[0]
+    width = model_width // 8
+
+    def kernel(*refs):
+        factor_ref, scale_ref, place_ref, rows_out, coeff_out, total = refs[len(parts) :]
+
+        def columns(k, _):
+            at = pl.ds(pl.multiple_of(k * width, width), width)
+            top = 0
+            for part in refs[: len(parts)]:
+                rows_out[top : top + part.shape[0], at] = part[:, at]
+                top += part.shape[0]
+            product = lax.dot_general(
+                rows_out[:, at],
+                factor_ref[:, at],
+                (((1,), (1,)), ((), ())),
+                preferred_element_type=jnp.float32,
+            )
+            total[...] = jnp.where(k == 0, product, total[...] + product)
+            return 0
+
+        lax.fori_loop(0, model_width // width, columns, 0)
+        scaled = total[...] * scale_ref[...]
+        coeff = scaled[:, :rank_limit]
+        for s in range(1, slots):
+            coeff = coeff + scaled[:, s * rank_limit : (s + 1) * rank_limit]
+        coeff_out[...] = jnp.dot(
+            place_ref[...], coeff.astype(jnp.bfloat16), preferred_element_type=jnp.float32
+        ).astype(jnp.bfloat16)
+
     return call(
-        functools.partial(shrink_kernel, own_rows, size, len(parts)),
+        kernel,
         (
             jax.ShapeDtypeStruct((batch_rows, model_width), jnp.bfloat16),
             jax.ShapeDtypeStruct((batch_rows, rank_limit), jnp.bfloat16),
         ),
-        [me, *tables, *parts, factor],
+        [*parts, factor, scale, to_place],
         "shrink_rows",
         scratch_shapes=[pltpu.VMEM((batch_rows, slots * rank_limit), jnp.float32)],
         cost_estimate=pl.CostEstimate(
@@ -213,84 +237,77 @@
     )
 
 
+def streamed(source, pieces, buffers, arrived):
+    slots = buffers.shape[0]
+    copies = [
+        pltpu.make_async_copy(source.at[piece], buffers.at[i % slots], arrived.at[i % slots])
+        for i, piece in enumerate(pieces)
+    ]
+    for copy in copies[:slots]:
+        copy.start()
+    for i, copy in enumerate(copies):
+        copy.wait()
+        yield i, buffers[i % slots]
+        if i + slots < len(copies):
+            copies[i + slots].start()
+
+
 def matmul(rows, weight, name, first, last, ordered=()):
-    batch_rows, depth = rows.shape
+    batch_rows = rows.shape[0]
     width = weight.shape[1]
-    block = depth // DEPTH_BLOCKS
+    starts = range(first, last, DEPTH_BLOCK)
+    pieces = [(slice(at, at + DEPTH_BLOCK), slice(None)) for at in starts]
 
     def kernel(rows_ref, weight_ref, *rest):
-        out = rest[-1]
-        k = pl.program_id(0)
-        at = pl.ds(pl.multiple_of((k + first) * block, block), block)
-        product = jnp.dot(rows_ref[:, at], weight_ref[...], preferred_element_type=jnp.float32)
-
-        @pl.when(k == 0)
-        def _():
-            out[...] = product
-
-        @pl.when(k > 0)
-        def _():
-            out[...] += product
+        out, buffers, arrived = rest[-3:]
+        for i, block in streamed(weight_ref, pieces, buffers, arrived):
+            product = jnp.dot(
+                rows_ref[:, pieces[i][0]], block, preferred_element_type=jnp.float32
+            )
+            out[...] = product if i == 0 else out[...] + product
 
     return pl.pallas_call(
         kernel,
         out_shape=jax.ShapeDtypeStruct((batch_rows, width), jnp.float32),
-        grid=(last - first,),
-        in_specs=[whole(), pl.BlockSpec((block, width), lambda k: (k + first, 0))]
-        + [whole(pl.ANY)] * len(ordered),
-        out_specs=pl.BlockSpec((batch_rows, width), lambda k: (0, 0)),
+        in_specs=[whole(), whole(pltpu.HBM)] + [whole(pl.ANY)] * len(ordered),
+        out_specs=whole(),
+        scratch_shapes=[
+            pltpu.VMEM((IN_FLIGHT, DEPTH_BLOCK, width), weight.dtype),
+            pltpu.SemaphoreType.DMA((IN_FLIGHT,)),
+        ],
         compiler_params=pltpu.CompilerParams(vmem_limit_bytes=STREAM_LIMIT),
         cost_estimate=pl.CostEstimate(
-            flops=2 * batch_rows * (last - first) * block * width,
-            bytes_accessed=2 * (last - first) * block * width,
+            flops=2 * batch_rows * (last - first) * width,
+            bytes_accessed=2 * (last - first) * width,
             transcendentals=0,
         ),
         name=name,
     )(rows, weight, *ordered)
 
 
-def hidden_kernel(
-    own_rows, size, me_ref, start, adapters, coeff, recv, expand, gate, up, more, out, spread
-):
-    me = me_ref[0]
-    batch_rows, rank_limit = coeff.shape
-    row = lax.broadcasted_iota(jnp.int32, (batch_rows, 1), 0)
-    position = row_positions(me, row, own_rows, size)
-    adapter = row_adapters(position, start[...], adapters[...])
-    from_place = position == lax.broadcasted_iota(jnp.int32, (1, batch_rows), 1)
+def hidden_kernel(coeff, recv, from_place, hot, expand, gate, up, more, out, spread):
+    rank_limit = coeff.shape[1]
     own = jnp.dot(
-        from_place.astype(jnp.bfloat16),
-        coeff[...] + recv[...],
-        preferred_element_type=jnp.float32,
-    )
+        from_place[...], coeff[...] + recv[...], preferred_element_type=jnp.float32
+    ).astype(jnp.bfloat16)
     pair = jnp.concatenate([own, own], axis=1)
-    second = lax.broadcasted_iota(jnp.int32, (1, 2 * rank_limit), 1) // rank_limit
     for p in range(spread.shape[1] // (2 * rank_limit)):
-        spread[:, p * 2 * rank_limit : (p + 1) * 2 * rank_limit] = jnp.where(
-            adapter == second + 2 * p, pair, 0.0
-        ).astype(jnp.bfloat16)
+        at = slice(p * 2 * rank_limit, (p + 1) * 2 * rank_limit)
+        spread[:, at] = hot[:, at] * pair
     lora = jnp.dot(spread[...], expand[...], preferred_element_type=jnp.float32)
     value = gate[...]
     total = up[...] + more[...] + lora
     out[...] = (value / (1.0 + jnp.exp(-value)) * total).astype(jnp.bfloat16)
 
 
-def hidden_rows(gate, up, more, coeff, recv, expand_factors, tables, me, own_rows, size):
+def hidden_rows(gate, up, more, coeff, recv, expand_factors, from_place, hot):
     adapters, rank_limit, width = expand_factors.shape
     batch_rows = gate.shape[0]
+    expand = expand_factors.reshape(adapters * rank_limit, width)
     return call(
-        functools.partial(hidden_kernel, own_rows, size),
+        hidden_kernel,
         jax.ShapeDtypeStruct((batch_rows, width), jnp.bfloat16),
-        [
-            me,
-            *tables,
-            coeff,
-            recv,
-            expand_factors.reshape(adapters * rank_limit, width),
-            gate,
-            up,
-            more,
-        ],
+        [coeff, recv, from_place, hot, expand, gate, up, more],
         "hidden_rows",
         scratch_shapes=[pltpu.VMEM((batch_rows, adapters * rank_limit), jnp.bfloat16)],
         cost_estimate=pl.CostEstimate(
@@ -304,29 +321,30 @@
 def down_rows(hidden, down_weight, half, ordered=()):
     batch_rows, hidden_width = hidden.shape
     width = down_weight.shape[1] // HALVES
-    steps = 8
-    block = width // steps
     core_rows = batch_rows // 2
+    starts = range(half * width, (half + 1) * width, WIDTH_BLOCK)
+    pieces = [(slice(None), slice(at, at + WIDTH_BLOCK)) for at in starts]
 
     def kernel(hidden_ref, weight, *rest):
-        mine, theirs = rest[-2:]
-        product = jnp.dot(
-            hidden_ref[...], weight[...], preferred_element_type=jnp.float32
-        ).astype(jnp.bfloat16)
-        theirs[...] = product[core_rows:]
-        mine[...] = product[:core_rows]
+        mine, theirs, buffers, arrived = rest[-4:]
+        for i, block in streamed(weight, pieces, buffers, arrived):
+            product = jnp.dot(
+                hidden_ref[...], block, preferred_element_type=jnp.float32
+            ).astype(jnp.bfloat16)
+            at = slice(i * WIDTH_BLOCK, (i + 1) * WIDTH_BLOCK)
+            theirs[:, at] = product[core_rows:]
+            mine[:, at] = product[:core_rows]
 
     part = jax.ShapeDtypeStruct((core_rows, width), jnp.bfloat16)
     return pl.pallas_call(
         kernel,
         out_shape=(part, part),
-        grid=(steps,),
-        in_specs=[
-            whole(),
-            pl.BlockSpec((hidden_width, block), lambda n: (0, n + half * steps)),
-        ]
-        + [whole(pl.ANY)] * len(ordered),
-        out_specs=[pl.BlockSpec((core_rows, block), lambda n: (0, n))] * 2,
+        in_specs=[whole(), whole(pltpu.HBM)] + [whole(pl.ANY)] * len(ordered),
+        out_specs=[whole()] * 2,
+        scratch_shapes=[
+            pltpu.VMEM((IN_FLIGHT, hidden_width, WIDTH_BLOCK), down_weight.dtype),
+            pltpu.SemaphoreType.DMA((IN_FLIGHT,)),
+        ],
         compiler_params=pltpu.CompilerParams(vmem_limit_bytes=STREAM_LIMIT),
         cost_estimate=pl.CostEstimate(
             flops=2 * batch_rows * hidden_width * width,
@@ -362,26 +380,22 @@
     last = chips // 2
     right, left = [None] * HALVES, [None] * HALVES
     ordered = []
-    for step in range(last, 0, -1):
-        for r in range(HALVES):
-            if step == last and r == 1:
-                continue
-            l = 1 - r
-            if step == last:
-                at_right = at_left = chips - 1
-            else:
-                at_right, at_left = 2 * step, 2 * step - 1
-            sums = add_blocks(
-                [
-                    (mine[r], theirs[r], at_right, right[r]),
-                    (mine[l], theirs[l], at_left, left[l]),
-                ],
-                own_rows,
-                ordered,
-            )
+    for turn in range(last):
+        for h in range(HALVES):
+            steps_right = last - turn - (h == 1)
+            steps_left = last - turn - (h == 0)
+            sides = []
+            if steps_right > 0:
+                index = min(2 * steps_right, chips - 1)
+                sides.append((mine[h], theirs[h], index, right[h]))
+            if steps_left > 0:
+                sides.append((mine[h], theirs[h], 2 * steps_left - 1, left[h]))
+            sums = list(add_blocks(sides, own_rows, ordered))
             ordered = [sums[0]]
-            right[r] = lax.ppermute(sums[0], AXIS, ring(size, 1))
-            left[l] = lax.ppermute(sums[1], AXIS, ring(size, -1))
+            if steps_right > 0:
+                right[h] = lax.ppermute(sums.pop(0), AXIS, ring(size, 1))
+            if steps_left > 0:
+                left[h] = lax.ppermute(sums.pop(0), AXIS, ring(size, -1))
     return list(zip(mine, theirs, right, left))
 
 
@@ -433,29 +447,31 @@
     size = lax.axis_size(AXIS)
     me = lax.axis_index(AXIS).astype(jnp.int32).reshape(1)
     own_rows, model_width = activations.shape
+    slots, _, rank_limit = shrink_factors.shape
     assert size & (size - 1) == 0 and own_rows & (own_rows - 1) == 0
-    rows_tables = (segment_start[None], segment_adapter[None])
-    all_tables = rows_tables + (adapter_ranks[None], adapter_storage_slot[None])
-
-    parts = gather_rows(activations, size)
-    rows, coeff = shrink_rows(parts, shrink_factors, all_tables, me, own_rows, size)
+    tables = [
+        table[None]
+        for table in (segment_start, segment_adapter, adapter_ranks, adapter_storage_slot)
+    ]
+    scale, to_place, from_place, hot = row_masks(me, tables, own_rows, size, slots, rank_limit)
+
+    parts = gather_rows(activations, size, [scale])
+    rows, coeff = shrink_rows(parts, shrink_factors, scale, to_place)
 
     bits = [1 << b for b in range(size.bit_length() - 1)]
     work = []
     for bit in bits[:-1]:
         received = lax.ppermute(coeff, AXIS, flip(size, bit))
         if bit == bits[1]:
-            work = [matmul(rows, gate_weight, "gate_rows", 0, DEPTH_BLOCKS, [coeff])]
+            work = [matmul(rows, gate_weight, "gate_rows", 0, model_width, [coeff])]
             gate = work[0]
         if bit == bits[2]:
-            work = [matmul(rows, up_weight, "up_rows", 0, DEPTH_BLOCKS // 2, [coeff])]
+            work = [matmul(rows, up_weight, "up_rows", 0, model_width // 2, [coeff])]
             up = work[0]
         coeff = add_coefficients(coeff, received, work)
     received = lax.ppermute(coeff, AXIS, flip(size, bits[-1]))
-    more = matmul(rows, up_weight, "up_rows", DEPTH_BLOCKS // 2, DEPTH_BLOCKS, [coeff])
-    hidden = hidden_rows(
-        gate, up, more, coeff, received, expand_factors, rows_tables, me, own_rows, size
-    )
+    more = matmul(rows, up_weight, "up_rows", model_width // 2, model_width, [coeff])
+    hidden = hidden_rows(gate, up, more, coeff, received, expand_factors, from_place, hot)
 
     mine, theirs = [None] * HALVES, [None] * HALVES
     ordered = []

time: 119 us -> 102 us (0.86)
  Pallas kernels: 43 us -> 33.4 us
  waiting for transfers between devices: 32.4 us -> 26.2 us
  local copies, waits for them, and re-layouts: 5.79 us -> 3.6 us
  starting transfers between devices: 36 us -> 37.6 us
    ppermute x3, starting transfers between devices: 0.18 us -> 7.08 us  [gather_rows(): left[1] = lax.ppermute(left[1], AXIS, ring(size, -1))]
    ppermute x3, starting transfers between devices: 7.36 us -> 0.52 us  [gather_rows(): right[0] = lax.ppermute(right[0], AXIS, ring(size, 1))]
    ppermute x3, starting transfers between devices: 5.43 us -> 0.35 us  [gather_rows(): right[1] = lax.ppermute(right[1], AXIS, ring(size, 1))]
    ppermute x3, starting transfers between devices: 0.7 us -> 5.78 us  [gather_rows(): left[0] = lax.ppermute(left[0], AXIS, ring(size, -1))]
    pallas_call x2 -> x3, Pallas kernels: 14.5 us -> 10.2 us  [the longest x2 9.63 us: down_rows(): pl.pallas_call(kernel, out_shape=(part, part), in_specs=[whole(), whole(p...]
    pallas_call x3, Pallas kernels: 21.4 us -> 17.7 us  [matmul(): pl.pallas_call(kernel, out_shape=jax.ShapeDtypeStruct((batch_rows, width)...]
    ppermute x3, waiting for transfers between devices: 3.54 us -> 0.01 us  [gather_rows(): right[0] = lax.ppermute(right[0], AXIS, ring(size, 1))]
    ppermute x2, waiting for transfers between devices: 3.65 us -> 0.14 us  [body(): theirs[h] = lax.ppermute(part, AXIS, flip(size, 1))]
  transfers between devices with their start and end apart: 37 -> 37, of which waited for: 25 -> 19; matrix products, arithmetic and copies ran while one was open for 0% -> 0% of each run, Pallas kernels for 19% -> 23%
where the time goes in v4:
time: 102 us
  starting transfers between devices  37.6 us (37%)
  Pallas kernels  33.4 us (33%)
  waiting for transfers between devices  26.2 us (26%)
  local copies, waits for them, and re-layouts  3.6 us (4%)
    pallas_call x3, Pallas kernels, matmul(): pl.pallas_call(kernel, out_shape=jax.ShapeDtypeStruct((batch_rows, width)...  17.7 us
    ppermute x7, starting transfers between devices, scatter_rows(): left[h] = lax.ppermute(sums.pop(0), AXIS, ring(size, -1))  11.2 us
    pallas_call x2, Pallas kernels, down_rows(): pl.pallas_call(kernel, out_shape=(part, part), in_specs=[whole(), whole(p...  9.63 us
    ppermute x3, starting transfers between devices, gather_rows(): left[1] = lax.ppermute(left[1], AXIS, ring(size, -1))  7.08 us
    ppermute x7, waiting for transfers between devices, scatter_rows(): right[h] = lax.ppermute(sums.pop(0), AXIS, ring(size, 1))  6.5 us
    ppermute x7, waiting for transfers between devices, scatter_rows(): left[h] = lax.ppermute(sums.pop(0), AXIS, ring(size, -1))  6.3 us
    ppermute x3, starting transfers between devices, gather_rows(): left[0] = lax.ppermute(left[0], AXIS, ring(size, -1))  5.78 us
    pallas_call x17, Pallas kernels, call(): pl.pallas_call(run, out_shape=out_shape, in_specs=[whole(pltpu.SMEM if op...  5.59 us
  transfers between devices with their start and end apart: 37, of which 19 were waited for; matrix products, arithmetic and copies ran while one was open for 0% of the time, Pallas kernels for 23%

profile of v4, /device:TPU:0, one launch (start us, length us, event | category | flops | bytes accessed | tf_op | source)
XLA Modules:
  0.0 101.7 jit_solution(4670560424687341791)
XLA Ops:
  0.6 0.9 copy-done
  1.6 3.0 %collective-permute-start.3 = (bf16[16,4096]{1,0:T(8,128)(2,1)S(1)}, bf16[16,4096]{1,0:T(8,128)(2,1)S(1)}, u32[]{:S(2)}, u32[]{:S(2)}) collective-permute-start(bf16[16,4096]{1,0:T(8,128)(2,1)S(1)} %get-tuple-element.27), channel_id=1, source_target_pairs={{0,2},{1,3},{4,0},{5,1},{8,4},{9,5},{12,8},{13,9},{14,12},{15,13},... | collective-permute-start | bytes 393224 | tf_op jit(solution)/shard_map/ppermute | solution.py:129
  4.8 1.9 %collective-permute-start.2 = (bf16[16,4096]{1,0:T(8,128)(2,1)S(1)}, bf16[16,4096]{1,0:T(8,128)(2,1)S(1)}, u32[]{:S(2)}, u32[]{:S(2)}) collective-permute-start(bf16[16,4096]{1,0:T(8,128)(2,1)S(1)} %get-tuple-element.26), channel_id=1, source_target_pairs={{0,2},{1,3},{4,0},{5,1},{8,4},{9,5},{12,8},{13,9},{14,12},{15,13},... | collective-permute-start | bytes 393224 | tf_op jit(solution)/shard_map/ppermute | solution.py:131
  6.8 2.2 %collective-permute-done.3.refs_3_ = bf16[16,4096]{1,0:T(8,128)(2,1)S(1)} collective-permute-done((bf16[16,4096]{1,0:T(8,128)(2,1)S(1)}, bf16[16,4096]{1,0:T(8,128)(2,1)S(1)}, u32[]{:S(2)}, u32[]{:S(2)}) %collective-permute-start.3) | collective-permute-done | bytes 131104 | tf_op jit(solution)/shard_map/ppermute | solution.py:129
  9.0 2.0 %collective-permute-start.7 = (bf16[16,4096]{1,0:T(8,128)(2,1)S(1)}, bf16[16,4096]{1,0:T(8,128)(2,1)S(1)}, u32[]{:S(2)}, u32[]{:S(2)}) collective-permute-start(bf16[16,4096]{1,0:T(8,128)(2,1)S(1)} %collective-permute-done.3.refs_3_), channel_id=1, source_target_pairs={{0,2},{1,3},{4,0},{5,1},{8,4},{9,5},{12,8},{13,9},{14,12},{15,13},... | collective-permute-start | bytes 393224 | tf_op jit(solution)/shard_map/ppermute | solution.py:129
  11.1 0.7 collective-permute-done.2.refs_2_
  11.8 2.0 %collective-permute-start.6 = (bf16[16,4096]{1,0:T(8,128)(2,1)S(1)}, bf16[16,4096]{1,0:T(8,128)(2,1)S(1)}, u32[]{:S(2)}, u32[]{:S(2)}) collective-permute-start(bf16[16,4096]{1,0:T(8,128)(2,1)S(1)} %collective-permute-done.2.refs_2_), channel_id=1, source_target_pairs={{0,2},{1,3},{4,0},{5,1},{8,4},{9,5},{12,8},{13,9},{14,12},{15,13},... | collective-permute-start | bytes 393224 | tf_op jit(solution)/shard_map/ppermute | solution.py:131
  13.9 1.3 %collective-permute-done.7.refs_7_ = bf16[16,4096]{1,0:T(8,128)(2,1)S(1)} collective-permute-done((bf16[16,4096]{1,0:T(8,128)(2,1)S(1)}, bf16[16,4096]{1,0:T(8,128)(2,1)S(1)}, u32[]{:S(2)}, u32[]{:S(2)}) %collective-permute-start.7) | collective-permute-done | bytes 131104 | tf_op jit(solution)/shard_map/ppermute | solution.py:129
  15.2 2.1 %collective-permute-start.11 = (bf16[16,4096]{1,0:T(8,128)(2,1)S(1)}, bf16[16,4096]{1,0:T(8,128)(2,1)S(1)}, u32[]{:S(2)}, u32[]{:S(2)}) collective-permute-start(bf16[16,4096]{1,0:T(8,128)(2,1)S(1)} %collective-permute-done.7.refs_7_), channel_id=1, source_target_pairs={{0,2},{1,3},{4,0},{5,1},{8,4},{9,5},{12,8},{13,9},{14,12},{15,13},... | collective-permute-start | bytes 393224 | tf_op jit(solution)/shard_map/ppermute | solution.py:129
  17.5 0.8 collective-permute-done.6.refs_6_
  18.3 1.9 %collective-permute-start.10 = (bf16[16,4096]{1,0:T(8,128)(2,1)S(1)}, bf16[16,4096]{1,0:T(8,128)(2,1)S(1)}, u32[]{:S(2)}, u32[]{:S(2)}) collective-permute-start(bf16[16,4096]{1,0:T(8,128)(2,1)S(1)} %collective-permute-done.6.refs_6_), channel_id=1, source_target_pairs={{0,2},{1,3},{4,0},{5,1},{8,4},{9,5},{12,8},{13,9},{14,12},{15,13},... | collective-permute-start | bytes 393224 | tf_op jit(solution)/shard_map/ppermute | solution.py:131
  20.3 0.7 copy-done.4
  21.0 0.7 copy-done.5
  21.6 0.7 copy-done.6
  22.3 0.7 copy-done.7
  23.5 1.6 %collective-permute-done.9.refs_9_ = bf16[16,4096]{1,0:T(8,128)(2,1)S(1)} collective-permute-done((bf16[16,4096]{1,0:T(8,128)(2,1)S(1)}, bf16[16,4096]{1,0:T(8,128)(2,1)S(1)}, u32[]{:S(2)}, u32[]{:S(2)}) %collective-permute-start.9) | collective-permute-done | bytes 131104 | tf_op jit(solution)/shard_map/ppermute | solution.py:130
  25.8 1.6 %collective-permute-start.13 = (bf16[16,4096]{1,0:T(8,128)(2,1)S(1)}, bf16[16,4096]{1,0:T(8,128)(2,1)S(1)}, u32[]{:S(2)}, u32[]{:S(2)}) collective-permute-start(bf16[16,4096]{1,0:T(8,128)(2,1)S(1)} %collective-permute-done.11.refs_11_), channel_id=1, source_target_pairs={{0,2},{1,3},{4,0},{5,1},{8,4},{9,5},{12,8},{13,9},{14,12},{15,13},... | collective-permute-start | bytes 393224 | tf_op jit(solution)/shard_map/ppermute | solution.py:135
  27.4 3.8 %collective-permute-done.12.refs_0_ = bf16[16,4096]{1,0:T(8,128)(2,1)S(1)} collective-permute-done((bf16[16,4096]{1,0:T(8,128)(2,1)S(1)}, bf16[16,4096]{1,0:T(8,128)(2,1)S(1)}, u32[]{:S(2)}, u32[]{:S(2)}) %collective-permute-start.12) | collective-permute-done | bytes 131104 | tf_op jit(solution)/shard_map/ppermute | solution.py:134
  31.5 1.5 %collective-permute-done.16.refs_5_ = bf16[16,8192]{1,0:T(8,128)(2,1)S(1)} collective-permute-done((bf16[16,8192]{1,0:T(8,128)(2,1)S(1)}, bf16[16,8192]{1,0:T(8,128)(2,1)S(1)}, u32[]{:S(2)}, u32[]{:S(2)}) %collective-permute-start.16) | collective-permute-done | bytes 262176 | tf_op jit(solution)/shard_map/ppermute | solution.py:140
  33.0 2.8 %shrink_rows.1 = (bf16[256,8192]{1,0:T(8,128)(2,1)S(1)}, bf16[256,64]{1,0:T(8,128)(2,1)S(1)}) custom-call(bf16[16,8192]{1,0:T(8,128)(2,1)S(1)} %copy-done.1, bf16[96,8192]{1,0:T(8,128)(2,1)S(1)} %join_pieces.2.refs_1_, bf16[16,8192]{1,0:T(8,128)(2,1)S(1)} %join_pieces.3.refs_2_, bf16[16,8192]{1,0:T(8,128)(2,1)S(1)} %collective-permute-done.14.refs_3_, ...), custom_call_target="tpu_custom_call" | custom-call | flops 268435456 | bytes 8388608 | tf_op jit(solution)/shard_map/shrink_rows/pallas_call | solution.py:77
  36.0 1.1 %collective-permute-done.17.refs_1_ = bf16[256,64]{1,0:T(8,128)(2,1)S(1)} collective-permute-done((bf16[256,64]{1,0:T(8,128)(2,1)S(1)}, bf16[256,64]{1,0:T(8,128)(2,1)S(1)}, u32[]{:S(2)}, u32[]{:S(2)}) %collective-permute-start.17) | collective-permute-done | bytes 32800 | tf_op jit(solution)/shard_map/ppermute | solution.py:464
  37.1 1.6 %collective-permute-start.18 = (bf16[256,64]{1,0:T(8,128)(2,1)S(1)}, bf16[256,64]{1,0:T(8,128)(2,1)S(1)}, u32[]{:S(2)}, u32[]{:S(2)}) collective-permute-start(bf16[256,64]{1,0:T(8,128)(2,1)S(1)} %add_coefficients.3.rest_0_.refs_0_), channel_id=1, source_target_pairs={{0,2},{1,3},{2,0},{3,1},{4,6},{5,7},{6,4},{7,5},{8,10},{9,11},{10,... | collective-permute-start | bytes 98312 | tf_op jit(solution)/shard_map/ppermute | solution.py:464
  38.8 8.2 %gate_rows.1.refs_2_.refs_5_ = f32[256,896]{1,0:T(8,128)S(1)} custom-call(bf16[256,8192]{1,0:T(8,128)(2,1)S(1)} %get-tuple-element.31.rows_ref, bf16[8192,896]{1,0:T(8,128)(2,1)} %weight_ref.3, bf16[256,64]{1,0:T(8,128)(2,1)S(1)} %add_coefficients.3.rest_0_.refs_0_), custom_call_target="tpu_custom_call" | custom-call | flops 3758096384 | bytes 14680064 | tf_op jit(solution)/shard_map/gate_rows/pallas_call | solution.py:269
  47.0 1.6 %collective-permute-start.19 = (bf16[256,64]{1,0:T(8,128)(2,1)S(1)}, bf16[256,64]{1,0:T(8,128)(2,1)S(1)}, u32[]{:S(2)}, u32[]{:S(2)}) collective-permute-start(bf16[256,64]{1,0:T(8,128)(2,1)S(1)} %add_coefficients.4.rest_0_.refs_0_), channel_id=1, source_target_pairs={{0,4},{1,5},{2,6},{3,7},{4,0},{5,1},{6,2},{7,3},{8,12},{9,13},{10,... | collective-permute-start | bytes 98312 | tf_op jit(solution)/shard_map/ppermute | solution.py:464
  48.7 4.7 %up_rows.2.refs_2_.refs_6_ = f32[256,896]{1,0:T(8,128)S(1)} custom-call(bf16[256,8192]{1,0:T(8,128)(2,1)S(1)} %get-tuple-element.31.rows_ref, bf16[8192,896]{1,0:T(8,128)(2,1)} %weight_ref.5, bf16[256,64]{1,0:T(8,128)(2,1)S(1)} %add_coefficients.4.rest_0_.refs_0_), custom_call_target="tpu_custom_call" | custom-call | flops 1879048192 | bytes 7340032 | tf_op jit(solution)/shard_map/up_rows/pallas_call | solution.py:269
  53.5 2.6 %collective-permute-start.20 = (bf16[256,64]{1,0:T(8,128)(2,1)S(1)}, bf16[256,64]{1,0:T(8,128)(2,1)S(1)}, u32[]{:S(2)}, u32[]{:S(2)}) collective-permute-start(bf16[256,64]{1,0:T(8,128)(2,1)S(1)} %add_coefficients.5.rest_0_.refs_0_), channel_id=1, source_target_pairs={{0,8},{1,9},{2,10},{3,11},{4,12},{5,13},{6,14},{7,15},{8,0},{9,1},... | collective-permute-start | bytes 98312 | tf_op jit(solution)/shard_map/ppermute | solution.py:472
  56.1 4.7 %up_rows.3.refs_7_ = f32[256,896]{1,0:T(8,128)S(1)} custom-call(bf16[256,8192]{1,0:T(8,128)(2,1)S(1)} %get-tuple-element.31.rows_ref, bf16[8192,896]{1,0:T(8,128)(2,1)} %weight_ref.5, bf16[256,64]{1,0:T(8,128)(2,1)S(1)} %add_coefficients.5.rest_0_.refs_0_), custom_call_target="tpu_custom_call" | custom-call | flops 1879048192 | bytes 7340032 | tf_op jit(solution)/shard_map/up_rows/pallas_call | solution.py:269
  60.9 1.0 hidden_rows.1.hidden_ref
  61.8 4.9 %down_rows.2 = (bf16[128,4096]{1,0:T(8,128)(2,1)S(1)}, bf16[128,4096]{1,0:T(8,128)(2,1)S(1)}) custom-call(bf16[256,896]{1,0:T(8,128)(2,1)S(1)} %hidden_rows.1.hidden_ref, bf16[896,8192]{1,0:T(8,128)(2,1)} %weight.3), custom_call_target="tpu_custom_call" | custom-call | flops 1879048192 | bytes 7340032 | tf_op jit(solution)/shard_map/down_rows/pallas_call | solution.py:339
  66.8 4.7 %down_rows.3 = (bf16[128,4096]{1,0:T(8,128)(2,1)S(1)}, bf16[128,4096]{1,0:T(8,128)(2,1)S(1)}) custom-call(bf16[256,896]{1,0:T(8,128)(2,1)S(1)} %hidden_rows.1.hidden_ref, bf16[896,8192]{1,0:T(8,128)(2,1)} %weight.3, bf16[128,4096]{1,0:T(8,128)(2,1)S(1)} %get-tuple-element.35.rest_0_), custom_call_target="tpu_custom_call" | custom-call | flops 1879048192 | bytes 7340032 | tf_op jit(solution)/shard_map/down_rows/pallas_call | solution.py:339
  72.7 1.6 %collective-permute-start.23 = (bf16[16,4096]{1,0:T(8,128)(2,1)S(1)}, bf16[16,4096]{1,0:T(8,128)(2,1)S(1)}, u32[]{:S(2)}, u32[]{:S(2)}) collective-permute-start(bf16[16,4096]{1,0:T(8,128)(2,1)S(1)} %get-tuple-element.37), channel_id=1, source_target_pairs={{0,2},{1,3},{4,0},{5,1},{8,4},{9,5},{12,8},{13,9},{14,12},{15,13},... | collective-permute-start | bytes 393224 | tf_op jit(solution)/shard_map/ppermute | solution.py:398
  75.0 1.6 %collective-permute-start.28 = (bf16[16,4096]{1,0:T(8,128)(2,1)S(1)}, bf16[16,4096]{1,0:T(8,128)(2,1)S(1)}, u32[]{:S(2)}, u32[]{:S(2)}) collective-permute-start(bf16[16,4096]{1,0:T(8,128)(2,1)S(1)} %get-tuple-element.43), channel_id=1, source_target_pairs={{0,2},{1,3},{4,0},{5,1},{8,4},{9,5},{12,8},{13,9},{14,12},{15,13},... | collective-permute-start | bytes 393224 | tf_op jit(solution)/shard_map/ppermute | solution.py:398
  76.6 1.2 %collective-permute-done.22.refs_2_ = bf16[16,4096]{1,0:T(8,128)(2,1)S(1)} collective-permute-done((bf16[16,4096]{1,0:T(8,128)(2,1)S(1)}, bf16[16,4096]{1,0:T(8,128)(2,1)S(1)}, u32[]{:S(2)}, u32[]{:S(2)}) %collective-permute-start.22) | collective-permute-done | bytes 131104 | tf_op jit(solution)/shard_map/ppermute | solution.py:396
  78.1 0.6 collective-permute-start.25
  78.7 1.4 %collective-permute-start.26 = (bf16[16,4096]{1,0:T(8,128)(2,1)S(1)}, bf16[16,4096]{1,0:T(8,128)(2,1)S(1)}, u32[]{:S(2)}, u32[]{:S(2)}) collective-permute-start(bf16[16,4096]{1,0:T(8,128)(2,1)S(1)} %get-tuple-element.42), channel_id=1, source_target_pairs={{0,2},{1,3},{4,0},{5,1},{8,4},{9,5},{12,8},{13,9},{14,12},{15,13},... | collective-permute-start | bytes 393224 | tf_op jit(solution)/shard_map/ppermute | solution.py:398
  80.2 0.7 collective-permute-done.27.refs_2_
  81.5 0.6 collective-permute-start.30
  82.1 1.4 %collective-permute-start.31 = (bf16[16,4096]{1,0:T(8,128)(2,1)S(1)}, bf16[16,4096]{1,0:T(8,128)(2,1)S(1)}, u32[]{:S(2)}, u32[]{:S(2)}) collective-permute-start(bf16[16,4096]{1,0:T(8,128)(2,1)S(1)} %get-tuple-element.46), channel_id=1, source_target_pairs={{0,2},{1,3},{4,0},{5,1},{8,4},{9,5},{12,8},{13,9},{14,12},{15,13},... | collective-permute-start | bytes 393224 | tf_op jit(solution)/shard_map/ppermute | solution.py:398
  83.6 0.7 collective-permute-done.26.refs_5_
  84.3 0.8 collective-permute-start.29
  85.2 2.6 %collective-permute-done.30.refs_2_ = bf16[16,4096]{1,0:T(8,128)(2,1)S(1)} collective-permute-done((bf16[16,4096]{1,0:T(8,128)(2,1)S(1)}, bf16[16,4096]{1,0:T(8,128)(2,1)S(1)}, u32[]{:S(2)}, u32[]{:S(2)}) %collective-permute-start.30) | collective-permute-done | bytes 131104 | tf_op jit(solution)/shard_map/ppermute | solution.py:396
  87.9 1.6 %collective-permute-start.35 = (bf16[16,4096]{1,0:T(8,128)(2,1)S(1)}, bf16[16,4096]{1,0:T(8,128)(2,1)S(1)}, u32[]{:S(2)}, u32[]{:S(2)}) collective-permute-start(bf16[16,4096]{1,0:T(8,128)(2,1)S(1)} %get-tuple-element.49), channel_id=1, source_target_pairs={{0,2},{1,3},{4,0},{5,1},{8,4},{9,5},{12,8},{13,9},{14,12},{15,13},... | collective-permute-start | bytes 393224 | tf_op jit(solution)/shard_map/ppermute | solution.py:398
  89.9 1.6 %collective-permute-start.33 = (bf16[16,4096]{1,0:T(8,128)(2,1)S(1)}, bf16[16,4096]{1,0:T(8,128)(2,1)S(1)}, u32[]{:S(2)}, u32[]{:S(2)}) collective-permute-start(bf16[16,4096]{1,0:T(8,128)(2,1)S(1)} %get-tuple-element.48), channel_id=1, source_target_pairs={{0,2},{1,3},{4,0},{5,1},{8,4},{9,5},{12,8},{13,9},{14,12},{15,13},... | collective-permute-start | bytes 393224 | tf_op jit(solution)/shard_map/ppermute | solution.py:398
  91.6 2.1 %collective-permute-done.35.refs_2_ = bf16[16,4096]{1,0:T(8,128)(2,1)S(1)} collective-permute-done((bf16[16,4096]{1,0:T(8,128)(2,1)S(1)}, bf16[16,4096]{1,0:T(8,128)(2,1)S(1)}, u32[]{:S(2)}, u32[]{:S(2)}) %collective-permute-start.35) | collective-permute-done | bytes 131104 | tf_op jit(solution)/shard_map/ppermute | solution.py:398
  93.7 2.0 %collective-permute-start.36 = (bf16[16,4096]{1,0:T(8,128)(2,1)S(1)}, bf16[16,4096]{1,0:T(8,128)(2,1)S(1)}, u32[]{:S(2)}, u32[]{:S(2)}) collective-permute-start(bf16[16,4096]{1,0:T(8,128)(2,1)S(1)} %add_blocks.15), channel_id=1, source_target_pairs={{0,2},{1,3},{4,0},{5,1},{8,4},{9,5},{12,8},{13,9},{14,12},{15,13},... | collective-permute-start | bytes 393224 | tf_op jit(solution)/shard_map/ppermute | solution.py:398
  95.8 2.9 %collective-permute-done.36.refs_7_ = bf16[16,4096]{1,0:T(8,128)(2,1)S(1)} collective-permute-done((bf16[16,4096]{1,0:T(8,128)(2,1)S(1)}, bf16[16,4096]{1,0:T(8,128)(2,1)S(1)}, u32[]{:S(2)}, u32[]{:S(2)}) %collective-permute-start.36) | collective-permute-done | bytes 131104 | tf_op jit(solution)/shard_map/ppermute | solution.py:398
  98.7 1.9 %collective-permute-done.32.refs_2_ = bf16[16,4096]{1,0:T(8,128)(2,1)S(1)} collective-permute-done((bf16[16,4096]{1,0:T(8,128)(2,1)S(1)}, bf16[16,4096]{1,0:T(8,128)(2,1)S(1)}, u32[]{:S(2)}, u32[]{:S(2)}) %collective-permute-start.32) | collective-permute-done | bytes 131104 | tf_op jit(solution)/shard_map/ppermute | solution.py:396
  100.6 1.0 %finish_rows.1 = (bf16[16,8192]{1,0:T(8,128)(2,1)}, bf16[16,8192]{1,0:T(8,128)(2,1)}) custom-call(bf16[128,4096]{1,0:T(8,128)(2,1)S(1)} %get-tuple-element.34.refs_0_.refs_2_.refs_3_, bf16[128,4096]{1,0:T(8,128)(2,1)S(1)} %collective-permute-done.21.refs_1_.refs_3_.refs_4_, bf16[16,4096]{1,0:T(8,128)(2,1)S(1)} %collective-permute-done.32.refs_2_, ...), custom_call_target="tpu_custom_call" | custom-call | tf_op jit(solution)/shard_map/finish_rows/pallas_call | solution.py:77
  (68 shorter events, 6.4 us)
Async XLA Ops:
  0.6 1.0 copy-start
  1.6 31.4 %copy-start.1 = (bf16[16,8192]{1,0:T(8,128)(2,1)S(1)}, bf16[16,8192]{1,0:T(8,128)(2,1)}, u32[]{:S(2)}) copy-start(bf16[16,8192]{1,0:T(8,128)(2,1)} %refs_8_.1) | copy-start | bytes 786436
  1.6 31.4 %copy-start.3 = (bf16[1,8192,64]{1,2,0:T(8,128)(2,1)S(1)}, bf16[1,8192,64]{1,2,0:T(8,128)(2,1)}, u32[]{:S(2)}) copy-start(bf16[1,8192,64]{1,2,0:T(8,128)(2,1)} %param.16) | copy-start | bytes 3145732
  1.6 7.4 %collective-permute-start.3 = (bf16[16,4096]{1,0:T(8,128)(2,1)S(1)}, bf16[16,4096]{1,0:T(8,128)(2,1)S(1)}, u32[]{:S(2)}, u32[]{:S(2)}) collective-permute-start(bf16[16,4096]{1,0:T(8,128)(2,1)S(1)} %get-tuple-element.27), channel_id=1, source_target_pairs={{0,2},{1,3},{4,0},{5,1},{8,4},{9,5},{12,8},{13,9},{14,12},{15,13},... | collective-permute-start | bytes 393224 | tf_op jit(solution)/shard_map/ppermute | solution.py:129
  4.6 6.4 %collective-permute-start = (bf16[16,4096]{1,0:T(8,128)(2,1)S(1)}, bf16[16,4096]{1,0:T(8,128)(2,1)S(1)}, u32[]{:S(2)}, u32[]{:S(2)}) collective-permute-start(bf16[16,4096]{1,0:T(8,128)(2,1)S(1)} %get-tuple-element.26), channel_id=1, source_target_pairs={{0,4},{1,5},{4,8},{5,9},{8,12},{9,13},{12,14},{13,15},{14,10},{15,... | collective-permute-start | bytes 393224 | tf_op jit(solution)/shard_map/ppermute | solution.py:128
  4.8 7.1 %collective-permute-start.2 = (bf16[16,4096]{1,0:T(8,128)(2,1)S(1)}, bf16[16,4096]{1,0:T(8,128)(2,1)S(1)}, u32[]{:S(2)}, u32[]{:S(2)}) collective-permute-start(bf16[16,4096]{1,0:T(8,128)(2,1)S(1)} %get-tuple-element.26), channel_id=1, source_target_pairs={{0,2},{1,3},{4,0},{5,1},{8,4},{9,5},{12,8},{13,9},{14,12},{15,13},... | collective-permute-start | bytes 393224 | tf_op jit(solution)/shard_map/ppermute | solution.py:131
  6.7 7.2 %collective-permute-start.1 = (bf16[16,4096]{1,0:T(8,128)(2,1)S(1)}, bf16[16,4096]{1,0:T(8,128)(2,1)S(1)}, u32[]{:S(2)}, u32[]{:S(2)}) collective-permute-start(bf16[16,4096]{1,0:T(8,128)(2,1)S(1)} %get-tuple-element.27), channel_id=1, source_target_pairs={{0,4},{1,5},{4,8},{5,9},{8,12},{9,13},{12,14},{13,15},{14,10},{15,... | collective-permute-start | bytes 393224 | tf_op jit(solution)/shard_map/ppermute | solution.py:130
  9.0 6.2 %collective-permute-start.7 = (bf16[16,4096]{1,0:T(8,128)(2,1)S(1)}, bf16[16,4096]{1,0:T(8,128)(2,1)S(1)}, u32[]{:S(2)}, u32[]{:S(2)}) collective-permute-start(bf16[16,4096]{1,0:T(8,128)(2,1)S(1)} %collective-permute-done.3.refs_3_), channel_id=1, source_target_pairs={{0,2},{1,3},{4,0},{5,1},{8,4},{9,5},{12,8},{13,9},{14,12},{15,13},... | collective-permute-start | bytes 393224 | tf_op jit(solution)/shard_map/ppermute | solution.py:129
  11.0 6.2 %collective-permute-start.4 = (bf16[16,4096]{1,0:T(8,128)(2,1)S(1)}, bf16[16,4096]{1,0:T(8,128)(2,1)S(1)}, u32[]{:S(2)}, u32[]{:S(2)}) collective-permute-start(bf16[16,4096]{1,0:T(8,128)(2,1)S(1)} %collective-permute-done.refs_0_), channel_id=1, source_target_pairs={{0,4},{1,5},{4,8},{5,9},{8,12},{9,13},{12,14},{13,15},{14,10},{15,... | collective-permute-start | bytes 393224 | tf_op jit(solution)/shard_map/ppermute | solution.py:128
  11.8 6.5 %collective-permute-start.6 = (bf16[16,4096]{1,0:T(8,128)(2,1)S(1)}, bf16[16,4096]{1,0:T(8,128)(2,1)S(1)}, u32[]{:S(2)}, u32[]{:S(2)}) collective-permute-start(bf16[16,4096]{1,0:T(8,128)(2,1)S(1)} %collective-permute-done.2.refs_2_), channel_id=1, source_target_pairs={{0,2},{1,3},{4,0},{5,1},{8,4},{9,5},{12,8},{13,9},{14,12},{15,13},... | collective-permute-start | bytes 393224 | tf_op jit(solution)/shard_map/ppermute | solution.py:131
  13.8 6.3 %collective-permute-start.5 = (bf16[16,4096]{1,0:T(8,128)(2,1)S(1)}, bf16[16,4096]{1,0:T(8,128)(2,1)S(1)}, u32[]{:S(2)}, u32[]{:S(2)}) collective-permute-start(bf16[16,4096]{1,0:T(8,128)(2,1)S(1)} %collective-permute-done.1.refs_1_), channel_id=1, source_target_pairs={{0,4},{1,5},{4,8},{5,9},{8,12},{9,13},{12,14},{13,15},{14,10},{15,... | collective-permute-start | bytes 393224 | tf_op jit(solution)/shard_map/ppermute | solution.py:130
  15.2 8.4 %collective-permute-start.11 = (bf16[16,4096]{1,0:T(8,128)(2,1)S(1)}, bf16[16,4096]{1,0:T(8,128)(2,1)S(1)}, u32[]{:S(2)}, u32[]{:S(2)}) collective-permute-start(bf16[16,4096]{1,0:T(8,128)(2,1)S(1)} %collective-permute-done.7.refs_7_), channel_id=1, source_target_pairs={{0,2},{1,3},{4,0},{5,1},{8,4},{9,5},{12,8},{13,9},{14,12},{15,13},... | collective-permute-start | bytes 393224 | tf_op jit(solution)/shard_map/ppermute | solution.py:129
  17.2 6.3 %collective-permute-start.8 = (bf16[16,4096]{1,0:T(8,128)(2,1)S(1)}, bf16[16,4096]{1,0:T(8,128)(2,1)S(1)}, u32[]{:S(2)}, u32[]{:S(2)}) collective-permute-start(bf16[16,4096]{1,0:T(8,128)(2,1)S(1)} %collective-permute-done.4.refs_4_), channel_id=1, source_target_pairs={{0,4},{1,5},{4,8},{5,9},{8,12},{9,13},{12,14},{13,15},{14,10},{15,... | collective-permute-start | bytes 393224 | tf_op jit(solution)/shard_map/ppermute | solution.py:128
  18.3 5.2 %collective-permute-start.10 = (bf16[16,4096]{1,0:T(8,128)(2,1)S(1)}, bf16[16,4096]{1,0:T(8,128)(2,1)S(1)}, u32[]{:S(2)}, u32[]{:S(2)}) collective-permute-start(bf16[16,4096]{1,0:T(8,128)(2,1)S(1)} %collective-permute-done.6.refs_6_), channel_id=1, source_target_pairs={{0,2},{1,3},{4,0},{5,1},{8,4},{9,5},{12,8},{13,9},{14,12},{15,13},... | collective-permute-start | bytes 393224 | tf_op jit(solution)/shard_map/ppermute | solution.py:131
  20.2 5.0 %collective-permute-start.9 = (bf16[16,4096]{1,0:T(8,128)(2,1)S(1)}, bf16[16,4096]{1,0:T(8,128)(2,1)S(1)}, u32[]{:S(2)}, u32[]{:S(2)}) collective-permute-start(bf16[16,4096]{1,0:T(8,128)(2,1)S(1)} %collective-permute-done.5.refs_5_), channel_id=1, source_target_pairs={{0,4},{1,5},{4,8},{5,9},{8,12},{9,13},{12,14},{13,15},{14,10},{15,... | collective-permute-start | bytes 393224 | tf_op jit(solution)/shard_map/ppermute | solution.py:130
  20.3 0.7 copy-start.4
  21.0 0.7 copy-start.5
  21.6 0.7 copy-start.6
  22.3 0.7 copy-start.7
  25.2 7.8 %collective-permute-start.15 = (bf16[96,8192]{1,0:T(8,128)(2,1)S(1)}, bf16[96,8192]{1,0:T(8,128)(2,1)S(1)}, u32[]{:S(2)}, u32[]{:S(2)}) collective-permute-start(bf16[96,8192]{1,0:T(8,128)(2,1)S(1)} %join_pieces.2.refs_1_), channel_id=1, source_target_pairs={{0,1},{1,0},{2,3},{3,2},{4,5},{5,4},{6,7},{7,6},{8,9},{9,8},{10,11... | collective-permute-start | bytes 4718600 | tf_op jit(solution)/shard_map/ppermute | solution.py:140
  25.3 5.9 %collective-permute-start.12 = (bf16[16,4096]{1,0:T(8,128)(2,1)S(1)}, bf16[16,4096]{1,0:T(8,128)(2,1)S(1)}, u32[]{:S(2)}, u32[]{:S(2)}) collective-permute-start(bf16[16,4096]{1,0:T(8,128)(2,1)S(1)} %collective-permute-done.8.refs_8_), channel_id=1, source_target_pairs={{0,4},{1,5},{4,8},{5,9},{8,12},{9,13},{12,14},{13,15},{14,10},{15,... | collective-permute-start | bytes 393224 | tf_op jit(solution)/shard_map/ppermute | solution.py:134
  25.8 5.6 %collective-permute-start.13 = (bf16[16,4096]{1,0:T(8,128)(2,1)S(1)}, bf16[16,4096]{1,0:T(8,128)(2,1)S(1)}, u32[]{:S(2)}, u32[]{:S(2)}) collective-permute-start(bf16[16,4096]{1,0:T(8,128)(2,1)S(1)} %collective-permute-done.11.refs_11_), channel_id=1, source_target_pairs={{0,2},{1,3},{4,0},{5,1},{8,4},{9,5},{12,8},{13,9},{14,12},{15,13},... | collective-permute-start | bytes 393224 | tf_op jit(solution)/shard_map/ppermute | solution.py:135
  27.4 4.1 %collective-permute-start.14 = (bf16[16,8192]{1,0:T(8,128)(2,1)}, bf16[16,8192]{1,0:T(8,128)(2,1)S(1)}, u32[]{:S(2)}, u32[]{:S(2)}) collective-permute-start(bf16[16,8192]{1,0:T(8,128)(2,1)} %refs_8_.1), channel_id=1, source_target_pairs={{0,1},{1,0},{2,3},{3,2},{4,5},{5,4},{6,7},{7,6},{8,9},{9,8},{10,11... | collective-permute-start | bytes 786440 | tf_op jit(solution)/shard_map/ppermute | solution.py:121
  31.4 1.6 %collective-permute-start.16 = (bf16[16,8192]{1,0:T(8,128)(2,1)S(1)}, bf16[16,8192]{1,0:T(8,128)(2,1)S(1)}, u32[]{:S(2)}, u32[]{:S(2)}) collective-permute-start(bf16[16,8192]{1,0:T(8,128)(2,1)S(1)} %join_pieces.3.refs_2_), channel_id=1, source_target_pairs={{0,1},{1,0},{2,3},{3,2},{4,5},{5,4},{6,7},{7,6},{8,9},{9,8},{10,11... | collective-permute-start | bytes 786440 | tf_op jit(solution)/shard_map/ppermute | solution.py:140
  35.8 1.3 %collective-permute-start.17 = (bf16[256,64]{1,0:T(8,128)(2,1)S(1)}, bf16[256,64]{1,0:T(8,128)(2,1)S(1)}, u32[]{:S(2)}, u32[]{:S(2)}) collective-permute-start(bf16[256,64]{1,0:T(8,128)(2,1)S(1)} %get-tuple-element.30.refs_0_), channel_id=1, source_target_pairs={{0,1},{1,0},{2,3},{3,2},{4,5},{5,4},{6,7},{7,6},{8,9},{9,8},{10,11... | collective-permute-start | bytes 98312 | tf_op jit(solution)/shard_map/ppermute | solution.py:464
  37.1 9.9 %collective-permute-start.18 = (bf16[256,64]{1,0:T(8,128)(2,1)S(1)}, bf16[256,64]{1,0:T(8,128)(2,1)S(1)}, u32[]{:S(2)}, u32[]{:S(2)}) collective-permute-start(bf16[256,64]{1,0:T(8,128)(2,1)S(1)} %add_coefficients.3.rest_0_.refs_0_), channel_id=1, source_target_pairs={{0,2},{1,3},{2,0},{3,1},{4,6},{5,7},{6,4},{7,5},{8,10},{9,11},{10,... | collective-permute-start | bytes 98312 | tf_op jit(solution)/shard_map/ppermute | solution.py:464
  47.0 6.4 %collective-permute-start.19 = (bf16[256,64]{1,0:T(8,128)(2,1)S(1)}, bf16[256,64]{1,0:T(8,128)(2,1)S(1)}, u32[]{:S(2)}, u32[]{:S(2)}) collective-permute-start(bf16[256,64]{1,0:T(8,128)(2,1)S(1)} %add_coefficients.4.rest_0_.refs_0_), channel_id=1, source_target_pairs={{0,4},{1,5},{2,6},{3,7},{4,0},{5,1},{6,2},{7,3},{8,12},{9,13},{10,... | collective-permute-start | bytes 98312 | tf_op jit(solution)/shard_map/ppermute | solution.py:464
  53.4 7.4 %copy-start.2 = (bf16[16,64,896]{2,1,0:T(8,128)(2,1)S(1)}, bf16[16,64,896]{2,1,0:T(8,128)(2,1)}, u32[]{:S(2)}) copy-start(bf16[16,64,896]{2,1,0:T(8,128)(2,1)} %param.17) | copy-start | bytes 5505028
  53.5 7.4 %collective-permute-start.20 = (bf16[256,64]{1,0:T(8,128)(2,1)S(1)}, bf16[256,64]{1,0:T(8,128)(2,1)S(1)}, u32[]{:S(2)}, u32[]{:S(2)}) collective-permute-start(bf16[256,64]{1,0:T(8,128)(2,1)S(1)} %add_coefficients.5.rest_0_.refs_0_), channel_id=1, source_target_pairs={{0,8},{1,9},{2,10},{3,11},{4,12},{5,13},{6,14},{7,15},{8,0},{9,1},... | collective-permute-start | bytes 98312 | tf_op jit(solution)/shard_map/ppermute | solution.py:472
  66.8 5.4 %collective-permute-start.21 = (bf16[128,4096]{1,0:T(8,128)(2,1)S(1)}, bf16[128,4096]{1,0:T(8,128)(2,1)S(1)}, u32[]{:S(2)}, u32[]{:S(2)}) collective-permute-start(bf16[128,4096]{1,0:T(8,128)(2,1)S(1)} %get-tuple-element.35.rest_0_), channel_id=1, source_target_pairs={{0,1},{1,0},{2,3},{3,2},{4,5},{5,4},{6,7},{7,6},{8,9},{9,8},{10,11... | collective-permute-start | bytes 3145736 | tf_op jit(solution)/shard_map/ppermute | solution.py:481
  71.6 2.8 %collective-permute-start.24 = (bf16[128,4096]{1,0:T(8,128)(2,1)S(1)}, bf16[128,4096]{1,0:T(8,128)(2,1)S(1)}, u32[]{:S(2)}, u32[]{:S(2)}) collective-permute-start(bf16[128,4096]{1,0:T(8,128)(2,1)S(1)} %get-tuple-element.39), channel_id=1, source_target_pairs={{0,1},{1,0},{2,3},{3,2},{4,5},{5,4},{6,7},{7,6},{8,9},{9,8},{10,11... | collective-permute-start | bytes 3145736 | tf_op jit(solution)/shard_map/ppermute | solution.py:481
  72.2 5.6 %collective-permute-start.22 = (bf16[16,4096]{1,0:T(8,128)(2,1)S(1)}, bf16[16,4096]{1,0:T(8,128)(2,1)S(1)}, u32[]{:S(2)}, u32[]{:S(2)}) collective-permute-start(bf16[16,4096]{1,0:T(8,128)(2,1)S(1)} %get-tuple-element.36.refs_4_), channel_id=1, source_target_pairs={{0,4},{1,5},{4,8},{5,9},{8,12},{9,13},{12,14},{13,15},{14,10},{15,... | collective-permute-start | bytes 393224 | tf_op jit(solution)/shard_map/ppermute | solution.py:396
  72.7 5.3 %collective-permute-start.23 = (bf16[16,4096]{1,0:T(8,128)(2,1)S(1)}, bf16[16,4096]{1,0:T(8,128)(2,1)S(1)}, u32[]{:S(2)}, u32[]{:S(2)}) collective-permute-start(bf16[16,4096]{1,0:T(8,128)(2,1)S(1)} %get-tuple-element.37), channel_id=1, source_target_pairs={{0,2},{1,3},{4,0},{5,1},{8,4},{9,5},{12,8},{13,9},{14,12},{15,13},... | collective-permute-start | bytes 393224 | tf_op jit(solution)/shard_map/ppermute | solution.py:398
  74.5 6.4 %collective-permute-start.27 = (bf16[16,4096]{1,0:T(8,128)(2,1)S(1)}, bf16[16,4096]{1,0:T(8,128)(2,1)S(1)}, u32[]{:S(2)}, u32[]{:S(2)}) collective-permute-start(bf16[16,4096]{1,0:T(8,128)(2,1)S(1)} %get-tuple-element.40.refs_6_), channel_id=1, source_target_pairs={{0,4},{1,5},{4,8},{5,9},{8,12},{9,13},{12,14},{13,15},{14,10},{15,... | collective-permute-start | bytes 393224 | tf_op jit(solution)/shard_map/ppermute | solution.py:396
  75.0 6.4 %collective-permute-start.28 = (bf16[16,4096]{1,0:T(8,128)(2,1)S(1)}, bf16[16,4096]{1,0:T(8,128)(2,1)S(1)}, u32[]{:S(2)}, u32[]{:S(2)}) collective-permute-start(bf16[16,4096]{1,0:T(8,128)(2,1)S(1)} %get-tuple-element.43), channel_id=1, source_target_pairs={{0,2},{1,3},{4,0},{5,1},{8,4},{9,5},{12,8},{13,9},{14,12},{15,13},... | collective-permute-start | bytes 393224 | tf_op jit(solution)/shard_map/ppermute | solution.py:398
  78.1 5.5 %collective-permute-start.25 = (bf16[16,4096]{1,0:T(8,128)(2,1)S(1)}, bf16[16,4096]{1,0:T(8,128)(2,1)S(1)}, u32[]{:S(2)}, u32[]{:S(2)}) collective-permute-start(bf16[16,4096]{1,0:T(8,128)(2,1)S(1)} %get-tuple-element.41.refs_6_), channel_id=1, source_target_pairs={{0,4},{1,5},{4,8},{5,9},{8,12},{9,13},{12,14},{13,15},{14,10},{15,... | collective-permute-start | bytes 393224 | tf_op jit(solution)/shard_map/ppermute | solution.py:396
  78.7 5.5 %collective-permute-start.26 = (bf16[16,4096]{1,0:T(8,128)(2,1)S(1)}, bf16[16,4096]{1,0:T(8,128)(2,1)S(1)}, u32[]{:S(2)}, u32[]{:S(2)}) collective-permute-start(bf16[16,4096]{1,0:T(8,128)(2,1)S(1)} %get-tuple-element.42), channel_id=1, source_target_pairs={{0,2},{1,3},{4,0},{5,1},{8,4},{9,5},{12,8},{13,9},{14,12},{15,13},... | collective-permute-start | bytes 393224 | tf_op jit(solution)/shard_map/ppermute | solution.py:398
  81.5 6.3 %collective-permute-start.30 = (bf16[16,4096]{1,0:T(8,128)(2,1)S(1)}, bf16[16,4096]{1,0:T(8,128)(2,1)S(1)}, u32[]{:S(2)}, u32[]{:S(2)}) collective-permute-start(bf16[16,4096]{1,0:T(8,128)(2,1)S(1)} %get-tuple-element.44.refs_6_), channel_id=1, source_target_pairs={{0,4},{1,5},{4,8},{5,9},{8,12},{9,13},{12,14},{13,15},{14,10},{15,... | collective-permute-start | bytes 393224 | tf_op jit(solution)/shard_map/ppermute | solution.py:396
  82.1 5.7 %collective-permute-start.31 = (bf16[16,4096]{1,0:T(8,128)(2,1)S(1)}, bf16[16,4096]{1,0:T(8,128)(2,1)S(1)}, u32[]{:S(2)}, u32[]{:S(2)}) collective-permute-start(bf16[16,4096]{1,0:T(8,128)(2,1)S(1)} %get-tuple-element.46), channel_id=1, source_target_pairs={{0,2},{1,3},{4,0},{5,1},{8,4},{9,5},{12,8},{13,9},{14,12},{15,13},... | collective-permute-start | bytes 393224 | tf_op jit(solution)/shard_map/ppermute | solution.py:398
  84.3 11.4 %copy-start.8 = (bf16[8192]{0:T(1024)(128)(2,1)S(1)}, bf16[8192]{0:T(1024)(128)(2,1)}, u32[]{:S(2)}) copy-start(bf16[8192]{0:T(1024)(128)(2,1)} %param.15) | copy-start | bytes 49156
  84.3 7.2 %collective-permute-start.29 = (bf16[16,4096]{1,0:T(8,128)(2,1)S(1)}, bf16[16,4096]{1,0:T(8,128)(2,1)S(1)}, u32[]{:S(2)}, u32[]{:S(2)}) collective-permute-start(bf16[16,4096]{1,0:T(8,128)(2,1)S(1)} %get-tuple-element.45.refs_6_), channel_id=1, source_target_pairs={{0,4},{1,5},{4,8},{5,9},{8,12},{9,13},{12,14},{13,15},{14,10},{15,... | collective-permute-start | bytes 393224 | tf_op jit(solution)/shard_map/ppermute | solution.py:396
  87.9 5.8 %collective-permute-start.35 = (bf16[16,4096]{1,0:T(8,128)(2,1)S(1)}, bf16[16,4096]{1,0:T(8,128)(2,1)S(1)}, u32[]{:S(2)}, u32[]{:S(2)}) collective-permute-start(bf16[16,4096]{1,0:T(8,128)(2,1)S(1)} %get-tuple-element.49), channel_id=1, source_target_pairs={{0,2},{1,3},{4,0},{5,1},{8,4},{9,5},{12,8},{13,9},{14,12},{15,13},... | collective-permute-start | bytes 393224 | tf_op jit(solution)/shard_map/ppermute | solution.py:398
  89.5 6.3 %collective-permute-start.34 = (bf16[16,4096]{1,0:T(8,128)(2,1)S(1)}, bf16[16,4096]{1,0:T(8,128)(2,1)S(1)}, u32[]{:S(2)}, u32[]{:S(2)}) collective-permute-start(bf16[16,4096]{1,0:T(8,128)(2,1)S(1)} %get-tuple-element.47.refs_3_), channel_id=1, source_target_pairs={{0,4},{1,5},{4,8},{5,9},{8,12},{9,13},{12,14},{13,15},{14,10},{15,... | collective-permute-start | bytes 393224 | tf_op jit(solution)/shard_map/ppermute | solution.py:396
  89.9 5.9 %collective-permute-start.33 = (bf16[16,4096]{1,0:T(8,128)(2,1)S(1)}, bf16[16,4096]{1,0:T(8,128)(2,1)S(1)}, u32[]{:S(2)}, u32[]{:S(2)}) collective-permute-start(bf16[16,4096]{1,0:T(8,128)(2,1)S(1)} %get-tuple-element.48), channel_id=1, source_target_pairs={{0,2},{1,3},{4,0},{5,1},{8,4},{9,5},{12,8},{13,9},{14,12},{15,13},... | collective-permute-start | bytes 393224 | tf_op jit(solution)/shard_map/ppermute | solution.py:398
  93.7 5.0 %collective-permute-start.36 = (bf16[16,4096]{1,0:T(8,128)(2,1)S(1)}, bf16[16,4096]{1,0:T(8,128)(2,1)S(1)}, u32[]{:S(2)}, u32[]{:S(2)}) collective-permute-start(bf16[16,4096]{1,0:T(8,128)(2,1)S(1)} %add_blocks.15), channel_id=1, source_target_pairs={{0,2},{1,3},{4,0},{5,1},{8,4},{9,5},{12,8},{13,9},{14,12},{15,13},... | collective-permute-start | bytes 393224 | tf_op jit(solution)/shard_map/ppermute | solution.py:398
  95.7 5.0 %collective-permute-start.32 = (bf16[16,4096]{1,0:T(8,128)(2,1)S(1)}, bf16[16,4096]{1,0:T(8,128)(2,1)S(1)}, u32[]{:S(2)}, u32[]{:S(2)}) collective-permute-start(bf16[16,4096]{1,0:T(8,128)(2,1)S(1)} %add_blocks.14.refs_3_), channel_id=1, source_target_pairs={{0,4},{1,5},{4,8},{5,9},{8,12},{9,13},{12,14},{13,15},{14,10},{15,... | collective-permute-start | bytes 393224 | tf_op jit(solution)/shard_map/ppermute | solution.py:396

commit v5 on v4

--- a/solution.py
+++ b/solution.py
@@ -10,9 +10,8 @@
 adapter_alpha = 32.0
 AXIS = "mp"
 HALVES = 2
-DEPTH_BLOCK = 512
+DEPTH_BLOCK = 1024
 WIDTH_BLOCK = 512
-IN_FLIGHT = 4
 VMEM_LIMIT = 16 * 1024 * 1024
 STREAM_LIMIT = 46 * 1024 * 1024
 
@@ -115,7 +114,7 @@
     )
 
 
-def gather_rows(own, size, ordered):
+def gather_rows(own, size, masks_after):
     chips = size // 2
     last = chips // 2
     other = lax.ppermute(own, AXIS, flip(size, 1))
@@ -134,18 +133,21 @@
             pieces.append(lax.ppermute(right[0], AXIS, ring(size, 1)))
             pieces.append(lax.ppermute(left[1], AXIS, ring(size, -1)))
         if step >= last - 1:
-            part = join(pieces, ordered if step < last else [])
+            part = join(pieces, [masks[0]] if step == last else [])
             pieces = []
             mine.append(part)
             theirs.append(lax.ppermute(part, AXIS, flip(size, 1)))
-    return mine + theirs
-
-
-def row_masks(me, tables, own_rows, size, slots, rank_limit):
+            if step < last:
+                masks = masks_after(part)
+    return mine + theirs, masks
+
+
+def row_masks(me, tables, own_rows, size, slots, rank_limit, ordered):
     batch_rows = own_rows * size
     adapters = tables[2].shape[1]
 
-    def kernel(me_ref, start, segment_adapter, ranks, slot_of, scale, to_place, from_place, hot):
+    def kernel(me_ref, start, segment_adapter, ranks, slot_of, *rest):
+        scale, to_place, from_place, hot = rest[-4:]
         me = me_ref[0]
         row = lax.broadcasted_iota(jnp.int32, (batch_rows, 1), 0)
         column = lax.broadcasted_iota(jnp.int32, (1, batch_rows), 1)
@@ -171,11 +173,13 @@
         kernel,
         out_shape=shapes,
         grid=(1,),
-        in_specs=[whole(pltpu.SMEM)] + [pl.BlockSpec(t.shape, lambda i: (0, 0)) for t in tables],
+        in_specs=[whole(pltpu.SMEM)]
+        + [pl.BlockSpec(t.shape, lambda i: (0, 0)) for t in tables]
+        + [whole(pl.ANY)] * len(ordered),
         out_specs=[pl.BlockSpec(shape.shape, lambda i: (0, 0)) for shape in shapes],
         compiler_params=pltpu.CompilerParams(vmem_limit_bytes=VMEM_LIMIT),
         name="row_masks",
-    )(me, *tables)
+    )(me, *tables, *ordered)
 
 
 def shrink_rows(parts, shrink_factors, scale, to_place):
@@ -237,33 +241,47 @@
     )
 
 
-def streamed(source, pieces, buffers, arrived):
-    slots = buffers.shape[0]
-    copies = [
-        pltpu.make_async_copy(source.at[piece], buffers.at[i % slots], arrived.at[i % slots])
-        for i, piece in enumerate(pieces)
-    ]
-    for copy in copies[:slots]:
-        copy.start()
-    for i, copy in enumerate(copies):
-        copy.wait()
+def streamed(source, blocks, buffers, arrived):
+    slots, depth = buffers.shape[:2]
+    parts = arrived.shape[1]
+    step = depth // parts
+
+    def copies(i):
+        rows, columns = blocks[i]
+        return [
+            pltpu.make_async_copy(
+                source.at[rows + p * step : rows + (p + 1) * step, columns],
+                buffers.at[i % slots, p * step : (p + 1) * step],
+                arrived.at[i % slots, p],
+            )
+            for p in range(parts)
+        ]
+
+    def start(i):
+        for copy in copies(i):
+            copy.start()
+
+    for i in range(min(slots, len(blocks))):
+        start(i)
+    for i in range(len(blocks)):
+        for copy in copies(i):
+            copy.wait()
         yield i, buffers[i % slots]
-        if i + slots < len(copies):
-            copies[i + slots].start()
+        if i + slots < len(blocks):
+            start(i + slots)
 
 
 def matmul(rows, weight, name, first, last, ordered=()):
     batch_rows = rows.shape[0]
     width = weight.shape[1]
     starts = range(first, last, DEPTH_BLOCK)
-    pieces = [(slice(at, at + DEPTH_BLOCK), slice(None)) for at in starts]
+    blocks = [(at, slice(None)) for at in starts]
 
     def kernel(rows_ref, weight_ref, *rest):
         out, buffers, arrived = rest[-3:]
-        for i, block in streamed(weight_ref, pieces, buffers, arrived):
-            product = jnp.dot(
-                rows_ref[:, pieces[i][0]], block, preferred_element_type=jnp.float32
-            )
+        for i, block in streamed(weight_ref, blocks, buffers, arrived):
+            at = slice(blocks[i][0], blocks[i][0] + DEPTH_BLOCK)
+            product = jnp.dot(rows_ref[:, at], block, preferred_element_type=jnp.float32)
             out[...] = product if i == 0 else out[...] + product
 
     return pl.pallas_call(
@@ -272,8 +290,8 @@
         in_specs=[whole(), whole(pltpu.HBM)] + [whole(pl.ANY)] * len(ordered),
         out_specs=whole(),
         scratch_shapes=[
-            pltpu.VMEM((IN_FLIGHT, DEPTH_BLOCK, width), weight.dtype),
-            pltpu.SemaphoreType.DMA((IN_FLIGHT,)),
+            pltpu.VMEM((3, DEPTH_BLOCK, width), weight.dtype),
+            pltpu.SemaphoreType.DMA((3, 4)),
         ],
         compiler_params=pltpu.CompilerParams(vmem_limit_bytes=STREAM_LIMIT),
         cost_estimate=pl.CostEstimate(
@@ -323,11 +341,11 @@
     width = down_weight.shape[1] // HALVES
     core_rows = batch_rows // 2
     starts = range(half * width, (half + 1) * width, WIDTH_BLOCK)
-    pieces = [(slice(None), slice(at, at + WIDTH_BLOCK)) for at in starts]
+    blocks = [(0, slice(at, at + WIDTH_BLOCK)) for at in starts]
 
     def kernel(hidden_ref, weight, *rest):
         mine, theirs, buffers, arrived = rest[-4:]
-        for i, block in streamed(weight, pieces, buffers, arrived):
+        for i, block in streamed(weight, blocks, buffers, arrived):
             product = jnp.dot(
                 hidden_ref[...], block, preferred_element_type=jnp.float32
             ).astype(jnp.bfloat16)
@@ -342,8 +360,8 @@
         in_specs=[whole(), whole(pltpu.HBM)] + [whole(pl.ANY)] * len(ordered),
         out_specs=[whole()] * 2,
         scratch_shapes=[
-            pltpu.VMEM((IN_FLIGHT, hidden_width, WIDTH_BLOCK), down_weight.dtype),
-            pltpu.SemaphoreType.DMA((IN_FLIGHT,)),
+            pltpu.VMEM((6, hidden_width, WIDTH_BLOCK), down_weight.dtype),
+            pltpu.SemaphoreType.DMA((6, 2)),
         ],
         compiler_params=pltpu.CompilerParams(vmem_limit_bytes=STREAM_LIMIT),
         cost_estimate=pl.CostEstimate(
@@ -387,15 +405,19 @@
             sides = []
             if steps_right > 0:
                 index = min(2 * steps_right, chips - 1)
-                sides.append((mine[h], theirs[h], index, right[h]))
+                sides.append((right, 1, index))
             if steps_left > 0:
-                sides.append((mine[h], theirs[h], 2 * steps_left - 1, left[h]))
-            sums = list(add_blocks(sides, own_rows, ordered))
+                sides.append((left, -1, 2 * steps_left - 1))
+            if h == 1:
+                sides.reverse()
+            sums = add_blocks(
+                [(mine[h], theirs[h], index, chain[h]) for chain, _, index in sides],
+                own_rows,
+                ordered,
+            )
             ordered = [sums[0]]
-            if steps_right > 0:
-                right[h] = lax.ppermute(sums.pop(0), AXIS, ring(size, 1))
-            if steps_left > 0:
-                left[h] = lax.ppermute(sums.pop(0), AXIS, ring(size, -1))
+            for (chain, by, _), value in zip(sides, sums):
+                chain[h] = lax.ppermute(value, AXIS, ring(size, by))
     return list(zip(mine, theirs, right, left))
 
 
@@ -453,9 +475,11 @@
         table[None]
         for table in (segment_start, segment_adapter, adapter_ranks, adapter_storage_slot)
     ]
-    scale, to_place, from_place, hot = row_masks(me, tables, own_rows, size, slots, rank_limit)
-
-    parts = gather_rows(activations, size, [scale])
+    parts, (scale, to_place, from_place, hot) = gather_rows(
+        activations,
+        size,
+        lambda part: row_masks(me, tables, own_rows, size, slots, rank_limit, [part]),
+    )
     rows, coeff = shrink_rows(parts, shrink_factors, scale, to_place)
 
     bits = [1 << b for b in range(size.bit_length() - 1)]

time: 102 us -> 105 us (1.029)
  Pallas kernels: 33.4 us -> 34.7 us
  local copies, waits for them, and re-layouts: 3.6 us -> 4.82 us
    ppermute x1, waiting for transfers between devices: 3.82 us -> 0.94 us  [gather_rows(): pieces.append(lax.ppermute(right[0], AXIS, ring(size, 1)))]
    pallas_call x17, Pallas kernels: 5.59 us -> 8.36 us  [call(): pl.pallas_call(run, out_shape=out_shape, in_specs=[whole(pltpu.SMEM if op...]
    pallas_call x3, Pallas kernels: 17.7 us -> 16 us  [matmul(): pl.pallas_call(kernel, out_shape=jax.ShapeDtypeStruct((batch_rows, width)...]
    ppermute x3, waiting for transfers between devices: 0.01 us -> 1.46 us  [gather_rows(): right[0] = lax.ppermute(right[0], AXIS, ring(size, 1))]
    unnamed x18, local copies, waits for them, and re-layouts: 3.58 us -> 4.8 us
  transfers between devices with their start and end apart: 37 -> 37, of which waited for: 19 -> 24; matrix products, arithmetic and copies ran while one was open for 0% -> 0% of each run, Pallas kernels for 23% -> 22%
where the time goes in v5:
time: 105 us
  starting transfers between devices  38.3 us (36%)
  Pallas kernels  34.7 us (33%)
  waiting for transfers between devices  26.2 us (25%)
  local copies, waits for them, and re-layouts  4.82 us (5%)
    pallas_call x3, Pallas kernels, matmul(): pl.pallas_call(kernel, out_shape=jax.ShapeDtypeStruct((batch_rows, width)...  16 us
    ppermute x14, starting transfers between devices, scatter_rows(): chain[h] = lax.ppermute(value, AXIS, ring(size, by))  15.6 us
    ppermute x14, waiting for transfers between devices, scatter_rows(): chain[h] = lax.ppermute(value, AXIS, ring(size, by))  12.7 us
    pallas_call x2, Pallas kernels, down_rows(): pl.pallas_call(kernel, out_shape=(part, part), in_specs=[whole(), whole(p...  9.78 us
    pallas_call x17, Pallas kernels, call(): pl.pallas_call(run, out_shape=out_shape, in_specs=[whole(pltpu.SMEM if op...  8.36 us
    ppermute x3, starting transfers between devices, gather_rows(): left[1] = lax.ppermute(left[1], AXIS, ring(size, -1))  7.08 us
    ppermute x3, starting transfers between devices, gather_rows(): left[0] = lax.ppermute(left[0], AXIS, ring(size, -1))  5.78 us
    unnamed x18, local copies, waits for them, and re-layouts  4.8 us
  transfers between devices with their start and end apart: 37, of which 24 were waited for; matrix products, arithmetic and copies ran while one was open for 0% of the time, Pallas kernels for 22%

profile of v5, /device:TPU:0, one launch (start us, length us, event | category | flops | bytes accessed | tf_op | source)
XLA Modules:
  0.0 105.0 jit_solution(4839748342328839555)
XLA Ops:
  0.6 0.9 copy-done
  1.6 3.0 %collective-permute-start.3 = (bf16[16,4096]{1,0:T(8,128)(2,1)S(1)}, bf16[16,4096]{1,0:T(8,128)(2,1)S(1)}, u32[]{:S(2)}, u32[]{:S(2)}) collective-permute-start(bf16[16,4096]{1,0:T(8,128)(2,1)S(1)} %get-tuple-element.27), channel_id=1, source_target_pairs={{0,2},{1,3},{4,0},{5,1},{8,4},{9,5},{12,8},{13,9},{14,12},{15,13},... | collective-permute-start | bytes 393224 | tf_op jit(solution)/shard_map/ppermute | solution.py:128
  4.7 1.9 %collective-permute-start.2 = (bf16[16,4096]{1,0:T(8,128)(2,1)S(1)}, bf16[16,4096]{1,0:T(8,128)(2,1)S(1)}, u32[]{:S(2)}, u32[]{:S(2)}) collective-permute-start(bf16[16,4096]{1,0:T(8,128)(2,1)S(1)} %get-tuple-element.26), channel_id=1, source_target_pairs={{0,2},{1,3},{4,0},{5,1},{8,4},{9,5},{12,8},{13,9},{14,12},{15,13},... | collective-permute-start | bytes 393224 | tf_op jit(solution)/shard_map/ppermute | solution.py:130
  6.8 2.2 %collective-permute-done.3.refs_3_ = bf16[16,4096]{1,0:T(8,128)(2,1)S(1)} collective-permute-done((bf16[16,4096]{1,0:T(8,128)(2,1)S(1)}, bf16[16,4096]{1,0:T(8,128)(2,1)S(1)}, u32[]{:S(2)}, u32[]{:S(2)}) %collective-permute-start.3) | collective-permute-done | bytes 131104 | tf_op jit(solution)/shard_map/ppermute | solution.py:128
  9.0 2.0 %collective-permute-start.7 = (bf16[16,4096]{1,0:T(8,128)(2,1)S(1)}, bf16[16,4096]{1,0:T(8,128)(2,1)S(1)}, u32[]{:S(2)}, u32[]{:S(2)}) collective-permute-start(bf16[16,4096]{1,0:T(8,128)(2,1)S(1)} %collective-permute-done.3.refs_3_), channel_id=1, source_target_pairs={{0,2},{1,3},{4,0},{5,1},{8,4},{9,5},{12,8},{13,9},{14,12},{15,13},... | collective-permute-start | bytes 393224 | tf_op jit(solution)/shard_map/ppermute | solution.py:128
  11.1 0.7 collective-permute-done.2.refs_2_
  11.8 2.0 %collective-permute-start.6 = (bf16[16,4096]{1,0:T(8,128)(2,1)S(1)}, bf16[16,4096]{1,0:T(8,128)(2,1)S(1)}, u32[]{:S(2)}, u32[]{:S(2)}) collective-permute-start(bf16[16,4096]{1,0:T(8,128)(2,1)S(1)} %collective-permute-done.2.refs_2_), channel_id=1, source_target_pairs={{0,2},{1,3},{4,0},{5,1},{8,4},{9,5},{12,8},{13,9},{14,12},{15,13},... | collective-permute-start | bytes 393224 | tf_op jit(solution)/shard_map/ppermute | solution.py:130
  13.9 1.3 %collective-permute-done.7.refs_7_ = bf16[16,4096]{1,0:T(8,128)(2,1)S(1)} collective-permute-done((bf16[16,4096]{1,0:T(8,128)(2,1)S(1)}, bf16[16,4096]{1,0:T(8,128)(2,1)S(1)}, u32[]{:S(2)}, u32[]{:S(2)}) %collective-permute-start.7) | collective-permute-done | bytes 131104 | tf_op jit(solution)/shard_map/ppermute | solution.py:128
  15.2 2.1 %collective-permute-start.11 = (bf16[16,4096]{1,0:T(8,128)(2,1)S(1)}, bf16[16,4096]{1,0:T(8,128)(2,1)S(1)}, u32[]{:S(2)}, u32[]{:S(2)}) collective-permute-start(bf16[16,4096]{1,0:T(8,128)(2,1)S(1)} %collective-permute-done.7.refs_7_), channel_id=1, source_target_pairs={{0,2},{1,3},{4,0},{5,1},{8,4},{9,5},{12,8},{13,9},{14,12},{15,13},... | collective-permute-start | bytes 393224 | tf_op jit(solution)/shard_map/ppermute | solution.py:128
  17.5 0.8 collective-permute-done.6.refs_6_
  18.3 1.9 %collective-permute-start.10 = (bf16[16,4096]{1,0:T(8,128)(2,1)S(1)}, bf16[16,4096]{1,0:T(8,128)(2,1)S(1)}, u32[]{:S(2)}, u32[]{:S(2)}) collective-permute-start(bf16[16,4096]{1,0:T(8,128)(2,1)S(1)} %collective-permute-done.6.refs_6_), channel_id=1, source_target_pairs={{0,2},{1,3},{4,0},{5,1},{8,4},{9,5},{12,8},{13,9},{14,12},{15,13},... | collective-permute-start | bytes 393224 | tf_op jit(solution)/shard_map/ppermute | solution.py:130
  20.3 0.7 collective-permute-done.11.refs_11_
  21.0 1.4 %collective-permute-done.8.refs_8_ = bf16[16,4096]{1,0:T(8,128)(2,1)} collective-permute-done((bf16[16,4096]{1,0:T(8,128)(2,1)S(1)}, bf16[16,4096]{1,0:T(8,128)(2,1)}, u32[]{:S(2)}, u32[]{:S(2)}) %collective-permute-start.8) | collective-permute-done | bytes 131104 | tf_op jit(solution)/shard_map/ppermute | solution.py:127
  22.5 0.8 collective-permute-done.10.refs_10_
  23.3 1.9 %collective-permute-done.9.refs_9_ = bf16[16,4096]{1,0:T(8,128)(2,1)S(1)} collective-permute-done((bf16[16,4096]{1,0:T(8,128)(2,1)S(1)}, bf16[16,4096]{1,0:T(8,128)(2,1)S(1)}, u32[]{:S(2)}, u32[]{:S(2)}) %collective-permute-start.9) | collective-permute-done | bytes 131104 | tf_op jit(solution)/shard_map/ppermute | solution.py:129
  25.1 1.0 join_pieces.2.rest_0_.refs_1_
  26.4 1.9 %collective-permute-start.13 = (bf16[16,4096]{1,0:T(8,128)(2,1)S(1)}, bf16[16,4096]{1,0:T(8,128)(2,1)}, u32[]{:S(2)}, u32[]{:S(2)}) collective-permute-start(bf16[16,4096]{1,0:T(8,128)(2,1)S(1)} %collective-permute-done.11.refs_11_), channel_id=1, source_target_pairs={{0,2},{1,3},{4,0},{5,1},{8,4},{9,5},{12,8},{13,9},{14,12},{15,13},... | collective-permute-start | bytes 393224 | tf_op jit(solution)/shard_map/ppermute | solution.py:134
  31.5 0.9 collective-permute-done.12.refs_0_
  32.4 1.0 join_pieces.3.refs_2_
  33.5 1.5 %collective-permute-done.16.refs_5_ = bf16[16,8192]{1,0:T(8,128)(2,1)S(1)} collective-permute-done((bf16[16,8192]{1,0:T(8,128)(2,1)S(1)}, bf16[16,8192]{1,0:T(8,128)(2,1)S(1)}, u32[]{:S(2)}, u32[]{:S(2)}) %collective-permute-start.16) | collective-permute-done | bytes 262176 | tf_op jit(solution)/shard_map/ppermute | solution.py:139
  35.0 1.2 %copy-done.3 = bf16[1,8192,64]{1,2,0:T(8,128)(2,1)S(1)} copy-done((bf16[1,8192,64]{1,2,0:T(8,128)(2,1)S(1)}, bf16[1,8192,64]{1,2,0:T(8,128)(2,1)}, u32[]{:S(2)}) %copy-start.3) | copy-done | bytes 1048600
  36.2 3.7 %shrink_rows.1 = (bf16[256,8192]{1,0:T(8,128)(2,1)S(1)}, bf16[256,64]{1,0:T(8,128)(2,1)S(1)}) custom-call(bf16[16,8192]{1,0:T(8,128)(2,1)S(1)} %copy-done.1, bf16[96,8192]{1,0:T(8,128)(2,1)S(1)} %join_pieces.2.rest_0_.refs_1_, bf16[16,8192]{1,0:T(8,128)(2,1)S(1)} %join_pieces.3.refs_2_, bf16[16,8192]{1,0:T(8,128)(2,1)} %collective-permute-done.14.refs_3_, ...), custom_call_target="tpu_custom_call" | custom-call | flops 268435456 | bytes 8388608 | tf_op jit(solution)/shard_map/shrink_rows/pallas_call | solution.py:76
  40.1 1.1 %collective-permute-done.17.refs_1_ = bf16[256,64]{1,0:T(8,128)(2,1)S(1)} collective-permute-done((bf16[256,64]{1,0:T(8,128)(2,1)S(1)}, bf16[256,64]{1,0:T(8,128)(2,1)S(1)}, u32[]{:S(2)}, u32[]{:S(2)}) %collective-permute-start.17) | collective-permute-done | bytes 32800 | tf_op jit(solution)/shard_map/ppermute | solution.py:488
  41.3 1.7 %collective-permute-start.18 = (bf16[256,64]{1,0:T(8,128)(2,1)S(1)}, bf16[256,64]{1,0:T(8,128)(2,1)S(1)}, u32[]{:S(2)}, u32[]{:S(2)}) collective-permute-start(bf16[256,64]{1,0:T(8,128)(2,1)S(1)} %add_coefficients.3.rest_0_.refs_0_), channel_id=1, source_target_pairs={{0,2},{1,3},{2,0},{3,1},{4,6},{5,7},{6,4},{7,5},{8,10},{9,11},{10,... | collective-permute-start | bytes 98312 | tf_op jit(solution)/shard_map/ppermute | solution.py:488
  42.9 7.3 %gate_rows.1.refs_2_.refs_5_ = f32[256,896]{1,0:T(8,128)S(1)} custom-call(bf16[256,8192]{1,0:T(8,128)(2,1)S(1)} %get-tuple-element.31.rows_ref, bf16[8192,896]{1,0:T(8,128)(2,1)} %weight_ref.3, bf16[256,64]{1,0:T(8,128)(2,1)S(1)} %add_coefficients.3.rest_0_.refs_0_), custom_call_target="tpu_custom_call" | custom-call | flops 3758096384 | bytes 14680064 | tf_op jit(solution)/shard_map/gate_rows/pallas_call | solution.py:287
  50.2 1.6 %collective-permute-start.19 = (bf16[256,64]{1,0:T(8,128)(2,1)S(1)}, bf16[256,64]{1,0:T(8,128)(2,1)S(1)}, u32[]{:S(2)}, u32[]{:S(2)}) collective-permute-start(bf16[256,64]{1,0:T(8,128)(2,1)S(1)} %add_coefficients.4.rest_0_.refs_0_), channel_id=1, source_target_pairs={{0,4},{1,5},{2,6},{3,7},{4,0},{5,1},{6,2},{7,3},{8,12},{9,13},{10,... | collective-permute-start | bytes 98312 | tf_op jit(solution)/shard_map/ppermute | solution.py:488
  51.9 4.4 %up_rows.2.refs_2_.refs_6_ = f32[256,896]{1,0:T(8,128)S(1)} custom-call(bf16[256,8192]{1,0:T(8,128)(2,1)S(1)} %get-tuple-element.31.rows_ref, bf16[8192,896]{1,0:T(8,128)(2,1)} %weight_ref.5, bf16[256,64]{1,0:T(8,128)(2,1)S(1)} %add_coefficients.4.rest_0_.refs_0_), custom_call_target="tpu_custom_call" | custom-call | flops 1879048192 | bytes 7340032 | tf_op jit(solution)/shard_map/up_rows/pallas_call | solution.py:287
  56.3 2.6 %collective-permute-start.20 = (bf16[256,64]{1,0:T(8,128)(2,1)S(1)}, bf16[256,64]{1,0:T(8,128)(2,1)S(1)}, u32[]{:S(2)}, u32[]{:S(2)}) collective-permute-start(bf16[256,64]{1,0:T(8,128)(2,1)S(1)} %add_coefficients.5.rest_0_.refs_0_), channel_id=1, source_target_pairs={{0,8},{1,9},{2,10},{3,11},{4,12},{5,13},{6,14},{7,15},{8,0},{9,1},... | collective-permute-start | bytes 98312 | tf_op jit(solution)/shard_map/ppermute | solution.py:496
  58.9 4.4 %up_rows.3.refs_7_ = f32[256,896]{1,0:T(8,128)S(1)} custom-call(bf16[256,8192]{1,0:T(8,128)(2,1)S(1)} %get-tuple-element.31.rows_ref, bf16[8192,896]{1,0:T(8,128)(2,1)} %weight_ref.5, bf16[256,64]{1,0:T(8,128)(2,1)S(1)} %add_coefficients.5.rest_0_.refs_0_), custom_call_target="tpu_custom_call" | custom-call | flops 1879048192 | bytes 7340032 | tf_op jit(solution)/shard_map/up_rows/pallas_call | solution.py:287
  63.3 1.0 hidden_rows.1.hidden_ref
  64.3 5.0 %down_rows.2 = (bf16[128,4096]{1,0:T(8,128)(2,1)S(1)}, bf16[128,4096]{1,0:T(8,128)(2,1)S(1)}) custom-call(bf16[256,896]{1,0:T(8,128)(2,1)S(1)} %hidden_rows.1.hidden_ref, bf16[896,8192]{1,0:T(8,128)(2,1)} %weight.3), custom_call_target="tpu_custom_call" | custom-call | flops 1879048192 | bytes 7340032 | tf_op jit(solution)/shard_map/down_rows/pallas_call | solution.py:357
  69.4 4.8 %down_rows.3 = (bf16[128,4096]{1,0:T(8,128)(2,1)S(1)}, bf16[128,4096]{1,0:T(8,128)(2,1)S(1)}) custom-call(bf16[256,896]{1,0:T(8,128)(2,1)S(1)} %hidden_rows.1.hidden_ref, bf16[896,8192]{1,0:T(8,128)(2,1)} %weight.3, bf16[128,4096]{1,0:T(8,128)(2,1)S(1)} %get-tuple-element.35.rest_0_), custom_call_target="tpu_custom_call" | custom-call | flops 1879048192 | bytes 7340032 | tf_op jit(solution)/shard_map/down_rows/pallas_call | solution.py:357
  75.4 1.5 %collective-permute-start.23 = (bf16[16,4096]{1,0:T(8,128)(2,1)S(1)}, bf16[16,4096]{1,0:T(8,128)(2,1)S(1)}, u32[]{:S(2)}, u32[]{:S(2)}) collective-permute-start(bf16[16,4096]{1,0:T(8,128)(2,1)S(1)} %get-tuple-element.37), channel_id=1, source_target_pairs={{0,2},{1,3},{4,0},{5,1},{8,4},{9,5},{12,8},{13,9},{14,12},{15,13},... | collective-permute-start | bytes 393224 | tf_op jit(solution)/shard_map/ppermute | solution.py:420
  77.7 1.5 %collective-permute-start.28 = (bf16[16,4096]{1,0:T(8,128)(2,1)S(1)}, bf16[16,4096]{1,0:T(8,128)(2,1)S(1)}, u32[]{:S(2)}, u32[]{:S(2)}) collective-permute-start(bf16[16,4096]{1,0:T(8,128)(2,1)S(1)} %get-tuple-element.43), channel_id=1, source_target_pairs={{0,4},{1,5},{4,8},{5,9},{8,12},{9,13},{12,14},{13,15},{14,10},{15,... | collective-permute-start | bytes 393224 | tf_op jit(solution)/shard_map/ppermute | solution.py:420
  79.2 1.1 %collective-permute-done.22.refs_2_ = bf16[16,4096]{1,0:T(8,128)(2,1)S(1)} collective-permute-done((bf16[16,4096]{1,0:T(8,128)(2,1)S(1)}, bf16[16,4096]{1,0:T(8,128)(2,1)S(1)}, u32[]{:S(2)}, u32[]{:S(2)}) %collective-permute-start.22) | collective-permute-done | bytes 131104 | tf_op jit(solution)/shard_map/ppermute | solution.py:420
  81.0 1.3 %collective-permute-start.25 = (bf16[16,4096]{1,0:T(8,128)(2,1)S(1)}, bf16[16,4096]{1,0:T(8,128)(2,1)S(1)}, u32[]{:S(2)}, u32[]{:S(2)}) collective-permute-start(bf16[16,4096]{1,0:T(8,128)(2,1)S(1)} %get-tuple-element.41.refs_6_), channel_id=1, source_target_pairs={{0,4},{1,5},{4,8},{5,9},{8,12},{9,13},{12,14},{13,15},{14,10},{15,... | collective-permute-start | bytes 393224 | tf_op jit(solution)/shard_map/ppermute | solution.py:420
  82.3 1.2 %collective-permute-start.26 = (bf16[16,4096]{1,0:T(8,128)(2,1)S(1)}, bf16[16,4096]{1,0:T(8,128)(2,1)S(1)}, u32[]{:S(2)}, u32[]{:S(2)}) collective-permute-start(bf16[16,4096]{1,0:T(8,128)(2,1)S(1)} %get-tuple-element.42), channel_id=1, source_target_pairs={{0,2},{1,3},{4,0},{5,1},{8,4},{9,5},{12,8},{13,9},{14,12},{15,13},... | collective-permute-start | bytes 393224 | tf_op jit(solution)/shard_map/ppermute | solution.py:420
  84.2 1.7 %collective-permute-start.30 = (bf16[16,4096]{1,0:T(8,128)(2,1)S(1)}, bf16[16,4096]{1,0:T(8,128)(2,1)S(1)}, u32[]{:S(2)}, u32[]{:S(2)}) collective-permute-start(bf16[16,4096]{1,0:T(8,128)(2,1)S(1)} %get-tuple-element.44.refs_6_), channel_id=1, source_target_pairs={{0,2},{1,3},{4,0},{5,1},{8,4},{9,5},{12,8},{13,9},{14,12},{15,13},... | collective-permute-start | bytes 393224 | tf_op jit(solution)/shard_map/ppermute | solution.py:420
  86.6 2.0 %collective-permute-done.26.refs_5_ = bf16[16,4096]{1,0:T(8,128)(2,1)S(1)} collective-permute-done((bf16[16,4096]{1,0:T(8,128)(2,1)S(1)}, bf16[16,4096]{1,0:T(8,128)(2,1)S(1)}, u32[]{:S(2)}, u32[]{:S(2)}) %collective-permute-start.26) | collective-permute-done | bytes 131104 | tf_op jit(solution)/shard_map/ppermute | solution.py:420
  88.8 0.7 collective-permute-start.29
  90.1 0.8 collective-permute-done.31.refs_5_
  90.9 1.6 %collective-permute-start.35 = (bf16[16,4096]{1,0:T(8,128)(2,1)S(1)}, bf16[16,4096]{1,0:T(8,128)(2,1)S(1)}, u32[]{:S(2)}, u32[]{:S(2)}) collective-permute-start(bf16[16,4096]{1,0:T(8,128)(2,1)S(1)} %get-tuple-element.47.refs_3_), channel_id=1, source_target_pairs={{0,2},{1,3},{4,0},{5,1},{8,4},{9,5},{12,8},{13,9},{14,12},{15,13},... | collective-permute-start | bytes 393224 | tf_op jit(solution)/shard_map/ppermute | solution.py:420
  93.0 1.6 %collective-permute-start.33 = (bf16[16,4096]{1,0:T(8,128)(2,1)S(1)}, bf16[16,4096]{1,0:T(8,128)(2,1)S(1)}, u32[]{:S(2)}, u32[]{:S(2)}) collective-permute-start(bf16[16,4096]{1,0:T(8,128)(2,1)S(1)} %get-tuple-element.48), channel_id=1, source_target_pairs={{0,2},{1,3},{4,0},{5,1},{8,4},{9,5},{12,8},{13,9},{14,12},{15,13},... | collective-permute-start | bytes 393224 | tf_op jit(solution)/shard_map/ppermute | solution.py:420
  94.7 1.7 %collective-permute-done.35.refs_2_ = bf16[16,4096]{1,0:T(8,128)(2,1)S(1)} collective-permute-done((bf16[16,4096]{1,0:T(8,128)(2,1)S(1)}, bf16[16,4096]{1,0:T(8,128)(2,1)S(1)}, u32[]{:S(2)}, u32[]{:S(2)}) %collective-permute-start.35) | collective-permute-done | bytes 131104 | tf_op jit(solution)/shard_map/ppermute | solution.py:420
  96.5 2.5 %collective-permute-start.36 = (bf16[16,4096]{1,0:T(8,128)(2,1)S(1)}, bf16[16,4096]{1,0:T(8,128)(2,1)S(1)}, u32[]{:S(2)}, u32[]{:S(2)}) collective-permute-start(bf16[16,4096]{1,0:T(8,128)(2,1)S(1)} %add_blocks.15), channel_id=1, source_target_pairs={{0,2},{1,3},{4,0},{5,1},{8,4},{9,5},{12,8},{13,9},{14,12},{15,13},... | collective-permute-start | bytes 393224 | tf_op jit(solution)/shard_map/ppermute | solution.py:420
  99.0 2.5 %collective-permute-done.36.refs_7_ = bf16[16,4096]{1,0:T(8,128)(2,1)S(1)} collective-permute-done((bf16[16,4096]{1,0:T(8,128)(2,1)S(1)}, bf16[16,4096]{1,0:T(8,128)(2,1)S(1)}, u32[]{:S(2)}, u32[]{:S(2)}) %collective-permute-start.36) | collective-permute-done | bytes 131104 | tf_op jit(solution)/shard_map/ppermute | solution.py:420
  101.5 2.4 %collective-permute-done.32.refs_2_ = bf16[16,4096]{1,0:T(8,128)(2,1)S(1)} collective-permute-done((bf16[16,4096]{1,0:T(8,128)(2,1)S(1)}, bf16[16,4096]{1,0:T(8,128)(2,1)S(1)}, u32[]{:S(2)}, u32[]{:S(2)}) %collective-permute-start.32) | collective-permute-done | bytes 131104 | tf_op jit(solution)/shard_map/ppermute | solution.py:420
  103.9 1.0 finish_rows.1
  (68 shorter events, 10.4 us)
Async XLA Ops:
  0.6 1.0 copy-start
  1.6 33.4 %copy-start.1 = (bf16[16,8192]{1,0:T(8,128)(2,1)S(1)}, bf16[16,8192]{1,0:T(8,128)(2,1)}, u32[]{:S(2)}) copy-start(bf16[16,8192]{1,0:T(8,128)(2,1)} %refs_8_.1) | copy-start | bytes 786436
  1.6 7.4 %collective-permute-start.3 = (bf16[16,4096]{1,0:T(8,128)(2,1)S(1)}, bf16[16,4096]{1,0:T(8,128)(2,1)S(1)}, u32[]{:S(2)}, u32[]{:S(2)}) collective-permute-start(bf16[16,4096]{1,0:T(8,128)(2,1)S(1)} %get-tuple-element.27), channel_id=1, source_target_pairs={{0,2},{1,3},{4,0},{5,1},{8,4},{9,5},{12,8},{13,9},{14,12},{15,13},... | collective-permute-start | bytes 393224 | tf_op jit(solution)/shard_map/ppermute | solution.py:128
  4.6 6.4 %collective-permute-start = (bf16[16,4096]{1,0:T(8,128)(2,1)S(1)}, bf16[16,4096]{1,0:T(8,128)(2,1)S(1)}, u32[]{:S(2)}, u32[]{:S(2)}) collective-permute-start(bf16[16,4096]{1,0:T(8,128)(2,1)S(1)} %get-tuple-element.26), channel_id=1, source_target_pairs={{0,4},{1,5},{4,8},{5,9},{8,12},{9,13},{12,14},{13,15},{14,10},{15,... | collective-permute-start | bytes 393224 | tf_op jit(solution)/shard_map/ppermute | solution.py:127
  4.7 7.1 %collective-permute-start.2 = (bf16[16,4096]{1,0:T(8,128)(2,1)S(1)}, bf16[16,4096]{1,0:T(8,128)(2,1)S(1)}, u32[]{:S(2)}, u32[]{:S(2)}) collective-permute-start(bf16[16,4096]{1,0:T(8,128)(2,1)S(1)} %get-tuple-element.26), channel_id=1, source_target_pairs={{0,2},{1,3},{4,0},{5,1},{8,4},{9,5},{12,8},{13,9},{14,12},{15,13},... | collective-permute-start | bytes 393224 | tf_op jit(solution)/shard_map/ppermute | solution.py:130
  6.7 7.2 %collective-permute-start.1 = (bf16[16,4096]{1,0:T(8,128)(2,1)S(1)}, bf16[16,4096]{1,0:T(8,128)(2,1)S(1)}, u32[]{:S(2)}, u32[]{:S(2)}) collective-permute-start(bf16[16,4096]{1,0:T(8,128)(2,1)S(1)} %get-tuple-element.27), channel_id=1, source_target_pairs={{0,4},{1,5},{4,8},{5,9},{8,12},{9,13},{12,14},{13,15},{14,10},{15,... | collective-permute-start | bytes 393224 | tf_op jit(solution)/shard_map/ppermute | solution.py:129
  9.0 6.2 %collective-permute-start.7 = (bf16[16,4096]{1,0:T(8,128)(2,1)S(1)}, bf16[16,4096]{1,0:T(8,128)(2,1)S(1)}, u32[]{:S(2)}, u32[]{:S(2)}) collective-permute-start(bf16[16,4096]{1,0:T(8,128)(2,1)S(1)} %collective-permute-done.3.refs_3_), channel_id=1, source_target_pairs={{0,2},{1,3},{4,0},{5,1},{8,4},{9,5},{12,8},{13,9},{14,12},{15,13},... | collective-permute-start | bytes 393224 | tf_op jit(solution)/shard_map/ppermute | solution.py:128
  11.0 6.2 %collective-permute-start.4 = (bf16[16,4096]{1,0:T(8,128)(2,1)S(1)}, bf16[16,4096]{1,0:T(8,128)(2,1)S(1)}, u32[]{:S(2)}, u32[]{:S(2)}) collective-permute-start(bf16[16,4096]{1,0:T(8,128)(2,1)S(1)} %collective-permute-done.refs_0_), channel_id=1, source_target_pairs={{0,4},{1,5},{4,8},{5,9},{8,12},{9,13},{12,14},{13,15},{14,10},{15,... | collective-permute-start | bytes 393224 | tf_op jit(solution)/shard_map/ppermute | solution.py:127
  11.8 6.5 %collective-permute-start.6 = (bf16[16,4096]{1,0:T(8,128)(2,1)S(1)}, bf16[16,4096]{1,0:T(8,128)(2,1)S(1)}, u32[]{:S(2)}, u32[]{:S(2)}) collective-permute-start(bf16[16,4096]{1,0:T(8,128)(2,1)S(1)} %collective-permute-done.2.refs_2_), channel_id=1, source_target_pairs={{0,2},{1,3},{4,0},{5,1},{8,4},{9,5},{12,8},{13,9},{14,12},{15,13},... | collective-permute-start | bytes 393224 | tf_op jit(solution)/shard_map/ppermute | solution.py:130
  13.8 6.3 %collective-permute-start.5 = (bf16[16,4096]{1,0:T(8,128)(2,1)S(1)}, bf16[16,4096]{1,0:T(8,128)(2,1)S(1)}, u32[]{:S(2)}, u32[]{:S(2)}) collective-permute-start(bf16[16,4096]{1,0:T(8,128)(2,1)S(1)} %collective-permute-done.1.refs_1_), channel_id=1, source_target_pairs={{0,4},{1,5},{4,8},{5,9},{8,12},{9,13},{12,14},{13,15},{14,10},{15,... | collective-permute-start | bytes 393224 | tf_op jit(solution)/shard_map/ppermute | solution.py:129
  15.2 5.9 %collective-permute-start.11 = (bf16[16,4096]{1,0:T(8,128)(2,1)S(1)}, bf16[16,4096]{1,0:T(8,128)(2,1)S(1)}, u32[]{:S(2)}, u32[]{:S(2)}) collective-permute-start(bf16[16,4096]{1,0:T(8,128)(2,1)S(1)} %collective-permute-done.7.refs_7_), channel_id=1, source_target_pairs={{0,2},{1,3},{4,0},{5,1},{8,4},{9,5},{12,8},{13,9},{14,12},{15,13},... | collective-permute-start | bytes 393224 | tf_op jit(solution)/shard_map/ppermute | solution.py:128
  17.2 5.3 %collective-permute-start.8 = (bf16[16,4096]{1,0:T(8,128)(2,1)S(1)}, bf16[16,4096]{1,0:T(8,128)(2,1)}, u32[]{:S(2)}, u32[]{:S(2)}) collective-permute-start(bf16[16,4096]{1,0:T(8,128)(2,1)S(1)} %collective-permute-done.4.refs_4_), channel_id=1, source_target_pairs={{0,4},{1,5},{4,8},{5,9},{8,12},{9,13},{12,14},{13,15},{14,10},{15,... | collective-permute-start | bytes 393224 | tf_op jit(solution)/shard_map/ppermute | solution.py:127
  18.3 5.0 %collective-permute-start.10 = (bf16[16,4096]{1,0:T(8,128)(2,1)S(1)}, bf16[16,4096]{1,0:T(8,128)(2,1)S(1)}, u32[]{:S(2)}, u32[]{:S(2)}) collective-permute-start(bf16[16,4096]{1,0:T(8,128)(2,1)S(1)} %collective-permute-done.6.refs_6_), channel_id=1, source_target_pairs={{0,2},{1,3},{4,0},{5,1},{8,4},{9,5},{12,8},{13,9},{14,12},{15,13},... | collective-permute-start | bytes 393224 | tf_op jit(solution)/shard_map/ppermute | solution.py:130
  20.2 5.0 %collective-permute-start.9 = (bf16[16,4096]{1,0:T(8,128)(2,1)S(1)}, bf16[16,4096]{1,0:T(8,128)(2,1)S(1)}, u32[]{:S(2)}, u32[]{:S(2)}) collective-permute-start(bf16[16,4096]{1,0:T(8,128)(2,1)S(1)} %collective-permute-done.5.refs_5_), channel_id=1, source_target_pairs={{0,4},{1,5},{4,8},{5,9},{8,12},{9,13},{12,14},{13,15},{14,10},{15,... | collective-permute-start | bytes 393224 | tf_op jit(solution)/shard_map/ppermute | solution.py:129
  26.1 8.9 %collective-permute-start.15 = (bf16[96,8192]{1,0:T(8,128)(2,1)S(1)}, bf16[96,8192]{1,0:T(8,128)(2,1)S(1)}, u32[]{:S(2)}, u32[]{:S(2)}) collective-permute-start(bf16[96,8192]{1,0:T(8,128)(2,1)S(1)} %join_pieces.2.rest_0_.refs_1_), channel_id=1, source_target_pairs={{0,1},{1,0},{2,3},{3,2},{4,5},{5,4},{6,7},{7,6},{8,9},{9,8},{10,11... | collective-permute-start | bytes 4718600 | tf_op jit(solution)/shard_map/ppermute | solution.py:139
  26.2 6.2 %collective-permute-start.12 = (bf16[16,4096]{1,0:T(8,128)(2,1)}, bf16[16,4096]{1,0:T(8,128)(2,1)}, u32[]{:S(2)}, u32[]{:S(2)}) collective-permute-start(bf16[16,4096]{1,0:T(8,128)(2,1)} %collective-permute-done.8.refs_8_), channel_id=1, source_target_pairs={{0,4},{1,5},{4,8},{5,9},{8,12},{9,13},{12,14},{13,15},{14,10},{15,... | collective-permute-start | bytes 393224 | tf_op jit(solution)/shard_map/ppermute | solution.py:133
  26.4 6.0 %collective-permute-start.13 = (bf16[16,4096]{1,0:T(8,128)(2,1)S(1)}, bf16[16,4096]{1,0:T(8,128)(2,1)}, u32[]{:S(2)}, u32[]{:S(2)}) collective-permute-start(bf16[16,4096]{1,0:T(8,128)(2,1)S(1)} %collective-permute-done.11.refs_11_), channel_id=1, source_target_pairs={{0,2},{1,3},{4,0},{5,1},{8,4},{9,5},{12,8},{13,9},{14,12},{15,13},... | collective-permute-start | bytes 393224 | tf_op jit(solution)/shard_map/ppermute | solution.py:134
  28.3 5.2 %collective-permute-start.14 = (bf16[16,8192]{1,0:T(8,128)(2,1)}, bf16[16,8192]{1,0:T(8,128)(2,1)}, u32[]{:S(2)}, u32[]{:S(2)}) collective-permute-start(bf16[16,8192]{1,0:T(8,128)(2,1)} %refs_8_.1), channel_id=1, source_target_pairs={{0,1},{1,0},{2,3},{3,2},{4,5},{5,4},{6,7},{7,6},{8,9},{9,8},{10,11... | collective-permute-start | bytes 786440 | tf_op jit(solution)/shard_map/ppermute | solution.py:120
  28.3 0.7 copy-start.4
  28.9 0.7 copy-start.5
  29.6 0.7 copy-start.6
  30.3 0.7 copy-start.7
  33.4 1.6 %collective-permute-start.16 = (bf16[16,8192]{1,0:T(8,128)(2,1)S(1)}, bf16[16,8192]{1,0:T(8,128)(2,1)S(1)}, u32[]{:S(2)}, u32[]{:S(2)}) collective-permute-start(bf16[16,8192]{1,0:T(8,128)(2,1)S(1)} %join_pieces.3.refs_2_), channel_id=1, source_target_pairs={{0,1},{1,0},{2,3},{3,2},{4,5},{5,4},{6,7},{7,6},{8,9},{9,8},{10,11... | collective-permute-start | bytes 786440 | tf_op jit(solution)/shard_map/ppermute | solution.py:139
  35.0 1.2 %copy-start.3 = (bf16[1,8192,64]{1,2,0:T(8,128)(2,1)S(1)}, bf16[1,8192,64]{1,2,0:T(8,128)(2,1)}, u32[]{:S(2)}) copy-start(bf16[1,8192,64]{1,2,0:T(8,128)(2,1)} %param.16) | copy-start | bytes 3145732
  39.9 1.3 %collective-permute-start.17 = (bf16[256,64]{1,0:T(8,128)(2,1)S(1)}, bf16[256,64]{1,0:T(8,128)(2,1)S(1)}, u32[]{:S(2)}, u32[]{:S(2)}) collective-permute-start(bf16[256,64]{1,0:T(8,128)(2,1)S(1)} %get-tuple-element.30.refs_0_), channel_id=1, source_target_pairs={{0,1},{1,0},{2,3},{3,2},{4,5},{5,4},{6,7},{7,6},{8,9},{9,8},{10,11... | collective-permute-start | bytes 98312 | tf_op jit(solution)/shard_map/ppermute | solution.py:488
  41.3 8.9 %collective-permute-start.18 = (bf16[256,64]{1,0:T(8,128)(2,1)S(1)}, bf16[256,64]{1,0:T(8,128)(2,1)S(1)}, u32[]{:S(2)}, u32[]{:S(2)}) collective-permute-start(bf16[256,64]{1,0:T(8,128)(2,1)S(1)} %add_coefficients.3.rest_0_.refs_0_), channel_id=1, source_target_pairs={{0,2},{1,3},{2,0},{3,1},{4,6},{5,7},{6,4},{7,5},{8,10},{9,11},{10,... | collective-permute-start | bytes 98312 | tf_op jit(solution)/shard_map/ppermute | solution.py:488
  50.2 6.0 %collective-permute-start.19 = (bf16[256,64]{1,0:T(8,128)(2,1)S(1)}, bf16[256,64]{1,0:T(8,128)(2,1)S(1)}, u32[]{:S(2)}, u32[]{:S(2)}) collective-permute-start(bf16[256,64]{1,0:T(8,128)(2,1)S(1)} %add_coefficients.4.rest_0_.refs_0_), channel_id=1, source_target_pairs={{0,4},{1,5},{2,6},{3,7},{4,0},{5,1},{6,2},{7,3},{8,12},{9,13},{10,... | collective-permute-start | bytes 98312 | tf_op jit(solution)/shard_map/ppermute | solution.py:488
  56.3 7.0 %copy-start.2 = (bf16[16,64,896]{2,1,0:T(8,128)(2,1)S(1)}, bf16[16,64,896]{2,1,0:T(8,128)(2,1)}, u32[]{:S(2)}) copy-start(bf16[16,64,896]{2,1,0:T(8,128)(2,1)} %param.17) | copy-start | bytes 5505028
  56.3 7.0 %collective-permute-start.20 = (bf16[256,64]{1,0:T(8,128)(2,1)S(1)}, bf16[256,64]{1,0:T(8,128)(2,1)S(1)}, u32[]{:S(2)}, u32[]{:S(2)}) collective-permute-start(bf16[256,64]{1,0:T(8,128)(2,1)S(1)} %add_coefficients.5.rest_0_.refs_0_), channel_id=1, source_target_pairs={{0,8},{1,9},{2,10},{3,11},{4,12},{5,13},{6,14},{7,15},{8,0},{9,1},... | collective-permute-start | bytes 98312 | tf_op jit(solution)/shard_map/ppermute | solution.py:496
  69.3 5.4 %collective-permute-start.21 = (bf16[128,4096]{1,0:T(8,128)(2,1)S(1)}, bf16[128,4096]{1,0:T(8,128)(2,1)S(1)}, u32[]{:S(2)}, u32[]{:S(2)}) collective-permute-start(bf16[128,4096]{1,0:T(8,128)(2,1)S(1)} %get-tuple-element.35.rest_0_), channel_id=1, source_target_pairs={{0,1},{1,0},{2,3},{3,2},{4,5},{5,4},{6,7},{7,6},{8,9},{9,8},{10,11... | collective-permute-start | bytes 3145736 | tf_op jit(solution)/shard_map/ppermute | solution.py:505
  74.2 2.8 %collective-permute-start.24 = (bf16[128,4096]{1,0:T(8,128)(2,1)S(1)}, bf16[128,4096]{1,0:T(8,128)(2,1)S(1)}, u32[]{:S(2)}, u32[]{:S(2)}) collective-permute-start(bf16[128,4096]{1,0:T(8,128)(2,1)S(1)} %get-tuple-element.39), channel_id=1, source_target_pairs={{0,1},{1,0},{2,3},{3,2},{4,5},{5,4},{6,7},{7,6},{8,9},{9,8},{10,11... | collective-permute-start | bytes 3145736 | tf_op jit(solution)/shard_map/ppermute | solution.py:505
  74.8 5.5 %collective-permute-start.22 = (bf16[16,4096]{1,0:T(8,128)(2,1)S(1)}, bf16[16,4096]{1,0:T(8,128)(2,1)S(1)}, u32[]{:S(2)}, u32[]{:S(2)}) collective-permute-start(bf16[16,4096]{1,0:T(8,128)(2,1)S(1)} %get-tuple-element.36.refs_4_), channel_id=1, source_target_pairs={{0,4},{1,5},{4,8},{5,9},{8,12},{9,13},{12,14},{13,15},{14,10},{15,... | collective-permute-start | bytes 393224 | tf_op jit(solution)/shard_map/ppermute | solution.py:420
  75.4 5.5 %collective-permute-start.23 = (bf16[16,4096]{1,0:T(8,128)(2,1)S(1)}, bf16[16,4096]{1,0:T(8,128)(2,1)S(1)}, u32[]{:S(2)}, u32[]{:S(2)}) collective-permute-start(bf16[16,4096]{1,0:T(8,128)(2,1)S(1)} %get-tuple-element.37), channel_id=1, source_target_pairs={{0,2},{1,3},{4,0},{5,1},{8,4},{9,5},{12,8},{13,9},{14,12},{15,13},... | collective-permute-start | bytes 393224 | tf_op jit(solution)/shard_map/ppermute | solution.py:420
  77.1 6.6 %collective-permute-start.27 = (bf16[16,4096]{1,0:T(8,128)(2,1)S(1)}, bf16[16,4096]{1,0:T(8,128)(2,1)S(1)}, u32[]{:S(2)}, u32[]{:S(2)}) collective-permute-start(bf16[16,4096]{1,0:T(8,128)(2,1)S(1)} %get-tuple-element.40.refs_6_), channel_id=1, source_target_pairs={{0,2},{1,3},{4,0},{5,1},{8,4},{9,5},{12,8},{13,9},{14,12},{15,13},... | collective-permute-start | bytes 393224 | tf_op jit(solution)/shard_map/ppermute | solution.py:420
  77.7 6.4 %collective-permute-start.28 = (bf16[16,4096]{1,0:T(8,128)(2,1)S(1)}, bf16[16,4096]{1,0:T(8,128)(2,1)S(1)}, u32[]{:S(2)}, u32[]{:S(2)}) collective-permute-start(bf16[16,4096]{1,0:T(8,128)(2,1)S(1)} %get-tuple-element.43), channel_id=1, source_target_pairs={{0,4},{1,5},{4,8},{5,9},{8,12},{9,13},{12,14},{13,15},{14,10},{15,... | collective-permute-start | bytes 393224 | tf_op jit(solution)/shard_map/ppermute | solution.py:420
  81.0 5.6 %collective-permute-start.25 = (bf16[16,4096]{1,0:T(8,128)(2,1)S(1)}, bf16[16,4096]{1,0:T(8,128)(2,1)S(1)}, u32[]{:S(2)}, u32[]{:S(2)}) collective-permute-start(bf16[16,4096]{1,0:T(8,128)(2,1)S(1)} %get-tuple-element.41.refs_6_), channel_id=1, source_target_pairs={{0,4},{1,5},{4,8},{5,9},{8,12},{9,13},{12,14},{13,15},{14,10},{15,... | collective-permute-start | bytes 393224 | tf_op jit(solution)/shard_map/ppermute | solution.py:420
  82.3 6.3 %collective-permute-start.26 = (bf16[16,4096]{1,0:T(8,128)(2,1)S(1)}, bf16[16,4096]{1,0:T(8,128)(2,1)S(1)}, u32[]{:S(2)}, u32[]{:S(2)}) collective-permute-start(bf16[16,4096]{1,0:T(8,128)(2,1)S(1)} %get-tuple-element.42), channel_id=1, source_target_pairs={{0,2},{1,3},{4,0},{5,1},{8,4},{9,5},{12,8},{13,9},{14,12},{15,13},... | collective-permute-start | bytes 393224 | tf_op jit(solution)/shard_map/ppermute | solution.py:420
  84.2 5.9 %collective-permute-start.30 = (bf16[16,4096]{1,0:T(8,128)(2,1)S(1)}, bf16[16,4096]{1,0:T(8,128)(2,1)S(1)}, u32[]{:S(2)}, u32[]{:S(2)}) collective-permute-start(bf16[16,4096]{1,0:T(8,128)(2,1)S(1)} %get-tuple-element.44.refs_6_), channel_id=1, source_target_pairs={{0,2},{1,3},{4,0},{5,1},{8,4},{9,5},{12,8},{13,9},{14,12},{15,13},... | collective-permute-start | bytes 393224 | tf_op jit(solution)/shard_map/ppermute | solution.py:420
  85.8 5.0 %collective-permute-start.31 = (bf16[16,4096]{1,0:T(8,128)(2,1)S(1)}, bf16[16,4096]{1,0:T(8,128)(2,1)S(1)}, u32[]{:S(2)}, u32[]{:S(2)}) collective-permute-start(bf16[16,4096]{1,0:T(8,128)(2,1)S(1)} %get-tuple-element.46), channel_id=1, source_target_pairs={{0,4},{1,5},{4,8},{5,9},{8,12},{9,13},{12,14},{13,15},{14,10},{15,... | collective-permute-start | bytes 393224 | tf_op jit(solution)/shard_map/ppermute | solution.py:420
  88.8 10.2 %copy-start.8 = (bf16[8192]{0:T(1024)(128)(2,1)S(1)}, bf16[8192]{0:T(1024)(128)(2,1)}, u32[]{:S(2)}) copy-start(bf16[8192]{0:T(1024)(128)(2,1)} %param.15) | copy-start | bytes 49156
  88.8 5.9 %collective-permute-start.29 = (bf16[16,4096]{1,0:T(8,128)(2,1)S(1)}, bf16[16,4096]{1,0:T(8,128)(2,1)S(1)}, u32[]{:S(2)}, u32[]{:S(2)}) collective-permute-start(bf16[16,4096]{1,0:T(8,128)(2,1)S(1)} %get-tuple-element.45.refs_6_), channel_id=1, source_target_pairs={{0,4},{1,5},{4,8},{5,9},{8,12},{9,13},{12,14},{13,15},{14,10},{15,... | collective-permute-start | bytes 393224 | tf_op jit(solution)/shard_map/ppermute | solution.py:420
  90.9 5.5 %collective-permute-start.35 = (bf16[16,4096]{1,0:T(8,128)(2,1)S(1)}, bf16[16,4096]{1,0:T(8,128)(2,1)S(1)}, u32[]{:S(2)}, u32[]{:S(2)}) collective-permute-start(bf16[16,4096]{1,0:T(8,128)(2,1)S(1)} %get-tuple-element.47.refs_3_), channel_id=1, source_target_pairs={{0,2},{1,3},{4,0},{5,1},{8,4},{9,5},{12,8},{13,9},{14,12},{15,13},... | collective-permute-start | bytes 393224 | tf_op jit(solution)/shard_map/ppermute | solution.py:420
  92.5 6.5 %collective-permute-start.34 = (bf16[16,4096]{1,0:T(8,128)(2,1)S(1)}, bf16[16,4096]{1,0:T(8,128)(2,1)S(1)}, u32[]{:S(2)}, u32[]{:S(2)}) collective-permute-start(bf16[16,4096]{1,0:T(8,128)(2,1)S(1)} %get-tuple-element.49), channel_id=1, source_target_pairs={{0,4},{1,5},{4,8},{5,9},{8,12},{9,13},{12,14},{13,15},{14,10},{15,... | collective-permute-start | bytes 393224 | tf_op jit(solution)/shard_map/ppermute | solution.py:420
  93.0 6.0 %collective-permute-start.33 = (bf16[16,4096]{1,0:T(8,128)(2,1)S(1)}, bf16[16,4096]{1,0:T(8,128)(2,1)S(1)}, u32[]{:S(2)}, u32[]{:S(2)}) collective-permute-start(bf16[16,4096]{1,0:T(8,128)(2,1)S(1)} %get-tuple-element.48), channel_id=1, source_target_pairs={{0,2},{1,3},{4,0},{5,1},{8,4},{9,5},{12,8},{13,9},{14,12},{15,13},... | collective-permute-start | bytes 393224 | tf_op jit(solution)/shard_map/ppermute | solution.py:420
  96.5 5.0 %collective-permute-start.36 = (bf16[16,4096]{1,0:T(8,128)(2,1)S(1)}, bf16[16,4096]{1,0:T(8,128)(2,1)S(1)}, u32[]{:S(2)}, u32[]{:S(2)}) collective-permute-start(bf16[16,4096]{1,0:T(8,128)(2,1)S(1)} %add_blocks.15), channel_id=1, source_target_pairs={{0,2},{1,3},{4,0},{5,1},{8,4},{9,5},{12,8},{13,9},{14,12},{15,13},... | collective-permute-start | bytes 393224 | tf_op jit(solution)/shard_map/ppermute | solution.py:420
  99.0 5.0 %collective-permute-start.32 = (bf16[16,4096]{1,0:T(8,128)(2,1)S(1)}, bf16[16,4096]{1,0:T(8,128)(2,1)S(1)}, u32[]{:S(2)}, u32[]{:S(2)}) collective-permute-start(bf16[16,4096]{1,0:T(8,128)(2,1)S(1)} %add_blocks.14.refs_3_), channel_id=1, source_target_pairs={{0,4},{1,5},{4,8},{5,9},{8,12},{9,13},{12,14},{13,15},{14,10},{15,... | collective-permute-start | bytes 393224 | tf_op jit(solution)/shard_map/ppermute | solution.py:420

commit v6 on v4

--- a/solution.py
+++ b/solution.py
@@ -10,11 +10,9 @@
 adapter_alpha = 32.0
 AXIS = "mp"
 HALVES = 2
-DEPTH_BLOCK = 512
-WIDTH_BLOCK = 512
-IN_FLIGHT = 4
+DEPTH_BLOCK = 1024
 VMEM_LIMIT = 16 * 1024 * 1024
-STREAM_LIMIT = 46 * 1024 * 1024
+STREAM_LIMIT = 38 * 1024 * 1024
 
 
 def chip_at(place, chips):
@@ -141,18 +139,26 @@
     return mine + theirs
 
 
-def row_masks(me, tables, own_rows, size, slots, rank_limit):
+def row_masks(me, tables, shrink_factors, own_rows, size):
     batch_rows = own_rows * size
-    adapters = tables[2].shape[1]
-
-    def kernel(me_ref, start, segment_adapter, ranks, slot_of, scale, to_place, from_place, hot):
+    slots, model_width, rank_limit = shrink_factors.shape
+    factor = jnp.swapaxes(shrink_factors, 1, 2).reshape(slots * rank_limit, model_width)
+    lengths = [table.shape[0] for table in tables]
+    starts = [sum(lengths[:i]) for i in range(len(lengths))]
+    adapters = lengths[2]
+
+    def kernel(me_ref, all_tables, factor_in, scale, to_place, from_place, hot, factor_out):
+        factor_out[...] = factor_in[...]
         me = me_ref[0]
+        start, segment_adapter, ranks, slot_of = (
+            all_tables[:, at : at + length] for at, length in zip(starts, lengths)
+        )
         row = lax.broadcasted_iota(jnp.int32, (batch_rows, 1), 0)
         column = lax.broadcasted_iota(jnp.int32, (1, batch_rows), 1)
         position = row_positions(me, row, own_rows, size)
-        adapter = row_adapters(position, start[...], segment_adapter[...])
-        rank = pick(adapter, ranks[...])
-        slot = pick(adapter, slot_of[...]) - me * slots
+        adapter = row_adapters(position, start, segment_adapter)
+        rank = pick(adapter, ranks)
+        slot = pick(adapter, slot_of) - me * slots
         at = lax.broadcasted_iota(jnp.int32, (1, slots * rank_limit), 1)
         keep = (at // rank_limit == slot) & (at % rank_limit < rank)
         scale[...] = jnp.where(keep, adapter_alpha / rank.astype(jnp.float32), 0.0)
@@ -166,21 +172,14 @@
         jax.ShapeDtypeStruct((batch_rows, batch_rows), jnp.bfloat16),
         jax.ShapeDtypeStruct((batch_rows, batch_rows), jnp.bfloat16),
         jax.ShapeDtypeStruct((batch_rows, adapters * rank_limit), jnp.bfloat16),
-    )
-    return pl.pallas_call(
-        kernel,
-        out_shape=shapes,
-        grid=(1,),
-        in_specs=[whole(pltpu.SMEM)] + [pl.BlockSpec(t.shape, lambda i: (0, 0)) for t in tables],
-        out_specs=[pl.BlockSpec(shape.shape, lambda i: (0, 0)) for shape in shapes],
-        compiler_params=pltpu.CompilerParams(vmem_limit_bytes=VMEM_LIMIT),
-        name="row_masks",
-    )(me, *tables)
-
-
-def shrink_rows(parts, shrink_factors, scale, to_place):
-    slots, model_width, rank_limit = shrink_factors.shape
-    factor = jnp.swapaxes(shrink_factors, 1, 2).reshape(slots * rank_limit, model_width)
+        jax.ShapeDtypeStruct(factor.shape, factor.dtype),
+    )
+    return call(kernel, shapes, [me, jnp.concatenate(tables)[None], factor], "row_masks")
+
+
+def shrink_rows(parts, factor, scale, to_place, rank_limit):
+    model_width = factor.shape[1]
+    slots = factor.shape[0] // rank_limit
     batch_rows = to_place.shape[0]
     width = model_width // 8
 
@@ -237,55 +236,86 @@
     )
 
 
-def streamed(source, pieces, buffers, arrived):
-    slots = buffers.shape[0]
-    copies = [
-        pltpu.make_async_copy(source.at[piece], buffers.at[i % slots], arrived.at[i % slots])
-        for i, piece in enumerate(pieces)
-    ]
-    for copy in copies[:slots]:
-        copy.start()
-    for i, copy in enumerate(copies):
-        copy.wait()
-        yield i, buffers[i % slots]
-        if i + slots < len(copies):
-            copies[i + slots].start()
-
-
-def matmul(rows, weight, name, first, last, ordered=()):
+def lane_tiles(width):
+    return -(-width // 128) * 128
+
+
+def mixed_rows(rows, weights, before, first, last, ordered):
     batch_rows = rows.shape[0]
-    width = weight.shape[1]
-    starts = range(first, last, DEPTH_BLOCK)
-    pieces = [(slice(at, at + DEPTH_BLOCK), slice(None)) for at in starts]
-
-    def kernel(rows_ref, weight_ref, *rest):
-        out, buffers, arrived = rest[-3:]
-        for i, block in streamed(weight_ref, pieces, buffers, arrived):
-            product = jnp.dot(
-                rows_ref[:, pieces[i][0]], block, preferred_element_type=jnp.float32
-            )
-            out[...] = product if i == 0 else out[...] + product
+    widths = [weight.shape[1] for weight in weights]
+    lefts = [sum(lane_tiles(width) for width in widths[:w]) for w in range(len(weights))]
+    width = sum(lane_tiles(width) for width in widths)
+    if width == sum(widths):
+        buffer_of, offsets = [0] * len(weights), lefts
+        products = [(0, width)]
+    else:
+        buffer_of, offsets = list(range(len(weights))), [0] * len(weights)
+        products = list(zip(lefts, widths))
+    blocks = []
+    at = first
+    while at < last:
+        depth = min(DEPTH_BLOCK if blocks else DEPTH_BLOCK // 2, last - at)
+        blocks.append((at, depth))
+        at += depth
+
+    def kernel(rows_ref, *refs):
+        sources = refs[: len(weights)]
+        arrived = refs[-1]
+        buffers = refs[-1 - len(products) : -1]
+        out = refs[-2 - len(products)]
+        copies = []
+        for b, (at, depth) in enumerate(blocks):
+            copies.append([])
+            half = depth // 2
+            for p in range(2):
+                for w, source in enumerate(sources):
+                    top = at - first + p * half
+                    copy = pltpu.make_async_copy(
+                        source.at[at + p * half : at + (p + 1) * half, :],
+                        buffers[buffer_of[w]].at[
+                            top : top + half, offsets[w] : offsets[w] + widths[w]
+                        ],
+                        arrived.at[b, 2 * w + p],
+                    )
+                    copy.start()
+                    copies[-1].append(copy)
+        for (at, depth), group in zip(blocks, copies):
+            for copy in group:
+                copy.wait()
+            for (left, wide), buffer in zip(products, buffers):
+                columns = slice(left, left + wide)
+                product = jnp.dot(
+                    rows_ref[:, at : at + depth],
+                    buffer[at - first : at - first + depth, :],
+                    preferred_element_type=jnp.float32,
+                )
+                if at > first:
+                    product = out[:, columns] + product
+                elif before is not None:
+                    product = refs[len(weights)][:, columns] + product
+                out[:, columns] = product
 
     return pl.pallas_call(
         kernel,
         out_shape=jax.ShapeDtypeStruct((batch_rows, width), jnp.float32),
-        in_specs=[whole(), whole(pltpu.HBM)] + [whole(pl.ANY)] * len(ordered),
+        in_specs=[whole()]
+        + [whole(pltpu.HBM)] * len(weights)
+        + [whole()] * (before is not None)
+        + [whole(pl.ANY)] * len(ordered),
         out_specs=whole(),
-        scratch_shapes=[
-            pltpu.VMEM((IN_FLIGHT, DEPTH_BLOCK, width), weight.dtype),
-            pltpu.SemaphoreType.DMA((IN_FLIGHT,)),
-        ],
+        scratch_shapes=[pltpu.VMEM((last - first, wide), rows.dtype) for _, wide in products]
+        + [pltpu.SemaphoreType.DMA((len(blocks), 2 * len(weights)))],
         compiler_params=pltpu.CompilerParams(vmem_limit_bytes=STREAM_LIMIT),
         cost_estimate=pl.CostEstimate(
             flops=2 * batch_rows * (last - first) * width,
             bytes_accessed=2 * (last - first) * width,
             transcendentals=0,
         ),
-        name=name,
-    )(rows, weight, *ordered)
-
-
-def hidden_kernel(coeff, recv, from_place, hot, expand, gate, up, more, out, spread):
+        name="mixed_rows",
+    )(rows, *weights, *([] if before is None else [before]), *ordered)
+
+
+def hidden_kernel(coeff, recv, from_place, hot, expand, mixed, out, spread):
     rank_limit = coeff.shape[1]
     own = jnp.dot(
         from_place[...], coeff[...] + recv[...], preferred_element_type=jnp.float32
@@ -295,19 +325,20 @@
         at = slice(p * 2 * rank_limit, (p + 1) * 2 * rank_limit)
         spread[:, at] = hot[:, at] * pair
     lora = jnp.dot(spread[...], expand[...], preferred_element_type=jnp.float32)
-    value = gate[...]
-    total = up[...] + more[...] + lora
+    width = out.shape[1]
+    value = mixed[:, :width]
+    total = mixed[:, lane_tiles(width) : lane_tiles(width) + width] + lora
     out[...] = (value / (1.0 + jnp.exp(-value)) * total).astype(jnp.bfloat16)
 
 
-def hidden_rows(gate, up, more, coeff, recv, expand_factors, from_place, hot):
+def hidden_rows(mixed, coeff, recv, expand_factors, from_place, hot):
     adapters, rank_limit, width = expand_factors.shape
-    batch_rows = gate.shape[0]
+    batch_rows = mixed.shape[0]
     expand = expand_factors.reshape(adapters * rank_limit, width)
     return call(
         hidden_kernel,
         jax.ShapeDtypeStruct((batch_rows, width), jnp.bfloat16),
-        [coeff, recv, from_place, hot, expand, gate, up, more],
+        [coeff, recv, from_place, hot, expand, mixed],
         "hidden_rows",
         scratch_shapes=[pltpu.VMEM((batch_rows, adapters * rank_limit), jnp.bfloat16)],
         cost_estimate=pl.CostEstimate(
@@ -316,43 +347,6 @@
             transcendentals=batch_rows * width,
         ),
     )
-
-
-def down_rows(hidden, down_weight, half, ordered=()):
-    batch_rows, hidden_width = hidden.shape
-    width = down_weight.shape[1] // HALVES
-    core_rows = batch_rows // 2
-    starts = range(half * width, (half + 1) * width, WIDTH_BLOCK)
-    pieces = [(slice(None), slice(at, at + WIDTH_BLOCK)) for at in starts]
-
-    def kernel(hidden_ref, weight, *rest):
-        mine, theirs, buffers, arrived = rest[-4:]
-        for i, block in streamed(weight, pieces, buffers, arrived):
-            product = jnp.dot(
-                hidden_ref[...], block, preferred_element_type=jnp.float32
-            ).astype(jnp.bfloat16)
-            at = slice(i * WIDTH_BLOCK, (i + 1) * WIDTH_BLOCK)
-            theirs[:, at] = product[core_rows:]
-            mine[:, at] = product[:core_rows]
-
-    part = jax.ShapeDtypeStruct((core_rows, width), jnp.bfloat16)
-    return pl.pallas_call(
-        kernel,
-        out_shape=(part, part),
-        in_specs=[whole(), whole(pltpu.HBM)] + [whole(pl.ANY)] * len(ordered),
-        out_specs=[whole()] * 2,
-        scratch_shapes=[
-            pltpu.VMEM((IN_FLIGHT, hidden_width, WIDTH_BLOCK), down_weight.dtype),
-            pltpu.SemaphoreType.DMA((IN_FLIGHT,)),
-        ],
-        compiler_params=pltpu.CompilerParams(vmem_limit_bytes=STREAM_LIMIT),
-        cost_estimate=pl.CostEstimate(
-            flops=2 * batch_rows * hidden_width * width,
-            bytes_accessed=2 * hidden_width * width,
-            transcendentals=0,
-        ),
-        name="down_rows",
-    )(hidden, down_weight, *ordered)
 
 
 def add_blocks(sides, own_rows, ordered):
@@ -387,15 +381,19 @@
             sides = []
             if steps_right > 0:
                 index = min(2 * steps_right, chips - 1)
-                sides.append((mine[h], theirs[h], index, right[h]))
+                sides.append((right, 1, index))
             if steps_left > 0:
-                sides.append((mine[h], theirs[h], 2 * steps_left - 1, left[h]))
-            sums = list(add_blocks(sides, own_rows, ordered))
+                sides.append((left, -1, 2 * steps_left - 1))
+            if h == 1:
+                sides.reverse()
+            sums = add_blocks(
+                [(mine[h], theirs[h], index, chain[h]) for chain, _, index in sides],
+                own_rows,
+                ordered,
+            )
             ordered = [sums[0]]
-            if steps_right > 0:
-                right[h] = lax.ppermute(sums.pop(0), AXIS, ring(size, 1))
-            if steps_left > 0:
-                left[h] = lax.ppermute(sums.pop(0), AXIS, ring(size, -1))
+            for (chain, by, _), value in zip(sides, sums):
+                chain[h] = lax.ppermute(value, AXIS, ring(size, by))
     return list(zip(mine, theirs, right, left))
 
 
@@ -447,38 +445,41 @@
     size = lax.axis_size(AXIS)
     me = lax.axis_index(AXIS).astype(jnp.int32).reshape(1)
     own_rows, model_width = activations.shape
-    slots, _, rank_limit = shrink_factors.shape
     assert size & (size - 1) == 0 and own_rows & (own_rows - 1) == 0
-    tables = [
-        table[None]
-        for table in (segment_start, segment_adapter, adapter_ranks, adapter_storage_slot)
-    ]
-    scale, to_place, from_place, hot = row_masks(me, tables, own_rows, size, slots, rank_limit)
+    tables = (segment_start, segment_adapter, adapter_ranks, adapter_storage_slot)
+    scale, to_place, from_place, hot, factor = row_masks(
+        me, tables, shrink_factors, own_rows, size
+    )
 
     parts = gather_rows(activations, size, [scale])
-    rows, coeff = shrink_rows(parts, shrink_factors, scale, to_place)
+    rows, coeff = shrink_rows(parts, factor, scale, to_place, shrink_factors.shape[2])
 
     bits = [1 << b for b in range(size.bit_length() - 1)]
-    work = []
-    for bit in bits[:-1]:
+    units = model_width // (DEPTH_BLOCK // 2)
+    cuts = [0] + [(units - units * k // 3) * (DEPTH_BLOCK // 2) for k in (2, 1, 0)]
+    mixed = None
+    for step, bit in enumerate(bits):
         received = lax.ppermute(coeff, AXIS, flip(size, bit))
-        if bit == bits[1]:
-            work = [matmul(rows, gate_weight, "gate_rows", 0, model_width, [coeff])]
-            gate = work[0]
-        if bit == bits[2]:
-            work = [matmul(rows, up_weight, "up_rows", 0, model_width // 2, [coeff])]
-            up = work[0]
-        coeff = add_coefficients(coeff, received, work)
-    received = lax.ppermute(coeff, AXIS, flip(size, bits[-1]))
-    more = matmul(rows, up_weight, "up_rows", model_width // 2, model_width, [coeff])
-    hidden = hidden_rows(gate, up, more, coeff, received, expand_factors, from_place, hot)
-
+        part = step - (len(bits) - 3)
+        if part >= 0:
+            mixed = mixed_rows(
+                rows, (gate_weight, up_weight), mixed, cuts[part], cuts[part + 1], [coeff]
+            )
+        if bit < bits[-1]:
+            coeff = add_coefficients(coeff, received, [] if mixed is None else [mixed])
+    hidden = hidden_rows(mixed, coeff, received, expand_factors, from_place, hot)
+
+    half = size * own_rows // 2
+    width = model_width // HALVES
     mine, theirs = [None] * HALVES, [None] * HALVES
-    ordered = []
     for h in range(HALVES):
-        mine[h], part = down_rows(hidden, down_weight, h, ordered)
-        ordered = [part]
-        theirs[h] = lax.ppermute(part, AXIS, flip(size, 1))
+        term = jnp.dot(
+            hidden,
+            down_weight[:, h * width : (h + 1) * width],
+            preferred_element_type=jnp.float32,
+        ).astype(jnp.bfloat16)
+        mine[h] = term
+        theirs[h] = lax.ppermute(term[half:], AXIS, flip(size, 1))
     halves = scatter_rows(mine, theirs, own_rows, size)
     return finish_rows(halves, activations, norm_gain_vector[None], own_rows)
 

time: 102 us -> 96.9 us (0.950)
  Pallas kernels: 33.4 us -> 22.9 us
  matrix products: 0 us -> 5.06 us
  local copies, waits for them, and re-layouts: 3.6 us -> 2.41 us
    pallas_call x6 -> x3, Pallas kernels: 27.8 us -> 16.5 us  [mixed_rows(): pl.pallas_call(kernel, out_shape=jax.ShapeDtypeStruct((batch_rows, width)...]
    dot_general x0 -> x2, matrix products: none -> 5.06 us  [body(): jnp.dot(hidden, down_weight[:, h * width:(h + 1) * width], preferred_elem...]
    ppermute x3 -> x4, starting transfers between devices: 3.47 us -> 6.15 us  [body(): received = lax.ppermute(coeff, AXIS, flip(size, bit))]
    ppermute x17 -> x16, starting transfers between devices: 18.1 us -> 16.3 us  [the longest x14 15.7 us: scatter_rows(): chain[h] = lax.ppermute(value, AXIS, ring(size, by))]
    unnamed x18, local copies, waits for them, and re-layouts: 3.58 us -> 2.21 us
    pallas_call x17 -> x18, Pallas kernels: 5.59 us -> 6.43 us  [call(): pl.pallas_call(run, out_shape=out_shape, in_specs=[whole(pltpu.SMEM if op...]
    ppermute x17 -> x16, waiting for transfers between devices: 12.9 us -> 12.6 us  [the longest x14 12.4 us: scatter_rows(): chain[h] = lax.ppermute(value, AXIS, ring(size, by))]
  transfers between devices with their start and end apart: 37 -> 37, of which waited for: 19 -> 22; matrix products, arithmetic and copies ran while one was open for 0% -> 4% of each run, Pallas kernels for 23% -> 19%
where the time goes in v6:
time: 96.9 us; the launch traced here: 96.7 us
  starting transfers between devices  38.4 us (40%)
  waiting for transfers between devices  26.1 us (27%)
  Pallas kernels  22.9 us (24%)
  matrix products  5.06 us (5%)
  local copies, waits for them, and re-layouts  2.41 us (2%)
  between operations  0.99 us (1%)
    pallas_call x3, Pallas kernels, mixed_rows(): pl.pallas_call(kernel, out_shape=jax.ShapeDtypeStruct((batch_rows, width)...  16.5 us
    ppermute x14, starting transfers between devices, scatter_rows(): chain[h] = lax.ppermute(value, AXIS, ring(size, by))  15.7 us
    ppermute x14, waiting for transfers between devices, scatter_rows(): chain[h] = lax.ppermute(value, AXIS, ring(size, by))  12.4 us
    ppermute x3, starting transfers between devices, gather_rows(): left[1] = lax.ppermute(left[1], AXIS, ring(size, -1))  7.08 us
    pallas_call x18, Pallas kernels, call(): pl.pallas_call(run, out_shape=out_shape, in_specs=[whole(pltpu.SMEM if op...  6.43 us
    ppermute x4, starting transfers between devices, body(): received = lax.ppermute(coeff, AXIS, flip(size, bit))  6.15 us
    ppermute x3, starting transfers between devices, gather_rows(): left[0] = lax.ppermute(left[0], AXIS, ring(size, -1))  5.78 us
    dot_general x2, matrix products, body(): jnp.dot(hidden, down_weight[:, h * width:(h + 1) * width], preferred_elem...  5.06 us
  transfers between devices with their start and end apart: 37, of which 22 were waited for; matrix products, arithmetic and copies ran while one was open for 4% of the time, Pallas kernels for 19%

profile of v6, /device:TPU:0, one launch (start us, length us, event | category | flops | bytes accessed | tf_op | source)
XLA Modules:
  0.0 96.7 jit_solution(3348992022916040510)
XLA Ops:
  0.6 0.9 copy-done
  1.6 3.0 %collective-permute-start.3 = (bf16[16,4096]{1,0:T(8,128)(2,1)S(1)}, bf16[16,4096]{1,0:T(8,128)(2,1)S(1)}, u32[]{:S(2)}, u32[]{:S(2)}) collective-permute-start(bf16[16,4096]{1,0:T(8,128)(2,1)S(1)} %get-tuple-element.24), channel_id=1, source_target_pairs={{0,2},{1,3},{4,0},{5,1},{8,4},{9,5},{12,8},{13,9},{14,12},{15,13},... | collective-permute-start | bytes 393224 | tf_op jit(solution)/shard_map/ppermute | solution.py:127
  4.7 1.9 %collective-permute-start.2 = (bf16[16,4096]{1,0:T(8,128)(2,1)S(1)}, bf16[16,4096]{1,0:T(8,128)(2,1)S(1)}, u32[]{:S(2)}, u32[]{:S(2)}) collective-permute-start(bf16[16,4096]{1,0:T(8,128)(2,1)S(1)} %get-tuple-element.23), channel_id=1, source_target_pairs={{0,2},{1,3},{4,0},{5,1},{8,4},{9,5},{12,8},{13,9},{14,12},{15,13},... | collective-permute-start | bytes 393224 | tf_op jit(solution)/shard_map/ppermute | solution.py:129
  6.8 2.2 %collective-permute-done.3.refs_3_ = bf16[16,4096]{1,0:T(8,128)(2,1)S(1)} collective-permute-done((bf16[16,4096]{1,0:T(8,128)(2,1)S(1)}, bf16[16,4096]{1,0:T(8,128)(2,1)S(1)}, u32[]{:S(2)}, u32[]{:S(2)}) %collective-permute-start.3) | collective-permute-done | bytes 131104 | tf_op jit(solution)/shard_map/ppermute | solution.py:127
  9.0 2.0 %collective-permute-start.7 = (bf16[16,4096]{1,0:T(8,128)(2,1)S(1)}, bf16[16,4096]{1,0:T(8,128)(2,1)S(1)}, u32[]{:S(2)}, u32[]{:S(2)}) collective-permute-start(bf16[16,4096]{1,0:T(8,128)(2,1)S(1)} %collective-permute-done.3.refs_3_), channel_id=1, source_target_pairs={{0,2},{1,3},{4,0},{5,1},{8,4},{9,5},{12,8},{13,9},{14,12},{15,13},... | collective-permute-start | bytes 393224 | tf_op jit(solution)/shard_map/ppermute | solution.py:127
  11.1 0.7 collective-permute-done.2.refs_2_
  11.8 2.0 %collective-permute-start.6 = (bf16[16,4096]{1,0:T(8,128)(2,1)S(1)}, bf16[16,4096]{1,0:T(8,128)(2,1)S(1)}, u32[]{:S(2)}, u32[]{:S(2)}) collective-permute-start(bf16[16,4096]{1,0:T(8,128)(2,1)S(1)} %collective-permute-done.2.refs_2_), channel_id=1, source_target_pairs={{0,2},{1,3},{4,0},{5,1},{8,4},{9,5},{12,8},{13,9},{14,12},{15,13},... | collective-permute-start | bytes 393224 | tf_op jit(solution)/shard_map/ppermute | solution.py:129
  13.9 1.3 %collective-permute-done.7.refs_7_ = bf16[16,4096]{1,0:T(8,128)(2,1)S(1)} collective-permute-done((bf16[16,4096]{1,0:T(8,128)(2,1)S(1)}, bf16[16,4096]{1,0:T(8,128)(2,1)S(1)}, u32[]{:S(2)}, u32[]{:S(2)}) %collective-permute-start.7) | collective-permute-done | bytes 131104 | tf_op jit(solution)/shard_map/ppermute | solution.py:127
  15.2 2.1 %collective-permute-start.11 = (bf16[16,4096]{1,0:T(8,128)(2,1)S(1)}, bf16[16,4096]{1,0:T(8,128)(2,1)S(1)}, u32[]{:S(2)}, u32[]{:S(2)}) collective-permute-start(bf16[16,4096]{1,0:T(8,128)(2,1)S(1)} %collective-permute-done.7.refs_7_), channel_id=1, source_target_pairs={{0,2},{1,3},{4,0},{5,1},{8,4},{9,5},{12,8},{13,9},{14,12},{15,13},... | collective-permute-start | bytes 393224 | tf_op jit(solution)/shard_map/ppermute | solution.py:127
  17.5 0.8 collective-permute-done.6.refs_6_
  18.3 1.9 %collective-permute-start.10 = (bf16[16,4096]{1,0:T(8,128)(2,1)S(1)}, bf16[16,4096]{1,0:T(8,128)(2,1)S(1)}, u32[]{:S(2)}, u32[]{:S(2)}) collective-permute-start(bf16[16,4096]{1,0:T(8,128)(2,1)S(1)} %collective-permute-done.6.refs_6_), channel_id=1, source_target_pairs={{0,2},{1,3},{4,0},{5,1},{8,4},{9,5},{12,8},{13,9},{14,12},{15,13},... | collective-permute-start | bytes 393224 | tf_op jit(solution)/shard_map/ppermute | solution.py:129
  20.3 0.8 add_bitcast_fusion.refs_1_
  21.1 1.2 %copy-done.3 = bf16[1,8192,64]{1,2,0:T(8,128)(2,1)S(1)} copy-done((bf16[1,8192,64]{1,2,0:T(8,128)(2,1)S(1)}, bf16[1,8192,64]{1,2,0:T(8,128)(2,1)}, u32[]{:S(2)}) %copy-start.3) | copy-done | bytes 1048600
  22.3 0.8 row_masks.1
  23.3 1.9 %collective-permute-done.9.refs_9_ = bf16[16,4096]{1,0:T(8,128)(2,1)S(1)} collective-permute-done((bf16[16,4096]{1,0:T(8,128)(2,1)S(1)}, bf16[16,4096]{1,0:T(8,128)(2,1)S(1)}, u32[]{:S(2)}, u32[]{:S(2)}) %collective-permute-start.9) | collective-permute-done | bytes 131104 | tf_op jit(solution)/shard_map/ppermute | solution.py:128
  25.5 1.9 %collective-permute-start.13 = (bf16[16,4096]{1,0:T(8,128)(2,1)S(1)}, bf16[16,4096]{1,0:T(8,128)(2,1)S(1)}, u32[]{:S(2)}, u32[]{:S(2)}) collective-permute-start(bf16[16,4096]{1,0:T(8,128)(2,1)S(1)} %collective-permute-done.11.refs_11_), channel_id=1, source_target_pairs={{0,2},{1,3},{4,0},{5,1},{8,4},{9,5},{12,8},{13,9},{14,12},{15,13},... | collective-permute-start | bytes 393224 | tf_op jit(solution)/shard_map/ppermute | solution.py:133
  27.4 3.8 %collective-permute-done.12.refs_0_ = bf16[16,4096]{1,0:T(8,128)(2,1)S(1)} collective-permute-done((bf16[16,4096]{1,0:T(8,128)(2,1)S(1)}, bf16[16,4096]{1,0:T(8,128)(2,1)S(1)}, u32[]{:S(2)}, u32[]{:S(2)}) %collective-permute-start.12) | collective-permute-done | bytes 131104 | tf_op jit(solution)/shard_map/ppermute | solution.py:132
  31.5 1.5 %collective-permute-done.16.refs_5_ = bf16[16,8192]{1,0:T(8,128)(2,1)S(1)} collective-permute-done((bf16[16,8192]{1,0:T(8,128)(2,1)S(1)}, bf16[16,8192]{1,0:T(8,128)(2,1)S(1)}, u32[]{:S(2)}, u32[]{:S(2)}) %collective-permute-start.16) | collective-permute-done | bytes 262176 | tf_op jit(solution)/shard_map/ppermute | solution.py:138
  33.0 2.8 %shrink_rows.1 = (bf16[256,8192]{1,0:T(8,128)(2,1)S(1)}, bf16[256,64]{1,0:T(8,128)(2,1)S(1)}) custom-call(bf16[16,8192]{1,0:T(8,128)(2,1)S(1)} %copy-done.1, bf16[96,8192]{1,0:T(8,128)(2,1)S(1)} %join_pieces.2.refs_1_, bf16[16,8192]{1,0:T(8,128)(2,1)S(1)} %join_pieces.3.refs_2_, bf16[16,8192]{1,0:T(8,128)(2,1)S(1)} %collective-permute-done.14.refs_3_, ...), custom_call_target="tpu_custom_call" | custom-call | flops 268435456 | bytes 8388608 | tf_op jit(solution)/shard_map/shrink_rows/pallas_call | solution.py:75
  36.0 1.1 %collective-permute-done.17.refs_1_ = bf16[256,64]{1,0:T(8,128)(2,1)S(1)} collective-permute-done((bf16[256,64]{1,0:T(8,128)(2,1)S(1)}, bf16[256,64]{1,0:T(8,128)(2,1)S(1)}, u32[]{:S(2)}, u32[]{:S(2)}) %collective-permute-start.17) | collective-permute-done | bytes 32800 | tf_op jit(solution)/shard_map/ppermute | solution.py:462
  37.1 1.6 %collective-permute-start.18 = (bf16[256,64]{1,0:T(8,128)(2,1)S(1)}, bf16[256,64]{1,0:T(8,128)(2,1)S(1)}, u32[]{:S(2)}, u32[]{:S(2)}) collective-permute-start(bf16[256,64]{1,0:T(8,128)(2,1)S(1)} %add_coefficients.3.refs_2_.refs_0_), channel_id=1, source_target_pairs={{0,2},{1,3},{2,0},{3,1},{4,6},{5,7},{6,4},{7,5},{8,10},{9,11},{10,... | collective-permute-start | bytes 98312 | tf_op jit(solution)/shard_map/ppermute | solution.py:462
  38.8 5.7 %mixed_rows.3.refs_2_ = f32[256,1792]{1,0:T(8,128)S(1)} custom-call(bf16[256,8192]{1,0:T(8,128)(2,1)S(1)} %get-tuple-element.29.rows_ref, bf16[8192,896]{1,0:T(8,128)(2,1)} %refs_0_.9, bf16[8192,896]{1,0:T(8,128)(2,1)} %refs_1_.5, bf16[256,64]{1,0:T(8,128)(2,1)S(1)} %add_coefficients.3.refs_2_.refs_0_), custom_call_target="tpu_custom_call" | custom-call | flops 2818572288 | bytes 11010048 | tf_op jit(solution)/shard_map/mixed_rows/pallas_call | solution.py:298
  44.5 1.6 %collective-permute-start.19 = (bf16[256,64]{1,0:T(8,128)(2,1)S(1)}, bf16[256,64]{1,0:T(8,128)(2,1)S(1)}, u32[]{:S(2)}, u32[]{:S(2)}) collective-permute-start(bf16[256,64]{1,0:T(8,128)(2,1)S(1)} %add_coefficients.4.refs_3_.refs_0_), channel_id=1, source_target_pairs={{0,4},{1,5},{2,6},{3,7},{4,0},{5,1},{6,2},{7,3},{8,12},{9,13},{10,... | collective-permute-start | bytes 98312 | tf_op jit(solution)/shard_map/ppermute | solution.py:462
  46.1 5.0 %mixed_rows.4.refs_2_ = f32[256,1792]{1,0:T(8,128)S(1)} custom-call(bf16[256,8192]{1,0:T(8,128)(2,1)S(1)} %get-tuple-element.29.rows_ref, bf16[8192,896]{1,0:T(8,128)(2,1)} %refs_0_.9, bf16[8192,896]{1,0:T(8,128)(2,1)} %refs_1_.5, f32[256,1792]{1,0:T(8,128)S(1)} %mixed_rows.3.refs_2_, bf16[256,64]{1,0:T(8,128)(2,1)S(1)} %add_coefficients.4.refs_3_.refs_0_), custom_call_target="tpu_custom_call" | custom-call | flops 2348810240 | bytes 9175040 | tf_op jit(solution)/shard_map/mixed_rows/pallas_call | solution.py:298
  51.3 2.7 %collective-permute-start.20 = (bf16[256,64]{1,0:T(8,128)(2,1)S(1)}, bf16[256,64]{1,0:T(8,128)(2,1)S(1)}, u32[]{:S(2)}, u32[]{:S(2)}) collective-permute-start(bf16[256,64]{1,0:T(8,128)(2,1)S(1)} %add_coefficients.5.refs_3_.refs_0_), channel_id=1, source_target_pairs={{0,8},{1,9},{2,10},{3,11},{4,12},{5,13},{6,14},{7,15},{8,0},{9,1},... | collective-permute-start | bytes 98312 | tf_op jit(solution)/shard_map/ppermute | solution.py:462
  53.9 5.8 %mixed_rows.5.refs_5_ = f32[256,1792]{1,0:T(8,128)S(1)} custom-call(bf16[256,8192]{1,0:T(8,128)(2,1)S(1)} %get-tuple-element.29.rows_ref, bf16[8192,896]{1,0:T(8,128)(2,1)} %refs_0_.9, bf16[8192,896]{1,0:T(8,128)(2,1)} %refs_1_.5, f32[256,1792]{1,0:T(8,128)S(1)} %mixed_rows.4.refs_2_, bf16[256,64]{1,0:T(8,128)(2,1)S(1)} %add_coefficients.5.refs_3_.refs_0_), custom_call_target="tpu_custom_call" | custom-call | flops 2348810240 | bytes 9175040 | tf_op jit(solution)/shard_map/mixed_rows/pallas_call | solution.py:298
  59.8 1.0 %hidden_rows.1 = bf16[256,896]{1,0:T(8,128)(2,1)S(1)} custom-call(bf16[256,64]{1,0:T(8,128)(2,1)S(1)} %add_coefficients.5.refs_3_.refs_0_, bf16[256,64]{1,0:T(8,128)(2,1)S(1)} %collective-permute-done.20.refs_1_, bf16[256,256]{1,0:T(8,128)(2,1)S(1)} %get-tuple-element.30.refs_2_, bf16[256,1024]{1,0:T(8,128)(2,1)S(1)} %get-tuple-element.31.refs_3_, ...), custom_call_target="tpu_custom_call" | custom-call | flops 469762048 | bytes 1835008 | tf_op jit(solution)/shard_map/hidden_rows/pallas_call | solution.py:75
  60.8 2.4 %fusion.4.refs_0_.refs_2_.refs_3_ = bf16[256,4096]{1,0:T(8,128)(2,1)S(1)} fusion(bf16[256,896]{1,0:T(8,128)(2,1)S(1)} %hidden_rows.1, bf16[896,8192]{1,0:T(8,128)(2,1)S(1)} %bitcast.12), kind=kOutput, calls=%fused_computation.4 | convolution fusion | flops 1880096768 | bytes 9895936 | tf_op jit(solution)/shard_map/dot_general | solution.py:476
  63.4 2.6 %fusion.7.refs_0_.refs_2_.refs_3_.refs_4_ = bf16[256,4096]{1,0:T(8,128)(2,1)S(1)} fusion(bf16[256,896]{1,0:T(8,128)(2,1)S(1)} %hidden_rows.1, bf16[896,8192]{1,0:T(8,128)(2,1)S(1)} %bitcast.12), kind=kOutput, calls=%fused_computation.5 | convolution fusion | flops 1880096768 | bytes 9895936 | tf_op jit(solution)/shard_map/dot_general | solution.py:476
  66.1 0.6 collective-permute-start.24
  67.3 1.6 %collective-permute-start.23 = (bf16[16,4096]{1,0:T(8,128)(2,1)S(1)}, bf16[16,4096]{1,0:T(8,128)(2,1)S(1)}, u32[]{:S(2)}, u32[]{:S(2)}) collective-permute-start(bf16[16,4096]{1,0:T(8,128)(2,1)S(1)} %get-tuple-element.33), channel_id=1, source_target_pairs={{0,2},{1,3},{4,0},{5,1},{8,4},{9,5},{12,8},{13,9},{14,12},{15,13},... | collective-permute-start | bytes 393224 | tf_op jit(solution)/shard_map/ppermute | solution.py:396
  69.1 0.6 collective-permute-start.27
  69.7 1.5 %collective-permute-start.28 = (bf16[16,4096]{1,0:T(8,128)(2,1)S(1)}, bf16[16,4096]{1,0:T(8,128)(2,1)S(1)}, u32[]{:S(2)}, u32[]{:S(2)}) collective-permute-start(bf16[16,4096]{1,0:T(8,128)(2,1)S(1)} %get-tuple-element.37), channel_id=1, source_target_pairs={{0,4},{1,5},{4,8},{5,9},{8,12},{9,13},{12,14},{13,15},{14,10},{15,... | collective-permute-start | bytes 393224 | tf_op jit(solution)/shard_map/ppermute | solution.py:396
  71.1 1.1 %collective-permute-done.22.refs_2_ = bf16[16,4096]{1,0:T(8,128)(2,1)S(1)} collective-permute-done((bf16[16,4096]{1,0:T(8,128)(2,1)S(1)}, bf16[16,4096]{1,0:T(8,128)(2,1)S(1)}, u32[]{:S(2)}, u32[]{:S(2)}) %collective-permute-start.22) | collective-permute-done | bytes 131104 | tf_op jit(solution)/shard_map/ppermute | solution.py:396
  72.9 2.5 %collective-permute-start.25 = (bf16[16,4096]{1,0:T(8,128)(2,1)S(1)}, bf16[16,4096]{1,0:T(8,128)(2,1)S(1)}, u32[]{:S(2)}, u32[]{:S(2)}) collective-permute-start(bf16[16,4096]{1,0:T(8,128)(2,1)S(1)} %get-tuple-element.35.refs_6_), channel_id=1, source_target_pairs={{0,4},{1,5},{4,8},{5,9},{8,12},{9,13},{12,14},{13,15},{14,10},{15,... | collective-permute-start | bytes 393224 | tf_op jit(solution)/shard_map/ppermute | solution.py:396
  75.5 0.5 collective-permute-done.28.refs_5_
  76.1 1.6 %collective-permute-start.30 = (bf16[16,4096]{1,0:T(8,128)(2,1)S(1)}, bf16[16,4096]{1,0:T(8,128)(2,1)S(1)}, u32[]{:S(2)}, u32[]{:S(2)}) collective-permute-start(bf16[16,4096]{1,0:T(8,128)(2,1)S(1)} %get-tuple-element.38.refs_6_), channel_id=1, source_target_pairs={{0,2},{1,3},{4,0},{5,1},{8,4},{9,5},{12,8},{13,9},{14,12},{15,13},... | collective-permute-start | bytes 393224 | tf_op jit(solution)/shard_map/ppermute | solution.py:396
  78.2 0.6 collective-permute-done.25.refs_2_
  78.8 1.8 %collective-permute-done.26.refs_5_ = bf16[16,4096]{1,0:T(8,128)(2,1)S(1)} collective-permute-done((bf16[16,4096]{1,0:T(8,128)(2,1)S(1)}, bf16[16,4096]{1,0:T(8,128)(2,1)S(1)}, u32[]{:S(2)}, u32[]{:S(2)}) %collective-permute-start.26) | collective-permute-done | bytes 131104 | tf_op jit(solution)/shard_map/ppermute | solution.py:396
  80.7 0.9 collective-permute-start.29
  82.0 0.7 collective-permute-done.31.refs_5_
  82.9 1.8 %collective-permute-start.35 = (bf16[16,4096]{1,0:T(8,128)(2,1)S(1)}, bf16[16,4096]{1,0:T(8,128)(2,1)S(1)}, u32[]{:S(2)}, u32[]{:S(2)}) collective-permute-start(bf16[16,4096]{1,0:T(8,128)(2,1)S(1)} %get-tuple-element.41.refs_3_), channel_id=1, source_target_pairs={{0,2},{1,3},{4,0},{5,1},{8,4},{9,5},{12,8},{13,9},{14,12},{15,13},... | collective-permute-start | bytes 393224 | tf_op jit(solution)/shard_map/ppermute | solution.py:396
  84.9 1.8 %collective-permute-start.33 = (bf16[16,4096]{1,0:T(8,128)(2,1)S(1)}, bf16[16,4096]{1,0:T(8,128)(2,1)S(1)}, u32[]{:S(2)}, u32[]{:S(2)}) collective-permute-start(bf16[16,4096]{1,0:T(8,128)(2,1)S(1)} %get-tuple-element.42), channel_id=1, source_target_pairs={{0,2},{1,3},{4,0},{5,1},{8,4},{9,5},{12,8},{13,9},{14,12},{15,13},... | collective-permute-start | bytes 393224 | tf_op jit(solution)/shard_map/ppermute | solution.py:396
  87.1 1.6 %collective-permute-done.35.refs_2_ = bf16[16,4096]{1,0:T(8,128)(2,1)S(1)} collective-permute-done((bf16[16,4096]{1,0:T(8,128)(2,1)S(1)}, bf16[16,4096]{1,0:T(8,128)(2,1)S(1)}, u32[]{:S(2)}, u32[]{:S(2)}) %collective-permute-start.35) | collective-permute-done | bytes 131104 | tf_op jit(solution)/shard_map/ppermute | solution.py:396
  88.7 2.0 %collective-permute-start.36 = (bf16[16,4096]{1,0:T(8,128)(2,1)S(1)}, bf16[16,4096]{1,0:T(8,128)(2,1)S(1)}, u32[]{:S(2)}, u32[]{:S(2)}) collective-permute-start(bf16[16,4096]{1,0:T(8,128)(2,1)S(1)} %add_blocks.15), channel_id=1, source_target_pairs={{0,2},{1,3},{4,0},{5,1},{8,4},{9,5},{12,8},{13,9},{14,12},{15,13},... | collective-permute-start | bytes 393224 | tf_op jit(solution)/shard_map/ppermute | solution.py:396
  90.9 2.9 %collective-permute-done.36.refs_7_ = bf16[16,4096]{1,0:T(8,128)(2,1)S(1)} collective-permute-done((bf16[16,4096]{1,0:T(8,128)(2,1)S(1)}, bf16[16,4096]{1,0:T(8,128)(2,1)S(1)}, u32[]{:S(2)}, u32[]{:S(2)}) %collective-permute-start.36) | collective-permute-done | bytes 131104 | tf_op jit(solution)/shard_map/ppermute | solution.py:396
  93.7 2.0 %collective-permute-done.32.refs_2_ = bf16[16,4096]{1,0:T(8,128)(2,1)S(1)} collective-permute-done((bf16[16,4096]{1,0:T(8,128)(2,1)S(1)}, bf16[16,4096]{1,0:T(8,128)(2,1)S(1)}, u32[]{:S(2)}, u32[]{:S(2)}) %collective-permute-start.32) | collective-permute-done | bytes 131104 | tf_op jit(solution)/shard_map/ppermute | solution.py:396
  95.7 1.0 %finish_rows.1 = (bf16[16,8192]{1,0:T(8,128)(2,1)}, bf16[16,8192]{1,0:T(8,128)(2,1)}) custom-call(bf16[256,4096]{1,0:T(8,128)(2,1)S(1)} %fusion.4.refs_0_.refs_2_.refs_3_, bf16[128,4096]{1,0:T(8,128)(2,1)S(1)} %collective-permute-done.21.refs_1_.refs_3_.refs_4_, bf16[16,4096]{1,0:T(8,128)(2,1)S(1)} %collective-permute-done.32.refs_2_, ...), custom_call_target="tpu_custom_call" | custom-call | tf_op jit(solution)/shard_map/finish_rows/pallas_call | solution.py:75
  (72 shorter events, 5.6 us)
Async XLA Ops:
  0.6 1.0 copy-start
  1.6 25.8 %copy-start.1 = (bf16[16,8192]{1,0:T(8,128)(2,1)S(1)}, bf16[16,8192]{1,0:T(8,128)(2,1)}, u32[]{:S(2)}) copy-start(bf16[16,8192]{1,0:T(8,128)(2,1)} %refs_8_.1) | copy-start | bytes 786436
  1.6 7.4 %collective-permute-start.3 = (bf16[16,4096]{1,0:T(8,128)(2,1)S(1)}, bf16[16,4096]{1,0:T(8,128)(2,1)S(1)}, u32[]{:S(2)}, u32[]{:S(2)}) collective-permute-start(bf16[16,4096]{1,0:T(8,128)(2,1)S(1)} %get-tuple-element.24), channel_id=1, source_target_pairs={{0,2},{1,3},{4,0},{5,1},{8,4},{9,5},{12,8},{13,9},{14,12},{15,13},... | collective-permute-start | bytes 393224 | tf_op jit(solution)/shard_map/ppermute | solution.py:127
  4.6 6.4 %collective-permute-start = (bf16[16,4096]{1,0:T(8,128)(2,1)S(1)}, bf16[16,4096]{1,0:T(8,128)(2,1)S(1)}, u32[]{:S(2)}, u32[]{:S(2)}) collective-permute-start(bf16[16,4096]{1,0:T(8,128)(2,1)S(1)} %get-tuple-element.23), channel_id=1, source_target_pairs={{0,4},{1,5},{4,8},{5,9},{8,12},{9,13},{12,14},{13,15},{14,10},{15,... | collective-permute-start | bytes 393224 | tf_op jit(solution)/shard_map/ppermute | solution.py:126
  4.7 7.1 %collective-permute-start.2 = (bf16[16,4096]{1,0:T(8,128)(2,1)S(1)}, bf16[16,4096]{1,0:T(8,128)(2,1)S(1)}, u32[]{:S(2)}, u32[]{:S(2)}) collective-permute-start(bf16[16,4096]{1,0:T(8,128)(2,1)S(1)} %get-tuple-element.23), channel_id=1, source_target_pairs={{0,2},{1,3},{4,0},{5,1},{8,4},{9,5},{12,8},{13,9},{14,12},{15,13},... | collective-permute-start | bytes 393224 | tf_op jit(solution)/shard_map/ppermute | solution.py:129
  6.6 7.2 %collective-permute-start.1 = (bf16[16,4096]{1,0:T(8,128)(2,1)S(1)}, bf16[16,4096]{1,0:T(8,128)(2,1)S(1)}, u32[]{:S(2)}, u32[]{:S(2)}) collective-permute-start(bf16[16,4096]{1,0:T(8,128)(2,1)S(1)} %get-tuple-element.24), channel_id=1, source_target_pairs={{0,4},{1,5},{4,8},{5,9},{8,12},{9,13},{12,14},{13,15},{14,10},{15,... | collective-permute-start | bytes 393224 | tf_op jit(solution)/shard_map/ppermute | solution.py:128
  9.0 6.2 %collective-permute-start.7 = (bf16[16,4096]{1,0:T(8,128)(2,1)S(1)}, bf16[16,4096]{1,0:T(8,128)(2,1)S(1)}, u32[]{:S(2)}, u32[]{:S(2)}) collective-permute-start(bf16[16,4096]{1,0:T(8,128)(2,1)S(1)} %collective-permute-done.3.refs_3_), channel_id=1, source_target_pairs={{0,2},{1,3},{4,0},{5,1},{8,4},{9,5},{12,8},{13,9},{14,12},{15,13},... | collective-permute-start | bytes 393224 | tf_op jit(solution)/shard_map/ppermute | solution.py:127
  11.0 6.2 %collective-permute-start.4 = (bf16[16,4096]{1,0:T(8,128)(2,1)S(1)}, bf16[16,4096]{1,0:T(8,128)(2,1)S(1)}, u32[]{:S(2)}, u32[]{:S(2)}) collective-permute-start(bf16[16,4096]{1,0:T(8,128)(2,1)S(1)} %collective-permute-done.refs_0_), channel_id=1, source_target_pairs={{0,4},{1,5},{4,8},{5,9},{8,12},{9,13},{12,14},{13,15},{14,10},{15,... | collective-permute-start | bytes 393224 | tf_op jit(solution)/shard_map/ppermute | solution.py:126
  11.8 6.5 %collective-permute-start.6 = (bf16[16,4096]{1,0:T(8,128)(2,1)S(1)}, bf16[16,4096]{1,0:T(8,128)(2,1)S(1)}, u32[]{:S(2)}, u32[]{:S(2)}) collective-permute-start(bf16[16,4096]{1,0:T(8,128)(2,1)S(1)} %collective-permute-done.2.refs_2_), channel_id=1, source_target_pairs={{0,2},{1,3},{4,0},{5,1},{8,4},{9,5},{12,8},{13,9},{14,12},{15,13},... | collective-permute-start | bytes 393224 | tf_op jit(solution)/shard_map/ppermute | solution.py:129
  13.8 6.3 %collective-permute-start.5 = (bf16[16,4096]{1,0:T(8,128)(2,1)S(1)}, bf16[16,4096]{1,0:T(8,128)(2,1)S(1)}, u32[]{:S(2)}, u32[]{:S(2)}) collective-permute-start(bf16[16,4096]{1,0:T(8,128)(2,1)S(1)} %collective-permute-done.1.refs_1_), channel_id=1, source_target_pairs={{0,4},{1,5},{4,8},{5,9},{8,12},{9,13},{12,14},{13,15},{14,10},{15,... | collective-permute-start | bytes 393224 | tf_op jit(solution)/shard_map/ppermute | solution.py:128
  15.2 8.0 %collective-permute-start.11 = (bf16[16,4096]{1,0:T(8,128)(2,1)S(1)}, bf16[16,4096]{1,0:T(8,128)(2,1)S(1)}, u32[]{:S(2)}, u32[]{:S(2)}) collective-permute-start(bf16[16,4096]{1,0:T(8,128)(2,1)S(1)} %collective-permute-done.7.refs_7_), channel_id=1, source_target_pairs={{0,2},{1,3},{4,0},{5,1},{8,4},{9,5},{12,8},{13,9},{14,12},{15,13},... | collective-permute-start | bytes 393224 | tf_op jit(solution)/shard_map/ppermute | solution.py:127
  17.2 5.9 %collective-permute-start.8 = (bf16[16,4096]{1,0:T(8,128)(2,1)S(1)}, bf16[16,4096]{1,0:T(8,128)(2,1)S(1)}, u32[]{:S(2)}, u32[]{:S(2)}) collective-permute-start(bf16[16,4096]{1,0:T(8,128)(2,1)S(1)} %collective-permute-done.4.refs_4_), channel_id=1, source_target_pairs={{0,4},{1,5},{4,8},{5,9},{8,12},{9,13},{12,14},{13,15},{14,10},{15,... | collective-permute-start | bytes 393224 | tf_op jit(solution)/shard_map/ppermute | solution.py:126
  18.3 5.0 %collective-permute-start.10 = (bf16[16,4096]{1,0:T(8,128)(2,1)S(1)}, bf16[16,4096]{1,0:T(8,128)(2,1)S(1)}, u32[]{:S(2)}, u32[]{:S(2)}) collective-permute-start(bf16[16,4096]{1,0:T(8,128)(2,1)S(1)} %collective-permute-done.6.refs_6_), channel_id=1, source_target_pairs={{0,2},{1,3},{4,0},{5,1},{8,4},{9,5},{12,8},{13,9},{14,12},{15,13},... | collective-permute-start | bytes 393224 | tf_op jit(solution)/shard_map/ppermute | solution.py:129
  20.1 5.0 %collective-permute-start.9 = (bf16[16,4096]{1,0:T(8,128)(2,1)S(1)}, bf16[16,4096]{1,0:T(8,128)(2,1)S(1)}, u32[]{:S(2)}, u32[]{:S(2)}) collective-permute-start(bf16[16,4096]{1,0:T(8,128)(2,1)S(1)} %collective-permute-done.5.refs_5_), channel_id=1, source_target_pairs={{0,4},{1,5},{4,8},{5,9},{8,12},{9,13},{12,14},{13,15},{14,10},{15,... | collective-permute-start | bytes 393224 | tf_op jit(solution)/shard_map/ppermute | solution.py:128
  21.1 1.2 %copy-start.3 = (bf16[1,8192,64]{1,2,0:T(8,128)(2,1)S(1)}, bf16[1,8192,64]{1,2,0:T(8,128)(2,1)}, u32[]{:S(2)}) copy-start(bf16[1,8192,64]{1,2,0:T(8,128)(2,1)} %param.16) | copy-start | bytes 3145732
  25.2 7.8 %collective-permute-start.15 = (bf16[96,8192]{1,0:T(8,128)(2,1)S(1)}, bf16[96,8192]{1,0:T(8,128)(2,1)S(1)}, u32[]{:S(2)}, u32[]{:S(2)}) collective-permute-start(bf16[96,8192]{1,0:T(8,128)(2,1)S(1)} %join_pieces.2.refs_1_), channel_id=1, source_target_pairs={{0,1},{1,0},{2,3},{3,2},{4,5},{5,4},{6,7},{7,6},{8,9},{9,8},{10,11... | collective-permute-start | bytes 4718600 | tf_op jit(solution)/shard_map/ppermute | solution.py:138
  25.3 5.9 %collective-permute-start.12 = (bf16[16,4096]{1,0:T(8,128)(2,1)S(1)}, bf16[16,4096]{1,0:T(8,128)(2,1)S(1)}, u32[]{:S(2)}, u32[]{:S(2)}) collective-permute-start(bf16[16,4096]{1,0:T(8,128)(2,1)S(1)} %collective-permute-done.8.refs_8_), channel_id=1, source_target_pairs={{0,4},{1,5},{4,8},{5,9},{8,12},{9,13},{12,14},{13,15},{14,10},{15,... | collective-permute-start | bytes 393224 | tf_op jit(solution)/shard_map/ppermute | solution.py:132
  25.5 5.8 %collective-permute-start.13 = (bf16[16,4096]{1,0:T(8,128)(2,1)S(1)}, bf16[16,4096]{1,0:T(8,128)(2,1)S(1)}, u32[]{:S(2)}, u32[]{:S(2)}) collective-permute-start(bf16[16,4096]{1,0:T(8,128)(2,1)S(1)} %collective-permute-done.11.refs_11_), channel_id=1, source_target_pairs={{0,2},{1,3},{4,0},{5,1},{8,4},{9,5},{12,8},{13,9},{14,12},{15,13},... | collective-permute-start | bytes 393224 | tf_op jit(solution)/shard_map/ppermute | solution.py:133
  27.4 4.1 %collective-permute-start.14 = (bf16[16,8192]{1,0:T(8,128)(2,1)S(1)}, bf16[16,8192]{1,0:T(8,128)(2,1)S(1)}, u32[]{:S(2)}, u32[]{:S(2)}) collective-permute-start(bf16[16,8192]{1,0:T(8,128)(2,1)S(1)} %copy-done.1), channel_id=1, source_target_pairs={{0,1},{1,0},{2,3},{3,2},{4,5},{5,4},{6,7},{7,6},{8,9},{9,8},{10,11... | collective-permute-start | bytes 786440 | tf_op jit(solution)/shard_map/ppermute | solution.py:119
  31.4 1.6 %collective-permute-start.16 = (bf16[16,8192]{1,0:T(8,128)(2,1)S(1)}, bf16[16,8192]{1,0:T(8,128)(2,1)S(1)}, u32[]{:S(2)}, u32[]{:S(2)}) collective-permute-start(bf16[16,8192]{1,0:T(8,128)(2,1)S(1)} %join_pieces.3.refs_2_), channel_id=1, source_target_pairs={{0,1},{1,0},{2,3},{3,2},{4,5},{5,4},{6,7},{7,6},{8,9},{9,8},{10,11... | collective-permute-start | bytes 786440 | tf_op jit(solution)/shard_map/ppermute | solution.py:138
  35.8 1.3 %collective-permute-start.17 = (bf16[256,64]{1,0:T(8,128)(2,1)S(1)}, bf16[256,64]{1,0:T(8,128)(2,1)S(1)}, u32[]{:S(2)}, u32[]{:S(2)}) collective-permute-start(bf16[256,64]{1,0:T(8,128)(2,1)S(1)} %get-tuple-element.28.refs_0_), channel_id=1, source_target_pairs={{0,1},{1,0},{2,3},{3,2},{4,5},{5,4},{6,7},{7,6},{8,9},{9,8},{10,11... | collective-permute-start | bytes 98312 | tf_op jit(solution)/shard_map/ppermute | solution.py:462
  37.1 7.3 %collective-permute-start.18 = (bf16[256,64]{1,0:T(8,128)(2,1)S(1)}, bf16[256,64]{1,0:T(8,128)(2,1)S(1)}, u32[]{:S(2)}, u32[]{:S(2)}) collective-permute-start(bf16[256,64]{1,0:T(8,128)(2,1)S(1)} %add_coefficients.3.refs_2_.refs_0_), channel_id=1, source_target_pairs={{0,2},{1,3},{2,0},{3,1},{4,6},{5,7},{6,4},{7,5},{8,10},{9,11},{10,... | collective-permute-start | bytes 98312 | tf_op jit(solution)/shard_map/ppermute | solution.py:462
  44.5 6.7 %collective-permute-start.19 = (bf16[256,64]{1,0:T(8,128)(2,1)S(1)}, bf16[256,64]{1,0:T(8,128)(2,1)S(1)}, u32[]{:S(2)}, u32[]{:S(2)}) collective-permute-start(bf16[256,64]{1,0:T(8,128)(2,1)S(1)} %add_coefficients.4.refs_3_.refs_0_), channel_id=1, source_target_pairs={{0,4},{1,5},{2,6},{3,7},{4,0},{5,1},{6,2},{7,3},{8,12},{9,13},{10,... | collective-permute-start | bytes 98312 | tf_op jit(solution)/shard_map/ppermute | solution.py:462
  51.2 9.6 %slice-start = ((s8[14680064]{0:T(1024)(128)(4,1)}), s8[4194304]{0:T(1024)(128)(4,1)S(1)}, s32[]{:S(2)}) async-start(s8[14680064]{0:T(1024)(128)(4,1)} %bitcast.11), calls=%async_computation | async-start | bytes 8388608
  51.2 8.5 %copy-start.2 = (bf16[16,64,896]{2,1,0:T(8,128)(2,1)S(1)}, bf16[16,64,896]{2,1,0:T(8,128)(2,1)}, u32[]{:S(2)}) copy-start(bf16[16,64,896]{2,1,0:T(8,128)(2,1)} %param.17) | copy-start | bytes 5505028
  51.2 9.5 %slice-start.1 = ((s8[14680064]{0:T(1024)(128)(4,1)}), s8[4194304]{0:T(1024)(128)(4,1)S(1)}, s32[]{:S(2)}) async-start(s8[14680064]{0:T(1024)(128)(4,1)} %bitcast.11), calls=%async_computation.1 | async-start | bytes 8388608
  51.2 9.5 %slice-start.2 = ((s8[14680064]{0:T(1024)(128)(4,1)}), s8[4194304]{0:T(1024)(128)(4,1)S(1)}, s32[]{:S(2)}) async-start(s8[14680064]{0:T(1024)(128)(4,1)} %bitcast.11), calls=%async_computation.2 | async-start | bytes 8388608
  51.2 9.5 %slice-start.3 = ((s8[14680064]{0:T(1024)(128)(4,1)}), s8[2097152]{0:T(1024)(128)(4,1)S(1)}, s32[]{:S(2)}) async-start(s8[14680064]{0:T(1024)(128)(4,1)} %bitcast.11), calls=%async_computation.3 | async-start | bytes 4194304
  51.3 8.5 %collective-permute-start.20 = (bf16[256,64]{1,0:T(8,128)(2,1)S(1)}, bf16[256,64]{1,0:T(8,128)(2,1)S(1)}, u32[]{:S(2)}, u32[]{:S(2)}) collective-permute-start(bf16[256,64]{1,0:T(8,128)(2,1)S(1)} %add_coefficients.5.refs_3_.refs_0_), channel_id=1, source_target_pairs={{0,8},{1,9},{2,10},{3,11},{4,12},{5,13},{6,14},{7,15},{8,0},{9,1},... | collective-permute-start | bytes 98312 | tf_op jit(solution)/shard_map/ppermute | solution.py:462
  63.3 3.4 %collective-permute-start.21 = (bf16[128,4096]{1,0:T(8,128)(2,1)S(1)}, bf16[128,4096]{1,0:T(8,128)(2,1)S(1)}, u32[]{:S(2)}, u32[]{:S(2)}) collective-permute-start(bf16[128,4096]{1,0:T(8,128)(2,1)S(1)} %slice.16), channel_id=1, source_target_pairs={{0,1},{1,0},{2,3},{3,2},{4,5},{5,4},{6,7},{7,6},{8,9},{9,8},{10,11... | collective-permute-start | bytes 3145736 | tf_op jit(solution)/shard_map/ppermute | solution.py:482
  66.1 2.8 %collective-permute-start.24 = (bf16[128,4096]{1,0:T(8,128)(2,1)S(1)}, bf16[128,4096]{1,0:T(8,128)(2,1)S(1)}, u32[]{:S(2)}, u32[]{:S(2)}) collective-permute-start(bf16[128,4096]{1,0:T(8,128)(2,1)S(1)} %slice.17), channel_id=1, source_target_pairs={{0,1},{1,0},{2,3},{3,2},{4,5},{5,4},{6,7},{7,6},{8,9},{9,8},{10,11... | collective-permute-start | bytes 3145736 | tf_op jit(solution)/shard_map/ppermute | solution.py:482
  66.8 5.5 %collective-permute-start.22 = (bf16[16,4096]{1,0:T(8,128)(2,1)S(1)}, bf16[16,4096]{1,0:T(8,128)(2,1)S(1)}, u32[]{:S(2)}, u32[]{:S(2)}) collective-permute-start(bf16[16,4096]{1,0:T(8,128)(2,1)S(1)} %get-tuple-element.32.refs_4_), channel_id=1, source_target_pairs={{0,4},{1,5},{4,8},{5,9},{8,12},{9,13},{12,14},{13,15},{14,10},{15,... | collective-permute-start | bytes 393224 | tf_op jit(solution)/shard_map/ppermute | solution.py:396
  67.3 5.5 %collective-permute-start.23 = (bf16[16,4096]{1,0:T(8,128)(2,1)S(1)}, bf16[16,4096]{1,0:T(8,128)(2,1)S(1)}, u32[]{:S(2)}, u32[]{:S(2)}) collective-permute-start(bf16[16,4096]{1,0:T(8,128)(2,1)S(1)} %get-tuple-element.33), channel_id=1, source_target_pairs={{0,2},{1,3},{4,0},{5,1},{8,4},{9,5},{12,8},{13,9},{14,12},{15,13},... | collective-permute-start | bytes 393224 | tf_op jit(solution)/shard_map/ppermute | solution.py:396
  69.1 6.4 %collective-permute-start.27 = (bf16[16,4096]{1,0:T(8,128)(2,1)S(1)}, bf16[16,4096]{1,0:T(8,128)(2,1)S(1)}, u32[]{:S(2)}, u32[]{:S(2)}) collective-permute-start(bf16[16,4096]{1,0:T(8,128)(2,1)S(1)} %get-tuple-element.34.refs_6_), channel_id=1, source_target_pairs={{0,2},{1,3},{4,0},{5,1},{8,4},{9,5},{12,8},{13,9},{14,12},{15,13},... | collective-permute-start | bytes 393224 | tf_op jit(solution)/shard_map/ppermute | solution.py:396
  69.7 6.4 %collective-permute-start.28 = (bf16[16,4096]{1,0:T(8,128)(2,1)S(1)}, bf16[16,4096]{1,0:T(8,128)(2,1)S(1)}, u32[]{:S(2)}, u32[]{:S(2)}) collective-permute-start(bf16[16,4096]{1,0:T(8,128)(2,1)S(1)} %get-tuple-element.37), channel_id=1, source_target_pairs={{0,4},{1,5},{4,8},{5,9},{8,12},{9,13},{12,14},{13,15},{14,10},{15,... | collective-permute-start | bytes 393224 | tf_op jit(solution)/shard_map/ppermute | solution.py:396
  72.9 6.0 %collective-permute-start.25 = (bf16[16,4096]{1,0:T(8,128)(2,1)S(1)}, bf16[16,4096]{1,0:T(8,128)(2,1)S(1)}, u32[]{:S(2)}, u32[]{:S(2)}) collective-permute-start(bf16[16,4096]{1,0:T(8,128)(2,1)S(1)} %get-tuple-element.35.refs_6_), channel_id=1, source_target_pairs={{0,4},{1,5},{4,8},{5,9},{8,12},{9,13},{12,14},{13,15},{14,10},{15,... | collective-permute-start | bytes 393224 | tf_op jit(solution)/shard_map/ppermute | solution.py:396
  75.4 5.2 %collective-permute-start.26 = (bf16[16,4096]{1,0:T(8,128)(2,1)S(1)}, bf16[16,4096]{1,0:T(8,128)(2,1)S(1)}, u32[]{:S(2)}, u32[]{:S(2)}) collective-permute-start(bf16[16,4096]{1,0:T(8,128)(2,1)S(1)} %get-tuple-element.36), channel_id=1, source_target_pairs={{0,2},{1,3},{4,0},{5,1},{8,4},{9,5},{12,8},{13,9},{14,12},{15,13},... | collective-permute-start | bytes 393224 | tf_op jit(solution)/shard_map/ppermute | solution.py:396
  76.1 5.9 %collective-permute-start.30 = (bf16[16,4096]{1,0:T(8,128)(2,1)S(1)}, bf16[16,4096]{1,0:T(8,128)(2,1)S(1)}, u32[]{:S(2)}, u32[]{:S(2)}) collective-permute-start(bf16[16,4096]{1,0:T(8,128)(2,1)S(1)} %get-tuple-element.38.refs_6_), channel_id=1, source_target_pairs={{0,2},{1,3},{4,0},{5,1},{8,4},{9,5},{12,8},{13,9},{14,12},{15,13},... | collective-permute-start | bytes 393224 | tf_op jit(solution)/shard_map/ppermute | solution.py:396
  77.8 5.0 %collective-permute-start.31 = (bf16[16,4096]{1,0:T(8,128)(2,1)S(1)}, bf16[16,4096]{1,0:T(8,128)(2,1)S(1)}, u32[]{:S(2)}, u32[]{:S(2)}) collective-permute-start(bf16[16,4096]{1,0:T(8,128)(2,1)S(1)} %get-tuple-element.40), channel_id=1, source_target_pairs={{0,4},{1,5},{4,8},{5,9},{8,12},{9,13},{12,14},{13,15},{14,10},{15,... | collective-permute-start | bytes 393224 | tf_op jit(solution)/shard_map/ppermute | solution.py:396
  80.7 6.3 %collective-permute-start.29 = (bf16[16,4096]{1,0:T(8,128)(2,1)S(1)}, bf16[16,4096]{1,0:T(8,128)(2,1)S(1)}, u32[]{:S(2)}, u32[]{:S(2)}) collective-permute-start(bf16[16,4096]{1,0:T(8,128)(2,1)S(1)} %get-tuple-element.39.refs_6_), channel_id=1, source_target_pairs={{0,4},{1,5},{4,8},{5,9},{8,12},{9,13},{12,14},{13,15},{14,10},{15,... | collective-permute-start | bytes 393224 | tf_op jit(solution)/shard_map/ppermute | solution.py:396
  82.8 8.0 %copy-start.4 = (bf16[8192]{0:T(1024)(128)(2,1)S(1)}, bf16[8192]{0:T(1024)(128)(2,1)}, u32[]{:S(2)}) copy-start(bf16[8192]{0:T(1024)(128)(2,1)} %param.15) | copy-start | bytes 49156
  82.9 5.8 %collective-permute-start.35 = (bf16[16,4096]{1,0:T(8,128)(2,1)S(1)}, bf16[16,4096]{1,0:T(8,128)(2,1)S(1)}, u32[]{:S(2)}, u32[]{:S(2)}) collective-permute-start(bf16[16,4096]{1,0:T(8,128)(2,1)S(1)} %get-tuple-element.41.refs_3_), channel_id=1, source_target_pairs={{0,2},{1,3},{4,0},{5,1},{8,4},{9,5},{12,8},{13,9},{14,12},{15,13},... | collective-permute-start | bytes 393224 | tf_op jit(solution)/shard_map/ppermute | solution.py:396
  84.7 6.2 %collective-permute-start.34 = (bf16[16,4096]{1,0:T(8,128)(2,1)S(1)}, bf16[16,4096]{1,0:T(8,128)(2,1)S(1)}, u32[]{:S(2)}, u32[]{:S(2)}) collective-permute-start(bf16[16,4096]{1,0:T(8,128)(2,1)S(1)} %get-tuple-element.43), channel_id=1, source_target_pairs={{0,4},{1,5},{4,8},{5,9},{8,12},{9,13},{12,14},{13,15},{14,10},{15,... | collective-permute-start | bytes 393224 | tf_op jit(solution)/shard_map/ppermute | solution.py:396
  84.9 5.9 %collective-permute-start.33 = (bf16[16,4096]{1,0:T(8,128)(2,1)S(1)}, bf16[16,4096]{1,0:T(8,128)(2,1)S(1)}, u32[]{:S(2)}, u32[]{:S(2)}) collective-permute-start(bf16[16,4096]{1,0:T(8,128)(2,1)S(1)} %get-tuple-element.42), channel_id=1, source_target_pairs={{0,2},{1,3},{4,0},{5,1},{8,4},{9,5},{12,8},{13,9},{14,12},{15,13},... | collective-permute-start | bytes 393224 | tf_op jit(solution)/shard_map/ppermute | solution.py:396
  88.7 5.0 %collective-permute-start.36 = (bf16[16,4096]{1,0:T(8,128)(2,1)S(1)}, bf16[16,4096]{1,0:T(8,128)(2,1)S(1)}, u32[]{:S(2)}, u32[]{:S(2)}) collective-permute-start(bf16[16,4096]{1,0:T(8,128)(2,1)S(1)} %add_blocks.15), channel_id=1, source_target_pairs={{0,2},{1,3},{4,0},{5,1},{8,4},{9,5},{12,8},{13,9},{14,12},{15,13},... | collective-permute-start | bytes 393224 | tf_op jit(solution)/shard_map/ppermute | solution.py:396
  90.7 5.0 %collective-permute-start.32 = (bf16[16,4096]{1,0:T(8,128)(2,1)S(1)}, bf16[16,4096]{1,0:T(8,128)(2,1)S(1)}, u32[]{:S(2)}, u32[]{:S(2)}) collective-permute-start(bf16[16,4096]{1,0:T(8,128)(2,1)S(1)} %add_blocks.14.refs_3_), channel_id=1, source_target_pairs={{0,4},{1,5},{4,8},{5,9},{8,12},{9,13},{12,14},{13,15},{14,10},{15,... | collective-permute-start | bytes 393224 | tf_op jit(solution)/shard_map/ppermute | solution.py:396

commit v7 on v6

--- a/solution.py
+++ b/solution.py
@@ -10,9 +10,12 @@
 adapter_alpha = 32.0
 AXIS = "mp"
 HALVES = 2
-DEPTH_BLOCK = 1024
-VMEM_LIMIT = 16 * 1024 * 1024
-STREAM_LIMIT = 38 * 1024 * 1024
+DEPTH_BLOCK = 256
+LOADS = 2
+VMEM_LIMIT = 12 * 1024 * 1024
+LOAD_LIMITS = [mb * 1024 * 1024 for mb in (42, 37)]
+STREAM_LIMIT = 34 * 1024 * 1024
+STREAM_COST = 4
 
 
 def chip_at(place, chips):
@@ -86,57 +89,73 @@
     )(*operands, *ordered)
 
 
-def split_columns(array):
+def column_half(array, h):
     rows, columns = array.shape
     width = columns // HALVES
-    half = jax.ShapeDtypeStruct((rows, width), array.dtype)
-
-    def kernel(ref, *outs):
-        for h, out in enumerate(outs):
-            out[...] = ref[:, h * width : (h + 1) * width]
-
-    return call(kernel, (half,) * HALVES, [array], "split_columns")
-
-
-def join(pieces, ordered=()):
+
+    def kernel(ref, out):
+        out[...] = ref[:, h * width : (h + 1) * width]
+
+    return call(
+        kernel, jax.ShapeDtypeStruct((rows, width), array.dtype), [array], "column_half"
+    )
+
+
+def pass_on(array, ordered):
+    def kernel(ref, out):
+        out[...] = ref[...]
+
+    return call(
+        kernel, jax.ShapeDtypeStruct(array.shape, array.dtype), [array], "pass_on", ordered
+    )
+
+
+def join(pieces, columns, ordered=()):
     rows, width = pieces[0].shape
+    across = columns // width
 
     def kernel(*refs):
         out = refs[-1]
         for i, ref in enumerate(refs[:-1]):
-            top, left = i // HALVES * rows, i % HALVES * width
+            top, left = i // across * rows, i % across * width
             out[top : top + rows, left : left + width] = ref[...]
 
-    shape = (rows * len(pieces) // HALVES, HALVES * width)
+    shape = (rows * len(pieces) // across, columns)
     return call(
         kernel, jax.ShapeDtypeStruct(shape, pieces[0].dtype), pieces, "join_pieces", ordered
     )
 
 
-def gather_rows(own, size, ordered):
+def gather_rows(own, size, weights, ordered):
     chips = size // 2
     last = chips // 2
-    other = lax.ppermute(own, AXIS, flip(size, 1))
-    halves = split_columns(own)
-    right, left = list(halves), list(halves)
-    pieces = []
-    mine, theirs = [own], [other]
-    for step in range(1, last + 1):
-        if step < last:
-            right[0] = lax.ppermute(right[0], AXIS, ring(size, 1))
-            left[1] = lax.ppermute(left[1], AXIS, ring(size, -1))
-            right[1] = lax.ppermute(right[1], AXIS, ring(size, 1))
-            left[0] = lax.ppermute(left[0], AXIS, ring(size, -1))
-            pieces += right + left
-        else:
-            pieces.append(lax.ppermute(right[0], AXIS, ring(size, 1)))
-            pieces.append(lax.ppermute(left[1], AXIS, ring(size, -1)))
-        if step >= last - 1:
-            part = join(pieces, ordered if step < last else [])
-            pieces = []
-            mine.append(part)
-            theirs.append(lax.ppermute(part, AXIS, flip(size, 1)))
-    return mine + theirs
+    columns = own.shape[1]
+    right = left = own
+    pieces, loads = [], []
+    mine, theirs = [own], []
+    for step in range(1, last):
+        before = right
+        right = lax.ppermute(right, AXIS, ring(size, 1))
+        left = lax.ppermute(left, AXIS, ring(size, -1))
+        if step == 1:
+            theirs.append(lax.ppermute(own, AXIS, flip(size, 1)))
+        pieces += [right, left]
+        if step <= LOADS:
+            loads.append(load_rows(weights, step - 1, [before] if step > 1 else []))
+            right = pass_on(right, loads[-1])
+    part = join(pieces, columns, ordered)
+    mine.append(part)
+    theirs.append(lax.ppermute(part, AXIS, flip(size, 1)))
+    part = join(
+        [
+            lax.ppermute(column_half(right, 0), AXIS, ring(size, 1)),
+            lax.ppermute(column_half(left, 1), AXIS, ring(size, -1)),
+        ],
+        columns,
+    )
+    mine.append(part)
+    theirs.append(lax.ppermute(part, AXIS, flip(size, 1)))
+    return mine + theirs, loads
 
 
 def row_masks(me, tables, shrink_factors, own_rows, size):
@@ -240,7 +259,88 @@
     return -(-width // 128) * 128
 
 
-def mixed_rows(rows, weights, before, first, last, ordered):
+def depth_cuts(depth):
+    part = -(-3 * depth // 8 // DEPTH_BLOCK) * DEPTH_BLOCK
+    return [part * p for p in range(LOADS + 1)] + [depth]
+
+
+def load_rows(weights, part, ordered):
+    depth = weights[0].shape[0]
+    first, last = depth_cuts(depth)[part : part + 2]
+    widths = [weight.shape[1] for weight in weights]
+    if all(width % 128 == 0 for width in widths):
+        places = [(0, sum(widths[:w])) for w in range(len(weights))]
+        shapes = [(last - first, sum(widths))]
+    else:
+        places = [(w, 0) for w in range(len(weights))]
+        shapes = [(last - first, width) for width in widths]
+
+    def kernel(*refs):
+        sources = refs[: len(weights)]
+        outs = refs[len(weights) + len(ordered) : -1]
+        arrived = refs[-1]
+        copies = []
+        for i, top in enumerate(range(0, last - first, DEPTH_BLOCK)):
+            for w, (out, left) in enumerate(places):
+                copy = pltpu.make_async_copy(
+                    sources[w].at[first + top : first + top + DEPTH_BLOCK, :],
+                    outs[out].at[top : top + DEPTH_BLOCK, left : left + widths[w]],
+                    arrived.at[i, w],
+                )
+                copy.start()
+                copies.append(copy)
+        for copy in copies:
+            copy.wait()
+
+    return pl.pallas_call(
+        kernel,
+        out_shape=[jax.ShapeDtypeStruct(shape, weights[0].dtype) for shape in shapes],
+        in_specs=[whole(pltpu.HBM)] * len(weights) + [whole(pl.ANY)] * len(ordered),
+        out_specs=[whole()] * len(shapes),
+        scratch_shapes=[
+            pltpu.SemaphoreType.DMA(((last - first) // DEPTH_BLOCK, len(weights)))
+        ],
+        compiler_params=pltpu.CompilerParams(vmem_limit_bytes=LOAD_LIMITS[part]),
+        cost_estimate=pl.CostEstimate(
+            flops=0, bytes_accessed=4 * (last - first) * sum(widths), transcendentals=0
+        ),
+        name="load_rows",
+    )(*weights, *ordered)
+
+
+def mixed_rows(rows, loaded, part, before, ordered):
+    batch_rows, depth = rows.shape
+    first, last = depth_cuts(depth)[part : part + 2]
+    widths = [block.shape[1] for block in loaded]
+    lefts = [sum(lane_tiles(width) for width in widths[:w]) for w in range(len(widths))]
+    width = sum(lane_tiles(width) for width in widths)
+
+    def kernel(rows_ref, *refs):
+        out = refs[-1]
+        for block, left, wide in zip(refs, lefts, widths):
+            columns = slice(left, left + wide)
+            product = jnp.dot(
+                rows_ref[:, first:last], block[...], preferred_element_type=jnp.float32
+            )
+            if before is not None:
+                product = refs[len(widths)][:, columns] + product
+            out[:, columns] = product
+
+    return call(
+        kernel,
+        jax.ShapeDtypeStruct((batch_rows, width), jnp.float32),
+        [rows, *loaded] + ([] if before is None else [before]),
+        "mixed_rows",
+        ordered,
+        cost_estimate=pl.CostEstimate(
+            flops=2 * batch_rows * (last - first) * width,
+            bytes_accessed=2 * (last - first) * width,
+            transcendentals=0,
+        ),
+    )
+
+
+def stream_rows(rows, weights, before, first, last, ordered):
     batch_rows = rows.shape[0]
     widths = [weight.shape[1] for weight in weights]
     lefts = [sum(lane_tiles(width) for width in widths[:w]) for w in range(len(weights))]
@@ -254,7 +354,7 @@
     blocks = []
     at = first
     while at < last:
-        depth = min(DEPTH_BLOCK if blocks else DEPTH_BLOCK // 2, last - at)
+        depth = min(4 * DEPTH_BLOCK if blocks else 2 * DEPTH_BLOCK, last - at)
         blocks.append((at, depth))
         at += depth
 
@@ -308,10 +408,10 @@
         compiler_params=pltpu.CompilerParams(vmem_limit_bytes=STREAM_LIMIT),
         cost_estimate=pl.CostEstimate(
             flops=2 * batch_rows * (last - first) * width,
-            bytes_accessed=2 * (last - first) * width,
+            bytes_accessed=STREAM_COST * (last - first) * width,
             transcendentals=0,
         ),
-        name="mixed_rows",
+        name="stream_rows",
     )(rows, *weights, *([] if before is None else [before]), *ordered)
 
 
@@ -451,20 +551,21 @@
         me, tables, shrink_factors, own_rows, size
     )
 
-    parts = gather_rows(activations, size, [scale])
+    parts, loads = gather_rows(activations, size, (gate_weight, up_weight), [scale])
     rows, coeff = shrink_rows(parts, factor, scale, to_place, shrink_factors.shape[2])
 
     bits = [1 << b for b in range(size.bit_length() - 1)]
-    units = model_width // (DEPTH_BLOCK // 2)
-    cuts = [0] + [(units - units * k // 3) * (DEPTH_BLOCK // 2) for k in (2, 1, 0)]
     mixed = None
     for step, bit in enumerate(bits):
         received = lax.ppermute(coeff, AXIS, flip(size, bit))
-        part = step - (len(bits) - 3)
-        if part >= 0:
-            mixed = mixed_rows(
+        part = step - (len(bits) - LOADS - 1)
+        if part == LOADS:
+            cuts = depth_cuts(model_width)
+            mixed = stream_rows(
                 rows, (gate_weight, up_weight), mixed, cuts[part], cuts[part + 1], [coeff]
             )
+        elif part >= 0:
+            mixed = mixed_rows(rows, loads[part], part, mixed, [coeff])
         if bit < bits[-1]:
             coeff = add_coefficients(coeff, received, [] if mixed is None else [mixed])
     hidden = hidden_rows(mixed, coeff, received, expand_factors, from_place, hot)

time: 96.9 us -> 103 us (1.063)
  starting transfers between devices: 38.4 us -> 27.8 us
  local copies, waits for them, and re-layouts: 2.41 us -> 12.6 us
  waiting for transfers between devices: 26.1 us -> 30.5 us
  Pallas kernels: 22.9 us -> 26.2 us
    unnamed x18 -> x32, local copies, waits for them, and re-layouts: 2.21 us -> 12.4 us
    ppermute x15 -> x9, starting transfers between devices: 15.8 us -> 9.27 us  [the longest x3 6.35 us: gather_rows(): right = lax.ppermute(right, AXIS, ring(size, 1))]
    pallas_call x18 -> x23, Pallas kernels: 6.43 us -> 12.3 us  [call(): pl.pallas_call(run, out_shape=out_shape, in_specs=[whole(pltpu.SMEM if op...]
    pallas_call x3, Pallas kernels: 16.5 us -> 13.9 us  [the longest x2 8.64 us: load_rows(): pl.pallas_call(kernel, out_shape=[jax.ShapeDtypeStruct(shape, weights[0]....]
    ppermute x15 -> x9, waiting for transfers between devices: 10.9 us -> 13.3 us  [the longest x3 6.82 us: gather_rows(): right = lax.ppermute(right, AXIS, ring(size, 1))]
    ppermute x4, starting transfers between devices: 6.15 us -> 4.09 us  [body(): received = lax.ppermute(coeff, AXIS, flip(size, bit))]
    ppermute x14, starting transfers between devices: 15.7 us -> 13.7 us  [scatter_rows(): chain[h] = lax.ppermute(value, AXIS, ring(size, by))]
    ppermute x14, waiting for transfers between devices: 12.4 us -> 14.4 us  [scatter_rows(): chain[h] = lax.ppermute(value, AXIS, ring(size, by))]
  transfers between devices with their start and end apart: 37 -> 31, of which waited for: 22 -> 20; matrix products, arithmetic and copies ran while one was open for 4% -> 3% of each run, Pallas kernels for 19% -> 21%
where the time goes in v7:
time: 103 us
  waiting for transfers between devices  30.5 us (30%)
  starting transfers between devices  27.8 us (27%)
  Pallas kernels  26.2 us (25%)
  local copies, waits for them, and re-layouts  12.6 us (12%)
  matrix products  4.84 us (5%)
  between operations  1.05 us (1%)
    ppermute x14, waiting for transfers between devices, scatter_rows(): chain[h] = lax.ppermute(value, AXIS, ring(size, by))  14.4 us
    ppermute x14, starting transfers between devices, scatter_rows(): chain[h] = lax.ppermute(value, AXIS, ring(size, by))  13.7 us
    unnamed x32, local copies, waits for them, and re-layouts  12.4 us
    pallas_call x23, Pallas kernels, call(): pl.pallas_call(run, out_shape=out_shape, in_specs=[whole(pltpu.SMEM if op...  12.3 us
    pallas_call x2, Pallas kernels, load_rows(): pl.pallas_call(kernel, out_shape=[jax.ShapeDtypeStruct(shape, weights[0]....  8.64 us
    ppermute x3, waiting for transfers between devices, gather_rows(): right = lax.ppermute(right, AXIS, ring(size, 1))  6.82 us
    ppermute x3, starting transfers between devices, gather_rows(): right = lax.ppermute(right, AXIS, ring(size, 1))  6.35 us
    pallas_call x1, Pallas kernels, stream_rows(): pl.pallas_call(kernel, out_shape=jax.ShapeDtypeStruct((batch_rows, width)...  5.27 us
  transfers between devices with their start and end apart: 31, of which 20 were waited for; matrix products, arithmetic and copies ran while one was open for 3% of the time, Pallas kernels for 21%

profile of v7, /device:TPU:0, one launch (start us, length us, event | category | flops | bytes accessed | tf_op | source)
XLA Modules:
  0.0 103.0 jit_solution(1130253626783679855)
XLA Ops:
  0.6 3.1 %collective-permute-start = (bf16[16,8192]{1,0:T(8,128)(2,1)}, bf16[16,8192]{1,0:T(8,128)(2,1)S(1)}, u32[]{:S(2)}, u32[]{:S(2)}) collective-permute-start(bf16[16,8192]{1,0:T(8,128)(2,1)} %refs_8_.1), channel_id=1, source_target_pairs={{0,4},{1,5},{4,8},{5,9},{8,12},{9,13},{12,14},{13,15},{14,10},{15,... | collective-permute-start | bytes 786440 | tf_op jit(solution)/shard_map/ppermute | solution.py:138
  3.7 4.3 %load_rows.2.refs_1_ = bf16[3072,1792]{1,0:T(8,128)(2,1)S(1)} custom-call(bf16[8192,896]{1,0:T(8,128)(2,1)} %refs_0_.7, bf16[8192,896]{1,0:T(8,128)(2,1)} %refs_1_.5), custom_call_target="tpu_custom_call" | custom-call | bytes 22020096 | tf_op jit(solution)/shard_map/load_rows/pallas_call | solution.py:295
  8.0 2.1 %collective-permute-done.refs_0_ = bf16[16,8192]{1,0:T(8,128)(2,1)S(1)} collective-permute-done((bf16[16,8192]{1,0:T(8,128)(2,1)}, bf16[16,8192]{1,0:T(8,128)(2,1)S(1)}, u32[]{:S(2)}, u32[]{:S(2)}) %collective-permute-start) | collective-permute-done | bytes 262176 | tf_op jit(solution)/shard_map/ppermute | solution.py:138
  10.2 4.1 %copy-done = bf16[3072,1792]{1,0:T(8,128)(2,1)} copy-done((bf16[3072,1792]{1,0:T(8,128)(2,1)}, bf16[3072,1792]{1,0:T(8,128)(2,1)S(1)}, u32[]{:S(2)}) %copy-start) | copy-done | bytes 11010072
  14.3 1.8 %collective-permute-start.2 = (bf16[16,8192]{1,0:T(8,128)(2,1)S(1)}, bf16[16,8192]{1,0:T(8,128)(2,1)S(1)}, u32[]{:S(2)}, u32[]{:S(2)}) collective-permute-start(bf16[16,8192]{1,0:T(8,128)(2,1)S(1)} %pass_on.2.refs_2_), channel_id=1, source_target_pairs={{0,4},{1,5},{4,8},{5,9},{8,12},{9,13},{12,14},{13,15},{14,10},{15,... | collective-permute-start | bytes 786440 | tf_op jit(solution)/shard_map/ppermute | solution.py:138
  16.4 4.3 %load_rows.3.refs_1_ = bf16[3072,1792]{1,0:T(8,128)(2,1)S(1)} custom-call(bf16[8192,896]{1,0:T(8,128)(2,1)} %refs_0_.7, bf16[8192,896]{1,0:T(8,128)(2,1)} %refs_1_.5, bf16[16,8192]{1,0:T(8,128)(2,1)S(1)} %pass_on.2.refs_2_), custom_call_target="tpu_custom_call" | custom-call | bytes 22020096 | tf_op jit(solution)/shard_map/load_rows/pallas_call | solution.py:295
  20.8 1.1 %collective-permute-done.2.refs_0_.refs_2_ = bf16[16,8192]{1,0:T(8,128)(2,1)S(1)} collective-permute-done((bf16[16,8192]{1,0:T(8,128)(2,1)S(1)}, bf16[16,8192]{1,0:T(8,128)(2,1)S(1)}, u32[]{:S(2)}, u32[]{:S(2)}) %collective-permute-start.2) | collective-permute-done | bytes 262176 | tf_op jit(solution)/shard_map/ppermute | solution.py:138
  21.9 4.0 %copy-done.2 = bf16[3072,1792]{1,0:T(8,128)(2,1)} copy-done((bf16[3072,1792]{1,0:T(8,128)(2,1)}, bf16[3072,1792]{1,0:T(8,128)(2,1)S(1)}, u32[]{:S(2)}) %copy-start.2) | copy-done | bytes 11010072
  25.9 1.5 %collective-permute-start.4 = (bf16[16,8192]{1,0:T(8,128)(2,1)S(1)}, bf16[16,8192]{1,0:T(8,128)(2,1)S(1)}, u32[]{:S(2)}, u32[]{:S(2)}) collective-permute-start(bf16[16,8192]{1,0:T(8,128)(2,1)S(1)} %pass_on.3), channel_id=1, source_target_pairs={{0,4},{1,5},{4,8},{5,9},{8,12},{9,13},{12,14},{13,15},{14,10},{15,... | collective-permute-start | bytes 786440 | tf_op jit(solution)/shard_map/ppermute | solution.py:138
  28.0 0.8 row_masks.1
  28.8 3.6 %collective-permute-done.4.refs_4_.refs_0_ = bf16[16,8192]{1,0:T(8,128)(2,1)S(1)} collective-permute-done((bf16[16,8192]{1,0:T(8,128)(2,1)S(1)}, bf16[16,8192]{1,0:T(8,128)(2,1)S(1)}, u32[]{:S(2)}, u32[]{:S(2)}) %collective-permute-start.4) | collective-permute-done | bytes 262176 | tf_op jit(solution)/shard_map/ppermute | solution.py:138
  32.5 1.3 %collective-permute-done.5.refs_5_.refs_0_ = bf16[16,8192]{1,0:T(8,128)(2,1)S(1)} collective-permute-done((bf16[16,8192]{1,0:T(8,128)(2,1)S(1)}, bf16[16,8192]{1,0:T(8,128)(2,1)S(1)}, u32[]{:S(2)}, u32[]{:S(2)}) %collective-permute-start.5) | collective-permute-done | bytes 262176 | tf_op jit(solution)/shard_map/ppermute | solution.py:139
  34.0 1.6 %collective-permute-start.6 = (bf16[16,4096]{1,0:T(8,128)(2,1)S(1)}, bf16[16,4096]{1,0:T(8,128)(2,1)S(1)}, u32[]{:S(2)}, u32[]{:S(2)}) collective-permute-start(bf16[16,4096]{1,0:T(8,128)(2,1)S(1)} %column_half.2), channel_id=1, source_target_pairs={{0,4},{1,5},{4,8},{5,9},{8,12},{9,13},{12,14},{13,15},{14,10},{15,... | collective-permute-start | bytes 393224 | tf_op jit(solution)/shard_map/ppermute | solution.py:151
  36.1 3.8 %collective-permute-done.6.refs_0_ = bf16[16,4096]{1,0:T(8,128)(2,1)S(1)} collective-permute-done((bf16[16,4096]{1,0:T(8,128)(2,1)S(1)}, bf16[16,4096]{1,0:T(8,128)(2,1)S(1)}, u32[]{:S(2)}, u32[]{:S(2)}) %collective-permute-start.6) | collective-permute-done | bytes 131104 | tf_op jit(solution)/shard_map/ppermute | solution.py:151
  39.9 1.4 %collective-permute-done.7.refs_1_ = bf16[16,4096]{1,0:T(8,128)(2,1)S(1)} collective-permute-done((bf16[16,4096]{1,0:T(8,128)(2,1)S(1)}, bf16[16,4096]{1,0:T(8,128)(2,1)S(1)}, u32[]{:S(2)}, u32[]{:S(2)}) %collective-permute-start.7) | collective-permute-done | bytes 131104 | tf_op jit(solution)/shard_map/ppermute | solution.py:152
  41.4 1.5 %collective-permute-done.10.refs_5_ = bf16[16,8192]{1,0:T(8,128)(2,1)S(1)} collective-permute-done((bf16[16,8192]{1,0:T(8,128)(2,1)S(1)}, bf16[16,8192]{1,0:T(8,128)(2,1)S(1)}, u32[]{:S(2)}, u32[]{:S(2)}) %collective-permute-start.10) | collective-permute-done | bytes 262176 | tf_op jit(solution)/shard_map/ppermute | solution.py:157
  42.9 2.6 %shrink_rows.1 = (bf16[256,8192]{1,0:T(8,128)(2,1)S(1)}, bf16[256,64]{1,0:T(8,128)(2,1)S(1)}) custom-call(bf16[16,8192]{1,0:T(8,128)(2,1)S(1)} %copy-done.5, bf16[96,8192]{1,0:T(8,128)(2,1)S(1)} %join_pieces.2.refs_1_, bf16[16,8192]{1,0:T(8,128)(2,1)S(1)} %join_pieces.3.refs_2_, bf16[16,8192]{1,0:T(8,128)(2,1)S(1)} %collective-permute-done.8.refs_3_, ...), custom_call_target="tpu_custom_call" | custom-call | flops 268435456 | bytes 8388608 | tf_op jit(solution)/shard_map/shrink_rows/pallas_call | solution.py:78
  45.7 1.1 %collective-permute-done.11.refs_1_ = bf16[256,64]{1,0:T(8,128)(2,1)S(1)} collective-permute-done((bf16[256,64]{1,0:T(8,128)(2,1)S(1)}, bf16[256,64]{1,0:T(8,128)(2,1)S(1)}, u32[]{:S(2)}, u32[]{:S(2)}) %collective-permute-start.11) | collective-permute-done | bytes 32800 | tf_op jit(solution)/shard_map/ppermute | solution.py:560
  47.4 4.1 %copy-done.1 = bf16[3072,1792]{1,0:T(8,128)(2,1)S(1)} copy-done((bf16[3072,1792]{1,0:T(8,128)(2,1)S(1)}, bf16[3072,1792]{1,0:T(8,128)(2,1)}, u32[]{:S(2)}) %copy-start.1) | copy-done | bytes 11010072
  51.5 3.0 %mixed_rows.2.refs_2_ = f32[256,1792]{1,0:T(8,128)S(1)} custom-call(bf16[256,8192]{1,0:T(8,128)(2,1)S(1)} %get-tuple-element.25.refs_0_.rows_ref, bf16[3072,1792]{1,0:T(8,128)(2,1)S(1)} %copy-done.1, bf16[256,64]{1,0:T(8,128)(2,1)S(1)} %add_coefficients.3.refs_2_.refs_0_), custom_call_target="tpu_custom_call" | custom-call | flops 2818572288 | bytes 11010048 | tf_op jit(solution)/shard_map/mixed_rows/pallas_call | solution.py:78
  54.5 1.2 %collective-permute-start.13 = (bf16[256,64]{1,0:T(8,128)(2,1)S(1)}, bf16[256,64]{1,0:T(8,128)(2,1)S(1)}, u32[]{:S(2)}, u32[]{:S(2)}) collective-permute-start(bf16[256,64]{1,0:T(8,128)(2,1)S(1)} %add_coefficients.4.refs_3_.refs_0_), channel_id=1, source_target_pairs={{0,4},{1,5},{2,6},{3,7},{4,0},{5,1},{6,2},{7,3},{8,12},{9,13},{10,... | collective-permute-start | bytes 98312 | tf_op jit(solution)/shard_map/ppermute | solution.py:560
  55.8 3.0 %mixed_rows.3.refs_2_ = f32[256,1792]{1,0:T(8,128)S(1)} custom-call(bf16[256,8192]{1,0:T(8,128)(2,1)S(1)} %get-tuple-element.25.refs_0_.rows_ref, bf16[3072,1792]{1,0:T(8,128)(2,1)S(1)} %copy-done.3, f32[256,1792]{1,0:T(8,128)S(1)} %mixed_rows.2.refs_2_, bf16[256,64]{1,0:T(8,128)(2,1)S(1)} %add_coefficients.4.refs_3_.refs_0_), custom_call_target="tpu_custom_call" | custom-call | flops 2818572288 | bytes 11010048 | tf_op jit(solution)/shard_map/mixed_rows/pallas_call | solution.py:78
  59.0 2.2 %collective-permute-start.14 = (bf16[256,64]{1,0:T(8,128)(2,1)S(1)}, bf16[256,64]{1,0:T(8,128)(2,1)S(1)}, u32[]{:S(2)}, u32[]{:S(2)}) collective-permute-start(bf16[256,64]{1,0:T(8,128)(2,1)S(1)} %add_coefficients.5.refs_3_.refs_0_), channel_id=1, source_target_pairs={{0,8},{1,9},{2,10},{3,11},{4,12},{5,13},{6,14},{7,15},{8,0},{9,1},... | collective-permute-start | bytes 98312 | tf_op jit(solution)/shard_map/ppermute | solution.py:560
  61.1 5.3 %stream_rows.1.refs_5_ = f32[256,1792]{1,0:T(8,128)S(1)} custom-call(bf16[256,8192]{1,0:T(8,128)(2,1)S(1)} %get-tuple-element.25.refs_0_.rows_ref, bf16[8192,896]{1,0:T(8,128)(2,1)} %refs_0_.7, bf16[8192,896]{1,0:T(8,128)(2,1)} %refs_1_.5, f32[256,1792]{1,0:T(8,128)S(1)} %mixed_rows.3.refs_2_, bf16[256,64]{1,0:T(8,128)(2,1)S(1)} %add_coefficients.5.refs_3_.refs_0_), custom_call_target="tpu_custom_call" | custom-call | flops 1879048192 | bytes 14680064 | tf_op jit(solution)/shard_map/stream_rows/pallas_call | solution.py:398
  66.4 1.0 hidden_rows.1
  67.4 2.4 %fusion.4.refs_0_.refs_2_.refs_3_ = bf16[256,4096]{1,0:T(8,128)(2,1)S(1)} fusion(bf16[256,896]{1,0:T(8,128)(2,1)S(1)} %hidden_rows.1, bf16[896,8192]{1,0:T(8,128)(2,1)S(1)} %bitcast.12), kind=kOutput, calls=%fused_computation.4 | convolution fusion | flops 1880096768 | bytes 9895936 | tf_op jit(solution)/shard_map/dot_general | solution.py:577
  70.0 2.4 %fusion.7.refs_0_.refs_2_.refs_3_.refs_4_ = bf16[256,4096]{1,0:T(8,128)(2,1)S(1)} fusion(bf16[256,896]{1,0:T(8,128)(2,1)S(1)} %hidden_rows.1, bf16[896,8192]{1,0:T(8,128)(2,1)S(1)} %bitcast.12), kind=kOutput, calls=%fused_computation.5 | convolution fusion | flops 1880096768 | bytes 9895936 | tf_op jit(solution)/shard_map/dot_general | solution.py:577
  72.5 0.6 collective-permute-start.18
  73.2 0.9 collective-permute-start.16
  74.1 1.2 %collective-permute-start.17 = (bf16[16,4096]{1,0:T(8,128)(2,1)S(1)}, bf16[16,4096]{1,0:T(8,128)(2,1)S(1)}, u32[]{:S(2)}, u32[]{:S(2)}) collective-permute-start(bf16[16,4096]{1,0:T(8,128)(2,1)S(1)} %get-tuple-element.29), channel_id=1, source_target_pairs={{0,2},{1,3},{4,0},{5,1},{8,4},{9,5},{12,8},{13,9},{14,12},{15,13},... | collective-permute-start | bytes 393224 | tf_op jit(solution)/shard_map/ppermute | solution.py:496
  75.5 2.1 %collective-permute-start.21 = (bf16[16,4096]{1,0:T(8,128)(2,1)S(1)}, bf16[16,4096]{1,0:T(8,128)(2,1)S(1)}, u32[]{:S(2)}, u32[]{:S(2)}) collective-permute-start(bf16[16,4096]{1,0:T(8,128)(2,1)S(1)} %get-tuple-element.30.refs_6_), channel_id=1, source_target_pairs={{0,2},{1,3},{4,0},{5,1},{8,4},{9,5},{12,8},{13,9},{14,12},{15,13},... | collective-permute-start | bytes 393224 | tf_op jit(solution)/shard_map/ppermute | solution.py:496
  77.6 1.4 %collective-permute-done.16.refs_2_ = bf16[16,4096]{1,0:T(8,128)(2,1)S(1)} collective-permute-done((bf16[16,4096]{1,0:T(8,128)(2,1)S(1)}, bf16[16,4096]{1,0:T(8,128)(2,1)S(1)}, u32[]{:S(2)}, u32[]{:S(2)}) %collective-permute-start.16) | collective-permute-done | bytes 131104 | tf_op jit(solution)/shard_map/ppermute | solution.py:496
  78.9 1.1 %collective-permute-done.17.refs_5_ = bf16[16,4096]{1,0:T(8,128)(2,1)S(1)} collective-permute-done((bf16[16,4096]{1,0:T(8,128)(2,1)S(1)}, bf16[16,4096]{1,0:T(8,128)(2,1)S(1)}, u32[]{:S(2)}, u32[]{:S(2)}) %collective-permute-start.17) | collective-permute-done | bytes 131104 | tf_op jit(solution)/shard_map/ppermute | solution.py:496
  80.2 1.5 %collective-permute-start.19 = (bf16[16,4096]{1,0:T(8,128)(2,1)S(1)}, bf16[16,4096]{1,0:T(8,128)(2,1)S(1)}, u32[]{:S(2)}, u32[]{:S(2)}) collective-permute-start(bf16[16,4096]{1,0:T(8,128)(2,1)S(1)} %get-tuple-element.31.refs_6_), channel_id=1, source_target_pairs={{0,4},{1,5},{4,8},{5,9},{8,12},{9,13},{12,14},{13,15},{14,10},{15,... | collective-permute-start | bytes 393224 | tf_op jit(solution)/shard_map/ppermute | solution.py:496
  81.7 0.6 collective-permute-start.20
  82.3 1.6 %collective-permute-done.22.refs_5_ = bf16[16,4096]{1,0:T(8,128)(2,1)S(1)} collective-permute-done((bf16[16,4096]{1,0:T(8,128)(2,1)S(1)}, bf16[16,4096]{1,0:T(8,128)(2,1)S(1)}, u32[]{:S(2)}, u32[]{:S(2)}) %collective-permute-start.22) | collective-permute-done | bytes 131104 | tf_op jit(solution)/shard_map/ppermute | solution.py:496
  84.0 0.8 collective-permute-start.24
  84.9 1.2 %collective-permute-start.25 = (bf16[16,4096]{1,0:T(8,128)(2,1)S(1)}, bf16[16,4096]{1,0:T(8,128)(2,1)S(1)}, u32[]{:S(2)}, u32[]{:S(2)}) collective-permute-start(bf16[16,4096]{1,0:T(8,128)(2,1)S(1)} %get-tuple-element.36), channel_id=1, source_target_pairs={{0,4},{1,5},{4,8},{5,9},{8,12},{9,13},{12,14},{13,15},{14,10},{15,... | collective-permute-start | bytes 393224 | tf_op jit(solution)/shard_map/ppermute | solution.py:496
  86.1 1.7 %collective-permute-done.20.refs_5_ = bf16[16,4096]{1,0:T(8,128)(2,1)S(1)} collective-permute-done((bf16[16,4096]{1,0:T(8,128)(2,1)S(1)}, bf16[16,4096]{1,0:T(8,128)(2,1)S(1)}, u32[]{:S(2)}, u32[]{:S(2)}) %collective-permute-start.20) | collective-permute-done | bytes 131104 | tf_op jit(solution)/shard_map/ppermute | solution.py:496
  88.0 0.7 collective-permute-start.23
  88.6 0.6 collective-permute-done.24.refs_2_
  89.2 1.4 %collective-permute-done.25.refs_5_ = bf16[16,4096]{1,0:T(8,128)(2,1)S(1)} collective-permute-done((bf16[16,4096]{1,0:T(8,128)(2,1)S(1)}, bf16[16,4096]{1,0:T(8,128)(2,1)S(1)}, u32[]{:S(2)}, u32[]{:S(2)}) %collective-permute-start.25) | collective-permute-done | bytes 131104 | tf_op jit(solution)/shard_map/ppermute | solution.py:496
  91.3 1.6 %collective-permute-start.28 = (bf16[16,4096]{1,0:T(8,128)(2,1)S(1)}, bf16[16,4096]{1,0:T(8,128)(2,1)S(1)}, u32[]{:S(2)}, u32[]{:S(2)}) collective-permute-start(bf16[16,4096]{1,0:T(8,128)(2,1)S(1)} %get-tuple-element.39), channel_id=1, source_target_pairs={{0,4},{1,5},{4,8},{5,9},{8,12},{9,13},{12,14},{13,15},{14,10},{15,... | collective-permute-start | bytes 393224 | tf_op jit(solution)/shard_map/ppermute | solution.py:496
  93.3 0.9 collective-permute-done.23.refs_2_
  94.2 2.6 %collective-permute-done.29.refs_2_ = bf16[16,4096]{1,0:T(8,128)(2,1)S(1)} collective-permute-done((bf16[16,4096]{1,0:T(8,128)(2,1)S(1)}, bf16[16,4096]{1,0:T(8,128)(2,1)S(1)}, u32[]{:S(2)}, u32[]{:S(2)}) %collective-permute-start.29) | collective-permute-done | bytes 131104 | tf_op jit(solution)/shard_map/ppermute | solution.py:496
  97.0 2.0 %collective-permute-start.26 = (bf16[16,4096]{1,0:T(8,128)(2,1)S(1)}, bf16[16,4096]{1,0:T(8,128)(2,1)S(1)}, u32[]{:S(2)}, u32[]{:S(2)}) collective-permute-start(bf16[16,4096]{1,0:T(8,128)(2,1)S(1)} %add_blocks.14.refs_3_), channel_id=1, source_target_pairs={{0,4},{1,5},{4,8},{5,9},{8,12},{9,13},{12,14},{13,15},{14,10},{15,... | collective-permute-start | bytes 393224 | tf_op jit(solution)/shard_map/ppermute | solution.py:496
  99.0 2.9 %collective-permute-done.30.refs_7_ = bf16[16,4096]{1,0:T(8,128)(2,1)S(1)} collective-permute-done((bf16[16,4096]{1,0:T(8,128)(2,1)S(1)}, bf16[16,4096]{1,0:T(8,128)(2,1)S(1)}, u32[]{:S(2)}, u32[]{:S(2)}) %collective-permute-start.30) | collective-permute-done | bytes 131104 | tf_op jit(solution)/shard_map/ppermute | solution.py:496
  102.0 1.0 %finish_rows.1 = (bf16[16,8192]{1,0:T(8,128)(2,1)}, bf16[16,8192]{1,0:T(8,128)(2,1)}) custom-call(bf16[256,4096]{1,0:T(8,128)(2,1)S(1)} %fusion.4.refs_0_.refs_2_.refs_3_, bf16[128,4096]{1,0:T(8,128)(2,1)S(1)} %collective-permute-done.15.refs_1_.refs_3_.refs_4_, bf16[16,4096]{1,0:T(8,128)(2,1)S(1)} %collective-permute-done.26.refs_2_, ...), custom_call_target="tpu_custom_call" | custom-call | tf_op jit(solution)/shard_map/finish_rows/pallas_call | solution.py:78
  (79 shorter events, 4.8 us)
Async XLA Ops:
  0.6 9.5 %collective-permute-start = (bf16[16,8192]{1,0:T(8,128)(2,1)}, bf16[16,8192]{1,0:T(8,128)(2,1)S(1)}, u32[]{:S(2)}, u32[]{:S(2)}) collective-permute-start(bf16[16,8192]{1,0:T(8,128)(2,1)} %refs_8_.1), channel_id=1, source_target_pairs={{0,4},{1,5},{4,8},{5,9},{8,12},{9,13},{12,14},{13,15},{14,10},{15,... | collective-permute-start | bytes 786440 | tf_op jit(solution)/shard_map/ppermute | solution.py:138
  3.7 12.4 %collective-permute-start.1 = (bf16[16,8192]{1,0:T(8,128)(2,1)}, bf16[16,8192]{1,0:T(8,128)(2,1)S(1)}, u32[]{:S(2)}, u32[]{:S(2)}) collective-permute-start(bf16[16,8192]{1,0:T(8,128)(2,1)} %refs_8_.1), channel_id=1, source_target_pairs={{0,2},{1,3},{4,0},{5,1},{8,4},{9,5},{12,8},{13,9},{14,12},{15,13},... | collective-permute-start | bytes 786440 | tf_op jit(solution)/shard_map/ppermute | solution.py:139
  10.2 4.2 %copy-start = (bf16[3072,1792]{1,0:T(8,128)(2,1)}, bf16[3072,1792]{1,0:T(8,128)(2,1)S(1)}, u32[]{:S(2)}) copy-start(bf16[3072,1792]{1,0:T(8,128)(2,1)S(1)} %load_rows.2.refs_1_) | copy-start | bytes 33030148
  14.3 7.5 %collective-permute-start.2 = (bf16[16,8192]{1,0:T(8,128)(2,1)S(1)}, bf16[16,8192]{1,0:T(8,128)(2,1)S(1)}, u32[]{:S(2)}, u32[]{:S(2)}) collective-permute-start(bf16[16,8192]{1,0:T(8,128)(2,1)S(1)} %pass_on.2.refs_2_), channel_id=1, source_target_pairs={{0,4},{1,5},{4,8},{5,9},{8,12},{9,13},{12,14},{13,15},{14,10},{15,... | collective-permute-start | bytes 786440 | tf_op jit(solution)/shard_map/ppermute | solution.py:138
  16.1 11.2 %collective-permute-start.3 = (bf16[16,8192]{1,0:T(8,128)(2,1)S(1)}, bf16[16,8192]{1,0:T(8,128)(2,1)S(1)}, u32[]{:S(2)}, u32[]{:S(2)}) collective-permute-start(bf16[16,8192]{1,0:T(8,128)(2,1)S(1)} %collective-permute-done.1.refs_1_), channel_id=1, source_target_pairs={{0,2},{1,3},{4,0},{5,1},{8,4},{9,5},{12,8},{13,9},{14,12},{15,13},... | collective-permute-start | bytes 786440 | tf_op jit(solution)/shard_map/ppermute | solution.py:139
  20.7 7.2 %copy-start.8 = (s32[16]{0:T(128)S(1)}, s32[16]{0:T(128)}, u32[]{:S(2)}) copy-start(s32[16]{0:T(128)} %param.19) | copy-start | bytes 196
  20.7 7.2 %copy-start.9 = (s32[16]{0:T(128)S(1)}, s32[16]{0:T(128)}, u32[]{:S(2)}) copy-start(s32[16]{0:T(128)} %param.18) | copy-start | bytes 196
  20.7 7.2 %copy-start.10 = (s32[32]{0:T(128)S(1)}, s32[32]{0:T(128)}, u32[]{:S(2)}) copy-start(s32[32]{0:T(128)} %param.21) | copy-start | bytes 388
  20.7 7.2 %copy-start.11 = (s32[32]{0:T(128)S(1)}, s32[32]{0:T(128)}, u32[]{:S(2)}) copy-start(s32[32]{0:T(128)} %param.20) | copy-start | bytes 388
  20.8 7.3 %copy-start.6 = (bf16[1,8192,64]{1,2,0:T(8,128)(2,1)S(1)}, bf16[1,8192,64]{1,2,0:T(8,128)(2,1)}, u32[]{:S(2)}) copy-start(bf16[1,8192,64]{1,2,0:T(8,128)(2,1)} %param.16) | copy-start | bytes 3145732
  20.8 15.4 %copy-start.5 = (bf16[16,8192]{1,0:T(8,128)(2,1)S(1)}, bf16[16,8192]{1,0:T(8,128)(2,1)}, u32[]{:S(2)}) copy-start(bf16[16,8192]{1,0:T(8,128)(2,1)} %refs_8_.1) | copy-start | bytes 786436
  21.9 4.1 %copy-start.2 = (bf16[3072,1792]{1,0:T(8,128)(2,1)}, bf16[3072,1792]{1,0:T(8,128)(2,1)S(1)}, u32[]{:S(2)}) copy-start(bf16[3072,1792]{1,0:T(8,128)(2,1)S(1)} %load_rows.3.refs_1_) | copy-start | bytes 33030148
  25.9 6.6 %collective-permute-start.4 = (bf16[16,8192]{1,0:T(8,128)(2,1)S(1)}, bf16[16,8192]{1,0:T(8,128)(2,1)S(1)}, u32[]{:S(2)}, u32[]{:S(2)}) collective-permute-start(bf16[16,8192]{1,0:T(8,128)(2,1)S(1)} %pass_on.3), channel_id=1, source_target_pairs={{0,4},{1,5},{4,8},{5,9},{8,12},{9,13},{12,14},{13,15},{14,10},{15,... | collective-permute-start | bytes 786440 | tf_op jit(solution)/shard_map/ppermute | solution.py:138
  27.4 6.4 %collective-permute-start.5 = (bf16[16,8192]{1,0:T(8,128)(2,1)S(1)}, bf16[16,8192]{1,0:T(8,128)(2,1)S(1)}, u32[]{:S(2)}, u32[]{:S(2)}) collective-permute-start(bf16[16,8192]{1,0:T(8,128)(2,1)S(1)} %collective-permute-done.3.refs_3_), channel_id=1, source_target_pairs={{0,2},{1,3},{4,0},{5,1},{8,4},{9,5},{12,8},{13,9},{14,12},{15,13},... | collective-permute-start | bytes 786440 | tf_op jit(solution)/shard_map/ppermute | solution.py:139
  33.9 9.0 %collective-permute-start.9 = (bf16[96,8192]{1,0:T(8,128)(2,1)S(1)}, bf16[96,8192]{1,0:T(8,128)(2,1)S(1)}, u32[]{:S(2)}, u32[]{:S(2)}) collective-permute-start(bf16[96,8192]{1,0:T(8,128)(2,1)S(1)} %join_pieces.2.refs_1_), channel_id=1, source_target_pairs={{0,1},{1,0},{2,3},{3,2},{4,5},{5,4},{6,7},{7,6},{8,9},{9,8},{10,11... | collective-permute-start | bytes 4718600 | tf_op jit(solution)/shard_map/ppermute | solution.py:148
  34.0 5.9 %collective-permute-start.6 = (bf16[16,4096]{1,0:T(8,128)(2,1)S(1)}, bf16[16,4096]{1,0:T(8,128)(2,1)S(1)}, u32[]{:S(2)}, u32[]{:S(2)}) collective-permute-start(bf16[16,4096]{1,0:T(8,128)(2,1)S(1)} %column_half.2), channel_id=1, source_target_pairs={{0,4},{1,5},{4,8},{5,9},{8,12},{9,13},{12,14},{13,15},{14,10},{15,... | collective-permute-start | bytes 393224 | tf_op jit(solution)/shard_map/ppermute | solution.py:151
  35.6 5.7 %collective-permute-start.7 = (bf16[16,4096]{1,0:T(8,128)(2,1)S(1)}, bf16[16,4096]{1,0:T(8,128)(2,1)S(1)}, u32[]{:S(2)}, u32[]{:S(2)}) collective-permute-start(bf16[16,4096]{1,0:T(8,128)(2,1)S(1)} %column_half.3), channel_id=1, source_target_pairs={{0,2},{1,3},{4,0},{5,1},{8,4},{9,5},{12,8},{13,9},{14,12},{15,13},... | collective-permute-start | bytes 393224 | tf_op jit(solution)/shard_map/ppermute | solution.py:152
  36.1 5.3 %collective-permute-start.8 = (bf16[16,8192]{1,0:T(8,128)(2,1)S(1)}, bf16[16,8192]{1,0:T(8,128)(2,1)S(1)}, u32[]{:S(2)}, u32[]{:S(2)}) collective-permute-start(bf16[16,8192]{1,0:T(8,128)(2,1)S(1)} %copy-done.5), channel_id=1, source_target_pairs={{0,1},{1,0},{2,3},{3,2},{4,5},{5,4},{6,7},{7,6},{8,9},{9,8},{10,11... | collective-permute-start | bytes 786440 | tf_op jit(solution)/shard_map/ppermute | solution.py:141
  41.3 1.6 %collective-permute-start.10 = (bf16[16,8192]{1,0:T(8,128)(2,1)S(1)}, bf16[16,8192]{1,0:T(8,128)(2,1)S(1)}, u32[]{:S(2)}, u32[]{:S(2)}) collective-permute-start(bf16[16,8192]{1,0:T(8,128)(2,1)S(1)} %join_pieces.3.refs_2_), channel_id=1, source_target_pairs={{0,1},{1,0},{2,3},{3,2},{4,5},{5,4},{6,7},{7,6},{8,9},{9,8},{10,11... | collective-permute-start | bytes 786440 | tf_op jit(solution)/shard_map/ppermute | solution.py:157
  45.5 1.3 %collective-permute-start.11 = (bf16[256,64]{1,0:T(8,128)(2,1)S(1)}, bf16[256,64]{1,0:T(8,128)(2,1)S(1)}, u32[]{:S(2)}, u32[]{:S(2)}) collective-permute-start(bf16[256,64]{1,0:T(8,128)(2,1)S(1)} %get-tuple-element.24.refs_0_), channel_id=1, source_target_pairs={{0,1},{1,0},{2,3},{3,2},{4,5},{5,4},{6,7},{7,6},{8,9},{9,8},{10,11... | collective-permute-start | bytes 98312 | tf_op jit(solution)/shard_map/ppermute | solution.py:560
  46.9 7.7 %collective-permute-start.12 = (bf16[256,64]{1,0:T(8,128)(2,1)S(1)}, bf16[256,64]{1,0:T(8,128)(2,1)S(1)}, u32[]{:S(2)}, u32[]{:S(2)}) collective-permute-start(bf16[256,64]{1,0:T(8,128)(2,1)S(1)} %add_coefficients.3.refs_2_.refs_0_), channel_id=1, source_target_pairs={{0,2},{1,3},{2,0},{3,1},{4,6},{5,7},{6,4},{7,5},{8,10},{9,11},{10,... | collective-permute-start | bytes 98312 | tf_op jit(solution)/shard_map/ppermute | solution.py:560
  47.4 4.1 %copy-start.1 = (bf16[3072,1792]{1,0:T(8,128)(2,1)S(1)}, bf16[3072,1792]{1,0:T(8,128)(2,1)}, u32[]{:S(2)}) copy-start(bf16[3072,1792]{1,0:T(8,128)(2,1)} %copy-done) | copy-start | bytes 33030148
  51.5 4.3 %copy-start.3 = (bf16[3072,1792]{1,0:T(8,128)(2,1)S(1)}, bf16[3072,1792]{1,0:T(8,128)(2,1)}, u32[]{:S(2)}) copy-start(bf16[3072,1792]{1,0:T(8,128)(2,1)} %copy-done.2) | copy-start | bytes 33030148
  54.5 4.3 %collective-permute-start.13 = (bf16[256,64]{1,0:T(8,128)(2,1)S(1)}, bf16[256,64]{1,0:T(8,128)(2,1)S(1)}, u32[]{:S(2)}, u32[]{:S(2)}) collective-permute-start(bf16[256,64]{1,0:T(8,128)(2,1)S(1)} %add_coefficients.4.refs_3_.refs_0_), channel_id=1, source_target_pairs={{0,4},{1,5},{2,6},{3,7},{4,0},{5,1},{6,2},{7,3},{8,12},{9,13},{10,... | collective-permute-start | bytes 98312 | tf_op jit(solution)/shard_map/ppermute | solution.py:560
  58.9 8.5 %slice-start = ((s8[14680064]{0:T(1024)(128)(4,1)}), s8[4194304]{0:T(1024)(128)(4,1)S(1)}, s32[]{:S(2)}) async-start(s8[14680064]{0:T(1024)(128)(4,1)} %bitcast.11), calls=%async_computation | async-start | bytes 8388608
  58.9 7.5 %copy-start.4 = (bf16[16,64,896]{2,1,0:T(8,128)(2,1)S(1)}, bf16[16,64,896]{2,1,0:T(8,128)(2,1)}, u32[]{:S(2)}) copy-start(bf16[16,64,896]{2,1,0:T(8,128)(2,1)} %param.17) | copy-start | bytes 5505028
  58.9 8.5 %slice-start.1 = ((s8[14680064]{0:T(1024)(128)(4,1)}), s8[4194304]{0:T(1024)(128)(4,1)S(1)}, s32[]{:S(2)}) async-start(s8[14680064]{0:T(1024)(128)(4,1)} %bitcast.11), calls=%async_computation.1 | async-start | bytes 8388608
  58.9 8.5 %slice-start.2 = ((s8[14680064]{0:T(1024)(128)(4,1)}), s8[4194304]{0:T(1024)(128)(4,1)S(1)}, s32[]{:S(2)}) async-start(s8[14680064]{0:T(1024)(128)(4,1)} %bitcast.11), calls=%async_computation.2 | async-start | bytes 8388608
  58.9 8.5 %slice-start.3 = ((s8[14680064]{0:T(1024)(128)(4,1)}), s8[2097152]{0:T(1024)(128)(4,1)S(1)}, s32[]{:S(2)}) async-start(s8[14680064]{0:T(1024)(128)(4,1)} %bitcast.11), calls=%async_computation.3 | async-start | bytes 4194304
  59.0 7.4 %collective-permute-start.14 = (bf16[256,64]{1,0:T(8,128)(2,1)S(1)}, bf16[256,64]{1,0:T(8,128)(2,1)S(1)}, u32[]{:S(2)}, u32[]{:S(2)}) collective-permute-start(bf16[256,64]{1,0:T(8,128)(2,1)S(1)} %add_coefficients.5.refs_3_.refs_0_), channel_id=1, source_target_pairs={{0,8},{1,9},{2,10},{3,11},{4,12},{5,13},{6,14},{7,15},{8,0},{9,1},... | collective-permute-start | bytes 98312 | tf_op jit(solution)/shard_map/ppermute | solution.py:560
  70.0 3.1 %collective-permute-start.15 = (bf16[128,4096]{1,0:T(8,128)(2,1)S(1)}, bf16[128,4096]{1,0:T(8,128)(2,1)S(1)}, u32[]{:S(2)}, u32[]{:S(2)}) collective-permute-start(bf16[128,4096]{1,0:T(8,128)(2,1)S(1)} %slice.16), channel_id=1, source_target_pairs={{0,1},{1,0},{2,3},{3,2},{4,5},{5,4},{6,7},{7,6},{8,9},{9,8},{10,11... | collective-permute-start | bytes 3145736 | tf_op jit(solution)/shard_map/ppermute | solution.py:583
  72.5 2.8 %collective-permute-start.18 = (bf16[128,4096]{1,0:T(8,128)(2,1)S(1)}, bf16[128,4096]{1,0:T(8,128)(2,1)S(1)}, u32[]{:S(2)}, u32[]{:S(2)}) collective-permute-start(bf16[128,4096]{1,0:T(8,128)(2,1)S(1)} %slice.17), channel_id=1, source_target_pairs={{0,1},{1,0},{2,3},{3,2},{4,5},{5,4},{6,7},{7,6},{8,9},{9,8},{10,11... | collective-permute-start | bytes 3145736 | tf_op jit(solution)/shard_map/ppermute | solution.py:583
  73.2 5.8 %collective-permute-start.16 = (bf16[16,4096]{1,0:T(8,128)(2,1)S(1)}, bf16[16,4096]{1,0:T(8,128)(2,1)S(1)}, u32[]{:S(2)}, u32[]{:S(2)}) collective-permute-start(bf16[16,4096]{1,0:T(8,128)(2,1)S(1)} %get-tuple-element.28.refs_4_), channel_id=1, source_target_pairs={{0,4},{1,5},{4,8},{5,9},{8,12},{9,13},{12,14},{13,15},{14,10},{15,... | collective-permute-start | bytes 393224 | tf_op jit(solution)/shard_map/ppermute | solution.py:496
  74.1 6.0 %collective-permute-start.17 = (bf16[16,4096]{1,0:T(8,128)(2,1)S(1)}, bf16[16,4096]{1,0:T(8,128)(2,1)S(1)}, u32[]{:S(2)}, u32[]{:S(2)}) collective-permute-start(bf16[16,4096]{1,0:T(8,128)(2,1)S(1)} %get-tuple-element.29), channel_id=1, source_target_pairs={{0,2},{1,3},{4,0},{5,1},{8,4},{9,5},{12,8},{13,9},{14,12},{15,13},... | collective-permute-start | bytes 393224 | tf_op jit(solution)/shard_map/ppermute | solution.py:496
  75.5 6.8 %collective-permute-start.21 = (bf16[16,4096]{1,0:T(8,128)(2,1)S(1)}, bf16[16,4096]{1,0:T(8,128)(2,1)S(1)}, u32[]{:S(2)}, u32[]{:S(2)}) collective-permute-start(bf16[16,4096]{1,0:T(8,128)(2,1)S(1)} %get-tuple-element.30.refs_6_), channel_id=1, source_target_pairs={{0,2},{1,3},{4,0},{5,1},{8,4},{9,5},{12,8},{13,9},{14,12},{15,13},... | collective-permute-start | bytes 393224 | tf_op jit(solution)/shard_map/ppermute | solution.py:496
  77.5 6.4 %collective-permute-start.22 = (bf16[16,4096]{1,0:T(8,128)(2,1)S(1)}, bf16[16,4096]{1,0:T(8,128)(2,1)S(1)}, u32[]{:S(2)}, u32[]{:S(2)}) collective-permute-start(bf16[16,4096]{1,0:T(8,128)(2,1)S(1)} %get-tuple-element.33), channel_id=1, source_target_pairs={{0,4},{1,5},{4,8},{5,9},{8,12},{9,13},{12,14},{13,15},{14,10},{15,... | collective-permute-start | bytes 393224 | tf_op jit(solution)/shard_map/ppermute | solution.py:496
  80.2 5.9 %collective-permute-start.19 = (bf16[16,4096]{1,0:T(8,128)(2,1)S(1)}, bf16[16,4096]{1,0:T(8,128)(2,1)S(1)}, u32[]{:S(2)}, u32[]{:S(2)}) collective-permute-start(bf16[16,4096]{1,0:T(8,128)(2,1)S(1)} %get-tuple-element.31.refs_6_), channel_id=1, source_target_pairs={{0,4},{1,5},{4,8},{5,9},{8,12},{9,13},{12,14},{13,15},{14,10},{15,... | collective-permute-start | bytes 393224 | tf_op jit(solution)/shard_map/ppermute | solution.py:496
  81.7 6.2 %collective-permute-start.20 = (bf16[16,4096]{1,0:T(8,128)(2,1)S(1)}, bf16[16,4096]{1,0:T(8,128)(2,1)S(1)}, u32[]{:S(2)}, u32[]{:S(2)}) collective-permute-start(bf16[16,4096]{1,0:T(8,128)(2,1)S(1)} %get-tuple-element.32), channel_id=1, source_target_pairs={{0,2},{1,3},{4,0},{5,1},{8,4},{9,5},{12,8},{13,9},{14,12},{15,13},... | collective-permute-start | bytes 393224 | tf_op jit(solution)/shard_map/ppermute | solution.py:496
  84.0 5.2 %collective-permute-start.24 = (bf16[16,4096]{1,0:T(8,128)(2,1)S(1)}, bf16[16,4096]{1,0:T(8,128)(2,1)S(1)}, u32[]{:S(2)}, u32[]{:S(2)}) collective-permute-start(bf16[16,4096]{1,0:T(8,128)(2,1)S(1)} %get-tuple-element.34.refs_6_), channel_id=1, source_target_pairs={{0,2},{1,3},{4,0},{5,1},{8,4},{9,5},{12,8},{13,9},{14,12},{15,13},... | collective-permute-start | bytes 393224 | tf_op jit(solution)/shard_map/ppermute | solution.py:496
  84.9 5.8 %collective-permute-start.25 = (bf16[16,4096]{1,0:T(8,128)(2,1)S(1)}, bf16[16,4096]{1,0:T(8,128)(2,1)S(1)}, u32[]{:S(2)}, u32[]{:S(2)}) collective-permute-start(bf16[16,4096]{1,0:T(8,128)(2,1)S(1)} %get-tuple-element.36), channel_id=1, source_target_pairs={{0,4},{1,5},{4,8},{5,9},{8,12},{9,13},{12,14},{13,15},{14,10},{15,... | collective-permute-start | bytes 393224 | tf_op jit(solution)/shard_map/ppermute | solution.py:496
  87.9 11.1 %copy-start.7 = (bf16[8192]{0:T(1024)(128)(2,1)S(1)}, bf16[8192]{0:T(1024)(128)(2,1)}, u32[]{:S(2)}) copy-start(bf16[8192]{0:T(1024)(128)(2,1)} %param.15) | copy-start | bytes 49156
  88.0 6.2 %collective-permute-start.23 = (bf16[16,4096]{1,0:T(8,128)(2,1)S(1)}, bf16[16,4096]{1,0:T(8,128)(2,1)S(1)}, u32[]{:S(2)}, u32[]{:S(2)}) collective-permute-start(bf16[16,4096]{1,0:T(8,128)(2,1)S(1)} %get-tuple-element.35.refs_6_), channel_id=1, source_target_pairs={{0,4},{1,5},{4,8},{5,9},{8,12},{9,13},{12,14},{13,15},{14,10},{15,... | collective-permute-start | bytes 393224 | tf_op jit(solution)/shard_map/ppermute | solution.py:496
  90.8 6.1 %collective-permute-start.29 = (bf16[16,4096]{1,0:T(8,128)(2,1)S(1)}, bf16[16,4096]{1,0:T(8,128)(2,1)S(1)}, u32[]{:S(2)}, u32[]{:S(2)}) collective-permute-start(bf16[16,4096]{1,0:T(8,128)(2,1)S(1)} %get-tuple-element.37.refs_3_), channel_id=1, source_target_pairs={{0,2},{1,3},{4,0},{5,1},{8,4},{9,5},{12,8},{13,9},{14,12},{15,13},... | collective-permute-start | bytes 393224 | tf_op jit(solution)/shard_map/ppermute | solution.py:496
  91.3 7.8 %collective-permute-start.28 = (bf16[16,4096]{1,0:T(8,128)(2,1)S(1)}, bf16[16,4096]{1,0:T(8,128)(2,1)S(1)}, u32[]{:S(2)}, u32[]{:S(2)}) collective-permute-start(bf16[16,4096]{1,0:T(8,128)(2,1)S(1)} %get-tuple-element.39), channel_id=1, source_target_pairs={{0,4},{1,5},{4,8},{5,9},{8,12},{9,13},{12,14},{13,15},{14,10},{15,... | collective-permute-start | bytes 393224 | tf_op jit(solution)/shard_map/ppermute | solution.py:496
  92.8 6.2 %collective-permute-start.27 = (bf16[16,4096]{1,0:T(8,128)(2,1)S(1)}, bf16[16,4096]{1,0:T(8,128)(2,1)S(1)}, u32[]{:S(2)}, u32[]{:S(2)}) collective-permute-start(bf16[16,4096]{1,0:T(8,128)(2,1)S(1)} %get-tuple-element.38), channel_id=1, source_target_pairs={{0,2},{1,3},{4,0},{5,1},{8,4},{9,5},{12,8},{13,9},{14,12},{15,13},... | collective-permute-start | bytes 393224 | tf_op jit(solution)/shard_map/ppermute | solution.py:496
  96.9 5.0 %collective-permute-start.30 = (bf16[16,4096]{1,0:T(8,128)(2,1)S(1)}, bf16[16,4096]{1,0:T(8,128)(2,1)S(1)}, u32[]{:S(2)}, u32[]{:S(2)}) collective-permute-start(bf16[16,4096]{1,0:T(8,128)(2,1)S(1)} %add_blocks.15), channel_id=1, source_target_pairs={{0,2},{1,3},{4,0},{5,1},{8,4},{9,5},{12,8},{13,9},{14,12},{15,13},... | collective-permute-start | bytes 393224 | tf_op jit(solution)/shard_map/ppermute | solution.py:496
  97.0 5.0 %collective-permute-start.26 = (bf16[16,4096]{1,0:T(8,128)(2,1)S(1)}, bf16[16,4096]{1,0:T(8,128)(2,1)S(1)}, u32[]{:S(2)}, u32[]{:S(2)}) collective-permute-start(bf16[16,4096]{1,0:T(8,128)(2,1)S(1)} %add_blocks.14.refs_3_), channel_id=1, source_target_pairs={{0,4},{1,5},{4,8},{5,9},{8,12},{9,13},{12,14},{13,15},{14,10},{15,... | collective-permute-start | bytes 393224 | tf_op jit(solution)/shard_map/ppermute | solution.py:496

commit v8 on v7

--- a/solution.py
+++ b/solution.py
@@ -158,20 +158,17 @@
     return mine + theirs, loads
 
 
-def row_masks(me, tables, shrink_factors, own_rows, size):
+def row_masks(tables, shrink_factors, own_rows, size):
     batch_rows = own_rows * size
     slots, model_width, rank_limit = shrink_factors.shape
     factor = jnp.swapaxes(shrink_factors, 1, 2).reshape(slots * rank_limit, model_width)
-    lengths = [table.shape[0] for table in tables]
-    starts = [sum(lengths[:i]) for i in range(len(lengths))]
-    adapters = lengths[2]
-
-    def kernel(me_ref, all_tables, factor_in, scale, to_place, from_place, hot, factor_out):
+    adapters = tables[2].shape[0]
+
+    def kernel(*refs):
+        start, segment_adapter, ranks, slot_of = (ref[...] for ref in refs[:4])
+        factor_in, scale, to_place, from_place, hot, factor_out = refs[4:]
         factor_out[...] = factor_in[...]
-        me = me_ref[0]
-        start, segment_adapter, ranks, slot_of = (
-            all_tables[:, at : at + length] for at, length in zip(starts, lengths)
-        )
+        me = lax.axis_index(AXIS)
         row = lax.broadcasted_iota(jnp.int32, (batch_rows, 1), 0)
         column = lax.broadcasted_iota(jnp.int32, (1, batch_rows), 1)
         position = row_positions(me, row, own_rows, size)
@@ -193,7 +190,7 @@
         jax.ShapeDtypeStruct((batch_rows, adapters * rank_limit), jnp.bfloat16),
         jax.ShapeDtypeStruct(factor.shape, factor.dtype),
     )
-    return call(kernel, shapes, [me, jnp.concatenate(tables)[None], factor], "row_masks")
+    return call(kernel, shapes, [*(table[None] for table in tables), factor], "row_masks")
 
 
 def shrink_rows(parts, factor, scale, to_place, rank_limit):
@@ -543,12 +540,11 @@
     segment_adapter,
 ):
     size = lax.axis_size(AXIS)
-    me = lax.axis_index(AXIS).astype(jnp.int32).reshape(1)
     own_rows, model_width = activations.shape
     assert size & (size - 1) == 0 and own_rows & (own_rows - 1) == 0
     tables = (segment_start, segment_adapter, adapter_ranks, adapter_storage_slot)
     scale, to_place, from_place, hot, factor = row_masks(
-        me, tables, shrink_factors, own_rows, size
+        tables, shrink_factors, own_rows, size
     )
 
     parts, loads = gather_rows(activations, size, (gate_weight, up_weight), [scale])

time: 103 us -> 92.2 us (0.90)
  local copies, waits for them, and re-layouts: 12.6 us -> 0.27 us
  starting transfers between devices: 27.8 us -> 29.9 us
    unnamed x32 -> x24, local copies, waits for them, and re-layouts: 12.4 us -> 0.08 us
    ppermute x14, waiting for transfers between devices: 14.4 us -> 12.9 us  [scatter_rows(): chain[h] = lax.ppermute(value, AXIS, ring(size, by))]
    ppermute x14, starting transfers between devices: 13.7 us -> 15.1 us  [scatter_rows(): chain[h] = lax.ppermute(value, AXIS, ring(size, by))]
  transfers between devices with their start and end apart: 31 -> 31, of which waited for: 20 -> 22; matrix products, arithmetic and copies ran while one was open for 3% -> 3% of each run, Pallas kernels for 21% -> 23%
where the time goes in v8:
time: 92.2 us; the launch traced here: 92.1 us
  waiting for transfers between devices  30 us (33%)
  starting transfers between devices  29.9 us (32%)
  Pallas kernels  26 us (28%)
  matrix products  4.84 us (5%)
  between operations  1.04 us (1%)
    ppermute x14, starting transfers between devices, scatter_rows(): chain[h] = lax.ppermute(value, AXIS, ring(size, by))  15.1 us
    ppermute x14, waiting for transfers between devices, scatter_rows(): chain[h] = lax.ppermute(value, AXIS, ring(size, by))  12.9 us
    pallas_call x23, Pallas kernels, call(): pl.pallas_call(run, out_shape=out_shape, in_specs=[whole(pltpu.SMEM if op...  12.1 us
    pallas_call x2, Pallas kernels, load_rows(): pl.pallas_call(kernel, out_shape=[jax.ShapeDtypeStruct(shape, weights[0]....  8.65 us
    ppermute x3, waiting for transfers between devices, gather_rows(): right = lax.ppermute(right, AXIS, ring(size, 1))  7.1 us
    ppermute x3, starting transfers between devices, gather_rows(): right = lax.ppermute(right, AXIS, ring(size, 1))  6.45 us
    pallas_call x1, Pallas kernels, stream_rows(): pl.pallas_call(kernel, out_shape=jax.ShapeDtypeStruct((batch_rows, width)...  5.27 us
    dot_general x2, matrix products, body(): jnp.dot(hidden, down_weight[:, h * width:(h + 1) * width], preferred_elem...  4.84 us
  transfers between devices with their start and end apart: 31, of which 22 were waited for; matrix products, arithmetic and copies ran while one was open for 3% of the time, Pallas kernels for 23%

profile of v8, /device:TPU:0, one launch (start us, length us, event | category | flops | bytes accessed | tf_op | source)
XLA Modules:
  0.0 92.1 jit_solution(10757943098448162276)
XLA Ops:
  0.6 3.1 %collective-permute-start = (bf16[16,8192]{1,0:T(8,128)(2,1)}, bf16[16,8192]{1,0:T(8,128)(2,1)S(1)}, u32[]{:S(2)}, u32[]{:S(2)}) collective-permute-start(bf16[16,8192]{1,0:T(8,128)(2,1)} %refs_8_.1), channel_id=1, source_target_pairs={{0,4},{1,5},{4,8},{5,9},{8,12},{9,13},{12,14},{13,15},{14,10},{15,... | collective-permute-start | bytes 786440 | tf_op jit(solution)/shard_map/ppermute | solution.py:138
  3.7 4.3 %load_rows.2.refs_1_ = bf16[3072,1792]{1,0:T(8,128)(2,1)S(1)} custom-call(bf16[8192,896]{1,0:T(8,128)(2,1)} %refs_0_.7, bf16[8192,896]{1,0:T(8,128)(2,1)} %refs_1_.5), custom_call_target="tpu_custom_call" | custom-call | bytes 22020096 | tf_op jit(solution)/shard_map/load_rows/pallas_call | solution.py:292
  8.0 2.1 %collective-permute-done.refs_0_ = bf16[16,8192]{1,0:T(8,128)(2,1)S(1)} collective-permute-done((bf16[16,8192]{1,0:T(8,128)(2,1)}, bf16[16,8192]{1,0:T(8,128)(2,1)S(1)}, u32[]{:S(2)}, u32[]{:S(2)}) %collective-permute-start) | collective-permute-done | bytes 262176 | tf_op jit(solution)/shard_map/ppermute | solution.py:138
  10.2 1.8 %collective-permute-start.2 = (bf16[16,8192]{1,0:T(8,128)(2,1)S(1)}, bf16[16,8192]{1,0:T(8,128)(2,1)S(1)}, u32[]{:S(2)}, u32[]{:S(2)}) collective-permute-start(bf16[16,8192]{1,0:T(8,128)(2,1)S(1)} %pass_on.2.refs_2_), channel_id=1, source_target_pairs={{0,4},{1,5},{4,8},{5,9},{8,12},{9,13},{12,14},{13,15},{14,10},{15,... | collective-permute-start | bytes 786440 | tf_op jit(solution)/shard_map/ppermute | solution.py:138
  12.3 4.3 %load_rows.3.refs_1_ = bf16[3072,1792]{1,0:T(8,128)(2,1)S(1)} custom-call(bf16[8192,896]{1,0:T(8,128)(2,1)} %refs_0_.7, bf16[8192,896]{1,0:T(8,128)(2,1)} %refs_1_.5, bf16[16,8192]{1,0:T(8,128)(2,1)S(1)} %pass_on.2.refs_2_), custom_call_target="tpu_custom_call" | custom-call | bytes 22020096 | tf_op jit(solution)/shard_map/load_rows/pallas_call | solution.py:292
  16.7 1.0 %collective-permute-done.2.refs_0_.refs_2_ = bf16[16,8192]{1,0:T(8,128)(2,1)S(1)} collective-permute-done((bf16[16,8192]{1,0:T(8,128)(2,1)S(1)}, bf16[16,8192]{1,0:T(8,128)(2,1)S(1)}, u32[]{:S(2)}, u32[]{:S(2)}) %collective-permute-start.2) | collective-permute-done | bytes 262176 | tf_op jit(solution)/shard_map/ppermute | solution.py:138
  17.8 1.5 %collective-permute-start.4 = (bf16[16,8192]{1,0:T(8,128)(2,1)S(1)}, bf16[16,8192]{1,0:T(8,128)(2,1)S(1)}, u32[]{:S(2)}, u32[]{:S(2)}) collective-permute-start(bf16[16,8192]{1,0:T(8,128)(2,1)S(1)} %pass_on.3), channel_id=1, source_target_pairs={{0,4},{1,5},{4,8},{5,9},{8,12},{9,13},{12,14},{13,15},{14,10},{15,... | collective-permute-start | bytes 786440 | tf_op jit(solution)/shard_map/ppermute | solution.py:138
  19.3 0.6 collective-permute-start.5
  19.9 0.6 row_masks.1
  20.4 3.9 %collective-permute-done.4.refs_4_.refs_0_ = bf16[16,8192]{1,0:T(8,128)(2,1)S(1)} collective-permute-done((bf16[16,8192]{1,0:T(8,128)(2,1)S(1)}, bf16[16,8192]{1,0:T(8,128)(2,1)S(1)}, u32[]{:S(2)}, u32[]{:S(2)}) %collective-permute-start.4) | collective-permute-done | bytes 262176 | tf_op jit(solution)/shard_map/ppermute | solution.py:138
  24.4 1.3 %collective-permute-done.5.refs_5_.refs_0_ = bf16[16,8192]{1,0:T(8,128)(2,1)S(1)} collective-permute-done((bf16[16,8192]{1,0:T(8,128)(2,1)S(1)}, bf16[16,8192]{1,0:T(8,128)(2,1)S(1)}, u32[]{:S(2)}, u32[]{:S(2)}) %collective-permute-start.5) | collective-permute-done | bytes 262176 | tf_op jit(solution)/shard_map/ppermute | solution.py:139
  25.9 1.6 %collective-permute-start.6 = (bf16[16,4096]{1,0:T(8,128)(2,1)S(1)}, bf16[16,4096]{1,0:T(8,128)(2,1)S(1)}, u32[]{:S(2)}, u32[]{:S(2)}) collective-permute-start(bf16[16,4096]{1,0:T(8,128)(2,1)S(1)} %column_half.2), channel_id=1, source_target_pairs={{0,4},{1,5},{4,8},{5,9},{8,12},{9,13},{12,14},{13,15},{14,10},{15,... | collective-permute-start | bytes 393224 | tf_op jit(solution)/shard_map/ppermute | solution.py:151
  28.0 3.8 %collective-permute-done.6.refs_0_ = bf16[16,4096]{1,0:T(8,128)(2,1)S(1)} collective-permute-done((bf16[16,4096]{1,0:T(8,128)(2,1)S(1)}, bf16[16,4096]{1,0:T(8,128)(2,1)S(1)}, u32[]{:S(2)}, u32[]{:S(2)}) %collective-permute-start.6) | collective-permute-done | bytes 131104 | tf_op jit(solution)/shard_map/ppermute | solution.py:151
  31.8 1.4 %collective-permute-done.7.refs_1_ = bf16[16,4096]{1,0:T(8,128)(2,1)S(1)} collective-permute-done((bf16[16,4096]{1,0:T(8,128)(2,1)S(1)}, bf16[16,4096]{1,0:T(8,128)(2,1)S(1)}, u32[]{:S(2)}, u32[]{:S(2)}) %collective-permute-start.7) | collective-permute-done | bytes 131104 | tf_op jit(solution)/shard_map/ppermute | solution.py:152
  33.3 1.5 %collective-permute-done.10.refs_5_ = bf16[16,8192]{1,0:T(8,128)(2,1)S(1)} collective-permute-done((bf16[16,8192]{1,0:T(8,128)(2,1)S(1)}, bf16[16,8192]{1,0:T(8,128)(2,1)S(1)}, u32[]{:S(2)}, u32[]{:S(2)}) %collective-permute-start.10) | collective-permute-done | bytes 262176 | tf_op jit(solution)/shard_map/ppermute | solution.py:157
  34.8 2.6 %shrink_rows.1 = (bf16[256,8192]{1,0:T(8,128)(2,1)S(1)}, bf16[256,64]{1,0:T(8,128)(2,1)S(1)}) custom-call(bf16[16,8192]{1,0:T(8,128)(2,1)S(1)} %copy-done.1, bf16[96,8192]{1,0:T(8,128)(2,1)S(1)} %join_pieces.2.refs_1_, bf16[16,8192]{1,0:T(8,128)(2,1)S(1)} %join_pieces.3.refs_2_, bf16[16,8192]{1,0:T(8,128)(2,1)S(1)} %collective-permute-done.8.refs_3_, ...), custom_call_target="tpu_custom_call" | custom-call | flops 268435456 | bytes 8388608 | tf_op jit(solution)/shard_map/shrink_rows/pallas_call | solution.py:78
  37.6 1.1 %collective-permute-done.11.refs_1_ = bf16[256,64]{1,0:T(8,128)(2,1)S(1)} collective-permute-done((bf16[256,64]{1,0:T(8,128)(2,1)S(1)}, bf16[256,64]{1,0:T(8,128)(2,1)S(1)}, u32[]{:S(2)}, u32[]{:S(2)}) %collective-permute-start.11) | collective-permute-done | bytes 32800 | tf_op jit(solution)/shard_map/ppermute | solution.py:556
  38.8 0.5 collective-permute-start.12
  39.3 3.0 %mixed_rows.2.refs_2_ = f32[256,1792]{1,0:T(8,128)S(1)} custom-call(bf16[256,8192]{1,0:T(8,128)(2,1)S(1)} %get-tuple-element.25.refs_0_.rows_ref, bf16[3072,1792]{1,0:T(8,128)(2,1)S(1)} %load_rows.2.refs_1_, bf16[256,64]{1,0:T(8,128)(2,1)S(1)} %add_coefficients.3.refs_2_.refs_0_), custom_call_target="tpu_custom_call" | custom-call | flops 2818572288 | bytes 11010048 | tf_op jit(solution)/shard_map/mixed_rows/pallas_call | solution.py:78
  42.3 0.8 collective-permute-done.12.refs_1_
  43.1 1.6 %collective-permute-start.13 = (bf16[256,64]{1,0:T(8,128)(2,1)S(1)}, bf16[256,64]{1,0:T(8,128)(2,1)S(1)}, u32[]{:S(2)}, u32[]{:S(2)}) collective-permute-start(bf16[256,64]{1,0:T(8,128)(2,1)S(1)} %add_coefficients.4.refs_3_.refs_0_), channel_id=1, source_target_pairs={{0,4},{1,5},{2,6},{3,7},{4,0},{5,1},{6,2},{7,3},{8,12},{9,13},{10,... | collective-permute-start | bytes 98312 | tf_op jit(solution)/shard_map/ppermute | solution.py:556
  44.8 3.0 %mixed_rows.3.refs_2_ = f32[256,1792]{1,0:T(8,128)S(1)} custom-call(bf16[256,8192]{1,0:T(8,128)(2,1)S(1)} %get-tuple-element.25.refs_0_.rows_ref, bf16[3072,1792]{1,0:T(8,128)(2,1)S(1)} %load_rows.3.refs_1_, f32[256,1792]{1,0:T(8,128)S(1)} %mixed_rows.2.refs_2_, bf16[256,64]{1,0:T(8,128)(2,1)S(1)} %add_coefficients.4.refs_3_.refs_0_), custom_call_target="tpu_custom_call" | custom-call | flops 2818572288 | bytes 11010048 | tf_op jit(solution)/shard_map/mixed_rows/pallas_call | solution.py:78
  47.9 2.3 %collective-permute-start.14 = (bf16[256,64]{1,0:T(8,128)(2,1)S(1)}, bf16[256,64]{1,0:T(8,128)(2,1)S(1)}, u32[]{:S(2)}, u32[]{:S(2)}) collective-permute-start(bf16[256,64]{1,0:T(8,128)(2,1)S(1)} %add_coefficients.5.refs_3_.refs_0_), channel_id=1, source_target_pairs={{0,8},{1,9},{2,10},{3,11},{4,12},{5,13},{6,14},{7,15},{8,0},{9,1},... | collective-permute-start | bytes 98312 | tf_op jit(solution)/shard_map/ppermute | solution.py:556
  50.1 5.3 %stream_rows.1.refs_5_ = f32[256,1792]{1,0:T(8,128)S(1)} custom-call(bf16[256,8192]{1,0:T(8,128)(2,1)S(1)} %get-tuple-element.25.refs_0_.rows_ref, bf16[8192,896]{1,0:T(8,128)(2,1)} %refs_0_.7, bf16[8192,896]{1,0:T(8,128)(2,1)} %refs_1_.5, f32[256,1792]{1,0:T(8,128)S(1)} %mixed_rows.3.refs_2_, bf16[256,64]{1,0:T(8,128)(2,1)S(1)} %add_coefficients.5.refs_3_.refs_0_), custom_call_target="tpu_custom_call" | custom-call | flops 1879048192 | bytes 14680064 | tf_op jit(solution)/shard_map/stream_rows/pallas_call | solution.py:395
  55.4 1.0 %hidden_rows.1 = bf16[256,896]{1,0:T(8,128)(2,1)S(1)} custom-call(bf16[256,64]{1,0:T(8,128)(2,1)S(1)} %add_coefficients.5.refs_3_.refs_0_, bf16[256,64]{1,0:T(8,128)(2,1)S(1)} %collective-permute-done.14.refs_1_, bf16[256,256]{1,0:T(8,128)(2,1)S(1)} %get-tuple-element.26.refs_2_, bf16[256,1024]{1,0:T(8,128)(2,1)S(1)} %get-tuple-element.27.refs_3_, ...), custom_call_target="tpu_custom_call" | custom-call | flops 469762048 | bytes 1835008 | tf_op jit(solution)/shard_map/hidden_rows/pallas_call | solution.py:78
  56.4 2.4 %fusion.4.refs_0_.refs_2_.refs_3_ = bf16[256,4096]{1,0:T(8,128)(2,1)S(1)} fusion(bf16[256,896]{1,0:T(8,128)(2,1)S(1)} %hidden_rows.1, bf16[896,8192]{1,0:T(8,128)(2,1)S(1)} %bitcast.17), kind=kOutput, calls=%fused_computation.4 | convolution fusion | flops 1880096768 | bytes 9895936 | tf_op jit(solution)/shard_map/dot_general | solution.py:573
  59.0 2.4 %fusion.7.refs_0_.refs_2_.refs_3_.refs_4_ = bf16[256,4096]{1,0:T(8,128)(2,1)S(1)} fusion(bf16[256,896]{1,0:T(8,128)(2,1)S(1)} %hidden_rows.1, bf16[896,8192]{1,0:T(8,128)(2,1)S(1)} %bitcast.17), kind=kOutput, calls=%fused_computation.5 | convolution fusion | flops 1880096768 | bytes 9895936 | tf_op jit(solution)/shard_map/dot_general | solution.py:573
  61.6 0.6 collective-permute-start.18
  62.2 0.8 collective-permute-start.16
  63.0 1.2 %collective-permute-start.17 = (bf16[16,4096]{1,0:T(8,128)(2,1)S(1)}, bf16[16,4096]{1,0:T(8,128)(2,1)S(1)}, u32[]{:S(2)}, u32[]{:S(2)}) collective-permute-start(bf16[16,4096]{1,0:T(8,128)(2,1)S(1)} %get-tuple-element.29), channel_id=1, source_target_pairs={{0,2},{1,3},{4,0},{5,1},{8,4},{9,5},{12,8},{13,9},{14,12},{15,13},... | collective-permute-start | bytes 393224 | tf_op jit(solution)/shard_map/ppermute | solution.py:493
  64.5 0.8 collective-permute-start.21
  65.3 1.2 %collective-permute-start.22 = (bf16[16,4096]{1,0:T(8,128)(2,1)S(1)}, bf16[16,4096]{1,0:T(8,128)(2,1)S(1)}, u32[]{:S(2)}, u32[]{:S(2)}) collective-permute-start(bf16[16,4096]{1,0:T(8,128)(2,1)S(1)} %get-tuple-element.33), channel_id=1, source_target_pairs={{0,4},{1,5},{4,8},{5,9},{8,12},{9,13},{12,14},{13,15},{14,10},{15,... | collective-permute-start | bytes 393224 | tf_op jit(solution)/shard_map/ppermute | solution.py:493
  66.6 1.1 %collective-permute-done.16.refs_2_ = bf16[16,4096]{1,0:T(8,128)(2,1)S(1)} collective-permute-done((bf16[16,4096]{1,0:T(8,128)(2,1)S(1)}, bf16[16,4096]{1,0:T(8,128)(2,1)S(1)}, u32[]{:S(2)}, u32[]{:S(2)}) %collective-permute-start.16) | collective-permute-done | bytes 131104 | tf_op jit(solution)/shard_map/ppermute | solution.py:493
  67.7 1.2 %collective-permute-done.17.refs_5_ = bf16[16,4096]{1,0:T(8,128)(2,1)S(1)} collective-permute-done((bf16[16,4096]{1,0:T(8,128)(2,1)S(1)}, bf16[16,4096]{1,0:T(8,128)(2,1)S(1)}, u32[]{:S(2)}, u32[]{:S(2)}) %collective-permute-start.17) | collective-permute-done | bytes 131104 | tf_op jit(solution)/shard_map/ppermute | solution.py:493
  69.0 1.8 %collective-permute-start.19 = (bf16[16,4096]{1,0:T(8,128)(2,1)S(1)}, bf16[16,4096]{1,0:T(8,128)(2,1)S(1)}, u32[]{:S(2)}, u32[]{:S(2)}) collective-permute-start(bf16[16,4096]{1,0:T(8,128)(2,1)S(1)} %get-tuple-element.31.refs_6_), channel_id=1, source_target_pairs={{0,4},{1,5},{4,8},{5,9},{8,12},{9,13},{12,14},{13,15},{14,10},{15,... | collective-permute-start | bytes 393224 | tf_op jit(solution)/shard_map/ppermute | solution.py:493
  71.1 0.6 collective-permute-done.22.refs_5_
  71.8 1.2 %collective-permute-start.24 = (bf16[16,4096]{1,0:T(8,128)(2,1)S(1)}, bf16[16,4096]{1,0:T(8,128)(2,1)S(1)}, u32[]{:S(2)}, u32[]{:S(2)}) collective-permute-start(bf16[16,4096]{1,0:T(8,128)(2,1)S(1)} %get-tuple-element.34.refs_6_), channel_id=1, source_target_pairs={{0,2},{1,3},{4,0},{5,1},{8,4},{9,5},{12,8},{13,9},{14,12},{15,13},... | collective-permute-start | bytes 393224 | tf_op jit(solution)/shard_map/ppermute | solution.py:493
  73.0 0.9 collective-permute-start.25
  74.3 1.7 %collective-permute-done.20.refs_5_ = bf16[16,4096]{1,0:T(8,128)(2,1)S(1)} collective-permute-done((bf16[16,4096]{1,0:T(8,128)(2,1)S(1)}, bf16[16,4096]{1,0:T(8,128)(2,1)S(1)}, u32[]{:S(2)}, u32[]{:S(2)}) %collective-permute-start.20) | collective-permute-done | bytes 131104 | tf_op jit(solution)/shard_map/ppermute | solution.py:493
  76.1 0.9 %collective-permute-start.23 = (bf16[16,4096]{1,0:T(8,128)(2,1)S(1)}, bf16[16,4096]{1,0:T(8,128)(2,1)S(1)}, u32[]{:S(2)}, u32[]{:S(2)}) collective-permute-start(bf16[16,4096]{1,0:T(8,128)(2,1)S(1)} %get-tuple-element.35.refs_6_), channel_id=1, source_target_pairs={{0,4},{1,5},{4,8},{5,9},{8,12},{9,13},{12,14},{13,15},{14,10},{15,... | collective-permute-start | bytes 393224 | tf_op jit(solution)/shard_map/ppermute | solution.py:493
  77.4 0.8 collective-permute-done.25.refs_5_
  78.3 1.7 %collective-permute-start.29 = (bf16[16,4096]{1,0:T(8,128)(2,1)S(1)}, bf16[16,4096]{1,0:T(8,128)(2,1)S(1)}, u32[]{:S(2)}, u32[]{:S(2)}) collective-permute-start(bf16[16,4096]{1,0:T(8,128)(2,1)S(1)} %get-tuple-element.37.refs_3_), channel_id=1, source_target_pairs={{0,2},{1,3},{4,0},{5,1},{8,4},{9,5},{12,8},{13,9},{14,12},{15,13},... | collective-permute-start | bytes 393224 | tf_op jit(solution)/shard_map/ppermute | solution.py:493
  80.4 1.7 %collective-permute-start.27 = (bf16[16,4096]{1,0:T(8,128)(2,1)S(1)}, bf16[16,4096]{1,0:T(8,128)(2,1)S(1)}, u32[]{:S(2)}, u32[]{:S(2)}) collective-permute-start(bf16[16,4096]{1,0:T(8,128)(2,1)S(1)} %get-tuple-element.38), channel_id=1, source_target_pairs={{0,2},{1,3},{4,0},{5,1},{8,4},{9,5},{12,8},{13,9},{14,12},{15,13},... | collective-permute-start | bytes 393224 | tf_op jit(solution)/shard_map/ppermute | solution.py:493
  82.5 1.7 %collective-permute-done.29.refs_2_ = bf16[16,4096]{1,0:T(8,128)(2,1)S(1)} collective-permute-done((bf16[16,4096]{1,0:T(8,128)(2,1)S(1)}, bf16[16,4096]{1,0:T(8,128)(2,1)S(1)}, u32[]{:S(2)}, u32[]{:S(2)}) %collective-permute-start.29) | collective-permute-done | bytes 131104 | tf_op jit(solution)/shard_map/ppermute | solution.py:493
  84.3 1.8 %collective-permute-start.30 = (bf16[16,4096]{1,0:T(8,128)(2,1)S(1)}, bf16[16,4096]{1,0:T(8,128)(2,1)S(1)}, u32[]{:S(2)}, u32[]{:S(2)}) collective-permute-start(bf16[16,4096]{1,0:T(8,128)(2,1)S(1)} %add_blocks.15), channel_id=1, source_target_pairs={{0,2},{1,3},{4,0},{5,1},{8,4},{9,5},{12,8},{13,9},{14,12},{15,13},... | collective-permute-start | bytes 393224 | tf_op jit(solution)/shard_map/ppermute | solution.py:493
  86.4 2.9 %collective-permute-done.30.refs_7_ = bf16[16,4096]{1,0:T(8,128)(2,1)S(1)} collective-permute-done((bf16[16,4096]{1,0:T(8,128)(2,1)S(1)}, bf16[16,4096]{1,0:T(8,128)(2,1)S(1)}, u32[]{:S(2)}, u32[]{:S(2)}) %collective-permute-start.30) | collective-permute-done | bytes 131104 | tf_op jit(solution)/shard_map/ppermute | solution.py:493
  89.3 1.7 %collective-permute-done.26.refs_2_ = bf16[16,4096]{1,0:T(8,128)(2,1)S(1)} collective-permute-done((bf16[16,4096]{1,0:T(8,128)(2,1)S(1)}, bf16[16,4096]{1,0:T(8,128)(2,1)S(1)}, u32[]{:S(2)}, u32[]{:S(2)}) %collective-permute-start.26) | collective-permute-done | bytes 131104 | tf_op jit(solution)/shard_map/ppermute | solution.py:493
  91.0 1.0 %finish_rows.1 = (bf16[16,8192]{1,0:T(8,128)(2,1)}, bf16[16,8192]{1,0:T(8,128)(2,1)}) custom-call(bf16[256,4096]{1,0:T(8,128)(2,1)S(1)} %fusion.4.refs_0_.refs_2_.refs_3_, bf16[128,4096]{1,0:T(8,128)(2,1)S(1)} %collective-permute-done.15.refs_1_.refs_3_.refs_4_, bf16[16,4096]{1,0:T(8,128)(2,1)S(1)} %collective-permute-done.26.refs_2_, ...), custom_call_target="tpu_custom_call" | custom-call | tf_op jit(solution)/shard_map/finish_rows/pallas_call | solution.py:78
  (70 shorter events, 4.7 us)
Async XLA Ops:
  0.6 9.5 %collective-permute-start = (bf16[16,8192]{1,0:T(8,128)(2,1)}, bf16[16,8192]{1,0:T(8,128)(2,1)S(1)}, u32[]{:S(2)}, u32[]{:S(2)}) collective-permute-start(bf16[16,8192]{1,0:T(8,128)(2,1)} %refs_8_.1), channel_id=1, source_target_pairs={{0,4},{1,5},{4,8},{5,9},{8,12},{9,13},{12,14},{13,15},{14,10},{15,... | collective-permute-start | bytes 786440 | tf_op jit(solution)/shard_map/ppermute | solution.py:138
  3.7 8.3 %collective-permute-start.1 = (bf16[16,8192]{1,0:T(8,128)(2,1)}, bf16[16,8192]{1,0:T(8,128)(2,1)S(1)}, u32[]{:S(2)}, u32[]{:S(2)}) collective-permute-start(bf16[16,8192]{1,0:T(8,128)(2,1)} %refs_8_.1), channel_id=1, source_target_pairs={{0,2},{1,3},{4,0},{5,1},{8,4},{9,5},{12,8},{13,9},{14,12},{15,13},... | collective-permute-start | bytes 786440 | tf_op jit(solution)/shard_map/ppermute | solution.py:139
  10.2 7.5 %collective-permute-start.2 = (bf16[16,8192]{1,0:T(8,128)(2,1)S(1)}, bf16[16,8192]{1,0:T(8,128)(2,1)S(1)}, u32[]{:S(2)}, u32[]{:S(2)}) collective-permute-start(bf16[16,8192]{1,0:T(8,128)(2,1)S(1)} %pass_on.2.refs_2_), channel_id=1, source_target_pairs={{0,4},{1,5},{4,8},{5,9},{8,12},{9,13},{12,14},{13,15},{14,10},{15,... | collective-permute-start | bytes 786440 | tf_op jit(solution)/shard_map/ppermute | solution.py:138
  12.0 7.2 %collective-permute-start.3 = (bf16[16,8192]{1,0:T(8,128)(2,1)S(1)}, bf16[16,8192]{1,0:T(8,128)(2,1)S(1)}, u32[]{:S(2)}, u32[]{:S(2)}) collective-permute-start(bf16[16,8192]{1,0:T(8,128)(2,1)S(1)} %collective-permute-done.1.refs_1_), channel_id=1, source_target_pairs={{0,2},{1,3},{4,0},{5,1},{8,4},{9,5},{12,8},{13,9},{14,12},{15,13},... | collective-permute-start | bytes 786440 | tf_op jit(solution)/shard_map/ppermute | solution.py:139
  16.6 3.2 %copy-start.2 = (bf16[1,8192,64]{1,2,0:T(8,128)(2,1)S(1)}, bf16[1,8192,64]{1,2,0:T(8,128)(2,1)}, u32[]{:S(2)}) copy-start(bf16[1,8192,64]{1,2,0:T(8,128)(2,1)} %param.16) | copy-start | bytes 3145732
  16.6 3.2 %copy-start.3 = (s32[32]{0:T(128)S(1)}, s32[32]{0:T(128)}, u32[]{:S(2)}) copy-start(s32[32]{0:T(128)} %param.20) | copy-start | bytes 388
  16.6 3.2 %copy-start.4 = (s32[32]{0:T(128)S(1)}, s32[32]{0:T(128)}, u32[]{:S(2)}) copy-start(s32[32]{0:T(128)} %param.21) | copy-start | bytes 388
  16.6 3.2 %copy-start.5 = (s32[16]{0:T(128)S(1)}, s32[16]{0:T(128)}, u32[]{:S(2)}) copy-start(s32[16]{0:T(128)} %param.18) | copy-start | bytes 196
  16.7 3.2 %copy-start.6 = (s32[16]{0:T(128)S(1)}, s32[16]{0:T(128)}, u32[]{:S(2)}) copy-start(s32[16]{0:T(128)} %param.19) | copy-start | bytes 196
  16.7 11.3 %copy-start.1 = (bf16[16,8192]{1,0:T(8,128)(2,1)S(1)}, bf16[16,8192]{1,0:T(8,128)(2,1)}, u32[]{:S(2)}) copy-start(bf16[16,8192]{1,0:T(8,128)(2,1)} %refs_8_.1) | copy-start | bytes 786436
  17.8 6.6 %collective-permute-start.4 = (bf16[16,8192]{1,0:T(8,128)(2,1)S(1)}, bf16[16,8192]{1,0:T(8,128)(2,1)S(1)}, u32[]{:S(2)}, u32[]{:S(2)}) collective-permute-start(bf16[16,8192]{1,0:T(8,128)(2,1)S(1)} %pass_on.3), channel_id=1, source_target_pairs={{0,4},{1,5},{4,8},{5,9},{8,12},{9,13},{12,14},{13,15},{14,10},{15,... | collective-permute-start | bytes 786440 | tf_op jit(solution)/shard_map/ppermute | solution.py:138
  19.3 6.4 %collective-permute-start.5 = (bf16[16,8192]{1,0:T(8,128)(2,1)S(1)}, bf16[16,8192]{1,0:T(8,128)(2,1)S(1)}, u32[]{:S(2)}, u32[]{:S(2)}) collective-permute-start(bf16[16,8192]{1,0:T(8,128)(2,1)S(1)} %collective-permute-done.3.refs_3_), channel_id=1, source_target_pairs={{0,2},{1,3},{4,0},{5,1},{8,4},{9,5},{12,8},{13,9},{14,12},{15,13},... | collective-permute-start | bytes 786440 | tf_op jit(solution)/shard_map/ppermute | solution.py:139
  25.8 9.0 %collective-permute-start.9 = (bf16[96,8192]{1,0:T(8,128)(2,1)S(1)}, bf16[96,8192]{1,0:T(8,128)(2,1)S(1)}, u32[]{:S(2)}, u32[]{:S(2)}) collective-permute-start(bf16[96,8192]{1,0:T(8,128)(2,1)S(1)} %join_pieces.2.refs_1_), channel_id=1, source_target_pairs={{0,1},{1,0},{2,3},{3,2},{4,5},{5,4},{6,7},{7,6},{8,9},{9,8},{10,11... | collective-permute-start | bytes 4718600 | tf_op jit(solution)/shard_map/ppermute | solution.py:148
  25.9 5.9 %collective-permute-start.6 = (bf16[16,4096]{1,0:T(8,128)(2,1)S(1)}, bf16[16,4096]{1,0:T(8,128)(2,1)S(1)}, u32[]{:S(2)}, u32[]{:S(2)}) collective-permute-start(bf16[16,4096]{1,0:T(8,128)(2,1)S(1)} %column_half.2), channel_id=1, source_target_pairs={{0,4},{1,5},{4,8},{5,9},{8,12},{9,13},{12,14},{13,15},{14,10},{15,... | collective-permute-start | bytes 393224 | tf_op jit(solution)/shard_map/ppermute | solution.py:151
  27.5 5.7 %collective-permute-start.7 = (bf16[16,4096]{1,0:T(8,128)(2,1)S(1)}, bf16[16,4096]{1,0:T(8,128)(2,1)S(1)}, u32[]{:S(2)}, u32[]{:S(2)}) collective-permute-start(bf16[16,4096]{1,0:T(8,128)(2,1)S(1)} %column_half.3), channel_id=1, source_target_pairs={{0,2},{1,3},{4,0},{5,1},{8,4},{9,5},{12,8},{13,9},{14,12},{15,13},... | collective-permute-start | bytes 393224 | tf_op jit(solution)/shard_map/ppermute | solution.py:152
  28.0 5.3 %collective-permute-start.8 = (bf16[16,8192]{1,0:T(8,128)(2,1)S(1)}, bf16[16,8192]{1,0:T(8,128)(2,1)S(1)}, u32[]{:S(2)}, u32[]{:S(2)}) collective-permute-start(bf16[16,8192]{1,0:T(8,128)(2,1)S(1)} %copy-done.1), channel_id=1, source_target_pairs={{0,1},{1,0},{2,3},{3,2},{4,5},{5,4},{6,7},{7,6},{8,9},{9,8},{10,11... | collective-permute-start | bytes 786440 | tf_op jit(solution)/shard_map/ppermute | solution.py:141
  33.2 1.6 %collective-permute-start.10 = (bf16[16,8192]{1,0:T(8,128)(2,1)S(1)}, bf16[16,8192]{1,0:T(8,128)(2,1)S(1)}, u32[]{:S(2)}, u32[]{:S(2)}) collective-permute-start(bf16[16,8192]{1,0:T(8,128)(2,1)S(1)} %join_pieces.3.refs_2_), channel_id=1, source_target_pairs={{0,1},{1,0},{2,3},{3,2},{4,5},{5,4},{6,7},{7,6},{8,9},{9,8},{10,11... | collective-permute-start | bytes 786440 | tf_op jit(solution)/shard_map/ppermute | solution.py:157
  37.4 1.3 %collective-permute-start.11 = (bf16[256,64]{1,0:T(8,128)(2,1)S(1)}, bf16[256,64]{1,0:T(8,128)(2,1)S(1)}, u32[]{:S(2)}, u32[]{:S(2)}) collective-permute-start(bf16[256,64]{1,0:T(8,128)(2,1)S(1)} %get-tuple-element.24.refs_0_), channel_id=1, source_target_pairs={{0,1},{1,0},{2,3},{3,2},{4,5},{5,4},{6,7},{7,6},{8,9},{9,8},{10,11... | collective-permute-start | bytes 98312 | tf_op jit(solution)/shard_map/ppermute | solution.py:556
  38.8 4.3 %collective-permute-start.12 = (bf16[256,64]{1,0:T(8,128)(2,1)S(1)}, bf16[256,64]{1,0:T(8,128)(2,1)S(1)}, u32[]{:S(2)}, u32[]{:S(2)}) collective-permute-start(bf16[256,64]{1,0:T(8,128)(2,1)S(1)} %add_coefficients.3.refs_2_.refs_0_), channel_id=1, source_target_pairs={{0,2},{1,3},{2,0},{3,1},{4,6},{5,7},{6,4},{7,5},{8,10},{9,11},{10,... | collective-permute-start | bytes 98312 | tf_op jit(solution)/shard_map/ppermute | solution.py:556
  43.1 4.7 %collective-permute-start.13 = (bf16[256,64]{1,0:T(8,128)(2,1)S(1)}, bf16[256,64]{1,0:T(8,128)(2,1)S(1)}, u32[]{:S(2)}, u32[]{:S(2)}) collective-permute-start(bf16[256,64]{1,0:T(8,128)(2,1)S(1)} %add_coefficients.4.refs_3_.refs_0_), channel_id=1, source_target_pairs={{0,4},{1,5},{2,6},{3,7},{4,0},{5,1},{6,2},{7,3},{8,12},{9,13},{10,... | collective-permute-start | bytes 98312 | tf_op jit(solution)/shard_map/ppermute | solution.py:556
  47.8 8.6 %slice-start = ((s8[14680064]{0:T(1024)(128)(4,1)}), s8[4194304]{0:T(1024)(128)(4,1)S(1)}, s32[]{:S(2)}) async-start(s8[14680064]{0:T(1024)(128)(4,1)} %bitcast.16), calls=%async_computation | async-start | bytes 8388608
  47.8 7.6 %copy-start = (bf16[16,64,896]{2,1,0:T(8,128)(2,1)S(1)}, bf16[16,64,896]{2,1,0:T(8,128)(2,1)}, u32[]{:S(2)}) copy-start(bf16[16,64,896]{2,1,0:T(8,128)(2,1)} %param.17) | copy-start | bytes 5505028
  47.8 8.6 %slice-start.1 = ((s8[14680064]{0:T(1024)(128)(4,1)}), s8[4194304]{0:T(1024)(128)(4,1)S(1)}, s32[]{:S(2)}) async-start(s8[14680064]{0:T(1024)(128)(4,1)} %bitcast.16), calls=%async_computation.1 | async-start | bytes 8388608
  47.8 8.6 %slice-start.2 = ((s8[14680064]{0:T(1024)(128)(4,1)}), s8[4194304]{0:T(1024)(128)(4,1)S(1)}, s32[]{:S(2)}) async-start(s8[14680064]{0:T(1024)(128)(4,1)} %bitcast.16), calls=%async_computation.2 | async-start | bytes 8388608
  47.8 8.6 %slice-start.3 = ((s8[14680064]{0:T(1024)(128)(4,1)}), s8[2097152]{0:T(1024)(128)(4,1)S(1)}, s32[]{:S(2)}) async-start(s8[14680064]{0:T(1024)(128)(4,1)} %bitcast.16), calls=%async_computation.3 | async-start | bytes 4194304
  47.9 7.5 %collective-permute-start.14 = (bf16[256,64]{1,0:T(8,128)(2,1)S(1)}, bf16[256,64]{1,0:T(8,128)(2,1)S(1)}, u32[]{:S(2)}, u32[]{:S(2)}) collective-permute-start(bf16[256,64]{1,0:T(8,128)(2,1)S(1)} %add_coefficients.5.refs_3_.refs_0_), channel_id=1, source_target_pairs={{0,8},{1,9},{2,10},{3,11},{4,12},{5,13},{6,14},{7,15},{8,0},{9,1},... | collective-permute-start | bytes 98312 | tf_op jit(solution)/shard_map/ppermute | solution.py:556
  59.0 3.2 %collective-permute-start.15 = (bf16[128,4096]{1,0:T(8,128)(2,1)S(1)}, bf16[128,4096]{1,0:T(8,128)(2,1)S(1)}, u32[]{:S(2)}, u32[]{:S(2)}) collective-permute-start(bf16[128,4096]{1,0:T(8,128)(2,1)S(1)} %slice.16), channel_id=1, source_target_pairs={{0,1},{1,0},{2,3},{3,2},{4,5},{5,4},{6,7},{7,6},{8,9},{9,8},{10,11... | collective-permute-start | bytes 3145736 | tf_op jit(solution)/shard_map/ppermute | solution.py:579
  61.6 2.8 %collective-permute-start.18 = (bf16[128,4096]{1,0:T(8,128)(2,1)S(1)}, bf16[128,4096]{1,0:T(8,128)(2,1)S(1)}, u32[]{:S(2)}, u32[]{:S(2)}) collective-permute-start(bf16[128,4096]{1,0:T(8,128)(2,1)S(1)} %slice.17), channel_id=1, source_target_pairs={{0,1},{1,0},{2,3},{3,2},{4,5},{5,4},{6,7},{7,6},{8,9},{9,8},{10,11... | collective-permute-start | bytes 3145736 | tf_op jit(solution)/shard_map/ppermute | solution.py:579
  62.2 5.5 %collective-permute-start.16 = (bf16[16,4096]{1,0:T(8,128)(2,1)S(1)}, bf16[16,4096]{1,0:T(8,128)(2,1)S(1)}, u32[]{:S(2)}, u32[]{:S(2)}) collective-permute-start(bf16[16,4096]{1,0:T(8,128)(2,1)S(1)} %get-tuple-element.28.refs_4_), channel_id=1, source_target_pairs={{0,4},{1,5},{4,8},{5,9},{8,12},{9,13},{12,14},{13,15},{14,10},{15,... | collective-permute-start | bytes 393224 | tf_op jit(solution)/shard_map/ppermute | solution.py:493
  63.0 5.8 %collective-permute-start.17 = (bf16[16,4096]{1,0:T(8,128)(2,1)S(1)}, bf16[16,4096]{1,0:T(8,128)(2,1)S(1)}, u32[]{:S(2)}, u32[]{:S(2)}) collective-permute-start(bf16[16,4096]{1,0:T(8,128)(2,1)S(1)} %get-tuple-element.29), channel_id=1, source_target_pairs={{0,2},{1,3},{4,0},{5,1},{8,4},{9,5},{12,8},{13,9},{14,12},{15,13},... | collective-permute-start | bytes 393224 | tf_op jit(solution)/shard_map/ppermute | solution.py:493
  64.5 6.6 %collective-permute-start.21 = (bf16[16,4096]{1,0:T(8,128)(2,1)S(1)}, bf16[16,4096]{1,0:T(8,128)(2,1)S(1)}, u32[]{:S(2)}, u32[]{:S(2)}) collective-permute-start(bf16[16,4096]{1,0:T(8,128)(2,1)S(1)} %get-tuple-element.30.refs_6_), channel_id=1, source_target_pairs={{0,2},{1,3},{4,0},{5,1},{8,4},{9,5},{12,8},{13,9},{14,12},{15,13},... | collective-permute-start | bytes 393224 | tf_op jit(solution)/shard_map/ppermute | solution.py:493
  65.3 6.4 %collective-permute-start.22 = (bf16[16,4096]{1,0:T(8,128)(2,1)S(1)}, bf16[16,4096]{1,0:T(8,128)(2,1)S(1)}, u32[]{:S(2)}, u32[]{:S(2)}) collective-permute-start(bf16[16,4096]{1,0:T(8,128)(2,1)S(1)} %get-tuple-element.33), channel_id=1, source_target_pairs={{0,4},{1,5},{4,8},{5,9},{8,12},{9,13},{12,14},{13,15},{14,10},{15,... | collective-permute-start | bytes 393224 | tf_op jit(solution)/shard_map/ppermute | solution.py:493
  69.0 5.3 %collective-permute-start.19 = (bf16[16,4096]{1,0:T(8,128)(2,1)S(1)}, bf16[16,4096]{1,0:T(8,128)(2,1)S(1)}, u32[]{:S(2)}, u32[]{:S(2)}) collective-permute-start(bf16[16,4096]{1,0:T(8,128)(2,1)S(1)} %get-tuple-element.31.refs_6_), channel_id=1, source_target_pairs={{0,4},{1,5},{4,8},{5,9},{8,12},{9,13},{12,14},{13,15},{14,10},{15,... | collective-permute-start | bytes 393224 | tf_op jit(solution)/shard_map/ppermute | solution.py:493
  70.8 5.2 %collective-permute-start.20 = (bf16[16,4096]{1,0:T(8,128)(2,1)S(1)}, bf16[16,4096]{1,0:T(8,128)(2,1)S(1)}, u32[]{:S(2)}, u32[]{:S(2)}) collective-permute-start(bf16[16,4096]{1,0:T(8,128)(2,1)S(1)} %get-tuple-element.32), channel_id=1, source_target_pairs={{0,2},{1,3},{4,0},{5,1},{8,4},{9,5},{12,8},{13,9},{14,12},{15,13},... | collective-permute-start | bytes 393224 | tf_op jit(solution)/shard_map/ppermute | solution.py:493
  71.8 5.6 %collective-permute-start.24 = (bf16[16,4096]{1,0:T(8,128)(2,1)S(1)}, bf16[16,4096]{1,0:T(8,128)(2,1)S(1)}, u32[]{:S(2)}, u32[]{:S(2)}) collective-permute-start(bf16[16,4096]{1,0:T(8,128)(2,1)S(1)} %get-tuple-element.34.refs_6_), channel_id=1, source_target_pairs={{0,2},{1,3},{4,0},{5,1},{8,4},{9,5},{12,8},{13,9},{14,12},{15,13},... | collective-permute-start | bytes 393224 | tf_op jit(solution)/shard_map/ppermute | solution.py:493
  73.0 5.2 %collective-permute-start.25 = (bf16[16,4096]{1,0:T(8,128)(2,1)S(1)}, bf16[16,4096]{1,0:T(8,128)(2,1)S(1)}, u32[]{:S(2)}, u32[]{:S(2)}) collective-permute-start(bf16[16,4096]{1,0:T(8,128)(2,1)S(1)} %get-tuple-element.36), channel_id=1, source_target_pairs={{0,4},{1,5},{4,8},{5,9},{8,12},{9,13},{12,14},{13,15},{14,10},{15,... | collective-permute-start | bytes 393224 | tf_op jit(solution)/shard_map/ppermute | solution.py:493
  76.1 10.3 %copy-start.7 = (bf16[8192]{0:T(1024)(128)(2,1)S(1)}, bf16[8192]{0:T(1024)(128)(2,1)}, u32[]{:S(2)}) copy-start(bf16[8192]{0:T(1024)(128)(2,1)} %param.15) | copy-start | bytes 49156
  76.1 6.4 %collective-permute-start.23 = (bf16[16,4096]{1,0:T(8,128)(2,1)S(1)}, bf16[16,4096]{1,0:T(8,128)(2,1)S(1)}, u32[]{:S(2)}, u32[]{:S(2)}) collective-permute-start(bf16[16,4096]{1,0:T(8,128)(2,1)S(1)} %get-tuple-element.35.refs_6_), channel_id=1, source_target_pairs={{0,4},{1,5},{4,8},{5,9},{8,12},{9,13},{12,14},{13,15},{14,10},{15,... | collective-permute-start | bytes 393224 | tf_op jit(solution)/shard_map/ppermute | solution.py:493
  78.3 5.9 %collective-permute-start.29 = (bf16[16,4096]{1,0:T(8,128)(2,1)S(1)}, bf16[16,4096]{1,0:T(8,128)(2,1)S(1)}, u32[]{:S(2)}, u32[]{:S(2)}) collective-permute-start(bf16[16,4096]{1,0:T(8,128)(2,1)S(1)} %get-tuple-element.37.refs_3_), channel_id=1, source_target_pairs={{0,2},{1,3},{4,0},{5,1},{8,4},{9,5},{12,8},{13,9},{14,12},{15,13},... | collective-permute-start | bytes 393224 | tf_op jit(solution)/shard_map/ppermute | solution.py:493
  80.1 6.3 %collective-permute-start.28 = (bf16[16,4096]{1,0:T(8,128)(2,1)S(1)}, bf16[16,4096]{1,0:T(8,128)(2,1)S(1)}, u32[]{:S(2)}, u32[]{:S(2)}) collective-permute-start(bf16[16,4096]{1,0:T(8,128)(2,1)S(1)} %get-tuple-element.39), channel_id=1, source_target_pairs={{0,4},{1,5},{4,8},{5,9},{8,12},{9,13},{12,14},{13,15},{14,10},{15,... | collective-permute-start | bytes 393224 | tf_op jit(solution)/shard_map/ppermute | solution.py:493
  80.4 6.0 %collective-permute-start.27 = (bf16[16,4096]{1,0:T(8,128)(2,1)S(1)}, bf16[16,4096]{1,0:T(8,128)(2,1)S(1)}, u32[]{:S(2)}, u32[]{:S(2)}) collective-permute-start(bf16[16,4096]{1,0:T(8,128)(2,1)S(1)} %get-tuple-element.38), channel_id=1, source_target_pairs={{0,2},{1,3},{4,0},{5,1},{8,4},{9,5},{12,8},{13,9},{14,12},{15,13},... | collective-permute-start | bytes 393224 | tf_op jit(solution)/shard_map/ppermute | solution.py:493
  84.3 5.0 %collective-permute-start.30 = (bf16[16,4096]{1,0:T(8,128)(2,1)S(1)}, bf16[16,4096]{1,0:T(8,128)(2,1)S(1)}, u32[]{:S(2)}, u32[]{:S(2)}) collective-permute-start(bf16[16,4096]{1,0:T(8,128)(2,1)S(1)} %add_blocks.15), channel_id=1, source_target_pairs={{0,2},{1,3},{4,0},{5,1},{8,4},{9,5},{12,8},{13,9},{14,12},{15,13},... | collective-permute-start | bytes 393224 | tf_op jit(solution)/shard_map/ppermute | solution.py:493
  86.1 5.0 %collective-permute-start.26 = (bf16[16,4096]{1,0:T(8,128)(2,1)S(1)}, bf16[16,4096]{1,0:T(8,128)(2,1)S(1)}, u32[]{:S(2)}, u32[]{:S(2)}) collective-permute-start(bf16[16,4096]{1,0:T(8,128)(2,1)S(1)} %add_blocks.14.refs_3_), channel_id=1, source_target_pairs={{0,4},{1,5},{4,8},{5,9},{8,12},{9,13},{12,14},{13,15},{14,10},{15,... | collective-permute-start | bytes 393224 | tf_op jit(solution)/shard_map/ppermute | solution.py:493

commit v9 on v8

--- a/solution.py
+++ b/solution.py
@@ -472,24 +472,20 @@
     right, left = [None] * HALVES, [None] * HALVES
     ordered = []
     for turn in range(last):
-        for h in range(HALVES):
-            steps_right = last - turn - (h == 1)
-            steps_left = last - turn - (h == 0)
+        chains = [(right, 1, 0), (left, -1, 1), (left, -1, 0), (right, 1, 1)]
+        if turn == 0:
+            chains = [chains[0], chains[2], chains[1], chains[3]]
+        groups = [[chain] for chain in chains] if turn < last - 1 else [chains[:2]]
+        for group in groups:
             sides = []
-            if steps_right > 0:
-                index = min(2 * steps_right, chips - 1)
-                sides.append((right, 1, index))
-            if steps_left > 0:
-                sides.append((left, -1, 2 * steps_left - 1))
-            if h == 1:
-                sides.reverse()
-            sums = add_blocks(
-                [(mine[h], theirs[h], index, chain[h]) for chain, _, index in sides],
-                own_rows,
-                ordered,
-            )
+            for chain, by, h in group:
+                longer = (by == 1) == (h == 0)
+                steps = last - turn - (not longer)
+                index = min(2 * steps, chips - 1) if by == 1 else 2 * steps - 1
+                sides.append((mine[h], theirs[h], index, chain[h]))
+            sums = add_blocks(sides, own_rows, ordered)
             ordered = [sums[0]]
-            for (chain, by, _), value in zip(sides, sums):
+            for (chain, by, h), value in zip(group, sums):
                 chain[h] = lax.ppermute(value, AXIS, ring(size, by))
     return list(zip(mine, theirs, right, left))
 

time: 92.2 us -> 91.3 us (level)
  starting transfers between devices: 29.9 us -> 28.8 us
    ppermute x2, waiting for transfers between devices: 0.14 us -> 1.38 us  [body(): theirs[h] = lax.ppermute(term[half:], AXIS, flip(size, 1))]
    ppermute x14, waiting for transfers between devices: 12.9 us -> 11.8 us  [scatter_rows(): chain[h] = lax.ppermute(value, AXIS, ring(size, by))]
    ppermute x14, starting transfers between devices: 15.1 us -> 14.1 us  [scatter_rows(): chain[h] = lax.ppermute(value, AXIS, ring(size, by))]
    pallas_call x23 -> x28, Pallas kernels: 12.1 us -> 12.1 us  [call(): pl.pallas_call(run, out_shape=out_shape, in_specs=[whole(pltpu.SMEM if op...]
  transfers between devices with their start and end apart: 31 -> 31, of which waited for: 22 -> 21; matrix products, arithmetic and copies ran while one was open for 3% -> 3% of each run, Pallas kernels for 23% -> 23%
where the time goes in v9:
time: 91.3 us; the launch traced here: 91.2 us
  waiting for transfers between devices  30.2 us (33%)
  starting transfers between devices  28.8 us (32%)
  Pallas kernels  26 us (28%)
  matrix products  4.84 us (5%)
  between operations  1.04 us (1%)
    ppermute x14, starting transfers between devices, scatter_rows(): chain[h] = lax.ppermute(value, AXIS, ring(size, by))  14.1 us
    pallas_call x28, Pallas kernels, call(): pl.pallas_call(run, out_shape=out_shape, in_specs=[whole(pltpu.SMEM if op...  12.1 us
    ppermute x14, waiting for transfers between devices, scatter_rows(): chain[h] = lax.ppermute(value, AXIS, ring(size, by))  11.8 us
    pallas_call x2, Pallas kernels, load_rows(): pl.pallas_call(kernel, out_shape=[jax.ShapeDtypeStruct(shape, weights[0]....  8.65 us
    ppermute x3, waiting for transfers between devices, gather_rows(): right = lax.ppermute(right, AXIS, ring(size, 1))  7.1 us
    ppermute x3, starting transfers between devices, gather_rows(): right = lax.ppermute(right, AXIS, ring(size, 1))  6.45 us
    pallas_call x1, Pallas kernels, stream_rows(): pl.pallas_call(kernel, out_shape=jax.ShapeDtypeStruct((batch_rows, width)...  5.27 us
    dot_general x2, matrix products, body(): jnp.dot(hidden, down_weight[:, h * width:(h + 1) * width], preferred_elem...  4.84 us
  transfers between devices with their start and end apart: 31, of which 21 were waited for; matrix products, arithmetic and copies ran while one was open for 3% of the time, Pallas kernels for 23%

profile of v9, /device:TPU:0, one launch (start us, length us, event | category | flops | bytes accessed | tf_op | source)
XLA Modules:
  0.0 91.2 jit_solution(16331414448108572898)
XLA Ops:
  0.6 3.1 %collective-permute-start = (bf16[16,8192]{1,0:T(8,128)(2,1)}, bf16[16,8192]{1,0:T(8,128)(2,1)S(1)}, u32[]{:S(2)}, u32[]{:S(2)}) collective-permute-start(bf16[16,8192]{1,0:T(8,128)(2,1)} %refs_8_.1), channel_id=1, source_target_pairs={{0,4},{1,5},{4,8},{5,9},{8,12},{9,13},{12,14},{13,15},{14,10},{15,... | collective-permute-start | bytes 786440 | tf_op jit(solution)/shard_map/ppermute | solution.py:138
  3.7 4.3 %load_rows.2.refs_1_ = bf16[3072,1792]{1,0:T(8,128)(2,1)S(1)} custom-call(bf16[8192,896]{1,0:T(8,128)(2,1)} %refs_0_.7, bf16[8192,896]{1,0:T(8,128)(2,1)} %refs_1_.5), custom_call_target="tpu_custom_call" | custom-call | bytes 22020096 | tf_op jit(solution)/shard_map/load_rows/pallas_call | solution.py:292
  8.0 2.1 %collective-permute-done.refs_0_ = bf16[16,8192]{1,0:T(8,128)(2,1)S(1)} collective-permute-done((bf16[16,8192]{1,0:T(8,128)(2,1)}, bf16[16,8192]{1,0:T(8,128)(2,1)S(1)}, u32[]{:S(2)}, u32[]{:S(2)}) %collective-permute-start) | collective-permute-done | bytes 262176 | tf_op jit(solution)/shard_map/ppermute | solution.py:138
  10.2 1.8 %collective-permute-start.2 = (bf16[16,8192]{1,0:T(8,128)(2,1)S(1)}, bf16[16,8192]{1,0:T(8,128)(2,1)S(1)}, u32[]{:S(2)}, u32[]{:S(2)}) collective-permute-start(bf16[16,8192]{1,0:T(8,128)(2,1)S(1)} %pass_on.2.refs_2_), channel_id=1, source_target_pairs={{0,4},{1,5},{4,8},{5,9},{8,12},{9,13},{12,14},{13,15},{14,10},{15,... | collective-permute-start | bytes 786440 | tf_op jit(solution)/shard_map/ppermute | solution.py:138
  12.3 4.3 %load_rows.3.refs_1_ = bf16[3072,1792]{1,0:T(8,128)(2,1)S(1)} custom-call(bf16[8192,896]{1,0:T(8,128)(2,1)} %refs_0_.7, bf16[8192,896]{1,0:T(8,128)(2,1)} %refs_1_.5, bf16[16,8192]{1,0:T(8,128)(2,1)S(1)} %pass_on.2.refs_2_), custom_call_target="tpu_custom_call" | custom-call | bytes 22020096 | tf_op jit(solution)/shard_map/load_rows/pallas_call | solution.py:292
  16.7 1.0 %collective-permute-done.2.refs_0_.refs_2_ = bf16[16,8192]{1,0:T(8,128)(2,1)S(1)} collective-permute-done((bf16[16,8192]{1,0:T(8,128)(2,1)S(1)}, bf16[16,8192]{1,0:T(8,128)(2,1)S(1)}, u32[]{:S(2)}, u32[]{:S(2)}) %collective-permute-start.2) | collective-permute-done | bytes 262176 | tf_op jit(solution)/shard_map/ppermute | solution.py:138
  17.8 1.5 %collective-permute-start.4 = (bf16[16,8192]{1,0:T(8,128)(2,1)S(1)}, bf16[16,8192]{1,0:T(8,128)(2,1)S(1)}, u32[]{:S(2)}, u32[]{:S(2)}) collective-permute-start(bf16[16,8192]{1,0:T(8,128)(2,1)S(1)} %pass_on.3), channel_id=1, source_target_pairs={{0,4},{1,5},{4,8},{5,9},{8,12},{9,13},{12,14},{13,15},{14,10},{15,... | collective-permute-start | bytes 786440 | tf_op jit(solution)/shard_map/ppermute | solution.py:138
  20.4 3.9 %collective-permute-done.4.refs_4_.refs_0_ = bf16[16,8192]{1,0:T(8,128)(2,1)S(1)} collective-permute-done((bf16[16,8192]{1,0:T(8,128)(2,1)S(1)}, bf16[16,8192]{1,0:T(8,128)(2,1)S(1)}, u32[]{:S(2)}, u32[]{:S(2)}) %collective-permute-start.4) | collective-permute-done | bytes 262176 | tf_op jit(solution)/shard_map/ppermute | solution.py:138
  24.4 1.3 %collective-permute-done.5.refs_5_.refs_0_ = bf16[16,8192]{1,0:T(8,128)(2,1)S(1)} collective-permute-done((bf16[16,8192]{1,0:T(8,128)(2,1)S(1)}, bf16[16,8192]{1,0:T(8,128)(2,1)S(1)}, u32[]{:S(2)}, u32[]{:S(2)}) %collective-permute-start.5) | collective-permute-done | bytes 262176 | tf_op jit(solution)/shard_map/ppermute | solution.py:139
  25.9 1.6 %collective-permute-start.6 = (bf16[16,4096]{1,0:T(8,128)(2,1)S(1)}, bf16[16,4096]{1,0:T(8,128)(2,1)S(1)}, u32[]{:S(2)}, u32[]{:S(2)}) collective-permute-start(bf16[16,4096]{1,0:T(8,128)(2,1)S(1)} %column_half.2), channel_id=1, source_target_pairs={{0,4},{1,5},{4,8},{5,9},{8,12},{9,13},{12,14},{13,15},{14,10},{15,... | collective-permute-start | bytes 393224 | tf_op jit(solution)/shard_map/ppermute | solution.py:151
  28.0 3.8 %collective-permute-done.6.refs_0_ = bf16[16,4096]{1,0:T(8,128)(2,1)S(1)} collective-permute-done((bf16[16,4096]{1,0:T(8,128)(2,1)S(1)}, bf16[16,4096]{1,0:T(8,128)(2,1)S(1)}, u32[]{:S(2)}, u32[]{:S(2)}) %collective-permute-start.6) | collective-permute-done | bytes 131104 | tf_op jit(solution)/shard_map/ppermute | solution.py:151
  31.8 1.4 %collective-permute-done.7.refs_1_ = bf16[16,4096]{1,0:T(8,128)(2,1)S(1)} collective-permute-done((bf16[16,4096]{1,0:T(8,128)(2,1)S(1)}, bf16[16,4096]{1,0:T(8,128)(2,1)S(1)}, u32[]{:S(2)}, u32[]{:S(2)}) %collective-permute-start.7) | collective-permute-done | bytes 131104 | tf_op jit(solution)/shard_map/ppermute | solution.py:152
  33.3 1.5 %collective-permute-done.10.refs_5_ = bf16[16,8192]{1,0:T(8,128)(2,1)S(1)} collective-permute-done((bf16[16,8192]{1,0:T(8,128)(2,1)S(1)}, bf16[16,8192]{1,0:T(8,128)(2,1)S(1)}, u32[]{:S(2)}, u32[]{:S(2)}) %collective-permute-start.10) | collective-permute-done | bytes 262176 | tf_op jit(solution)/shard_map/ppermute | solution.py:157
  34.8 2.6 %shrink_rows.1 = (bf16[256,8192]{1,0:T(8,128)(2,1)S(1)}, bf16[256,64]{1,0:T(8,128)(2,1)S(1)}) custom-call(bf16[16,8192]{1,0:T(8,128)(2,1)S(1)} %copy-done.1, bf16[96,8192]{1,0:T(8,128)(2,1)S(1)} %join_pieces.2.refs_1_, bf16[16,8192]{1,0:T(8,128)(2,1)S(1)} %join_pieces.3.refs_2_, bf16[16,8192]{1,0:T(8,128)(2,1)S(1)} %collective-permute-done.8.refs_3_, ...), custom_call_target="tpu_custom_call" | custom-call | flops 268435456 | bytes 8388608 | tf_op jit(solution)/shard_map/shrink_rows/pallas_call | solution.py:78
  37.6 1.1 %collective-permute-done.11.refs_1_ = bf16[256,64]{1,0:T(8,128)(2,1)S(1)} collective-permute-done((bf16[256,64]{1,0:T(8,128)(2,1)S(1)}, bf16[256,64]{1,0:T(8,128)(2,1)S(1)}, u32[]{:S(2)}, u32[]{:S(2)}) %collective-permute-start.11) | collective-permute-done | bytes 32800 | tf_op jit(solution)/shard_map/ppermute | solution.py:552
  39.3 3.0 %mixed_rows.2.refs_2_ = f32[256,1792]{1,0:T(8,128)S(1)} custom-call(bf16[256,8192]{1,0:T(8,128)(2,1)S(1)} %get-tuple-element.15.refs_0_.rows_ref, bf16[3072,1792]{1,0:T(8,128)(2,1)S(1)} %load_rows.2.refs_1_, bf16[256,64]{1,0:T(8,128)(2,1)S(1)} %add_coefficients.3.refs_2_.refs_0_), custom_call_target="tpu_custom_call" | custom-call | flops 2818572288 | bytes 11010048 | tf_op jit(solution)/shard_map/mixed_rows/pallas_call | solution.py:78
  42.3 0.8 collective-permute-done.12.refs_1_
  43.1 1.6 %collective-permute-start.13 = (bf16[256,64]{1,0:T(8,128)(2,1)S(1)}, bf16[256,64]{1,0:T(8,128)(2,1)S(1)}, u32[]{:S(2)}, u32[]{:S(2)}) collective-permute-start(bf16[256,64]{1,0:T(8,128)(2,1)S(1)} %add_coefficients.4.refs_3_.refs_0_), channel_id=1, source_target_pairs={{0,4},{1,5},{2,6},{3,7},{4,0},{5,1},{6,2},{7,3},{8,12},{9,13},{10,... | collective-permute-start | bytes 98312 | tf_op jit(solution)/shard_map/ppermute | solution.py:552
  44.8 3.0 %mixed_rows.3.refs_2_ = f32[256,1792]{1,0:T(8,128)S(1)} custom-call(bf16[256,8192]{1,0:T(8,128)(2,1)S(1)} %get-tuple-element.15.refs_0_.rows_ref, bf16[3072,1792]{1,0:T(8,128)(2,1)S(1)} %load_rows.3.refs_1_, f32[256,1792]{1,0:T(8,128)S(1)} %mixed_rows.2.refs_2_, bf16[256,64]{1,0:T(8,128)(2,1)S(1)} %add_coefficients.4.refs_3_.refs_0_), custom_call_target="tpu_custom_call" | custom-call | flops 2818572288 | bytes 11010048 | tf_op jit(solution)/shard_map/mixed_rows/pallas_call | solution.py:78
  47.9 2.3 %collective-permute-start.14 = (bf16[256,64]{1,0:T(8,128)(2,1)S(1)}, bf16[256,64]{1,0:T(8,128)(2,1)S(1)}, u32[]{:S(2)}, u32[]{:S(2)}) collective-permute-start(bf16[256,64]{1,0:T(8,128)(2,1)S(1)} %add_coefficients.5.refs_3_.refs_0_), channel_id=1, source_target_pairs={{0,8},{1,9},{2,10},{3,11},{4,12},{5,13},{6,14},{7,15},{8,0},{9,1},... | collective-permute-start | bytes 98312 | tf_op jit(solution)/shard_map/ppermute | solution.py:552
  50.1 5.3 %stream_rows.1.refs_5_ = f32[256,1792]{1,0:T(8,128)S(1)} custom-call(bf16[256,8192]{1,0:T(8,128)(2,1)S(1)} %get-tuple-element.15.refs_0_.rows_ref, bf16[8192,896]{1,0:T(8,128)(2,1)} %refs_0_.7, bf16[8192,896]{1,0:T(8,128)(2,1)} %refs_1_.5, f32[256,1792]{1,0:T(8,128)S(1)} %mixed_rows.3.refs_2_, bf16[256,64]{1,0:T(8,128)(2,1)S(1)} %add_coefficients.5.refs_3_.refs_0_), custom_call_target="tpu_custom_call" | custom-call | flops 1879048192 | bytes 14680064 | tf_op jit(solution)/shard_map/stream_rows/pallas_call | solution.py:395
  55.4 1.0 %hidden_rows.1 = bf16[256,896]{1,0:T(8,128)(2,1)S(1)} custom-call(bf16[256,64]{1,0:T(8,128)(2,1)S(1)} %add_coefficients.5.refs_3_.refs_0_, bf16[256,64]{1,0:T(8,128)(2,1)S(1)} %collective-permute-done.14.refs_1_, bf16[256,256]{1,0:T(8,128)(2,1)S(1)} %get-tuple-element.16.refs_2_, bf16[256,1024]{1,0:T(8,128)(2,1)S(1)} %get-tuple-element.17.refs_3_, ...), custom_call_target="tpu_custom_call" | custom-call | flops 469762048 | bytes 1835008 | tf_op jit(solution)/shard_map/hidden_rows/pallas_call | solution.py:78
  56.4 2.4 %fusion.4.refs_0_ = bf16[256,4096]{1,0:T(8,128)(2,1)S(1)} fusion(bf16[256,896]{1,0:T(8,128)(2,1)S(1)} %hidden_rows.1, bf16[896,8192]{1,0:T(8,128)(2,1)S(1)} %bitcast.17), kind=kOutput, calls=%fused_computation.4 | convolution fusion | flops 1880096768 | bytes 9895936 | tf_op jit(solution)/shard_map/dot_general | solution.py:569
  59.0 2.4 %fusion.7.refs_0_.refs_3_.refs_4_ = bf16[256,4096]{1,0:T(8,128)(2,1)S(1)} fusion(bf16[256,896]{1,0:T(8,128)(2,1)S(1)} %hidden_rows.1, bf16[896,8192]{1,0:T(8,128)(2,1)S(1)} %bitcast.17), kind=kOutput, calls=%fused_computation.5 | convolution fusion | flops 1880096768 | bytes 9895936 | tf_op jit(solution)/shard_map/dot_general | solution.py:569
  62.2 0.8 collective-permute-start.16
  63.0 1.4 %collective-permute-done.17.refs_1_.refs_4_.refs_5_ = bf16[128,4096]{1,0:T(8,128)(2,1)S(1)} collective-permute-done((bf16[128,4096]{1,0:T(8,128)(2,1)S(1)}, bf16[128,4096]{1,0:T(8,128)(2,1)S(1)}, u32[]{:S(2)}, u32[]{:S(2)}) %collective-permute-start.17) | collective-permute-done | bytes 1048608 | tf_op jit(solution)/shard_map/ppermute | solution.py:575
  64.5 0.8 collective-permute-start.21
  65.3 0.8 collective-permute-start.20
  66.1 1.3 %collective-permute-start.19 = (bf16[16,4096]{1,0:T(8,128)(2,1)S(1)}, bf16[16,4096]{1,0:T(8,128)(2,1)S(1)}, u32[]{:S(2)}, u32[]{:S(2)}) collective-permute-start(bf16[16,4096]{1,0:T(8,128)(2,1)S(1)} %add_blocks.16.refs_3_), channel_id=1, source_target_pairs={{0,4},{1,5},{4,8},{5,9},{8,12},{9,13},{12,14},{13,15},{14,10},{15,... | collective-permute-start | bytes 393224 | tf_op jit(solution)/shard_map/ppermute | solution.py:489
  67.7 1.1 %collective-permute-start.18 = (bf16[16,4096]{1,0:T(8,128)(2,1)S(1)}, bf16[16,4096]{1,0:T(8,128)(2,1)S(1)}, u32[]{:S(2)}, u32[]{:S(2)}) collective-permute-start(bf16[16,4096]{1,0:T(8,128)(2,1)S(1)} %add_blocks.17.refs_3_), channel_id=1, source_target_pairs={{0,4},{1,5},{4,8},{5,9},{8,12},{9,13},{12,14},{13,15},{14,10},{15,... | collective-permute-start | bytes 393224 | tf_op jit(solution)/shard_map/ppermute | solution.py:489
  68.8 2.1 %collective-permute-done.21.refs_2_ = bf16[16,4096]{1,0:T(8,128)(2,1)S(1)} collective-permute-done((bf16[16,4096]{1,0:T(8,128)(2,1)S(1)}, bf16[16,4096]{1,0:T(8,128)(2,1)S(1)}, u32[]{:S(2)}, u32[]{:S(2)}) %collective-permute-start.21) | collective-permute-done | bytes 131104 | tf_op jit(solution)/shard_map/ppermute | solution.py:489
  70.9 0.8 collective-permute-start.23
  71.7 1.8 %collective-permute-done.20.refs_2_ = bf16[16,4096]{1,0:T(8,128)(2,1)S(1)} collective-permute-done((bf16[16,4096]{1,0:T(8,128)(2,1)S(1)}, bf16[16,4096]{1,0:T(8,128)(2,1)S(1)}, u32[]{:S(2)}, u32[]{:S(2)}) %collective-permute-start.20) | collective-permute-done | bytes 131104 | tf_op jit(solution)/shard_map/ppermute | solution.py:489
  73.6 0.8 collective-permute-start.26
  74.5 1.3 %collective-permute-start.25 = (bf16[16,4096]{1,0:T(8,128)(2,1)S(1)}, bf16[16,4096]{1,0:T(8,128)(2,1)S(1)}, u32[]{:S(2)}, u32[]{:S(2)}) collective-permute-start(bf16[16,4096]{1,0:T(8,128)(2,1)S(1)} %add_blocks.20.refs_3_), channel_id=1, source_target_pairs={{0,4},{1,5},{4,8},{5,9},{8,12},{9,13},{12,14},{13,15},{14,10},{15,... | collective-permute-start | bytes 393224 | tf_op jit(solution)/shard_map/ppermute | solution.py:489
  75.9 0.6 collective-permute-done.23.refs_2_
  76.6 0.8 collective-permute-start.24
  77.4 1.2 %collective-permute-start.22 = (bf16[16,4096]{1,0:T(8,128)(2,1)S(1)}, bf16[16,4096]{1,0:T(8,128)(2,1)S(1)}, u32[]{:S(2)}, u32[]{:S(2)}) collective-permute-start(bf16[16,4096]{1,0:T(8,128)(2,1)S(1)} %add_blocks.21.refs_3_), channel_id=1, source_target_pairs={{0,4},{1,5},{4,8},{5,9},{8,12},{9,13},{12,14},{13,15},{14,10},{15,... | collective-permute-start | bytes 393224 | tf_op jit(solution)/shard_map/ppermute | solution.py:489
  78.6 1.5 %collective-permute-done.26.refs_2_ = bf16[16,4096]{1,0:T(8,128)(2,1)S(1)} collective-permute-done((bf16[16,4096]{1,0:T(8,128)(2,1)S(1)}, bf16[16,4096]{1,0:T(8,128)(2,1)S(1)}, u32[]{:S(2)}, u32[]{:S(2)}) %collective-permute-start.26) | collective-permute-done | bytes 131104 | tf_op jit(solution)/shard_map/ppermute | solution.py:489
  80.2 0.8 collective-permute-start.28
  81.1 1.3 %collective-permute-start.29 = (bf16[16,4096]{1,0:T(8,128)(2,1)S(1)}, bf16[16,4096]{1,0:T(8,128)(2,1)S(1)}, u32[]{:S(2)}, u32[]{:S(2)}) collective-permute-start(bf16[16,4096]{1,0:T(8,128)(2,1)S(1)} %add_blocks.24.refs_6_), channel_id=1, source_target_pairs={{0,4},{1,5},{4,8},{5,9},{8,12},{9,13},{12,14},{13,15},{14,10},{15,... | collective-permute-start | bytes 393224 | tf_op jit(solution)/shard_map/ppermute | solution.py:489
  82.4 0.6 collective-permute-done.24.refs_5_
  83.0 0.8 collective-permute-done.22.refs_2_
  83.9 1.3 %collective-permute-start.27 = (bf16[16,4096]{1,0:T(8,128)(2,1)S(1)}, bf16[16,4096]{1,0:T(8,128)(2,1)S(1)}, u32[]{:S(2)}, u32[]{:S(2)}) collective-permute-start(bf16[16,4096]{1,0:T(8,128)(2,1)S(1)} %get-tuple-element.18), channel_id=1, source_target_pairs={{0,4},{1,5},{4,8},{5,9},{8,12},{9,13},{12,14},{13,15},{14,10},{15,... | collective-permute-start | bytes 393224 | tf_op jit(solution)/shard_map/ppermute | solution.py:489
  85.2 0.8 collective-permute-start.30
  86.6 2.3 %collective-permute-done.27.refs_2_ = bf16[16,4096]{1,0:T(8,128)(2,1)S(1)} collective-permute-done((bf16[16,4096]{1,0:T(8,128)(2,1)S(1)}, bf16[16,4096]{1,0:T(8,128)(2,1)S(1)}, u32[]{:S(2)}, u32[]{:S(2)}) %collective-permute-start.27) | collective-permute-done | bytes 131104 | tf_op jit(solution)/shard_map/ppermute | solution.py:489
  88.9 1.2 %collective-permute-done.30.refs_7_ = bf16[16,4096]{1,0:T(8,128)(2,1)S(1)} collective-permute-done((bf16[16,4096]{1,0:T(8,128)(2,1)S(1)}, bf16[16,4096]{1,0:T(8,128)(2,1)S(1)}, u32[]{:S(2)}, u32[]{:S(2)}) %collective-permute-start.30) | collective-permute-done | bytes 131104 | tf_op jit(solution)/shard_map/ppermute | solution.py:489
  90.1 1.0 %finish_rows.1 = (bf16[16,8192]{1,0:T(8,128)(2,1)}, bf16[16,8192]{1,0:T(8,128)(2,1)}) custom-call(bf16[256,4096]{1,0:T(8,128)(2,1)S(1)} %fusion.4.refs_0_, bf16[128,4096]{1,0:T(8,128)(2,1)S(1)} %collective-permute-done.15.refs_1_, bf16[16,4096]{1,0:T(8,128)(2,1)S(1)} %collective-permute-done.27.refs_2_, ...), custom_call_target="tpu_custom_call" | custom-call | tf_op jit(solution)/shard_map/finish_rows/pallas_call | solution.py:78
  (75 shorter events, 5.4 us)
Async XLA Ops:
  0.6 9.5 %collective-permute-start = (bf16[16,8192]{1,0:T(8,128)(2,1)}, bf16[16,8192]{1,0:T(8,128)(2,1)S(1)}, u32[]{:S(2)}, u32[]{:S(2)}) collective-permute-start(bf16[16,8192]{1,0:T(8,128)(2,1)} %refs_8_.1), channel_id=1, source_target_pairs={{0,4},{1,5},{4,8},{5,9},{8,12},{9,13},{12,14},{13,15},{14,10},{15,... | collective-permute-start | bytes 786440 | tf_op jit(solution)/shard_map/ppermute | solution.py:138
  3.7 8.3 %collective-permute-start.1 = (bf16[16,8192]{1,0:T(8,128)(2,1)}, bf16[16,8192]{1,0:T(8,128)(2,1)S(1)}, u32[]{:S(2)}, u32[]{:S(2)}) collective-permute-start(bf16[16,8192]{1,0:T(8,128)(2,1)} %refs_8_.1), channel_id=1, source_target_pairs={{0,2},{1,3},{4,0},{5,1},{8,4},{9,5},{12,8},{13,9},{14,12},{15,13},... | collective-permute-start | bytes 786440 | tf_op jit(solution)/shard_map/ppermute | solution.py:139
  10.2 7.5 %collective-permute-start.2 = (bf16[16,8192]{1,0:T(8,128)(2,1)S(1)}, bf16[16,8192]{1,0:T(8,128)(2,1)S(1)}, u32[]{:S(2)}, u32[]{:S(2)}) collective-permute-start(bf16[16,8192]{1,0:T(8,128)(2,1)S(1)} %pass_on.2.refs_2_), channel_id=1, source_target_pairs={{0,4},{1,5},{4,8},{5,9},{8,12},{9,13},{12,14},{13,15},{14,10},{15,... | collective-permute-start | bytes 786440 | tf_op jit(solution)/shard_map/ppermute | solution.py:138
  12.0 7.2 %collective-permute-start.3 = (bf16[16,8192]{1,0:T(8,128)(2,1)S(1)}, bf16[16,8192]{1,0:T(8,128)(2,1)S(1)}, u32[]{:S(2)}, u32[]{:S(2)}) collective-permute-start(bf16[16,8192]{1,0:T(8,128)(2,1)S(1)} %collective-permute-done.1.refs_1_), channel_id=1, source_target_pairs={{0,2},{1,3},{4,0},{5,1},{8,4},{9,5},{12,8},{13,9},{14,12},{15,13},... | collective-permute-start | bytes 786440 | tf_op jit(solution)/shard_map/ppermute | solution.py:139
  16.6 3.2 %copy-start.2 = (bf16[1,8192,64]{1,2,0:T(8,128)(2,1)S(1)}, bf16[1,8192,64]{1,2,0:T(8,128)(2,1)}, u32[]{:S(2)}) copy-start(bf16[1,8192,64]{1,2,0:T(8,128)(2,1)} %param.16) | copy-start | bytes 3145732
  16.6 3.2 %copy-start.3 = (s32[32]{0:T(128)S(1)}, s32[32]{0:T(128)}, u32[]{:S(2)}) copy-start(s32[32]{0:T(128)} %param.20) | copy-start | bytes 388
  16.6 3.2 %copy-start.4 = (s32[32]{0:T(128)S(1)}, s32[32]{0:T(128)}, u32[]{:S(2)}) copy-start(s32[32]{0:T(128)} %param.21) | copy-start | bytes 388
  16.6 3.2 %copy-start.5 = (s32[16]{0:T(128)S(1)}, s32[16]{0:T(128)}, u32[]{:S(2)}) copy-start(s32[16]{0:T(128)} %param.18) | copy-start | bytes 196
  16.7 3.2 %copy-start.6 = (s32[16]{0:T(128)S(1)}, s32[16]{0:T(128)}, u32[]{:S(2)}) copy-start(s32[16]{0:T(128)} %param.19) | copy-start | bytes 196
  16.7 11.3 %copy-start.1 = (bf16[16,8192]{1,0:T(8,128)(2,1)S(1)}, bf16[16,8192]{1,0:T(8,128)(2,1)}, u32[]{:S(2)}) copy-start(bf16[16,8192]{1,0:T(8,128)(2,1)} %refs_8_.1) | copy-start | bytes 786436
  17.8 6.6 %collective-permute-start.4 = (bf16[16,8192]{1,0:T(8,128)(2,1)S(1)}, bf16[16,8192]{1,0:T(8,128)(2,1)S(1)}, u32[]{:S(2)}, u32[]{:S(2)}) collective-permute-start(bf16[16,8192]{1,0:T(8,128)(2,1)S(1)} %pass_on.3), channel_id=1, source_target_pairs={{0,4},{1,5},{4,8},{5,9},{8,12},{9,13},{12,14},{13,15},{14,10},{15,... | collective-permute-start | bytes 786440 | tf_op jit(solution)/shard_map/ppermute | solution.py:138
  19.3 6.4 %collective-permute-start.5 = (bf16[16,8192]{1,0:T(8,128)(2,1)S(1)}, bf16[16,8192]{1,0:T(8,128)(2,1)S(1)}, u32[]{:S(2)}, u32[]{:S(2)}) collective-permute-start(bf16[16,8192]{1,0:T(8,128)(2,1)S(1)} %collective-permute-done.3.refs_3_), channel_id=1, source_target_pairs={{0,2},{1,3},{4,0},{5,1},{8,4},{9,5},{12,8},{13,9},{14,12},{15,13},... | collective-permute-start | bytes 786440 | tf_op jit(solution)/shard_map/ppermute | solution.py:139
  25.8 9.0 %collective-permute-start.9 = (bf16[96,8192]{1,0:T(8,128)(2,1)S(1)}, bf16[96,8192]{1,0:T(8,128)(2,1)S(1)}, u32[]{:S(2)}, u32[]{:S(2)}) collective-permute-start(bf16[96,8192]{1,0:T(8,128)(2,1)S(1)} %join_pieces.2.refs_1_), channel_id=1, source_target_pairs={{0,1},{1,0},{2,3},{3,2},{4,5},{5,4},{6,7},{7,6},{8,9},{9,8},{10,11... | collective-permute-start | bytes 4718600 | tf_op jit(solution)/shard_map/ppermute | solution.py:148
  25.9 5.9 %collective-permute-start.6 = (bf16[16,4096]{1,0:T(8,128)(2,1)S(1)}, bf16[16,4096]{1,0:T(8,128)(2,1)S(1)}, u32[]{:S(2)}, u32[]{:S(2)}) collective-permute-start(bf16[16,4096]{1,0:T(8,128)(2,1)S(1)} %column_half.2), channel_id=1, source_target_pairs={{0,4},{1,5},{4,8},{5,9},{8,12},{9,13},{12,14},{13,15},{14,10},{15,... | collective-permute-start | bytes 393224 | tf_op jit(solution)/shard_map/ppermute | solution.py:151
  27.5 5.7 %collective-permute-start.7 = (bf16[16,4096]{1,0:T(8,128)(2,1)S(1)}, bf16[16,4096]{1,0:T(8,128)(2,1)S(1)}, u32[]{:S(2)}, u32[]{:S(2)}) collective-permute-start(bf16[16,4096]{1,0:T(8,128)(2,1)S(1)} %column_half.3), channel_id=1, source_target_pairs={{0,2},{1,3},{4,0},{5,1},{8,4},{9,5},{12,8},{13,9},{14,12},{15,13},... | collective-permute-start | bytes 393224 | tf_op jit(solution)/shard_map/ppermute | solution.py:152
  28.0 5.3 %collective-permute-start.8 = (bf16[16,8192]{1,0:T(8,128)(2,1)S(1)}, bf16[16,8192]{1,0:T(8,128)(2,1)S(1)}, u32[]{:S(2)}, u32[]{:S(2)}) collective-permute-start(bf16[16,8192]{1,0:T(8,128)(2,1)S(1)} %copy-done.1), channel_id=1, source_target_pairs={{0,1},{1,0},{2,3},{3,2},{4,5},{5,4},{6,7},{7,6},{8,9},{9,8},{10,11... | collective-permute-start | bytes 786440 | tf_op jit(solution)/shard_map/ppermute | solution.py:141
  33.2 1.6 %collective-permute-start.10 = (bf16[16,8192]{1,0:T(8,128)(2,1)S(1)}, bf16[16,8192]{1,0:T(8,128)(2,1)S(1)}, u32[]{:S(2)}, u32[]{:S(2)}) collective-permute-start(bf16[16,8192]{1,0:T(8,128)(2,1)S(1)} %join_pieces.3.refs_2_), channel_id=1, source_target_pairs={{0,1},{1,0},{2,3},{3,2},{4,5},{5,4},{6,7},{7,6},{8,9},{9,8},{10,11... | collective-permute-start | bytes 786440 | tf_op jit(solution)/shard_map/ppermute | solution.py:157
  37.4 1.3 %collective-permute-start.11 = (bf16[256,64]{1,0:T(8,128)(2,1)S(1)}, bf16[256,64]{1,0:T(8,128)(2,1)S(1)}, u32[]{:S(2)}, u32[]{:S(2)}) collective-permute-start(bf16[256,64]{1,0:T(8,128)(2,1)S(1)} %get-tuple-element.14.refs_0_), channel_id=1, source_target_pairs={{0,1},{1,0},{2,3},{3,2},{4,5},{5,4},{6,7},{7,6},{8,9},{9,8},{10,11... | collective-permute-start | bytes 98312 | tf_op jit(solution)/shard_map/ppermute | solution.py:552
  38.8 4.3 %collective-permute-start.12 = (bf16[256,64]{1,0:T(8,128)(2,1)S(1)}, bf16[256,64]{1,0:T(8,128)(2,1)S(1)}, u32[]{:S(2)}, u32[]{:S(2)}) collective-permute-start(bf16[256,64]{1,0:T(8,128)(2,1)S(1)} %add_coefficients.3.refs_2_.refs_0_), channel_id=1, source_target_pairs={{0,2},{1,3},{2,0},{3,1},{4,6},{5,7},{6,4},{7,5},{8,10},{9,11},{10,... | collective-permute-start | bytes 98312 | tf_op jit(solution)/shard_map/ppermute | solution.py:552
  43.1 4.7 %collective-permute-start.13 = (bf16[256,64]{1,0:T(8,128)(2,1)S(1)}, bf16[256,64]{1,0:T(8,128)(2,1)S(1)}, u32[]{:S(2)}, u32[]{:S(2)}) collective-permute-start(bf16[256,64]{1,0:T(8,128)(2,1)S(1)} %add_coefficients.4.refs_3_.refs_0_), channel_id=1, source_target_pairs={{0,4},{1,5},{2,6},{3,7},{4,0},{5,1},{6,2},{7,3},{8,12},{9,13},{10,... | collective-permute-start | bytes 98312 | tf_op jit(solution)/shard_map/ppermute | solution.py:552
  47.8 8.6 %slice-start = ((s8[14680064]{0:T(1024)(128)(4,1)}), s8[4194304]{0:T(1024)(128)(4,1)S(1)}, s32[]{:S(2)}) async-start(s8[14680064]{0:T(1024)(128)(4,1)} %bitcast.16), calls=%async_computation | async-start | bytes 8388608
  47.8 7.6 %copy-start = (bf16[16,64,896]{2,1,0:T(8,128)(2,1)S(1)}, bf16[16,64,896]{2,1,0:T(8,128)(2,1)}, u32[]{:S(2)}) copy-start(bf16[16,64,896]{2,1,0:T(8,128)(2,1)} %param.17) | copy-start | bytes 5505028
  47.8 8.6 %slice-start.1 = ((s8[14680064]{0:T(1024)(128)(4,1)}), s8[4194304]{0:T(1024)(128)(4,1)S(1)}, s32[]{:S(2)}) async-start(s8[14680064]{0:T(1024)(128)(4,1)} %bitcast.16), calls=%async_computation.1 | async-start | bytes 8388608
  47.8 8.6 %slice-start.2 = ((s8[14680064]{0:T(1024)(128)(4,1)}), s8[4194304]{0:T(1024)(128)(4,1)S(1)}, s32[]{:S(2)}) async-start(s8[14680064]{0:T(1024)(128)(4,1)} %bitcast.16), calls=%async_computation.2 | async-start | bytes 8388608
  47.8 8.6 %slice-start.3 = ((s8[14680064]{0:T(1024)(128)(4,1)}), s8[2097152]{0:T(1024)(128)(4,1)S(1)}, s32[]{:S(2)}) async-start(s8[14680064]{0:T(1024)(128)(4,1)} %bitcast.16), calls=%async_computation.3 | async-start | bytes 4194304
  47.9 7.5 %collective-permute-start.14 = (bf16[256,64]{1,0:T(8,128)(2,1)S(1)}, bf16[256,64]{1,0:T(8,128)(2,1)S(1)}, u32[]{:S(2)}, u32[]{:S(2)}) collective-permute-start(bf16[256,64]{1,0:T(8,128)(2,1)S(1)} %add_coefficients.5.refs_3_.refs_0_), channel_id=1, source_target_pairs={{0,8},{1,9},{2,10},{3,11},{4,12},{5,13},{6,14},{7,15},{8,0},{9,1},... | collective-permute-start | bytes 98312 | tf_op jit(solution)/shard_map/ppermute | solution.py:552
  59.0 3.2 %collective-permute-start.15 = (bf16[128,4096]{1,0:T(8,128)(2,1)S(1)}, bf16[128,4096]{1,0:T(8,128)(2,1)S(1)}, u32[]{:S(2)}, u32[]{:S(2)}) collective-permute-start(bf16[128,4096]{1,0:T(8,128)(2,1)S(1)} %slice.16), channel_id=1, source_target_pairs={{0,1},{1,0},{2,3},{3,2},{4,5},{5,4},{6,7},{7,6},{8,9},{9,8},{10,11... | collective-permute-start | bytes 3145736 | tf_op jit(solution)/shard_map/ppermute | solution.py:575
  61.6 2.8 %collective-permute-start.17 = (bf16[128,4096]{1,0:T(8,128)(2,1)S(1)}, bf16[128,4096]{1,0:T(8,128)(2,1)S(1)}, u32[]{:S(2)}, u32[]{:S(2)}) collective-permute-start(bf16[128,4096]{1,0:T(8,128)(2,1)S(1)} %slice.17), channel_id=1, source_target_pairs={{0,1},{1,0},{2,3},{3,2},{4,5},{5,4},{6,7},{7,6},{8,9},{9,8},{10,11... | collective-permute-start | bytes 3145736 | tf_op jit(solution)/shard_map/ppermute | solution.py:575
  62.2 5.5 %collective-permute-start.16 = (bf16[16,4096]{1,0:T(8,128)(2,1)S(1)}, bf16[16,4096]{1,0:T(8,128)(2,1)S(1)}, u32[]{:S(2)}, u32[]{:S(2)}) collective-permute-start(bf16[16,4096]{1,0:T(8,128)(2,1)S(1)} %add_blocks.13.refs_2_), channel_id=1, source_target_pairs={{0,4},{1,5},{4,8},{5,9},{8,12},{9,13},{12,14},{13,15},{14,10},{15,... | collective-permute-start | bytes 393224 | tf_op jit(solution)/shard_map/ppermute | solution.py:489
  64.5 6.4 %collective-permute-start.21 = (bf16[16,4096]{1,0:T(8,128)(2,1)S(1)}, bf16[16,4096]{1,0:T(8,128)(2,1)S(1)}, u32[]{:S(2)}, u32[]{:S(2)}) collective-permute-start(bf16[16,4096]{1,0:T(8,128)(2,1)S(1)} %add_blocks.15.refs_2_), channel_id=1, source_target_pairs={{0,2},{1,3},{4,0},{5,1},{8,4},{9,5},{12,8},{13,9},{14,12},{15,13},... | collective-permute-start | bytes 393224 | tf_op jit(solution)/shard_map/ppermute | solution.py:489
  65.3 8.3 %collective-permute-start.20 = (bf16[16,4096]{1,0:T(8,128)(2,1)S(1)}, bf16[16,4096]{1,0:T(8,128)(2,1)S(1)}, u32[]{:S(2)}, u32[]{:S(2)}) collective-permute-start(bf16[16,4096]{1,0:T(8,128)(2,1)S(1)} %add_blocks.14.refs_2_), channel_id=1, source_target_pairs={{0,2},{1,3},{4,0},{5,1},{8,4},{9,5},{12,8},{13,9},{14,12},{15,13},... | collective-permute-start | bytes 393224 | tf_op jit(solution)/shard_map/ppermute | solution.py:489
  66.1 8.3 %collective-permute-start.19 = (bf16[16,4096]{1,0:T(8,128)(2,1)S(1)}, bf16[16,4096]{1,0:T(8,128)(2,1)S(1)}, u32[]{:S(2)}, u32[]{:S(2)}) collective-permute-start(bf16[16,4096]{1,0:T(8,128)(2,1)S(1)} %add_blocks.16.refs_3_), channel_id=1, source_target_pairs={{0,4},{1,5},{4,8},{5,9},{8,12},{9,13},{12,14},{13,15},{14,10},{15,... | collective-permute-start | bytes 393224 | tf_op jit(solution)/shard_map/ppermute | solution.py:489
  67.7 8.1 %collective-permute-start.18 = (bf16[16,4096]{1,0:T(8,128)(2,1)S(1)}, bf16[16,4096]{1,0:T(8,128)(2,1)S(1)}, u32[]{:S(2)}, u32[]{:S(2)}) collective-permute-start(bf16[16,4096]{1,0:T(8,128)(2,1)S(1)} %add_blocks.17.refs_3_), channel_id=1, source_target_pairs={{0,4},{1,5},{4,8},{5,9},{8,12},{9,13},{12,14},{13,15},{14,10},{15,... | collective-permute-start | bytes 393224 | tf_op jit(solution)/shard_map/ppermute | solution.py:489
  70.9 5.6 %collective-permute-start.23 = (bf16[16,4096]{1,0:T(8,128)(2,1)S(1)}, bf16[16,4096]{1,0:T(8,128)(2,1)S(1)}, u32[]{:S(2)}, u32[]{:S(2)}) collective-permute-start(bf16[16,4096]{1,0:T(8,128)(2,1)S(1)} %add_blocks.18.refs_3_), channel_id=1, source_target_pairs={{0,2},{1,3},{4,0},{5,1},{8,4},{9,5},{12,8},{13,9},{14,12},{15,13},... | collective-permute-start | bytes 393224 | tf_op jit(solution)/shard_map/ppermute | solution.py:489
  73.6 6.5 %collective-permute-start.26 = (bf16[16,4096]{1,0:T(8,128)(2,1)S(1)}, bf16[16,4096]{1,0:T(8,128)(2,1)S(1)}, u32[]{:S(2)}, u32[]{:S(2)}) collective-permute-start(bf16[16,4096]{1,0:T(8,128)(2,1)S(1)} %add_blocks.19.refs_3_), channel_id=1, source_target_pairs={{0,2},{1,3},{4,0},{5,1},{8,4},{9,5},{12,8},{13,9},{14,12},{15,13},... | collective-permute-start | bytes 393224 | tf_op jit(solution)/shard_map/ppermute | solution.py:489
  74.5 6.5 %collective-permute-start.25 = (bf16[16,4096]{1,0:T(8,128)(2,1)S(1)}, bf16[16,4096]{1,0:T(8,128)(2,1)S(1)}, u32[]{:S(2)}, u32[]{:S(2)}) collective-permute-start(bf16[16,4096]{1,0:T(8,128)(2,1)S(1)} %add_blocks.20.refs_3_), channel_id=1, source_target_pairs={{0,4},{1,5},{4,8},{5,9},{8,12},{9,13},{12,14},{13,15},{14,10},{15,... | collective-permute-start | bytes 393224 | tf_op jit(solution)/shard_map/ppermute | solution.py:489
  76.6 9.4 %copy-start.7 = (bf16[8192]{0:T(1024)(128)(2,1)S(1)}, bf16[8192]{0:T(1024)(128)(2,1)}, u32[]{:S(2)}) copy-start(bf16[8192]{0:T(1024)(128)(2,1)} %param.15) | copy-start | bytes 49156
  76.6 6.4 %collective-permute-start.24 = (bf16[16,4096]{1,0:T(8,128)(2,1)S(1)}, bf16[16,4096]{1,0:T(8,128)(2,1)S(1)}, u32[]{:S(2)}, u32[]{:S(2)}) collective-permute-start(bf16[16,4096]{1,0:T(8,128)(2,1)S(1)} %add_blocks.22.refs_3_), channel_id=1, source_target_pairs={{0,2},{1,3},{4,0},{5,1},{8,4},{9,5},{12,8},{13,9},{14,12},{15,13},... | collective-permute-start | bytes 393224 | tf_op jit(solution)/shard_map/ppermute | solution.py:489
  77.4 6.4 %collective-permute-start.22 = (bf16[16,4096]{1,0:T(8,128)(2,1)S(1)}, bf16[16,4096]{1,0:T(8,128)(2,1)S(1)}, u32[]{:S(2)}, u32[]{:S(2)}) collective-permute-start(bf16[16,4096]{1,0:T(8,128)(2,1)S(1)} %add_blocks.21.refs_3_), channel_id=1, source_target_pairs={{0,4},{1,5},{4,8},{5,9},{8,12},{9,13},{12,14},{13,15},{14,10},{15,... | collective-permute-start | bytes 393224 | tf_op jit(solution)/shard_map/ppermute | solution.py:489
  80.2 6.4 %collective-permute-start.28 = (bf16[16,4096]{1,0:T(8,128)(2,1)S(1)}, bf16[16,4096]{1,0:T(8,128)(2,1)S(1)}, u32[]{:S(2)}, u32[]{:S(2)}) collective-permute-start(bf16[16,4096]{1,0:T(8,128)(2,1)S(1)} %add_blocks.23.refs_3_), channel_id=1, source_target_pairs={{0,2},{1,3},{4,0},{5,1},{8,4},{9,5},{12,8},{13,9},{14,12},{15,13},... | collective-permute-start | bytes 393224 | tf_op jit(solution)/shard_map/ppermute | solution.py:489
  81.1 5.3 %collective-permute-start.29 = (bf16[16,4096]{1,0:T(8,128)(2,1)S(1)}, bf16[16,4096]{1,0:T(8,128)(2,1)S(1)}, u32[]{:S(2)}, u32[]{:S(2)}) collective-permute-start(bf16[16,4096]{1,0:T(8,128)(2,1)S(1)} %add_blocks.24.refs_6_), channel_id=1, source_target_pairs={{0,4},{1,5},{4,8},{5,9},{8,12},{9,13},{12,14},{13,15},{14,10},{15,... | collective-permute-start | bytes 393224 | tf_op jit(solution)/shard_map/ppermute | solution.py:489
  83.9 5.0 %collective-permute-start.27 = (bf16[16,4096]{1,0:T(8,128)(2,1)S(1)}, bf16[16,4096]{1,0:T(8,128)(2,1)S(1)}, u32[]{:S(2)}, u32[]{:S(2)}) collective-permute-start(bf16[16,4096]{1,0:T(8,128)(2,1)S(1)} %get-tuple-element.18), channel_id=1, source_target_pairs={{0,4},{1,5},{4,8},{5,9},{8,12},{9,13},{12,14},{13,15},{14,10},{15,... | collective-permute-start | bytes 393224 | tf_op jit(solution)/shard_map/ppermute | solution.py:489
  85.2 5.0 %collective-permute-start.30 = (bf16[16,4096]{1,0:T(8,128)(2,1)S(1)}, bf16[16,4096]{1,0:T(8,128)(2,1)S(1)}, u32[]{:S(2)}, u32[]{:S(2)}) collective-permute-start(bf16[16,4096]{1,0:T(8,128)(2,1)S(1)} %get-tuple-element.19), channel_id=1, source_target_pairs={{0,2},{1,3},{4,0},{5,1},{8,4},{9,5},{12,8},{13,9},{14,12},{15,13},... | collective-permute-start | bytes 393224 | tf_op jit(solution)/shard_map/ppermute | solution.py:489

commit v10 on v9

--- a/solution.py
+++ b/solution.py
@@ -472,9 +472,9 @@
     right, left = [None] * HALVES, [None] * HALVES
     ordered = []
     for turn in range(last):
-        chains = [(right, 1, 0), (left, -1, 1), (left, -1, 0), (right, 1, 1)]
+        chains = [(right, 1, 0), (left, -1, 1), (right, 1, 1), (left, -1, 0)]
         if turn == 0:
-            chains = [chains[0], chains[2], chains[1], chains[3]]
+            chains = [chains[0], chains[3], chains[2], chains[1]]
         groups = [[chain] for chain in chains] if turn < last - 1 else [chains[:2]]
         for group in groups:
             sides = []

time: 91.3 us -> 90.1 us (0.987)
  transfers between devices with their start and end apart: 31 -> 31, of which waited for: 21 -> 19; matrix products, arithmetic and copies ran while one was open for 3% -> 3% of each run, Pallas kernels for 23% -> 24%
where the time goes in v10:
time: 90.1 us; the launch traced here: 89.9 us
  waiting for transfers between devices  29.5 us (33%)
  starting transfers between devices  28.3 us (31%)
  Pallas kernels  26 us (29%)
  matrix products  4.84 us (5%)
  between operations  1.04 us (1%)
    ppermute x14, starting transfers between devices, scatter_rows(): chain[h] = lax.ppermute(value, AXIS, ring(size, by))  13.5 us
    pallas_call x28, Pallas kernels, call(): pl.pallas_call(run, out_shape=out_shape, in_specs=[whole(pltpu.SMEM if op...  12.1 us
    ppermute x14, waiting for transfers between devices, scatter_rows(): chain[h] = lax.ppermute(value, AXIS, ring(size, by))  11.1 us
    pallas_call x2, Pallas kernels, load_rows(): pl.pallas_call(kernel, out_shape=[jax.ShapeDtypeStruct(shape, weights[0]....  8.65 us
    ppermute x3, waiting for transfers between devices, gather_rows(): right = lax.ppermute(right, AXIS, ring(size, 1))  7.1 us
    ppermute x3, starting transfers between devices, gather_rows(): right = lax.ppermute(right, AXIS, ring(size, 1))  6.45 us
    pallas_call x1, Pallas kernels, stream_rows(): pl.pallas_call(kernel, out_shape=jax.ShapeDtypeStruct((batch_rows, width)...  5.27 us
    dot_general x2, matrix products, body(): jnp.dot(hidden, down_weight[:, h * width:(h + 1) * width], preferred_elem...  4.84 us
  transfers between devices with their start and end apart: 31, of which 19 were waited for; matrix products, arithmetic and copies ran while one was open for 3% of the time, Pallas kernels for 24%

profile of v10, /device:TPU:0, one launch (start us, length us, event | category | flops | bytes accessed | tf_op | source)
XLA Modules:
  0.0 89.9 jit_solution(5365466934057408071)
XLA Ops:
  0.6 3.1 %collective-permute-start = (bf16[16,8192]{1,0:T(8,128)(2,1)}, bf16[16,8192]{1,0:T(8,128)(2,1)S(1)}, u32[]{:S(2)}, u32[]{:S(2)}) collective-permute-start(bf16[16,8192]{1,0:T(8,128)(2,1)} %refs_8_.1), channel_id=1, source_target_pairs={{0,4},{1,5},{4,8},{5,9},{8,12},{9,13},{12,14},{13,15},{14,10},{15,... | collective-permute-start | bytes 786440 | tf_op jit(solution)/shard_map/ppermute | solution.py:138
  3.7 4.3 %load_rows.2.refs_1_ = bf16[3072,1792]{1,0:T(8,128)(2,1)S(1)} custom-call(bf16[8192,896]{1,0:T(8,128)(2,1)} %refs_0_.7, bf16[8192,896]{1,0:T(8,128)(2,1)} %refs_1_.5), custom_call_target="tpu_custom_call" | custom-call | bytes 22020096 | tf_op jit(solution)/shard_map/load_rows/pallas_call | solution.py:292
  8.0 2.1 %collective-permute-done.refs_0_ = bf16[16,8192]{1,0:T(8,128)(2,1)S(1)} collective-permute-done((bf16[16,8192]{1,0:T(8,128)(2,1)}, bf16[16,8192]{1,0:T(8,128)(2,1)S(1)}, u32[]{:S(2)}, u32[]{:S(2)}) %collective-permute-start) | collective-permute-done | bytes 262176 | tf_op jit(solution)/shard_map/ppermute | solution.py:138
  10.2 1.8 %collective-permute-start.2 = (bf16[16,8192]{1,0:T(8,128)(2,1)S(1)}, bf16[16,8192]{1,0:T(8,128)(2,1)S(1)}, u32[]{:S(2)}, u32[]{:S(2)}) collective-permute-start(bf16[16,8192]{1,0:T(8,128)(2,1)S(1)} %pass_on.2.refs_2_), channel_id=1, source_target_pairs={{0,4},{1,5},{4,8},{5,9},{8,12},{9,13},{12,14},{13,15},{14,10},{15,... | collective-permute-start | bytes 786440 | tf_op jit(solution)/shard_map/ppermute | solution.py:138
  12.3 4.3 %load_rows.3.refs_1_ = bf16[3072,1792]{1,0:T(8,128)(2,1)S(1)} custom-call(bf16[8192,896]{1,0:T(8,128)(2,1)} %refs_0_.7, bf16[8192,896]{1,0:T(8,128)(2,1)} %refs_1_.5, bf16[16,8192]{1,0:T(8,128)(2,1)S(1)} %pass_on.2.refs_2_), custom_call_target="tpu_custom_call" | custom-call | bytes 22020096 | tf_op jit(solution)/shard_map/load_rows/pallas_call | solution.py:292
  16.7 1.0 %collective-permute-done.2.refs_0_.refs_2_ = bf16[16,8192]{1,0:T(8,128)(2,1)S(1)} collective-permute-done((bf16[16,8192]{1,0:T(8,128)(2,1)S(1)}, bf16[16,8192]{1,0:T(8,128)(2,1)S(1)}, u32[]{:S(2)}, u32[]{:S(2)}) %collective-permute-start.2) | collective-permute-done | bytes 262176 | tf_op jit(solution)/shard_map/ppermute | solution.py:138
  17.8 1.5 %collective-permute-start.4 = (bf16[16,8192]{1,0:T(8,128)(2,1)S(1)}, bf16[16,8192]{1,0:T(8,128)(2,1)S(1)}, u32[]{:S(2)}, u32[]{:S(2)}) collective-permute-start(bf16[16,8192]{1,0:T(8,128)(2,1)S(1)} %pass_on.3), channel_id=1, source_target_pairs={{0,4},{1,5},{4,8},{5,9},{8,12},{9,13},{12,14},{13,15},{14,10},{15,... | collective-permute-start | bytes 786440 | tf_op jit(solution)/shard_map/ppermute | solution.py:138
  19.9 0.6 row_masks.1
  20.4 3.9 %collective-permute-done.4.refs_4_.refs_0_ = bf16[16,8192]{1,0:T(8,128)(2,1)S(1)} collective-permute-done((bf16[16,8192]{1,0:T(8,128)(2,1)S(1)}, bf16[16,8192]{1,0:T(8,128)(2,1)S(1)}, u32[]{:S(2)}, u32[]{:S(2)}) %collective-permute-start.4) | collective-permute-done | bytes 262176 | tf_op jit(solution)/shard_map/ppermute | solution.py:138
  24.4 1.3 %collective-permute-done.5.refs_5_.refs_0_ = bf16[16,8192]{1,0:T(8,128)(2,1)S(1)} collective-permute-done((bf16[16,8192]{1,0:T(8,128)(2,1)S(1)}, bf16[16,8192]{1,0:T(8,128)(2,1)S(1)}, u32[]{:S(2)}, u32[]{:S(2)}) %collective-permute-start.5) | collective-permute-done | bytes 262176 | tf_op jit(solution)/shard_map/ppermute | solution.py:139
  25.9 1.6 %collective-permute-start.6 = (bf16[16,4096]{1,0:T(8,128)(2,1)S(1)}, bf16[16,4096]{1,0:T(8,128)(2,1)S(1)}, u32[]{:S(2)}, u32[]{:S(2)}) collective-permute-start(bf16[16,4096]{1,0:T(8,128)(2,1)S(1)} %column_half.2), channel_id=1, source_target_pairs={{0,4},{1,5},{4,8},{5,9},{8,12},{9,13},{12,14},{13,15},{14,10},{15,... | collective-permute-start | bytes 393224 | tf_op jit(solution)/shard_map/ppermute | solution.py:151
  28.0 3.8 %collective-permute-done.6.refs_0_ = bf16[16,4096]{1,0:T(8,128)(2,1)S(1)} collective-permute-done((bf16[16,4096]{1,0:T(8,128)(2,1)S(1)}, bf16[16,4096]{1,0:T(8,128)(2,1)S(1)}, u32[]{:S(2)}, u32[]{:S(2)}) %collective-permute-start.6) | collective-permute-done | bytes 131104 | tf_op jit(solution)/shard_map/ppermute | solution.py:151
  31.8 1.4 %collective-permute-done.7.refs_1_ = bf16[16,4096]{1,0:T(8,128)(2,1)S(1)} collective-permute-done((bf16[16,4096]{1,0:T(8,128)(2,1)S(1)}, bf16[16,4096]{1,0:T(8,128)(2,1)S(1)}, u32[]{:S(2)}, u32[]{:S(2)}) %collective-permute-start.7) | collective-permute-done | bytes 131104 | tf_op jit(solution)/shard_map/ppermute | solution.py:152
  33.3 1.5 %collective-permute-done.10.refs_5_ = bf16[16,8192]{1,0:T(8,128)(2,1)S(1)} collective-permute-done((bf16[16,8192]{1,0:T(8,128)(2,1)S(1)}, bf16[16,8192]{1,0:T(8,128)(2,1)S(1)}, u32[]{:S(2)}, u32[]{:S(2)}) %collective-permute-start.10) | collective-permute-done | bytes 262176 | tf_op jit(solution)/shard_map/ppermute | solution.py:157
  34.8 2.6 %shrink_rows.1 = (bf16[256,8192]{1,0:T(8,128)(2,1)S(1)}, bf16[256,64]{1,0:T(8,128)(2,1)S(1)}) custom-call(bf16[16,8192]{1,0:T(8,128)(2,1)S(1)} %copy-done.1, bf16[96,8192]{1,0:T(8,128)(2,1)S(1)} %join_pieces.2.refs_1_, bf16[16,8192]{1,0:T(8,128)(2,1)S(1)} %join_pieces.3.refs_2_, bf16[16,8192]{1,0:T(8,128)(2,1)S(1)} %collective-permute-done.8.refs_3_, ...), custom_call_target="tpu_custom_call" | custom-call | flops 268435456 | bytes 8388608 | tf_op jit(solution)/shard_map/shrink_rows/pallas_call | solution.py:78
  37.6 1.1 %collective-permute-done.11.refs_1_ = bf16[256,64]{1,0:T(8,128)(2,1)S(1)} collective-permute-done((bf16[256,64]{1,0:T(8,128)(2,1)S(1)}, bf16[256,64]{1,0:T(8,128)(2,1)S(1)}, u32[]{:S(2)}, u32[]{:S(2)}) %collective-permute-start.11) | collective-permute-done | bytes 32800 | tf_op jit(solution)/shard_map/ppermute | solution.py:552
  39.3 3.0 %mixed_rows.2.refs_2_ = f32[256,1792]{1,0:T(8,128)S(1)} custom-call(bf16[256,8192]{1,0:T(8,128)(2,1)S(1)} %get-tuple-element.15.refs_0_.rows_ref, bf16[3072,1792]{1,0:T(8,128)(2,1)S(1)} %load_rows.2.refs_1_, bf16[256,64]{1,0:T(8,128)(2,1)S(1)} %add_coefficients.3.refs_2_.refs_0_), custom_call_target="tpu_custom_call" | custom-call | flops 2818572288 | bytes 11010048 | tf_op jit(solution)/shard_map/mixed_rows/pallas_call | solution.py:78
  42.3 0.8 collective-permute-done.12.refs_1_
  43.1 1.6 %collective-permute-start.13 = (bf16[256,64]{1,0:T(8,128)(2,1)S(1)}, bf16[256,64]{1,0:T(8,128)(2,1)S(1)}, u32[]{:S(2)}, u32[]{:S(2)}) collective-permute-start(bf16[256,64]{1,0:T(8,128)(2,1)S(1)} %add_coefficients.4.refs_3_.refs_0_), channel_id=1, source_target_pairs={{0,4},{1,5},{2,6},{3,7},{4,0},{5,1},{6,2},{7,3},{8,12},{9,13},{10,... | collective-permute-start | bytes 98312 | tf_op jit(solution)/shard_map/ppermute | solution.py:552
  44.8 3.0 %mixed_rows.3.refs_2_ = f32[256,1792]{1,0:T(8,128)S(1)} custom-call(bf16[256,8192]{1,0:T(8,128)(2,1)S(1)} %get-tuple-element.15.refs_0_.rows_ref, bf16[3072,1792]{1,0:T(8,128)(2,1)S(1)} %load_rows.3.refs_1_, f32[256,1792]{1,0:T(8,128)S(1)} %mixed_rows.2.refs_2_, bf16[256,64]{1,0:T(8,128)(2,1)S(1)} %add_coefficients.4.refs_3_.refs_0_), custom_call_target="tpu_custom_call" | custom-call | flops 2818572288 | bytes 11010048 | tf_op jit(solution)/shard_map/mixed_rows/pallas_call | solution.py:78
  47.9 2.3 %collective-permute-start.14 = (bf16[256,64]{1,0:T(8,128)(2,1)S(1)}, bf16[256,64]{1,0:T(8,128)(2,1)S(1)}, u32[]{:S(2)}, u32[]{:S(2)}) collective-permute-start(bf16[256,64]{1,0:T(8,128)(2,1)S(1)} %add_coefficients.5.refs_3_.refs_0_), channel_id=1, source_target_pairs={{0,8},{1,9},{2,10},{3,11},{4,12},{5,13},{6,14},{7,15},{8,0},{9,1},... | collective-permute-start | bytes 98312 | tf_op jit(solution)/shard_map/ppermute | solution.py:552
  50.1 5.3 %stream_rows.1.refs_5_ = f32[256,1792]{1,0:T(8,128)S(1)} custom-call(bf16[256,8192]{1,0:T(8,128)(2,1)S(1)} %get-tuple-element.15.refs_0_.rows_ref, bf16[8192,896]{1,0:T(8,128)(2,1)} %refs_0_.7, bf16[8192,896]{1,0:T(8,128)(2,1)} %refs_1_.5, f32[256,1792]{1,0:T(8,128)S(1)} %mixed_rows.3.refs_2_, bf16[256,64]{1,0:T(8,128)(2,1)S(1)} %add_coefficients.5.refs_3_.refs_0_), custom_call_target="tpu_custom_call" | custom-call | flops 1879048192 | bytes 14680064 | tf_op jit(solution)/shard_map/stream_rows/pallas_call | solution.py:395
  55.4 1.0 %hidden_rows.1 = bf16[256,896]{1,0:T(8,128)(2,1)S(1)} custom-call(bf16[256,64]{1,0:T(8,128)(2,1)S(1)} %add_coefficients.5.refs_3_.refs_0_, bf16[256,64]{1,0:T(8,128)(2,1)S(1)} %collective-permute-done.14.refs_1_, bf16[256,256]{1,0:T(8,128)(2,1)S(1)} %get-tuple-element.16.refs_2_, bf16[256,1024]{1,0:T(8,128)(2,1)S(1)} %get-tuple-element.17.refs_3_, ...), custom_call_target="tpu_custom_call" | custom-call | flops 469762048 | bytes 1835008 | tf_op jit(solution)/shard_map/hidden_rows/pallas_call | solution.py:78
  56.4 2.4 %fusion.4.refs_0_ = bf16[256,4096]{1,0:T(8,128)(2,1)S(1)} fusion(bf16[256,896]{1,0:T(8,128)(2,1)S(1)} %hidden_rows.1, bf16[896,8192]{1,0:T(8,128)(2,1)S(1)} %bitcast.17), kind=kOutput, calls=%fused_computation.4 | convolution fusion | flops 1880096768 | bytes 9895936 | tf_op jit(solution)/shard_map/dot_general | solution.py:569
  59.0 2.4 %fusion.7.refs_0_.refs_3_.refs_4_ = bf16[256,4096]{1,0:T(8,128)(2,1)S(1)} fusion(bf16[256,896]{1,0:T(8,128)(2,1)S(1)} %hidden_rows.1, bf16[896,8192]{1,0:T(8,128)(2,1)S(1)} %bitcast.17), kind=kOutput, calls=%fused_computation.5 | convolution fusion | flops 1880096768 | bytes 9895936 | tf_op jit(solution)/shard_map/dot_general | solution.py:569
  62.2 0.8 collective-permute-start.16
  63.0 1.4 %collective-permute-done.17.refs_1_.refs_4_.refs_5_ = bf16[128,4096]{1,0:T(8,128)(2,1)S(1)} collective-permute-done((bf16[128,4096]{1,0:T(8,128)(2,1)S(1)}, bf16[128,4096]{1,0:T(8,128)(2,1)S(1)}, u32[]{:S(2)}, u32[]{:S(2)}) %collective-permute-start.17) | collective-permute-done | bytes 1048608 | tf_op jit(solution)/shard_map/ppermute | solution.py:575
  64.5 0.8 collective-permute-start.21
  65.3 1.2 %collective-permute-start.20 = (bf16[16,4096]{1,0:T(8,128)(2,1)S(1)}, bf16[16,4096]{1,0:T(8,128)(2,1)S(1)}, u32[]{:S(2)}, u32[]{:S(2)}) collective-permute-start(bf16[16,4096]{1,0:T(8,128)(2,1)S(1)} %add_blocks.15.refs_2_), channel_id=1, source_target_pairs={{0,4},{1,5},{4,8},{5,9},{8,12},{9,13},{12,14},{13,15},{14,10},{15,... | collective-permute-start | bytes 393224 | tf_op jit(solution)/shard_map/ppermute | solution.py:489
  66.6 0.8 collective-permute-start.19
  67.7 1.0 %collective-permute-start.18 = (bf16[16,4096]{1,0:T(8,128)(2,1)S(1)}, bf16[16,4096]{1,0:T(8,128)(2,1)S(1)}, u32[]{:S(2)}, u32[]{:S(2)}) collective-permute-start(bf16[16,4096]{1,0:T(8,128)(2,1)S(1)} %add_blocks.17.refs_3_), channel_id=1, source_target_pairs={{0,4},{1,5},{4,8},{5,9},{8,12},{9,13},{12,14},{13,15},{14,10},{15,... | collective-permute-start | bytes 393224 | tf_op jit(solution)/shard_map/ppermute | solution.py:489
  68.7 2.1 %collective-permute-done.21.refs_2_ = bf16[16,4096]{1,0:T(8,128)(2,1)S(1)} collective-permute-done((bf16[16,4096]{1,0:T(8,128)(2,1)S(1)}, bf16[16,4096]{1,0:T(8,128)(2,1)S(1)}, u32[]{:S(2)}, u32[]{:S(2)}) %collective-permute-start.21) | collective-permute-done | bytes 131104 | tf_op jit(solution)/shard_map/ppermute | solution.py:489
  70.9 0.8 collective-permute-start.23
  71.8 1.3 %collective-permute-start.26 = (bf16[16,4096]{1,0:T(8,128)(2,1)S(1)}, bf16[16,4096]{1,0:T(8,128)(2,1)S(1)}, u32[]{:S(2)}, u32[]{:S(2)}) collective-permute-start(bf16[16,4096]{1,0:T(8,128)(2,1)S(1)} %add_blocks.19.refs_3_), channel_id=1, source_target_pairs={{0,4},{1,5},{4,8},{5,9},{8,12},{9,13},{12,14},{13,15},{14,10},{15,... | collective-permute-start | bytes 393224 | tf_op jit(solution)/shard_map/ppermute | solution.py:489
  73.7 0.8 collective-permute-start.25
  74.6 2.0 %collective-permute-done.23.refs_2_ = bf16[16,4096]{1,0:T(8,128)(2,1)S(1)} collective-permute-done((bf16[16,4096]{1,0:T(8,128)(2,1)S(1)}, bf16[16,4096]{1,0:T(8,128)(2,1)S(1)}, u32[]{:S(2)}, u32[]{:S(2)}) %collective-permute-start.23) | collective-permute-done | bytes 131104 | tf_op jit(solution)/shard_map/ppermute | solution.py:489
  76.6 0.8 collective-permute-start.24
  77.4 1.2 %collective-permute-start.22 = (bf16[16,4096]{1,0:T(8,128)(2,1)S(1)}, bf16[16,4096]{1,0:T(8,128)(2,1)S(1)}, u32[]{:S(2)}, u32[]{:S(2)}) collective-permute-start(bf16[16,4096]{1,0:T(8,128)(2,1)S(1)} %add_blocks.21.refs_3_), channel_id=1, source_target_pairs={{0,4},{1,5},{4,8},{5,9},{8,12},{9,13},{12,14},{13,15},{14,10},{15,... | collective-permute-start | bytes 393224 | tf_op jit(solution)/shard_map/ppermute | solution.py:489
  78.7 0.8 collective-permute-start.29
  79.6 0.6 collective-permute-done.25.refs_2_
  80.2 0.8 collective-permute-start.28
  81.0 1.9 %collective-permute-done.24.refs_5_ = bf16[16,4096]{1,0:T(8,128)(2,1)S(1)} collective-permute-done((bf16[16,4096]{1,0:T(8,128)(2,1)S(1)}, bf16[16,4096]{1,0:T(8,128)(2,1)S(1)}, u32[]{:S(2)}, u32[]{:S(2)}) %collective-permute-start.24) | collective-permute-done | bytes 131104 | tf_op jit(solution)/shard_map/ppermute | solution.py:489
  83.1 0.8 collective-permute-start.27
  83.9 1.2 %collective-permute-start.30 = (bf16[16,4096]{1,0:T(8,128)(2,1)S(1)}, bf16[16,4096]{1,0:T(8,128)(2,1)S(1)}, u32[]{:S(2)}, u32[]{:S(2)}) collective-permute-start(bf16[16,4096]{1,0:T(8,128)(2,1)S(1)} %get-tuple-element.19), channel_id=1, source_target_pairs={{0,2},{1,3},{4,0},{5,1},{8,4},{9,5},{12,8},{13,9},{14,12},{15,13},... | collective-permute-start | bytes 393224 | tf_op jit(solution)/shard_map/ppermute | solution.py:489
  85.2 1.1 %collective-permute-done.28.refs_3_ = bf16[16,4096]{1,0:T(8,128)(2,1)S(1)} collective-permute-done((bf16[16,4096]{1,0:T(8,128)(2,1)S(1)}, bf16[16,4096]{1,0:T(8,128)(2,1)S(1)}, u32[]{:S(2)}, u32[]{:S(2)}) %collective-permute-start.28) | collective-permute-done | bytes 131104 | tf_op jit(solution)/shard_map/ppermute | solution.py:489
  86.3 1.8 %collective-permute-done.27.refs_2_ = bf16[16,4096]{1,0:T(8,128)(2,1)S(1)} collective-permute-done((bf16[16,4096]{1,0:T(8,128)(2,1)S(1)}, bf16[16,4096]{1,0:T(8,128)(2,1)S(1)}, u32[]{:S(2)}, u32[]{:S(2)}) %collective-permute-start.27) | collective-permute-done | bytes 131104 | tf_op jit(solution)/shard_map/ppermute | solution.py:489
  88.1 0.8 collective-permute-done.30.refs_7_
  88.9 1.0 %finish_rows.1 = (bf16[16,8192]{1,0:T(8,128)(2,1)}, bf16[16,8192]{1,0:T(8,128)(2,1)}) custom-call(bf16[256,4096]{1,0:T(8,128)(2,1)S(1)} %fusion.4.refs_0_, bf16[128,4096]{1,0:T(8,128)(2,1)S(1)} %collective-permute-done.15.refs_1_, bf16[16,4096]{1,0:T(8,128)(2,1)S(1)} %collective-permute-done.27.refs_2_, ...), custom_call_target="tpu_custom_call" | custom-call | tf_op jit(solution)/shard_map/finish_rows/pallas_call | solution.py:78
  (75 shorter events, 4.8 us)
Async XLA Ops:
  0.6 9.5 %collective-permute-start = (bf16[16,8192]{1,0:T(8,128)(2,1)}, bf16[16,8192]{1,0:T(8,128)(2,1)S(1)}, u32[]{:S(2)}, u32[]{:S(2)}) collective-permute-start(bf16[16,8192]{1,0:T(8,128)(2,1)} %refs_8_.1), channel_id=1, source_target_pairs={{0,4},{1,5},{4,8},{5,9},{8,12},{9,13},{12,14},{13,15},{14,10},{15,... | collective-permute-start | bytes 786440 | tf_op jit(solution)/shard_map/ppermute | solution.py:138
  3.7 8.3 %collective-permute-start.1 = (bf16[16,8192]{1,0:T(8,128)(2,1)}, bf16[16,8192]{1,0:T(8,128)(2,1)S(1)}, u32[]{:S(2)}, u32[]{:S(2)}) collective-permute-start(bf16[16,8192]{1,0:T(8,128)(2,1)} %refs_8_.1), channel_id=1, source_target_pairs={{0,2},{1,3},{4,0},{5,1},{8,4},{9,5},{12,8},{13,9},{14,12},{15,13},... | collective-permute-start | bytes 786440 | tf_op jit(solution)/shard_map/ppermute | solution.py:139
  10.2 7.5 %collective-permute-start.2 = (bf16[16,8192]{1,0:T(8,128)(2,1)S(1)}, bf16[16,8192]{1,0:T(8,128)(2,1)S(1)}, u32[]{:S(2)}, u32[]{:S(2)}) collective-permute-start(bf16[16,8192]{1,0:T(8,128)(2,1)S(1)} %pass_on.2.refs_2_), channel_id=1, source_target_pairs={{0,4},{1,5},{4,8},{5,9},{8,12},{9,13},{12,14},{13,15},{14,10},{15,... | collective-permute-start | bytes 786440 | tf_op jit(solution)/shard_map/ppermute | solution.py:138
  12.0 7.2 %collective-permute-start.3 = (bf16[16,8192]{1,0:T(8,128)(2,1)S(1)}, bf16[16,8192]{1,0:T(8,128)(2,1)S(1)}, u32[]{:S(2)}, u32[]{:S(2)}) collective-permute-start(bf16[16,8192]{1,0:T(8,128)(2,1)S(1)} %collective-permute-done.1.refs_1_), channel_id=1, source_target_pairs={{0,2},{1,3},{4,0},{5,1},{8,4},{9,5},{12,8},{13,9},{14,12},{15,13},... | collective-permute-start | bytes 786440 | tf_op jit(solution)/shard_map/ppermute | solution.py:139
  16.6 3.2 %copy-start.2 = (bf16[1,8192,64]{1,2,0:T(8,128)(2,1)S(1)}, bf16[1,8192,64]{1,2,0:T(8,128)(2,1)}, u32[]{:S(2)}) copy-start(bf16[1,8192,64]{1,2,0:T(8,128)(2,1)} %param.16) | copy-start | bytes 3145732
  16.6 3.2 %copy-start.3 = (s32[32]{0:T(128)S(1)}, s32[32]{0:T(128)}, u32[]{:S(2)}) copy-start(s32[32]{0:T(128)} %param.20) | copy-start | bytes 388
  16.6 3.2 %copy-start.4 = (s32[32]{0:T(128)S(1)}, s32[32]{0:T(128)}, u32[]{:S(2)}) copy-start(s32[32]{0:T(128)} %param.21) | copy-start | bytes 388
  16.6 3.2 %copy-start.5 = (s32[16]{0:T(128)S(1)}, s32[16]{0:T(128)}, u32[]{:S(2)}) copy-start(s32[16]{0:T(128)} %param.18) | copy-start | bytes 196
  16.7 3.2 %copy-start.6 = (s32[16]{0:T(128)S(1)}, s32[16]{0:T(128)}, u32[]{:S(2)}) copy-start(s32[16]{0:T(128)} %param.19) | copy-start | bytes 196
  16.7 11.3 %copy-start.1 = (bf16[16,8192]{1,0:T(8,128)(2,1)S(1)}, bf16[16,8192]{1,0:T(8,128)(2,1)}, u32[]{:S(2)}) copy-start(bf16[16,8192]{1,0:T(8,128)(2,1)} %refs_8_.1) | copy-start | bytes 786436
  17.8 6.6 %collective-permute-start.4 = (bf16[16,8192]{1,0:T(8,128)(2,1)S(1)}, bf16[16,8192]{1,0:T(8,128)(2,1)S(1)}, u32[]{:S(2)}, u32[]{:S(2)}) collective-permute-start(bf16[16,8192]{1,0:T(8,128)(2,1)S(1)} %pass_on.3), channel_id=1, source_target_pairs={{0,4},{1,5},{4,8},{5,9},{8,12},{9,13},{12,14},{13,15},{14,10},{15,... | collective-permute-start | bytes 786440 | tf_op jit(solution)/shard_map/ppermute | solution.py:138
  19.3 6.4 %collective-permute-start.5 = (bf16[16,8192]{1,0:T(8,128)(2,1)S(1)}, bf16[16,8192]{1,0:T(8,128)(2,1)S(1)}, u32[]{:S(2)}, u32[]{:S(2)}) collective-permute-start(bf16[16,8192]{1,0:T(8,128)(2,1)S(1)} %collective-permute-done.3.refs_3_), channel_id=1, source_target_pairs={{0,2},{1,3},{4,0},{5,1},{8,4},{9,5},{12,8},{13,9},{14,12},{15,13},... | collective-permute-start | bytes 786440 | tf_op jit(solution)/shard_map/ppermute | solution.py:139
  25.8 9.0 %collective-permute-start.9 = (bf16[96,8192]{1,0:T(8,128)(2,1)S(1)}, bf16[96,8192]{1,0:T(8,128)(2,1)S(1)}, u32[]{:S(2)}, u32[]{:S(2)}) collective-permute-start(bf16[96,8192]{1,0:T(8,128)(2,1)S(1)} %join_pieces.2.refs_1_), channel_id=1, source_target_pairs={{0,1},{1,0},{2,3},{3,2},{4,5},{5,4},{6,7},{7,6},{8,9},{9,8},{10,11... | collective-permute-start | bytes 4718600 | tf_op jit(solution)/shard_map/ppermute | solution.py:148
  25.9 5.9 %collective-permute-start.6 = (bf16[16,4096]{1,0:T(8,128)(2,1)S(1)}, bf16[16,4096]{1,0:T(8,128)(2,1)S(1)}, u32[]{:S(2)}, u32[]{:S(2)}) collective-permute-start(bf16[16,4096]{1,0:T(8,128)(2,1)S(1)} %column_half.2), channel_id=1, source_target_pairs={{0,4},{1,5},{4,8},{5,9},{8,12},{9,13},{12,14},{13,15},{14,10},{15,... | collective-permute-start | bytes 393224 | tf_op jit(solution)/shard_map/ppermute | solution.py:151
  27.5 5.7 %collective-permute-start.7 = (bf16[16,4096]{1,0:T(8,128)(2,1)S(1)}, bf16[16,4096]{1,0:T(8,128)(2,1)S(1)}, u32[]{:S(2)}, u32[]{:S(2)}) collective-permute-start(bf16[16,4096]{1,0:T(8,128)(2,1)S(1)} %column_half.3), channel_id=1, source_target_pairs={{0,2},{1,3},{4,0},{5,1},{8,4},{9,5},{12,8},{13,9},{14,12},{15,13},... | collective-permute-start | bytes 393224 | tf_op jit(solution)/shard_map/ppermute | solution.py:152
  28.0 5.3 %collective-permute-start.8 = (bf16[16,8192]{1,0:T(8,128)(2,1)S(1)}, bf16[16,8192]{1,0:T(8,128)(2,1)S(1)}, u32[]{:S(2)}, u32[]{:S(2)}) collective-permute-start(bf16[16,8192]{1,0:T(8,128)(2,1)S(1)} %copy-done.1), channel_id=1, source_target_pairs={{0,1},{1,0},{2,3},{3,2},{4,5},{5,4},{6,7},{7,6},{8,9},{9,8},{10,11... | collective-permute-start | bytes 786440 | tf_op jit(solution)/shard_map/ppermute | solution.py:141
  33.2 1.6 %collective-permute-start.10 = (bf16[16,8192]{1,0:T(8,128)(2,1)S(1)}, bf16[16,8192]{1,0:T(8,128)(2,1)S(1)}, u32[]{:S(2)}, u32[]{:S(2)}) collective-permute-start(bf16[16,8192]{1,0:T(8,128)(2,1)S(1)} %join_pieces.3.refs_2_), channel_id=1, source_target_pairs={{0,1},{1,0},{2,3},{3,2},{4,5},{5,4},{6,7},{7,6},{8,9},{9,8},{10,11... | collective-permute-start | bytes 786440 | tf_op jit(solution)/shard_map/ppermute | solution.py:157
  37.4 1.3 %collective-permute-start.11 = (bf16[256,64]{1,0:T(8,128)(2,1)S(1)}, bf16[256,64]{1,0:T(8,128)(2,1)S(1)}, u32[]{:S(2)}, u32[]{:S(2)}) collective-permute-start(bf16[256,64]{1,0:T(8,128)(2,1)S(1)} %get-tuple-element.14.refs_0_), channel_id=1, source_target_pairs={{0,1},{1,0},{2,3},{3,2},{4,5},{5,4},{6,7},{7,6},{8,9},{9,8},{10,11... | collective-permute-start | bytes 98312 | tf_op jit(solution)/shard_map/ppermute | solution.py:552
  38.8 4.3 %collective-permute-start.12 = (bf16[256,64]{1,0:T(8,128)(2,1)S(1)}, bf16[256,64]{1,0:T(8,128)(2,1)S(1)}, u32[]{:S(2)}, u32[]{:S(2)}) collective-permute-start(bf16[256,64]{1,0:T(8,128)(2,1)S(1)} %add_coefficients.3.refs_2_.refs_0_), channel_id=1, source_target_pairs={{0,2},{1,3},{2,0},{3,1},{4,6},{5,7},{6,4},{7,5},{8,10},{9,11},{10,... | collective-permute-start | bytes 98312 | tf_op jit(solution)/shard_map/ppermute | solution.py:552
  43.1 4.7 %collective-permute-start.13 = (bf16[256,64]{1,0:T(8,128)(2,1)S(1)}, bf16[256,64]{1,0:T(8,128)(2,1)S(1)}, u32[]{:S(2)}, u32[]{:S(2)}) collective-permute-start(bf16[256,64]{1,0:T(8,128)(2,1)S(1)} %add_coefficients.4.refs_3_.refs_0_), channel_id=1, source_target_pairs={{0,4},{1,5},{2,6},{3,7},{4,0},{5,1},{6,2},{7,3},{8,12},{9,13},{10,... | collective-permute-start | bytes 98312 | tf_op jit(solution)/shard_map/ppermute | solution.py:552
  47.8 8.6 %slice-start = ((s8[14680064]{0:T(1024)(128)(4,1)}), s8[4194304]{0:T(1024)(128)(4,1)S(1)}, s32[]{:S(2)}) async-start(s8[14680064]{0:T(1024)(128)(4,1)} %bitcast.16), calls=%async_computation | async-start | bytes 8388608
  47.8 7.6 %copy-start = (bf16[16,64,896]{2,1,0:T(8,128)(2,1)S(1)}, bf16[16,64,896]{2,1,0:T(8,128)(2,1)}, u32[]{:S(2)}) copy-start(bf16[16,64,896]{2,1,0:T(8,128)(2,1)} %param.17) | copy-start | bytes 5505028
  47.8 8.6 %slice-start.1 = ((s8[14680064]{0:T(1024)(128)(4,1)}), s8[4194304]{0:T(1024)(128)(4,1)S(1)}, s32[]{:S(2)}) async-start(s8[14680064]{0:T(1024)(128)(4,1)} %bitcast.16), calls=%async_computation.1 | async-start | bytes 8388608
  47.8 8.6 %slice-start.2 = ((s8[14680064]{0:T(1024)(128)(4,1)}), s8[4194304]{0:T(1024)(128)(4,1)S(1)}, s32[]{:S(2)}) async-start(s8[14680064]{0:T(1024)(128)(4,1)} %bitcast.16), calls=%async_computation.2 | async-start | bytes 8388608
  47.8 8.6 %slice-start.3 = ((s8[14680064]{0:T(1024)(128)(4,1)}), s8[2097152]{0:T(1024)(128)(4,1)S(1)}, s32[]{:S(2)}) async-start(s8[14680064]{0:T(1024)(128)(4,1)} %bitcast.16), calls=%async_computation.3 | async-start | bytes 4194304
  47.9 7.5 %collective-permute-start.14 = (bf16[256,64]{1,0:T(8,128)(2,1)S(1)}, bf16[256,64]{1,0:T(8,128)(2,1)S(1)}, u32[]{:S(2)}, u32[]{:S(2)}) collective-permute-start(bf16[256,64]{1,0:T(8,128)(2,1)S(1)} %add_coefficients.5.refs_3_.refs_0_), channel_id=1, source_target_pairs={{0,8},{1,9},{2,10},{3,11},{4,12},{5,13},{6,14},{7,15},{8,0},{9,1},... | collective-permute-start | bytes 98312 | tf_op jit(solution)/shard_map/ppermute | solution.py:552
  59.0 3.2 %collective-permute-start.15 = (bf16[128,4096]{1,0:T(8,128)(2,1)S(1)}, bf16[128,4096]{1,0:T(8,128)(2,1)S(1)}, u32[]{:S(2)}, u32[]{:S(2)}) collective-permute-start(bf16[128,4096]{1,0:T(8,128)(2,1)S(1)} %slice.16), channel_id=1, source_target_pairs={{0,1},{1,0},{2,3},{3,2},{4,5},{5,4},{6,7},{7,6},{8,9},{9,8},{10,11... | collective-permute-start | bytes 3145736 | tf_op jit(solution)/shard_map/ppermute | solution.py:575
  61.6 2.8 %collective-permute-start.17 = (bf16[128,4096]{1,0:T(8,128)(2,1)S(1)}, bf16[128,4096]{1,0:T(8,128)(2,1)S(1)}, u32[]{:S(2)}, u32[]{:S(2)}) collective-permute-start(bf16[128,4096]{1,0:T(8,128)(2,1)S(1)} %slice.17), channel_id=1, source_target_pairs={{0,1},{1,0},{2,3},{3,2},{4,5},{5,4},{6,7},{7,6},{8,9},{9,8},{10,11... | collective-permute-start | bytes 3145736 | tf_op jit(solution)/shard_map/ppermute | solution.py:575
  62.2 5.5 %collective-permute-start.16 = (bf16[16,4096]{1,0:T(8,128)(2,1)S(1)}, bf16[16,4096]{1,0:T(8,128)(2,1)S(1)}, u32[]{:S(2)}, u32[]{:S(2)}) collective-permute-start(bf16[16,4096]{1,0:T(8,128)(2,1)S(1)} %add_blocks.13.refs_2_), channel_id=1, source_target_pairs={{0,4},{1,5},{4,8},{5,9},{8,12},{9,13},{12,14},{13,15},{14,10},{15,... | collective-permute-start | bytes 393224 | tf_op jit(solution)/shard_map/ppermute | solution.py:489
  64.5 6.4 %collective-permute-start.21 = (bf16[16,4096]{1,0:T(8,128)(2,1)S(1)}, bf16[16,4096]{1,0:T(8,128)(2,1)S(1)}, u32[]{:S(2)}, u32[]{:S(2)}) collective-permute-start(bf16[16,4096]{1,0:T(8,128)(2,1)S(1)} %add_blocks.16.refs_3_), channel_id=1, source_target_pairs={{0,2},{1,3},{4,0},{5,1},{8,4},{9,5},{12,8},{13,9},{14,12},{15,13},... | collective-permute-start | bytes 393224 | tf_op jit(solution)/shard_map/ppermute | solution.py:489
  65.3 6.4 %collective-permute-start.20 = (bf16[16,4096]{1,0:T(8,128)(2,1)S(1)}, bf16[16,4096]{1,0:T(8,128)(2,1)S(1)}, u32[]{:S(2)}, u32[]{:S(2)}) collective-permute-start(bf16[16,4096]{1,0:T(8,128)(2,1)S(1)} %add_blocks.15.refs_2_), channel_id=1, source_target_pairs={{0,4},{1,5},{4,8},{5,9},{8,12},{9,13},{12,14},{13,15},{14,10},{15,... | collective-permute-start | bytes 393224 | tf_op jit(solution)/shard_map/ppermute | solution.py:489
  66.6 7.0 %collective-permute-start.19 = (bf16[16,4096]{1,0:T(8,128)(2,1)S(1)}, bf16[16,4096]{1,0:T(8,128)(2,1)S(1)}, u32[]{:S(2)}, u32[]{:S(2)}) collective-permute-start(bf16[16,4096]{1,0:T(8,128)(2,1)S(1)} %add_blocks.14.refs_2_), channel_id=1, source_target_pairs={{0,2},{1,3},{4,0},{5,1},{8,4},{9,5},{12,8},{13,9},{14,12},{15,13},... | collective-permute-start | bytes 393224 | tf_op jit(solution)/shard_map/ppermute | solution.py:489
  67.7 6.8 %collective-permute-start.18 = (bf16[16,4096]{1,0:T(8,128)(2,1)S(1)}, bf16[16,4096]{1,0:T(8,128)(2,1)S(1)}, u32[]{:S(2)}, u32[]{:S(2)}) collective-permute-start(bf16[16,4096]{1,0:T(8,128)(2,1)S(1)} %add_blocks.17.refs_3_), channel_id=1, source_target_pairs={{0,4},{1,5},{4,8},{5,9},{8,12},{9,13},{12,14},{13,15},{14,10},{15,... | collective-permute-start | bytes 393224 | tf_op jit(solution)/shard_map/ppermute | solution.py:489
  70.9 5.6 %collective-permute-start.23 = (bf16[16,4096]{1,0:T(8,128)(2,1)S(1)}, bf16[16,4096]{1,0:T(8,128)(2,1)S(1)}, u32[]{:S(2)}, u32[]{:S(2)}) collective-permute-start(bf16[16,4096]{1,0:T(8,128)(2,1)S(1)} %add_blocks.18.refs_3_), channel_id=1, source_target_pairs={{0,2},{1,3},{4,0},{5,1},{8,4},{9,5},{12,8},{13,9},{14,12},{15,13},... | collective-permute-start | bytes 393224 | tf_op jit(solution)/shard_map/ppermute | solution.py:489
  71.8 6.9 %collective-permute-start.26 = (bf16[16,4096]{1,0:T(8,128)(2,1)S(1)}, bf16[16,4096]{1,0:T(8,128)(2,1)S(1)}, u32[]{:S(2)}, u32[]{:S(2)}) collective-permute-start(bf16[16,4096]{1,0:T(8,128)(2,1)S(1)} %add_blocks.19.refs_3_), channel_id=1, source_target_pairs={{0,4},{1,5},{4,8},{5,9},{8,12},{9,13},{12,14},{13,15},{14,10},{15,... | collective-permute-start | bytes 393224 | tf_op jit(solution)/shard_map/ppermute | solution.py:489
  73.7 6.5 %collective-permute-start.25 = (bf16[16,4096]{1,0:T(8,128)(2,1)S(1)}, bf16[16,4096]{1,0:T(8,128)(2,1)S(1)}, u32[]{:S(2)}, u32[]{:S(2)}) collective-permute-start(bf16[16,4096]{1,0:T(8,128)(2,1)S(1)} %add_blocks.20.refs_3_), channel_id=1, source_target_pairs={{0,2},{1,3},{4,0},{5,1},{8,4},{9,5},{12,8},{13,9},{14,12},{15,13},... | collective-permute-start | bytes 393224 | tf_op jit(solution)/shard_map/ppermute | solution.py:489
  76.6 8.6 %copy-start.7 = (bf16[8192]{0:T(1024)(128)(2,1)S(1)}, bf16[8192]{0:T(1024)(128)(2,1)}, u32[]{:S(2)}) copy-start(bf16[8192]{0:T(1024)(128)(2,1)} %param.15) | copy-start | bytes 49156
  76.6 6.4 %collective-permute-start.24 = (bf16[16,4096]{1,0:T(8,128)(2,1)S(1)}, bf16[16,4096]{1,0:T(8,128)(2,1)S(1)}, u32[]{:S(2)}, u32[]{:S(2)}) collective-permute-start(bf16[16,4096]{1,0:T(8,128)(2,1)S(1)} %add_blocks.22.refs_3_), channel_id=1, source_target_pairs={{0,2},{1,3},{4,0},{5,1},{8,4},{9,5},{12,8},{13,9},{14,12},{15,13},... | collective-permute-start | bytes 393224 | tf_op jit(solution)/shard_map/ppermute | solution.py:489
  77.4 5.6 %collective-permute-start.22 = (bf16[16,4096]{1,0:T(8,128)(2,1)S(1)}, bf16[16,4096]{1,0:T(8,128)(2,1)S(1)}, u32[]{:S(2)}, u32[]{:S(2)}) collective-permute-start(bf16[16,4096]{1,0:T(8,128)(2,1)S(1)} %add_blocks.21.refs_3_), channel_id=1, source_target_pairs={{0,4},{1,5},{4,8},{5,9},{8,12},{9,13},{12,14},{13,15},{14,10},{15,... | collective-permute-start | bytes 393224 | tf_op jit(solution)/shard_map/ppermute | solution.py:489
  78.7 7.6 %collective-permute-start.29 = (bf16[16,4096]{1,0:T(8,128)(2,1)S(1)}, bf16[16,4096]{1,0:T(8,128)(2,1)S(1)}, u32[]{:S(2)}, u32[]{:S(2)}) collective-permute-start(bf16[16,4096]{1,0:T(8,128)(2,1)S(1)} %add_blocks.23.refs_3_), channel_id=1, source_target_pairs={{0,4},{1,5},{4,8},{5,9},{8,12},{9,13},{12,14},{13,15},{14,10},{15,... | collective-permute-start | bytes 393224 | tf_op jit(solution)/shard_map/ppermute | solution.py:489
  80.2 6.1 %collective-permute-start.28 = (bf16[16,4096]{1,0:T(8,128)(2,1)S(1)}, bf16[16,4096]{1,0:T(8,128)(2,1)S(1)}, u32[]{:S(2)}, u32[]{:S(2)}) collective-permute-start(bf16[16,4096]{1,0:T(8,128)(2,1)S(1)} %add_blocks.24.refs_6_), channel_id=1, source_target_pairs={{0,2},{1,3},{4,0},{5,1},{8,4},{9,5},{12,8},{13,9},{14,12},{15,13},... | collective-permute-start | bytes 393224 | tf_op jit(solution)/shard_map/ppermute | solution.py:489
  83.1 5.0 %collective-permute-start.27 = (bf16[16,4096]{1,0:T(8,128)(2,1)S(1)}, bf16[16,4096]{1,0:T(8,128)(2,1)S(1)}, u32[]{:S(2)}, u32[]{:S(2)}) collective-permute-start(bf16[16,4096]{1,0:T(8,128)(2,1)S(1)} %get-tuple-element.18), channel_id=1, source_target_pairs={{0,4},{1,5},{4,8},{5,9},{8,12},{9,13},{12,14},{13,15},{14,10},{15,... | collective-permute-start | bytes 393224 | tf_op jit(solution)/shard_map/ppermute | solution.py:489
  83.9 5.0 %collective-permute-start.30 = (bf16[16,4096]{1,0:T(8,128)(2,1)S(1)}, bf16[16,4096]{1,0:T(8,128)(2,1)S(1)}, u32[]{:S(2)}, u32[]{:S(2)}) collective-permute-start(bf16[16,4096]{1,0:T(8,128)(2,1)S(1)} %get-tuple-element.19), channel_id=1, source_target_pairs={{0,2},{1,3},{4,0},{5,1},{8,4},{9,5},{12,8},{13,9},{14,12},{15,13},... | collective-permute-start | bytes 393224 | tf_op jit(solution)/shard_map/ppermute | solution.py:489

commit v11 on v10

--- a/solution.py
+++ b/solution.py
@@ -13,7 +13,7 @@
 DEPTH_BLOCK = 256
 LOADS = 2
 VMEM_LIMIT = 12 * 1024 * 1024
-LOAD_LIMITS = [mb * 1024 * 1024 for mb in (42, 37)]
+LOAD_LIMITS = [mb * 1024 * 1024 for mb in (42, 36)]
 STREAM_LIMIT = 34 * 1024 * 1024
 STREAM_COST = 4
 
@@ -197,7 +197,7 @@
     model_width = factor.shape[1]
     slots = factor.shape[0] // rank_limit
     batch_rows = to_place.shape[0]
-    width = model_width // 8
+    width = model_width // 4
 
     def kernel(*refs):
         factor_ref, scale_ref, place_ref, rows_out, coeff_out, total = refs[len(parts) :]
@@ -257,7 +257,7 @@
 
 
 def depth_cuts(depth):
-    part = -(-3 * depth // 8 // DEPTH_BLOCK) * DEPTH_BLOCK
+    part = -(-13 * depth // 32 // DEPTH_BLOCK) * DEPTH_BLOCK
     return [part * p for p in range(LOADS + 1)] + [depth]
 
 

time: 90.1 us -> 89.1 us (0.989)
  waiting for transfers between devices: 29.5 us -> 27.5 us
  starting transfers between devices: 28.3 us -> 29.5 us
    ppermute x14, starting transfers between devices: 13.5 us -> 15 us  [scatter_rows(): chain[h] = lax.ppermute(value, AXIS, ring(size, by))]
where the time goes in v11:
time: 89.1 us; the launch traced here: 89 us
  starting transfers between devices  29.5 us (33%)
  waiting for transfers between devices  27.5 us (31%)
  Pallas kernels  25.8 us (29%)
  matrix products  4.84 us (5%)
  between operations  1.04 us (1%)
    ppermute x14, starting transfers between devices, scatter_rows(): chain[h] = lax.ppermute(value, AXIS, ring(size, by))  15 us
    pallas_call x28, Pallas kernels, call(): pl.pallas_call(run, out_shape=out_shape, in_specs=[whole(pltpu.SMEM if op...  12 us
    ppermute x14, waiting for transfers between devices, scatter_rows(): chain[h] = lax.ppermute(value, AXIS, ring(size, by))  10.3 us
    pallas_call x2, Pallas kernels, load_rows(): pl.pallas_call(kernel, out_shape=[jax.ShapeDtypeStruct(shape, weights[0]....  9.2 us
    ppermute x3, waiting for transfers between devices, gather_rows(): right = lax.ppermute(right, AXIS, ring(size, 1))  6.55 us
    ppermute x3, starting transfers between devices, gather_rows(): right = lax.ppermute(right, AXIS, ring(size, 1))  6.45 us
    dot_general x2, matrix products, body(): jnp.dot(hidden, down_weight[:, h * width:(h + 1) * width], preferred_elem...  4.84 us
    pallas_call x1, Pallas kernels, stream_rows(): pl.pallas_call(kernel, out_shape=jax.ShapeDtypeStruct((batch_rows, width)...  4.65 us
  transfers between devices with their start and end apart: 31, of which 19 were waited for; matrix products, arithmetic and copies ran while one was open for 3% of the time, Pallas kernels for 24%

profile of v11, /device:TPU:0, one launch (start us, length us, event | category | flops | bytes accessed | tf_op | source)
XLA Modules:
  0.0 89.0 jit_solution(17896829147038847916)
XLA Ops:
  0.6 3.1 %collective-permute-start = (bf16[16,8192]{1,0:T(8,128)(2,1)}, bf16[16,8192]{1,0:T(8,128)(2,1)S(1)}, u32[]{:S(2)}, u32[]{:S(2)}) collective-permute-start(bf16[16,8192]{1,0:T(8,128)(2,1)} %refs_8_.1), channel_id=1, source_target_pairs={{0,4},{1,5},{4,8},{5,9},{8,12},{9,13},{12,14},{13,15},{14,10},{15,... | collective-permute-start | bytes 786440 | tf_op jit(solution)/shard_map/ppermute | solution.py:138
  3.7 4.6 %load_rows.2.refs_1_ = bf16[3328,1792]{1,0:T(8,128)(2,1)S(1)} custom-call(bf16[8192,896]{1,0:T(8,128)(2,1)} %refs_0_.7, bf16[8192,896]{1,0:T(8,128)(2,1)} %refs_1_.5), custom_call_target="tpu_custom_call" | custom-call | bytes 23855104 | tf_op jit(solution)/shard_map/load_rows/pallas_call | solution.py:292
  8.3 1.8 %collective-permute-done.refs_0_ = bf16[16,8192]{1,0:T(8,128)(2,1)S(1)} collective-permute-done((bf16[16,8192]{1,0:T(8,128)(2,1)}, bf16[16,8192]{1,0:T(8,128)(2,1)S(1)}, u32[]{:S(2)}, u32[]{:S(2)}) %collective-permute-start) | collective-permute-done | bytes 262176 | tf_op jit(solution)/shard_map/ppermute | solution.py:138
  10.2 1.8 %collective-permute-start.2 = (bf16[16,8192]{1,0:T(8,128)(2,1)S(1)}, bf16[16,8192]{1,0:T(8,128)(2,1)S(1)}, u32[]{:S(2)}, u32[]{:S(2)}) collective-permute-start(bf16[16,8192]{1,0:T(8,128)(2,1)S(1)} %pass_on.2.refs_2_), channel_id=1, source_target_pairs={{0,4},{1,5},{4,8},{5,9},{8,12},{9,13},{12,14},{13,15},{14,10},{15,... | collective-permute-start | bytes 786440 | tf_op jit(solution)/shard_map/ppermute | solution.py:138
  12.3 4.6 %load_rows.3.refs_1_ = bf16[3328,1792]{1,0:T(8,128)(2,1)S(1)} custom-call(bf16[8192,896]{1,0:T(8,128)(2,1)} %refs_0_.7, bf16[8192,896]{1,0:T(8,128)(2,1)} %refs_1_.5, bf16[16,8192]{1,0:T(8,128)(2,1)S(1)} %pass_on.2.refs_2_), custom_call_target="tpu_custom_call" | custom-call | bytes 23855104 | tf_op jit(solution)/shard_map/load_rows/pallas_call | solution.py:292
  17.0 0.8 collective-permute-done.2.refs_0_.refs_2_
  17.8 1.5 %collective-permute-start.4 = (bf16[16,8192]{1,0:T(8,128)(2,1)S(1)}, bf16[16,8192]{1,0:T(8,128)(2,1)S(1)}, u32[]{:S(2)}, u32[]{:S(2)}) collective-permute-start(bf16[16,8192]{1,0:T(8,128)(2,1)S(1)} %pass_on.3), channel_id=1, source_target_pairs={{0,4},{1,5},{4,8},{5,9},{8,12},{9,13},{12,14},{13,15},{14,10},{15,... | collective-permute-start | bytes 786440 | tf_op jit(solution)/shard_map/ppermute | solution.py:138
  19.9 0.6 row_masks.1
  20.4 3.9 %collective-permute-done.4.refs_4_.refs_0_ = bf16[16,8192]{1,0:T(8,128)(2,1)S(1)} collective-permute-done((bf16[16,8192]{1,0:T(8,128)(2,1)S(1)}, bf16[16,8192]{1,0:T(8,128)(2,1)S(1)}, u32[]{:S(2)}, u32[]{:S(2)}) %collective-permute-start.4) | collective-permute-done | bytes 262176 | tf_op jit(solution)/shard_map/ppermute | solution.py:138
  24.4 1.3 %collective-permute-done.5.refs_5_.refs_0_ = bf16[16,8192]{1,0:T(8,128)(2,1)S(1)} collective-permute-done((bf16[16,8192]{1,0:T(8,128)(2,1)S(1)}, bf16[16,8192]{1,0:T(8,128)(2,1)S(1)}, u32[]{:S(2)}, u32[]{:S(2)}) %collective-permute-start.5) | collective-permute-done | bytes 262176 | tf_op jit(solution)/shard_map/ppermute | solution.py:139
  25.9 1.6 %collective-permute-start.6 = (bf16[16,4096]{1,0:T(8,128)(2,1)S(1)}, bf16[16,4096]{1,0:T(8,128)(2,1)S(1)}, u32[]{:S(2)}, u32[]{:S(2)}) collective-permute-start(bf16[16,4096]{1,0:T(8,128)(2,1)S(1)} %column_half.2), channel_id=1, source_target_pairs={{0,4},{1,5},{4,8},{5,9},{8,12},{9,13},{12,14},{13,15},{14,10},{15,... | collective-permute-start | bytes 393224 | tf_op jit(solution)/shard_map/ppermute | solution.py:151
  28.0 3.8 %collective-permute-done.6.refs_0_ = bf16[16,4096]{1,0:T(8,128)(2,1)S(1)} collective-permute-done((bf16[16,4096]{1,0:T(8,128)(2,1)S(1)}, bf16[16,4096]{1,0:T(8,128)(2,1)S(1)}, u32[]{:S(2)}, u32[]{:S(2)}) %collective-permute-start.6) | collective-permute-done | bytes 131104 | tf_op jit(solution)/shard_map/ppermute | solution.py:151
  31.8 1.4 %collective-permute-done.7.refs_1_ = bf16[16,4096]{1,0:T(8,128)(2,1)S(1)} collective-permute-done((bf16[16,4096]{1,0:T(8,128)(2,1)S(1)}, bf16[16,4096]{1,0:T(8,128)(2,1)S(1)}, u32[]{:S(2)}, u32[]{:S(2)}) %collective-permute-start.7) | collective-permute-done | bytes 131104 | tf_op jit(solution)/shard_map/ppermute | solution.py:152
  33.3 1.5 %collective-permute-done.10.refs_5_ = bf16[16,8192]{1,0:T(8,128)(2,1)S(1)} collective-permute-done((bf16[16,8192]{1,0:T(8,128)(2,1)S(1)}, bf16[16,8192]{1,0:T(8,128)(2,1)S(1)}, u32[]{:S(2)}, u32[]{:S(2)}) %collective-permute-start.10) | collective-permute-done | bytes 262176 | tf_op jit(solution)/shard_map/ppermute | solution.py:157
  34.8 2.0 %shrink_rows.1 = (bf16[256,8192]{1,0:T(8,128)(2,1)S(1)}, bf16[256,64]{1,0:T(8,128)(2,1)S(1)}) custom-call(bf16[16,8192]{1,0:T(8,128)(2,1)S(1)} %copy-done.1, bf16[96,8192]{1,0:T(8,128)(2,1)S(1)} %join_pieces.2.refs_1_, bf16[16,8192]{1,0:T(8,128)(2,1)S(1)} %join_pieces.3.refs_2_, bf16[16,8192]{1,0:T(8,128)(2,1)S(1)} %collective-permute-done.8.refs_3_, ...), custom_call_target="tpu_custom_call" | custom-call | flops 268435456 | bytes 8388608 | tf_op jit(solution)/shard_map/shrink_rows/pallas_call | solution.py:78
  37.0 1.1 %collective-permute-done.11.refs_1_ = bf16[256,64]{1,0:T(8,128)(2,1)S(1)} collective-permute-done((bf16[256,64]{1,0:T(8,128)(2,1)S(1)}, bf16[256,64]{1,0:T(8,128)(2,1)S(1)}, u32[]{:S(2)}, u32[]{:S(2)}) %collective-permute-start.11) | collective-permute-done | bytes 32800 | tf_op jit(solution)/shard_map/ppermute | solution.py:552
  38.7 3.2 %mixed_rows.2.refs_2_ = f32[256,1792]{1,0:T(8,128)S(1)} custom-call(bf16[256,8192]{1,0:T(8,128)(2,1)S(1)} %get-tuple-element.15.refs_0_.rows_ref, bf16[3328,1792]{1,0:T(8,128)(2,1)S(1)} %load_rows.2.refs_1_, bf16[256,64]{1,0:T(8,128)(2,1)S(1)} %add_coefficients.3.refs_2_.refs_0_), custom_call_target="tpu_custom_call" | custom-call | flops 3053453312 | bytes 11927552 | tf_op jit(solution)/shard_map/mixed_rows/pallas_call | solution.py:78
  41.9 0.6 collective-permute-done.12.refs_1_
  42.5 1.6 %collective-permute-start.13 = (bf16[256,64]{1,0:T(8,128)(2,1)S(1)}, bf16[256,64]{1,0:T(8,128)(2,1)S(1)}, u32[]{:S(2)}, u32[]{:S(2)}) collective-permute-start(bf16[256,64]{1,0:T(8,128)(2,1)S(1)} %add_coefficients.4.refs_3_.refs_0_), channel_id=1, source_target_pairs={{0,4},{1,5},{2,6},{3,7},{4,0},{5,1},{6,2},{7,3},{8,12},{9,13},{10,... | collective-permute-start | bytes 98312 | tf_op jit(solution)/shard_map/ppermute | solution.py:552
  44.1 3.2 %mixed_rows.3.refs_2_ = f32[256,1792]{1,0:T(8,128)S(1)} custom-call(bf16[256,8192]{1,0:T(8,128)(2,1)S(1)} %get-tuple-element.15.refs_0_.rows_ref, bf16[3328,1792]{1,0:T(8,128)(2,1)S(1)} %load_rows.3.refs_1_, f32[256,1792]{1,0:T(8,128)S(1)} %mixed_rows.2.refs_2_, bf16[256,64]{1,0:T(8,128)(2,1)S(1)} %add_coefficients.4.refs_3_.refs_0_), custom_call_target="tpu_custom_call" | custom-call | flops 3053453312 | bytes 11927552 | tf_op jit(solution)/shard_map/mixed_rows/pallas_call | solution.py:78
  47.5 2.0 %collective-permute-start.14 = (bf16[256,64]{1,0:T(8,128)(2,1)S(1)}, bf16[256,64]{1,0:T(8,128)(2,1)S(1)}, u32[]{:S(2)}, u32[]{:S(2)}) collective-permute-start(bf16[256,64]{1,0:T(8,128)(2,1)S(1)} %add_coefficients.5.refs_3_.refs_0_), channel_id=1, source_target_pairs={{0,8},{1,9},{2,10},{3,11},{4,12},{5,13},{6,14},{7,15},{8,0},{9,1},... | collective-permute-start | bytes 98312 | tf_op jit(solution)/shard_map/ppermute | solution.py:552
  49.5 4.6 %stream_rows.1.refs_5_ = f32[256,1792]{1,0:T(8,128)S(1)} custom-call(bf16[256,8192]{1,0:T(8,128)(2,1)S(1)} %get-tuple-element.15.refs_0_.rows_ref, bf16[8192,896]{1,0:T(8,128)(2,1)} %refs_0_.7, bf16[8192,896]{1,0:T(8,128)(2,1)} %refs_1_.5, f32[256,1792]{1,0:T(8,128)S(1)} %mixed_rows.3.refs_2_, bf16[256,64]{1,0:T(8,128)(2,1)S(1)} %add_coefficients.5.refs_3_.refs_0_), custom_call_target="tpu_custom_call" | custom-call | flops 1409286144 | bytes 11010048 | tf_op jit(solution)/shard_map/stream_rows/pallas_call | solution.py:395
  54.2 1.0 %hidden_rows.1 = bf16[256,896]{1,0:T(8,128)(2,1)S(1)} custom-call(bf16[256,64]{1,0:T(8,128)(2,1)S(1)} %add_coefficients.5.refs_3_.refs_0_, bf16[256,64]{1,0:T(8,128)(2,1)S(1)} %collective-permute-done.14.refs_1_, bf16[256,256]{1,0:T(8,128)(2,1)S(1)} %get-tuple-element.16.refs_2_, bf16[256,1024]{1,0:T(8,128)(2,1)S(1)} %get-tuple-element.17.refs_3_, ...), custom_call_target="tpu_custom_call" | custom-call | flops 469762048 | bytes 1835008 | tf_op jit(solution)/shard_map/hidden_rows/pallas_call | solution.py:78
  55.2 2.4 %fusion.4.refs_0_ = bf16[256,4096]{1,0:T(8,128)(2,1)S(1)} fusion(bf16[256,896]{1,0:T(8,128)(2,1)S(1)} %hidden_rows.1, bf16[896,8192]{1,0:T(8,128)(2,1)S(1)} %bitcast.17), kind=kOutput, calls=%fused_computation.4 | convolution fusion | flops 1880096768 | bytes 9895936 | tf_op jit(solution)/shard_map/dot_general | solution.py:569
  57.8 2.4 %fusion.7.refs_0_.refs_3_.refs_4_ = bf16[256,4096]{1,0:T(8,128)(2,1)S(1)} fusion(bf16[256,896]{1,0:T(8,128)(2,1)S(1)} %hidden_rows.1, bf16[896,8192]{1,0:T(8,128)(2,1)S(1)} %bitcast.17), kind=kOutput, calls=%fused_computation.5 | convolution fusion | flops 1880096768 | bytes 9895936 | tf_op jit(solution)/shard_map/dot_general | solution.py:569
  60.3 0.6 collective-permute-start.17
  60.9 1.3 %collective-permute-start.16 = (bf16[16,4096]{1,0:T(8,128)(2,1)S(1)}, bf16[16,4096]{1,0:T(8,128)(2,1)S(1)}, u32[]{:S(2)}, u32[]{:S(2)}) collective-permute-start(bf16[16,4096]{1,0:T(8,128)(2,1)S(1)} %add_blocks.13.refs_2_), channel_id=1, source_target_pairs={{0,4},{1,5},{4,8},{5,9},{8,12},{9,13},{12,14},{13,15},{14,10},{15,... | collective-permute-start | bytes 393224 | tf_op jit(solution)/shard_map/ppermute | solution.py:489
  62.2 0.9 %collective-permute-done.17.refs_1_.refs_4_.refs_5_ = bf16[128,4096]{1,0:T(8,128)(2,1)S(1)} collective-permute-done((bf16[128,4096]{1,0:T(8,128)(2,1)S(1)}, bf16[128,4096]{1,0:T(8,128)(2,1)S(1)}, u32[]{:S(2)}, u32[]{:S(2)}) %collective-permute-start.17) | collective-permute-done | bytes 1048608 | tf_op jit(solution)/shard_map/ppermute | solution.py:575
  63.3 1.1 %collective-permute-start.21 = (bf16[16,4096]{1,0:T(8,128)(2,1)S(1)}, bf16[16,4096]{1,0:T(8,128)(2,1)S(1)}, u32[]{:S(2)}, u32[]{:S(2)}) collective-permute-start(bf16[16,4096]{1,0:T(8,128)(2,1)S(1)} %add_blocks.16.refs_3_), channel_id=1, source_target_pairs={{0,2},{1,3},{4,0},{5,1},{8,4},{9,5},{12,8},{13,9},{14,12},{15,13},... | collective-permute-start | bytes 393224 | tf_op jit(solution)/shard_map/ppermute | solution.py:489
  64.3 1.0 %collective-permute-start.20 = (bf16[16,4096]{1,0:T(8,128)(2,1)S(1)}, bf16[16,4096]{1,0:T(8,128)(2,1)S(1)}, u32[]{:S(2)}, u32[]{:S(2)}) collective-permute-start(bf16[16,4096]{1,0:T(8,128)(2,1)S(1)} %add_blocks.15.refs_2_), channel_id=1, source_target_pairs={{0,4},{1,5},{4,8},{5,9},{8,12},{9,13},{12,14},{13,15},{14,10},{15,... | collective-permute-start | bytes 393224 | tf_op jit(solution)/shard_map/ppermute | solution.py:489
  65.4 1.0 %collective-permute-start.19 = (bf16[16,4096]{1,0:T(8,128)(2,1)S(1)}, bf16[16,4096]{1,0:T(8,128)(2,1)S(1)}, u32[]{:S(2)}, u32[]{:S(2)}) collective-permute-start(bf16[16,4096]{1,0:T(8,128)(2,1)S(1)} %add_blocks.14.refs_2_), channel_id=1, source_target_pairs={{0,2},{1,3},{4,0},{5,1},{8,4},{9,5},{12,8},{13,9},{14,12},{15,13},... | collective-permute-start | bytes 393224 | tf_op jit(solution)/shard_map/ppermute | solution.py:489
  66.6 1.1 %collective-permute-start.18 = (bf16[16,4096]{1,0:T(8,128)(2,1)S(1)}, bf16[16,4096]{1,0:T(8,128)(2,1)S(1)}, u32[]{:S(2)}, u32[]{:S(2)}) collective-permute-start(bf16[16,4096]{1,0:T(8,128)(2,1)S(1)} %add_blocks.17.refs_3_), channel_id=1, source_target_pairs={{0,4},{1,5},{4,8},{5,9},{8,12},{9,13},{12,14},{13,15},{14,10},{15,... | collective-permute-start | bytes 393224 | tf_op jit(solution)/shard_map/ppermute | solution.py:489
  67.7 1.9 %collective-permute-done.21.refs_2_ = bf16[16,4096]{1,0:T(8,128)(2,1)S(1)} collective-permute-done((bf16[16,4096]{1,0:T(8,128)(2,1)S(1)}, bf16[16,4096]{1,0:T(8,128)(2,1)S(1)}, u32[]{:S(2)}, u32[]{:S(2)}) %collective-permute-start.21) | collective-permute-done | bytes 131104 | tf_op jit(solution)/shard_map/ppermute | solution.py:489
  69.7 1.1 %collective-permute-start.23 = (bf16[16,4096]{1,0:T(8,128)(2,1)S(1)}, bf16[16,4096]{1,0:T(8,128)(2,1)S(1)}, u32[]{:S(2)}, u32[]{:S(2)}) collective-permute-start(bf16[16,4096]{1,0:T(8,128)(2,1)S(1)} %add_blocks.18.refs_3_), channel_id=1, source_target_pairs={{0,2},{1,3},{4,0},{5,1},{8,4},{9,5},{12,8},{13,9},{14,12},{15,13},... | collective-permute-start | bytes 393224 | tf_op jit(solution)/shard_map/ppermute | solution.py:489
  70.8 1.1 %collective-permute-start.26 = (bf16[16,4096]{1,0:T(8,128)(2,1)S(1)}, bf16[16,4096]{1,0:T(8,128)(2,1)S(1)}, u32[]{:S(2)}, u32[]{:S(2)}) collective-permute-start(bf16[16,4096]{1,0:T(8,128)(2,1)S(1)} %add_blocks.19.refs_3_), channel_id=1, source_target_pairs={{0,4},{1,5},{4,8},{5,9},{8,12},{9,13},{12,14},{13,15},{14,10},{15,... | collective-permute-start | bytes 393224 | tf_op jit(solution)/shard_map/ppermute | solution.py:489
  72.4 1.1 %collective-permute-start.25 = (bf16[16,4096]{1,0:T(8,128)(2,1)S(1)}, bf16[16,4096]{1,0:T(8,128)(2,1)S(1)}, u32[]{:S(2)}, u32[]{:S(2)}) collective-permute-start(bf16[16,4096]{1,0:T(8,128)(2,1)S(1)} %add_blocks.20.refs_3_), channel_id=1, source_target_pairs={{0,2},{1,3},{4,0},{5,1},{8,4},{9,5},{12,8},{13,9},{14,12},{15,13},... | collective-permute-start | bytes 393224 | tf_op jit(solution)/shard_map/ppermute | solution.py:489
  73.6 1.7 %collective-permute-done.23.refs_2_ = bf16[16,4096]{1,0:T(8,128)(2,1)S(1)} collective-permute-done((bf16[16,4096]{1,0:T(8,128)(2,1)S(1)}, bf16[16,4096]{1,0:T(8,128)(2,1)S(1)}, u32[]{:S(2)}, u32[]{:S(2)}) %collective-permute-start.23) | collective-permute-done | bytes 131104 | tf_op jit(solution)/shard_map/ppermute | solution.py:489
  75.4 1.1 %collective-permute-start.24 = (bf16[16,4096]{1,0:T(8,128)(2,1)S(1)}, bf16[16,4096]{1,0:T(8,128)(2,1)S(1)}, u32[]{:S(2)}, u32[]{:S(2)}) collective-permute-start(bf16[16,4096]{1,0:T(8,128)(2,1)S(1)} %add_blocks.22.refs_3_), channel_id=1, source_target_pairs={{0,2},{1,3},{4,0},{5,1},{8,4},{9,5},{12,8},{13,9},{14,12},{15,13},... | collective-permute-start | bytes 393224 | tf_op jit(solution)/shard_map/ppermute | solution.py:489
  76.4 1.0 %collective-permute-start.22 = (bf16[16,4096]{1,0:T(8,128)(2,1)S(1)}, bf16[16,4096]{1,0:T(8,128)(2,1)S(1)}, u32[]{:S(2)}, u32[]{:S(2)}) collective-permute-start(bf16[16,4096]{1,0:T(8,128)(2,1)S(1)} %add_blocks.21.refs_3_), channel_id=1, source_target_pairs={{0,4},{1,5},{4,8},{5,9},{8,12},{9,13},{12,14},{13,15},{14,10},{15,... | collective-permute-start | bytes 393224 | tf_op jit(solution)/shard_map/ppermute | solution.py:489
  77.5 1.1 %collective-permute-start.29 = (bf16[16,4096]{1,0:T(8,128)(2,1)S(1)}, bf16[16,4096]{1,0:T(8,128)(2,1)S(1)}, u32[]{:S(2)}, u32[]{:S(2)}) collective-permute-start(bf16[16,4096]{1,0:T(8,128)(2,1)S(1)} %add_blocks.23.refs_3_), channel_id=1, source_target_pairs={{0,4},{1,5},{4,8},{5,9},{8,12},{9,13},{12,14},{13,15},{14,10},{15,... | collective-permute-start | bytes 393224 | tf_op jit(solution)/shard_map/ppermute | solution.py:489
  79.0 1.1 %collective-permute-start.28 = (bf16[16,4096]{1,0:T(8,128)(2,1)S(1)}, bf16[16,4096]{1,0:T(8,128)(2,1)S(1)}, u32[]{:S(2)}, u32[]{:S(2)}) collective-permute-start(bf16[16,4096]{1,0:T(8,128)(2,1)S(1)} %add_blocks.24.refs_6_), channel_id=1, source_target_pairs={{0,2},{1,3},{4,0},{5,1},{8,4},{9,5},{12,8},{13,9},{14,12},{15,13},... | collective-permute-start | bytes 393224 | tf_op jit(solution)/shard_map/ppermute | solution.py:489
  80.0 1.7 %collective-permute-done.24.refs_5_ = bf16[16,4096]{1,0:T(8,128)(2,1)S(1)} collective-permute-done((bf16[16,4096]{1,0:T(8,128)(2,1)S(1)}, bf16[16,4096]{1,0:T(8,128)(2,1)S(1)}, u32[]{:S(2)}, u32[]{:S(2)}) %collective-permute-start.24) | collective-permute-done | bytes 131104 | tf_op jit(solution)/shard_map/ppermute | solution.py:489
  81.9 1.1 %collective-permute-start.27 = (bf16[16,4096]{1,0:T(8,128)(2,1)S(1)}, bf16[16,4096]{1,0:T(8,128)(2,1)S(1)}, u32[]{:S(2)}, u32[]{:S(2)}) collective-permute-start(bf16[16,4096]{1,0:T(8,128)(2,1)S(1)} %get-tuple-element.18), channel_id=1, source_target_pairs={{0,4},{1,5},{4,8},{5,9},{8,12},{9,13},{12,14},{13,15},{14,10},{15,... | collective-permute-start | bytes 393224 | tf_op jit(solution)/shard_map/ppermute | solution.py:489
  83.0 1.0 %collective-permute-start.30 = (bf16[16,4096]{1,0:T(8,128)(2,1)S(1)}, bf16[16,4096]{1,0:T(8,128)(2,1)S(1)}, u32[]{:S(2)}, u32[]{:S(2)}) collective-permute-start(bf16[16,4096]{1,0:T(8,128)(2,1)S(1)} %get-tuple-element.19), channel_id=1, source_target_pairs={{0,2},{1,3},{4,0},{5,1},{8,4},{9,5},{12,8},{13,9},{14,12},{15,13},... | collective-permute-start | bytes 393224 | tf_op jit(solution)/shard_map/ppermute | solution.py:489
  84.0 1.4 %collective-permute-done.28.refs_3_ = bf16[16,4096]{1,0:T(8,128)(2,1)S(1)} collective-permute-done((bf16[16,4096]{1,0:T(8,128)(2,1)S(1)}, bf16[16,4096]{1,0:T(8,128)(2,1)S(1)}, u32[]{:S(2)}, u32[]{:S(2)}) %collective-permute-start.28) | collective-permute-done | bytes 131104 | tf_op jit(solution)/shard_map/ppermute | solution.py:489
  85.4 1.5 %collective-permute-done.27.refs_2_ = bf16[16,4096]{1,0:T(8,128)(2,1)S(1)} collective-permute-done((bf16[16,4096]{1,0:T(8,128)(2,1)S(1)}, bf16[16,4096]{1,0:T(8,128)(2,1)S(1)}, u32[]{:S(2)}, u32[]{:S(2)}) %collective-permute-start.27) | collective-permute-done | bytes 131104 | tf_op jit(solution)/shard_map/ppermute | solution.py:489
  86.9 1.0 %collective-permute-done.30.refs_7_ = bf16[16,4096]{1,0:T(8,128)(2,1)S(1)} collective-permute-done((bf16[16,4096]{1,0:T(8,128)(2,1)S(1)}, bf16[16,4096]{1,0:T(8,128)(2,1)S(1)}, u32[]{:S(2)}, u32[]{:S(2)}) %collective-permute-start.30) | collective-permute-done | bytes 131104 | tf_op jit(solution)/shard_map/ppermute | solution.py:489
  87.9 1.0 %finish_rows.1 = (bf16[16,8192]{1,0:T(8,128)(2,1)}, bf16[16,8192]{1,0:T(8,128)(2,1)}) custom-call(bf16[256,4096]{1,0:T(8,128)(2,1)S(1)} %fusion.4.refs_0_, bf16[128,4096]{1,0:T(8,128)(2,1)S(1)} %collective-permute-done.15.refs_1_, bf16[16,4096]{1,0:T(8,128)(2,1)S(1)} %collective-permute-done.27.refs_2_, ...), custom_call_target="tpu_custom_call" | custom-call | tf_op jit(solution)/shard_map/finish_rows/pallas_call | solution.py:78
  (75 shorter events, 4.5 us)
Async XLA Ops:
  0.6 9.5 %collective-permute-start = (bf16[16,8192]{1,0:T(8,128)(2,1)}, bf16[16,8192]{1,0:T(8,128)(2,1)S(1)}, u32[]{:S(2)}, u32[]{:S(2)}) collective-permute-start(bf16[16,8192]{1,0:T(8,128)(2,1)} %refs_8_.1), channel_id=1, source_target_pairs={{0,4},{1,5},{4,8},{5,9},{8,12},{9,13},{12,14},{13,15},{14,10},{15,... | collective-permute-start | bytes 786440 | tf_op jit(solution)/shard_map/ppermute | solution.py:138
  3.7 8.3 %collective-permute-start.1 = (bf16[16,8192]{1,0:T(8,128)(2,1)}, bf16[16,8192]{1,0:T(8,128)(2,1)S(1)}, u32[]{:S(2)}, u32[]{:S(2)}) collective-permute-start(bf16[16,8192]{1,0:T(8,128)(2,1)} %refs_8_.1), channel_id=1, source_target_pairs={{0,2},{1,3},{4,0},{5,1},{8,4},{9,5},{12,8},{13,9},{14,12},{15,13},... | collective-permute-start | bytes 786440 | tf_op jit(solution)/shard_map/ppermute | solution.py:139
  10.2 7.5 %collective-permute-start.2 = (bf16[16,8192]{1,0:T(8,128)(2,1)S(1)}, bf16[16,8192]{1,0:T(8,128)(2,1)S(1)}, u32[]{:S(2)}, u32[]{:S(2)}) collective-permute-start(bf16[16,8192]{1,0:T(8,128)(2,1)S(1)} %pass_on.2.refs_2_), channel_id=1, source_target_pairs={{0,4},{1,5},{4,8},{5,9},{8,12},{9,13},{12,14},{13,15},{14,10},{15,... | collective-permute-start | bytes 786440 | tf_op jit(solution)/shard_map/ppermute | solution.py:138
  12.0 7.2 %collective-permute-start.3 = (bf16[16,8192]{1,0:T(8,128)(2,1)S(1)}, bf16[16,8192]{1,0:T(8,128)(2,1)S(1)}, u32[]{:S(2)}, u32[]{:S(2)}) collective-permute-start(bf16[16,8192]{1,0:T(8,128)(2,1)S(1)} %collective-permute-done.1.refs_1_), channel_id=1, source_target_pairs={{0,2},{1,3},{4,0},{5,1},{8,4},{9,5},{12,8},{13,9},{14,12},{15,13},... | collective-permute-start | bytes 786440 | tf_op jit(solution)/shard_map/ppermute | solution.py:139
  16.9 3.0 %copy-start.2 = (bf16[1,8192,64]{1,2,0:T(8,128)(2,1)S(1)}, bf16[1,8192,64]{1,2,0:T(8,128)(2,1)}, u32[]{:S(2)}) copy-start(bf16[1,8192,64]{1,2,0:T(8,128)(2,1)} %param.16) | copy-start | bytes 3145732
  16.9 3.0 %copy-start.3 = (s32[32]{0:T(128)S(1)}, s32[32]{0:T(128)}, u32[]{:S(2)}) copy-start(s32[32]{0:T(128)} %param.20) | copy-start | bytes 388
  16.9 2.9 %copy-start.4 = (s32[32]{0:T(128)S(1)}, s32[32]{0:T(128)}, u32[]{:S(2)}) copy-start(s32[32]{0:T(128)} %param.21) | copy-start | bytes 388
  16.9 2.9 %copy-start.5 = (s32[16]{0:T(128)S(1)}, s32[16]{0:T(128)}, u32[]{:S(2)}) copy-start(s32[16]{0:T(128)} %param.18) | copy-start | bytes 196
  16.9 2.9 %copy-start.6 = (s32[16]{0:T(128)S(1)}, s32[16]{0:T(128)}, u32[]{:S(2)}) copy-start(s32[16]{0:T(128)} %param.19) | copy-start | bytes 196
  16.9 11.1 %copy-start.1 = (bf16[16,8192]{1,0:T(8,128)(2,1)S(1)}, bf16[16,8192]{1,0:T(8,128)(2,1)}, u32[]{:S(2)}) copy-start(bf16[16,8192]{1,0:T(8,128)(2,1)} %refs_8_.1) | copy-start | bytes 786436
  17.8 6.6 %collective-permute-start.4 = (bf16[16,8192]{1,0:T(8,128)(2,1)S(1)}, bf16[16,8192]{1,0:T(8,128)(2,1)S(1)}, u32[]{:S(2)}, u32[]{:S(2)}) collective-permute-start(bf16[16,8192]{1,0:T(8,128)(2,1)S(1)} %pass_on.3), channel_id=1, source_target_pairs={{0,4},{1,5},{4,8},{5,9},{8,12},{9,13},{12,14},{13,15},{14,10},{15,... | collective-permute-start | bytes 786440 | tf_op jit(solution)/shard_map/ppermute | solution.py:138
  19.3 6.4 %collective-permute-start.5 = (bf16[16,8192]{1,0:T(8,128)(2,1)S(1)}, bf16[16,8192]{1,0:T(8,128)(2,1)S(1)}, u32[]{:S(2)}, u32[]{:S(2)}) collective-permute-start(bf16[16,8192]{1,0:T(8,128)(2,1)S(1)} %collective-permute-done.3.refs_3_), channel_id=1, source_target_pairs={{0,2},{1,3},{4,0},{5,1},{8,4},{9,5},{12,8},{13,9},{14,12},{15,13},... | collective-permute-start | bytes 786440 | tf_op jit(solution)/shard_map/ppermute | solution.py:139
  25.8 9.0 %collective-permute-start.9 = (bf16[96,8192]{1,0:T(8,128)(2,1)S(1)}, bf16[96,8192]{1,0:T(8,128)(2,1)S(1)}, u32[]{:S(2)}, u32[]{:S(2)}) collective-permute-start(bf16[96,8192]{1,0:T(8,128)(2,1)S(1)} %join_pieces.2.refs_1_), channel_id=1, source_target_pairs={{0,1},{1,0},{2,3},{3,2},{4,5},{5,4},{6,7},{7,6},{8,9},{9,8},{10,11... | collective-permute-start | bytes 4718600 | tf_op jit(solution)/shard_map/ppermute | solution.py:148
  25.9 5.9 %collective-permute-start.6 = (bf16[16,4096]{1,0:T(8,128)(2,1)S(1)}, bf16[16,4096]{1,0:T(8,128)(2,1)S(1)}, u32[]{:S(2)}, u32[]{:S(2)}) collective-permute-start(bf16[16,4096]{1,0:T(8,128)(2,1)S(1)} %column_half.2), channel_id=1, source_target_pairs={{0,4},{1,5},{4,8},{5,9},{8,12},{9,13},{12,14},{13,15},{14,10},{15,... | collective-permute-start | bytes 393224 | tf_op jit(solution)/shard_map/ppermute | solution.py:151
  27.5 5.7 %collective-permute-start.7 = (bf16[16,4096]{1,0:T(8,128)(2,1)S(1)}, bf16[16,4096]{1,0:T(8,128)(2,1)S(1)}, u32[]{:S(2)}, u32[]{:S(2)}) collective-permute-start(bf16[16,4096]{1,0:T(8,128)(2,1)S(1)} %column_half.3), channel_id=1, source_target_pairs={{0,2},{1,3},{4,0},{5,1},{8,4},{9,5},{12,8},{13,9},{14,12},{15,13},... | collective-permute-start | bytes 393224 | tf_op jit(solution)/shard_map/ppermute | solution.py:152
  28.0 5.3 %collective-permute-start.8 = (bf16[16,8192]{1,0:T(8,128)(2,1)S(1)}, bf16[16,8192]{1,0:T(8,128)(2,1)S(1)}, u32[]{:S(2)}, u32[]{:S(2)}) collective-permute-start(bf16[16,8192]{1,0:T(8,128)(2,1)S(1)} %copy-done.1), channel_id=1, source_target_pairs={{0,1},{1,0},{2,3},{3,2},{4,5},{5,4},{6,7},{7,6},{8,9},{9,8},{10,11... | collective-permute-start | bytes 786440 | tf_op jit(solution)/shard_map/ppermute | solution.py:141
  33.2 1.6 %collective-permute-start.10 = (bf16[16,8192]{1,0:T(8,128)(2,1)S(1)}, bf16[16,8192]{1,0:T(8,128)(2,1)S(1)}, u32[]{:S(2)}, u32[]{:S(2)}) collective-permute-start(bf16[16,8192]{1,0:T(8,128)(2,1)S(1)} %join_pieces.3.refs_2_), channel_id=1, source_target_pairs={{0,1},{1,0},{2,3},{3,2},{4,5},{5,4},{6,7},{7,6},{8,9},{9,8},{10,11... | collective-permute-start | bytes 786440 | tf_op jit(solution)/shard_map/ppermute | solution.py:157
  36.8 1.3 %collective-permute-start.11 = (bf16[256,64]{1,0:T(8,128)(2,1)S(1)}, bf16[256,64]{1,0:T(8,128)(2,1)S(1)}, u32[]{:S(2)}, u32[]{:S(2)}) collective-permute-start(bf16[256,64]{1,0:T(8,128)(2,1)S(1)} %get-tuple-element.14.refs_0_), channel_id=1, source_target_pairs={{0,1},{1,0},{2,3},{3,2},{4,5},{5,4},{6,7},{7,6},{8,9},{9,8},{10,11... | collective-permute-start | bytes 98312 | tf_op jit(solution)/shard_map/ppermute | solution.py:552
  38.1 4.3 %collective-permute-start.12 = (bf16[256,64]{1,0:T(8,128)(2,1)S(1)}, bf16[256,64]{1,0:T(8,128)(2,1)S(1)}, u32[]{:S(2)}, u32[]{:S(2)}) collective-permute-start(bf16[256,64]{1,0:T(8,128)(2,1)S(1)} %add_coefficients.3.refs_2_.refs_0_), channel_id=1, source_target_pairs={{0,2},{1,3},{2,0},{3,1},{4,6},{5,7},{6,4},{7,5},{8,10},{9,11},{10,... | collective-permute-start | bytes 98312 | tf_op jit(solution)/shard_map/ppermute | solution.py:552
  42.5 4.9 %collective-permute-start.13 = (bf16[256,64]{1,0:T(8,128)(2,1)S(1)}, bf16[256,64]{1,0:T(8,128)(2,1)S(1)}, u32[]{:S(2)}, u32[]{:S(2)}) collective-permute-start(bf16[256,64]{1,0:T(8,128)(2,1)S(1)} %add_coefficients.4.refs_3_.refs_0_), channel_id=1, source_target_pairs={{0,4},{1,5},{2,6},{3,7},{4,0},{5,1},{6,2},{7,3},{8,12},{9,13},{10,... | collective-permute-start | bytes 98312 | tf_op jit(solution)/shard_map/ppermute | solution.py:552
  47.4 7.8 %slice-start = ((s8[14680064]{0:T(1024)(128)(4,1)}), s8[4194304]{0:T(1024)(128)(4,1)S(1)}, s32[]{:S(2)}) async-start(s8[14680064]{0:T(1024)(128)(4,1)} %bitcast.16), calls=%async_computation | async-start | bytes 8388608
  47.4 6.7 %copy-start = (bf16[16,64,896]{2,1,0:T(8,128)(2,1)S(1)}, bf16[16,64,896]{2,1,0:T(8,128)(2,1)}, u32[]{:S(2)}) copy-start(bf16[16,64,896]{2,1,0:T(8,128)(2,1)} %param.17) | copy-start | bytes 5505028
  47.5 7.7 %slice-start.1 = ((s8[14680064]{0:T(1024)(128)(4,1)}), s8[4194304]{0:T(1024)(128)(4,1)S(1)}, s32[]{:S(2)}) async-start(s8[14680064]{0:T(1024)(128)(4,1)} %bitcast.16), calls=%async_computation.1 | async-start | bytes 8388608
  47.5 7.7 %slice-start.2 = ((s8[14680064]{0:T(1024)(128)(4,1)}), s8[4194304]{0:T(1024)(128)(4,1)S(1)}, s32[]{:S(2)}) async-start(s8[14680064]{0:T(1024)(128)(4,1)} %bitcast.16), calls=%async_computation.2 | async-start | bytes 8388608
  47.5 7.7 %slice-start.3 = ((s8[14680064]{0:T(1024)(128)(4,1)}), s8[2097152]{0:T(1024)(128)(4,1)S(1)}, s32[]{:S(2)}) async-start(s8[14680064]{0:T(1024)(128)(4,1)} %bitcast.16), calls=%async_computation.3 | async-start | bytes 4194304
  47.5 6.7 %collective-permute-start.14 = (bf16[256,64]{1,0:T(8,128)(2,1)S(1)}, bf16[256,64]{1,0:T(8,128)(2,1)S(1)}, u32[]{:S(2)}, u32[]{:S(2)}) collective-permute-start(bf16[256,64]{1,0:T(8,128)(2,1)S(1)} %add_coefficients.5.refs_3_.refs_0_), channel_id=1, source_target_pairs={{0,8},{1,9},{2,10},{3,11},{4,12},{5,13},{6,14},{7,15},{8,0},{9,1},... | collective-permute-start | bytes 98312 | tf_op jit(solution)/shard_map/ppermute | solution.py:552
  57.7 3.2 %collective-permute-start.15 = (bf16[128,4096]{1,0:T(8,128)(2,1)S(1)}, bf16[128,4096]{1,0:T(8,128)(2,1)S(1)}, u32[]{:S(2)}, u32[]{:S(2)}) collective-permute-start(bf16[128,4096]{1,0:T(8,128)(2,1)S(1)} %slice.16), channel_id=1, source_target_pairs={{0,1},{1,0},{2,3},{3,2},{4,5},{5,4},{6,7},{7,6},{8,9},{9,8},{10,11... | collective-permute-start | bytes 3145736 | tf_op jit(solution)/shard_map/ppermute | solution.py:575
  60.3 2.8 %collective-permute-start.17 = (bf16[128,4096]{1,0:T(8,128)(2,1)S(1)}, bf16[128,4096]{1,0:T(8,128)(2,1)S(1)}, u32[]{:S(2)}, u32[]{:S(2)}) collective-permute-start(bf16[128,4096]{1,0:T(8,128)(2,1)S(1)} %slice.17), channel_id=1, source_target_pairs={{0,1},{1,0},{2,3},{3,2},{4,5},{5,4},{6,7},{7,6},{8,9},{9,8},{10,11... | collective-permute-start | bytes 3145736 | tf_op jit(solution)/shard_map/ppermute | solution.py:575
  60.9 5.7 %collective-permute-start.16 = (bf16[16,4096]{1,0:T(8,128)(2,1)S(1)}, bf16[16,4096]{1,0:T(8,128)(2,1)S(1)}, u32[]{:S(2)}, u32[]{:S(2)}) collective-permute-start(bf16[16,4096]{1,0:T(8,128)(2,1)S(1)} %add_blocks.13.refs_2_), channel_id=1, source_target_pairs={{0,4},{1,5},{4,8},{5,9},{8,12},{9,13},{12,14},{13,15},{14,10},{15,... | collective-permute-start | bytes 393224 | tf_op jit(solution)/shard_map/ppermute | solution.py:489
  63.3 6.4 %collective-permute-start.21 = (bf16[16,4096]{1,0:T(8,128)(2,1)S(1)}, bf16[16,4096]{1,0:T(8,128)(2,1)S(1)}, u32[]{:S(2)}, u32[]{:S(2)}) collective-permute-start(bf16[16,4096]{1,0:T(8,128)(2,1)S(1)} %add_blocks.16.refs_3_), channel_id=1, source_target_pairs={{0,2},{1,3},{4,0},{5,1},{8,4},{9,5},{12,8},{13,9},{14,12},{15,13},... | collective-permute-start | bytes 393224 | tf_op jit(solution)/shard_map/ppermute | solution.py:489
  64.3 6.4 %collective-permute-start.20 = (bf16[16,4096]{1,0:T(8,128)(2,1)S(1)}, bf16[16,4096]{1,0:T(8,128)(2,1)S(1)}, u32[]{:S(2)}, u32[]{:S(2)}) collective-permute-start(bf16[16,4096]{1,0:T(8,128)(2,1)S(1)} %add_blocks.15.refs_2_), channel_id=1, source_target_pairs={{0,4},{1,5},{4,8},{5,9},{8,12},{9,13},{12,14},{13,15},{14,10},{15,... | collective-permute-start | bytes 393224 | tf_op jit(solution)/shard_map/ppermute | solution.py:489
  65.4 7.0 %collective-permute-start.19 = (bf16[16,4096]{1,0:T(8,128)(2,1)S(1)}, bf16[16,4096]{1,0:T(8,128)(2,1)S(1)}, u32[]{:S(2)}, u32[]{:S(2)}) collective-permute-start(bf16[16,4096]{1,0:T(8,128)(2,1)S(1)} %add_blocks.14.refs_2_), channel_id=1, source_target_pairs={{0,2},{1,3},{4,0},{5,1},{8,4},{9,5},{12,8},{13,9},{14,12},{15,13},... | collective-permute-start | bytes 393224 | tf_op jit(solution)/shard_map/ppermute | solution.py:489
  66.6 6.9 %collective-permute-start.18 = (bf16[16,4096]{1,0:T(8,128)(2,1)S(1)}, bf16[16,4096]{1,0:T(8,128)(2,1)S(1)}, u32[]{:S(2)}, u32[]{:S(2)}) collective-permute-start(bf16[16,4096]{1,0:T(8,128)(2,1)S(1)} %add_blocks.17.refs_3_), channel_id=1, source_target_pairs={{0,4},{1,5},{4,8},{5,9},{8,12},{9,13},{12,14},{13,15},{14,10},{15,... | collective-permute-start | bytes 393224 | tf_op jit(solution)/shard_map/ppermute | solution.py:489
  69.7 5.6 %collective-permute-start.23 = (bf16[16,4096]{1,0:T(8,128)(2,1)S(1)}, bf16[16,4096]{1,0:T(8,128)(2,1)S(1)}, u32[]{:S(2)}, u32[]{:S(2)}) collective-permute-start(bf16[16,4096]{1,0:T(8,128)(2,1)S(1)} %add_blocks.18.refs_3_), channel_id=1, source_target_pairs={{0,2},{1,3},{4,0},{5,1},{8,4},{9,5},{12,8},{13,9},{14,12},{15,13},... | collective-permute-start | bytes 393224 | tf_op jit(solution)/shard_map/ppermute | solution.py:489
  70.8 6.6 %collective-permute-start.26 = (bf16[16,4096]{1,0:T(8,128)(2,1)S(1)}, bf16[16,4096]{1,0:T(8,128)(2,1)S(1)}, u32[]{:S(2)}, u32[]{:S(2)}) collective-permute-start(bf16[16,4096]{1,0:T(8,128)(2,1)S(1)} %add_blocks.19.refs_3_), channel_id=1, source_target_pairs={{0,4},{1,5},{4,8},{5,9},{8,12},{9,13},{12,14},{13,15},{14,10},{15,... | collective-permute-start | bytes 393224 | tf_op jit(solution)/shard_map/ppermute | solution.py:489
  72.4 6.5 %collective-permute-start.25 = (bf16[16,4096]{1,0:T(8,128)(2,1)S(1)}, bf16[16,4096]{1,0:T(8,128)(2,1)S(1)}, u32[]{:S(2)}, u32[]{:S(2)}) collective-permute-start(bf16[16,4096]{1,0:T(8,128)(2,1)S(1)} %add_blocks.20.refs_3_), channel_id=1, source_target_pairs={{0,2},{1,3},{4,0},{5,1},{8,4},{9,5},{12,8},{13,9},{14,12},{15,13},... | collective-permute-start | bytes 393224 | tf_op jit(solution)/shard_map/ppermute | solution.py:489
  75.4 8.6 %copy-start.7 = (bf16[8192]{0:T(1024)(128)(2,1)S(1)}, bf16[8192]{0:T(1024)(128)(2,1)}, u32[]{:S(2)}) copy-start(bf16[8192]{0:T(1024)(128)(2,1)} %param.15) | copy-start | bytes 49156
  75.4 6.4 %collective-permute-start.24 = (bf16[16,4096]{1,0:T(8,128)(2,1)S(1)}, bf16[16,4096]{1,0:T(8,128)(2,1)S(1)}, u32[]{:S(2)}, u32[]{:S(2)}) collective-permute-start(bf16[16,4096]{1,0:T(8,128)(2,1)S(1)} %add_blocks.22.refs_3_), channel_id=1, source_target_pairs={{0,2},{1,3},{4,0},{5,1},{8,4},{9,5},{12,8},{13,9},{14,12},{15,13},... | collective-permute-start | bytes 393224 | tf_op jit(solution)/shard_map/ppermute | solution.py:489
  76.4 5.3 %collective-permute-start.22 = (bf16[16,4096]{1,0:T(8,128)(2,1)S(1)}, bf16[16,4096]{1,0:T(8,128)(2,1)S(1)}, u32[]{:S(2)}, u32[]{:S(2)}) collective-permute-start(bf16[16,4096]{1,0:T(8,128)(2,1)S(1)} %add_blocks.21.refs_3_), channel_id=1, source_target_pairs={{0,4},{1,5},{4,8},{5,9},{8,12},{9,13},{12,14},{13,15},{14,10},{15,... | collective-permute-start | bytes 393224 | tf_op jit(solution)/shard_map/ppermute | solution.py:489
  77.5 7.9 %collective-permute-start.29 = (bf16[16,4096]{1,0:T(8,128)(2,1)S(1)}, bf16[16,4096]{1,0:T(8,128)(2,1)S(1)}, u32[]{:S(2)}, u32[]{:S(2)}) collective-permute-start(bf16[16,4096]{1,0:T(8,128)(2,1)S(1)} %add_blocks.23.refs_3_), channel_id=1, source_target_pairs={{0,4},{1,5},{4,8},{5,9},{8,12},{9,13},{12,14},{13,15},{14,10},{15,... | collective-permute-start | bytes 393224 | tf_op jit(solution)/shard_map/ppermute | solution.py:489
  79.0 6.4 %collective-permute-start.28 = (bf16[16,4096]{1,0:T(8,128)(2,1)S(1)}, bf16[16,4096]{1,0:T(8,128)(2,1)S(1)}, u32[]{:S(2)}, u32[]{:S(2)}) collective-permute-start(bf16[16,4096]{1,0:T(8,128)(2,1)S(1)} %add_blocks.24.refs_6_), channel_id=1, source_target_pairs={{0,2},{1,3},{4,0},{5,1},{8,4},{9,5},{12,8},{13,9},{14,12},{15,13},... | collective-permute-start | bytes 393224 | tf_op jit(solution)/shard_map/ppermute | solution.py:489
  81.9 5.0 %collective-permute-start.27 = (bf16[16,4096]{1,0:T(8,128)(2,1)S(1)}, bf16[16,4096]{1,0:T(8,128)(2,1)S(1)}, u32[]{:S(2)}, u32[]{:S(2)}) collective-permute-start(bf16[16,4096]{1,0:T(8,128)(2,1)S(1)} %get-tuple-element.18), channel_id=1, source_target_pairs={{0,4},{1,5},{4,8},{5,9},{8,12},{9,13},{12,14},{13,15},{14,10},{15,... | collective-permute-start | bytes 393224 | tf_op jit(solution)/shard_map/ppermute | solution.py:489
  83.0 5.0 %collective-permute-start.30 = (bf16[16,4096]{1,0:T(8,128)(2,1)S(1)}, bf16[16,4096]{1,0:T(8,128)(2,1)S(1)}, u32[]{:S(2)}, u32[]{:S(2)}) collective-permute-start(bf16[16,4096]{1,0:T(8,128)(2,1)S(1)} %get-tuple-element.19), channel_id=1, source_target_pairs={{0,2},{1,3},{4,0},{5,1},{8,4},{9,5},{12,8},{13,9},{14,12},{15,13},... | collective-permute-start | bytes 393224 | tf_op jit(solution)/shard_map/ppermute | solution.py:489

commit v12 on v11

--- a/solution.py
+++ b/solution.py
@@ -197,7 +197,7 @@
     model_width = factor.shape[1]
     slots = factor.shape[0] // rank_limit
     batch_rows = to_place.shape[0]
-    width = model_width // 4
+    width = model_width // 2
 
     def kernel(*refs):
         factor_ref, scale_ref, place_ref, rows_out, coeff_out, total = refs[len(parts) :]
@@ -473,9 +473,11 @@
     ordered = []
     for turn in range(last):
         chains = [(right, 1, 0), (left, -1, 1), (right, 1, 1), (left, -1, 0)]
-        if turn == 0:
-            chains = [chains[0], chains[3], chains[2], chains[1]]
-        groups = [[chain] for chain in chains] if turn < last - 1 else [chains[:2]]
+        groups = [[chain] for chain in chains]
+        if turn < 2:
+            groups = [[chains[0], chains[3]], [chains[1]], [chains[2]]]
+        if turn == last - 1:
+            groups = [chains[:2]]
         for group in groups:
             sides = []
             for chain, by, h in group:

time: 89.1 us -> 90 us (1.010)
  waiting for transfers between devices: 27.5 us -> 28.8 us
    ppermute x14, waiting for transfers between devices: 10.3 us -> 12.4 us  [scatter_rows(): chain[h] = lax.ppermute(value, AXIS, ring(size, by))]
    pallas_call x28 -> x26, Pallas kernels: 12 us -> 11.7 us  [call(): pl.pallas_call(run, out_shape=out_shape, in_specs=[whole(pltpu.SMEM if op...]
  transfers between devices with their start and end apart: 31 -> 31, of which waited for: 19 -> 20; matrix products, arithmetic and copies ran while one was open for 3% -> 3% of each run, Pallas kernels for 24% -> 24%
where the time goes in v12:
time: 90 us; the launch traced here: 89.8 us
  starting transfers between devices  29.4 us (33%)
  waiting for transfers between devices  28.8 us (32%)
  Pallas kernels  25.6 us (28%)
  matrix products  4.84 us (5%)
  between operations  1.03 us (1%)
    ppermute x14, starting transfers between devices, scatter_rows(): chain[h] = lax.ppermute(value, AXIS, ring(size, by))  14.9 us
    ppermute x14, waiting for transfers between devices, scatter_rows(): chain[h] = lax.ppermute(value, AXIS, ring(size, by))  12.4 us
    pallas_call x26, Pallas kernels, call(): pl.pallas_call(run, out_shape=out_shape, in_specs=[whole(pltpu.SMEM if op...  11.7 us
    pallas_call x2, Pallas kernels, load_rows(): pl.pallas_call(kernel, out_shape=[jax.ShapeDtypeStruct(shape, weights[0]....  9.2 us
    ppermute x3, waiting for transfers between devices, gather_rows(): right = lax.ppermute(right, AXIS, ring(size, 1))  6.55 us
    ppermute x3, starting transfers between devices, gather_rows(): right = lax.ppermute(right, AXIS, ring(size, 1))  6.45 us
    dot_general x2, matrix products, body(): jnp.dot(hidden, down_weight[:, h * width:(h + 1) * width], preferred_elem...  4.84 us
    pallas_call x1, Pallas kernels, stream_rows(): pl.pallas_call(kernel, out_shape=jax.ShapeDtypeStruct((batch_rows, width)...  4.65 us
  transfers between devices with their start and end apart: 31, of which 20 were waited for; matrix products, arithmetic and copies ran while one was open for 3% of the time, Pallas kernels for 24%

profile of v12, /device:TPU:0, one launch (start us, length us, event | category | flops | bytes accessed | tf_op | source)
XLA Modules:
  0.0 89.8 jit_solution(1739412315781632393)
XLA Ops:
  0.6 3.1 %collective-permute-start = (bf16[16,8192]{1,0:T(8,128)(2,1)}, bf16[16,8192]{1,0:T(8,128)(2,1)S(1)}, u32[]{:S(2)}, u32[]{:S(2)}) collective-permute-start(bf16[16,8192]{1,0:T(8,128)(2,1)} %refs_8_.1), channel_id=1, source_target_pairs={{0,4},{1,5},{4,8},{5,9},{8,12},{9,13},{12,14},{13,15},{14,10},{15,... | collective-permute-start | bytes 786440 | tf_op jit(solution)/shard_map/ppermute | solution.py:138
  3.7 4.6 %load_rows.2.refs_1_ = bf16[3328,1792]{1,0:T(8,128)(2,1)S(1)} custom-call(bf16[8192,896]{1,0:T(8,128)(2,1)} %refs_0_.7, bf16[8192,896]{1,0:T(8,128)(2,1)} %refs_1_.5), custom_call_target="tpu_custom_call" | custom-call | bytes 23855104 | tf_op jit(solution)/shard_map/load_rows/pallas_call | solution.py:292
  8.3 1.8 %collective-permute-done.refs_0_ = bf16[16,8192]{1,0:T(8,128)(2,1)S(1)} collective-permute-done((bf16[16,8192]{1,0:T(8,128)(2,1)}, bf16[16,8192]{1,0:T(8,128)(2,1)S(1)}, u32[]{:S(2)}, u32[]{:S(2)}) %collective-permute-start) | collective-permute-done | bytes 262176 | tf_op jit(solution)/shard_map/ppermute | solution.py:138
  10.2 1.8 %collective-permute-start.2 = (bf16[16,8192]{1,0:T(8,128)(2,1)S(1)}, bf16[16,8192]{1,0:T(8,128)(2,1)S(1)}, u32[]{:S(2)}, u32[]{:S(2)}) collective-permute-start(bf16[16,8192]{1,0:T(8,128)(2,1)S(1)} %pass_on.2.refs_2_), channel_id=1, source_target_pairs={{0,4},{1,5},{4,8},{5,9},{8,12},{9,13},{12,14},{13,15},{14,10},{15,... | collective-permute-start | bytes 786440 | tf_op jit(solution)/shard_map/ppermute | solution.py:138
  12.3 4.6 %load_rows.3.refs_1_ = bf16[3328,1792]{1,0:T(8,128)(2,1)S(1)} custom-call(bf16[8192,896]{1,0:T(8,128)(2,1)} %refs_0_.7, bf16[8192,896]{1,0:T(8,128)(2,1)} %refs_1_.5, bf16[16,8192]{1,0:T(8,128)(2,1)S(1)} %pass_on.2.refs_2_), custom_call_target="tpu_custom_call" | custom-call | bytes 23855104 | tf_op jit(solution)/shard_map/load_rows/pallas_call | solution.py:292
  17.0 0.8 collective-permute-done.2.refs_0_.refs_2_
  17.8 1.5 %collective-permute-start.4 = (bf16[16,8192]{1,0:T(8,128)(2,1)S(1)}, bf16[16,8192]{1,0:T(8,128)(2,1)S(1)}, u32[]{:S(2)}, u32[]{:S(2)}) collective-permute-start(bf16[16,8192]{1,0:T(8,128)(2,1)S(1)} %pass_on.3), channel_id=1, source_target_pairs={{0,4},{1,5},{4,8},{5,9},{8,12},{9,13},{12,14},{13,15},{14,10},{15,... | collective-permute-start | bytes 786440 | tf_op jit(solution)/shard_map/ppermute | solution.py:138
  19.9 0.6 row_masks.1
  20.4 3.9 %collective-permute-done.4.refs_4_.refs_0_ = bf16[16,8192]{1,0:T(8,128)(2,1)S(1)} collective-permute-done((bf16[16,8192]{1,0:T(8,128)(2,1)S(1)}, bf16[16,8192]{1,0:T(8,128)(2,1)S(1)}, u32[]{:S(2)}, u32[]{:S(2)}) %collective-permute-start.4) | collective-permute-done | bytes 262176 | tf_op jit(solution)/shard_map/ppermute | solution.py:138
  24.4 1.3 %collective-permute-done.5.refs_5_.refs_0_ = bf16[16,8192]{1,0:T(8,128)(2,1)S(1)} collective-permute-done((bf16[16,8192]{1,0:T(8,128)(2,1)S(1)}, bf16[16,8192]{1,0:T(8,128)(2,1)S(1)}, u32[]{:S(2)}, u32[]{:S(2)}) %collective-permute-start.5) | collective-permute-done | bytes 262176 | tf_op jit(solution)/shard_map/ppermute | solution.py:139
  25.9 1.6 %collective-permute-start.6 = (bf16[16,4096]{1,0:T(8,128)(2,1)S(1)}, bf16[16,4096]{1,0:T(8,128)(2,1)S(1)}, u32[]{:S(2)}, u32[]{:S(2)}) collective-permute-start(bf16[16,4096]{1,0:T(8,128)(2,1)S(1)} %column_half.2), channel_id=1, source_target_pairs={{0,4},{1,5},{4,8},{5,9},{8,12},{9,13},{12,14},{13,15},{14,10},{15,... | collective-permute-start | bytes 393224 | tf_op jit(solution)/shard_map/ppermute | solution.py:151
  28.0 3.8 %collective-permute-done.6.refs_0_ = bf16[16,4096]{1,0:T(8,128)(2,1)S(1)} collective-permute-done((bf16[16,4096]{1,0:T(8,128)(2,1)S(1)}, bf16[16,4096]{1,0:T(8,128)(2,1)S(1)}, u32[]{:S(2)}, u32[]{:S(2)}) %collective-permute-start.6) | collective-permute-done | bytes 131104 | tf_op jit(solution)/shard_map/ppermute | solution.py:151
  31.8 1.4 %collective-permute-done.7.refs_1_ = bf16[16,4096]{1,0:T(8,128)(2,1)S(1)} collective-permute-done((bf16[16,4096]{1,0:T(8,128)(2,1)S(1)}, bf16[16,4096]{1,0:T(8,128)(2,1)S(1)}, u32[]{:S(2)}, u32[]{:S(2)}) %collective-permute-start.7) | collective-permute-done | bytes 131104 | tf_op jit(solution)/shard_map/ppermute | solution.py:152
  33.3 1.5 %collective-permute-done.10.refs_5_ = bf16[16,8192]{1,0:T(8,128)(2,1)S(1)} collective-permute-done((bf16[16,8192]{1,0:T(8,128)(2,1)S(1)}, bf16[16,8192]{1,0:T(8,128)(2,1)S(1)}, u32[]{:S(2)}, u32[]{:S(2)}) %collective-permute-start.10) | collective-permute-done | bytes 262176 | tf_op jit(solution)/shard_map/ppermute | solution.py:157
  34.8 1.8 %shrink_rows.1 = (bf16[256,8192]{1,0:T(8,128)(2,1)S(1)}, bf16[256,64]{1,0:T(8,128)(2,1)S(1)}) custom-call(bf16[16,8192]{1,0:T(8,128)(2,1)S(1)} %copy-done.1, bf16[96,8192]{1,0:T(8,128)(2,1)S(1)} %join_pieces.2.refs_1_, bf16[16,8192]{1,0:T(8,128)(2,1)S(1)} %join_pieces.3.refs_2_, bf16[16,8192]{1,0:T(8,128)(2,1)S(1)} %collective-permute-done.8.refs_3_, ...), custom_call_target="tpu_custom_call" | custom-call | flops 268435456 | bytes 8388608 | tf_op jit(solution)/shard_map/shrink_rows/pallas_call | solution.py:78
  36.8 1.1 %collective-permute-done.11.refs_1_ = bf16[256,64]{1,0:T(8,128)(2,1)S(1)} collective-permute-done((bf16[256,64]{1,0:T(8,128)(2,1)S(1)}, bf16[256,64]{1,0:T(8,128)(2,1)S(1)}, u32[]{:S(2)}, u32[]{:S(2)}) %collective-permute-start.11) | collective-permute-done | bytes 32800 | tf_op jit(solution)/shard_map/ppermute | solution.py:554
  38.4 3.2 %mixed_rows.2.refs_2_ = f32[256,1792]{1,0:T(8,128)S(1)} custom-call(bf16[256,8192]{1,0:T(8,128)(2,1)S(1)} %get-tuple-element.19.refs_0_.rows_ref, bf16[3328,1792]{1,0:T(8,128)(2,1)S(1)} %load_rows.2.refs_1_, bf16[256,64]{1,0:T(8,128)(2,1)S(1)} %add_coefficients.3.refs_2_.refs_0_), custom_call_target="tpu_custom_call" | custom-call | flops 3053453312 | bytes 11927552 | tf_op jit(solution)/shard_map/mixed_rows/pallas_call | solution.py:78
  41.7 0.6 collective-permute-done.12.refs_1_
  42.3 1.6 %collective-permute-start.13 = (bf16[256,64]{1,0:T(8,128)(2,1)S(1)}, bf16[256,64]{1,0:T(8,128)(2,1)S(1)}, u32[]{:S(2)}, u32[]{:S(2)}) collective-permute-start(bf16[256,64]{1,0:T(8,128)(2,1)S(1)} %add_coefficients.4.refs_3_.refs_0_), channel_id=1, source_target_pairs={{0,4},{1,5},{2,6},{3,7},{4,0},{5,1},{6,2},{7,3},{8,12},{9,13},{10,... | collective-permute-start | bytes 98312 | tf_op jit(solution)/shard_map/ppermute | solution.py:554
  43.9 3.2 %mixed_rows.3.refs_2_ = f32[256,1792]{1,0:T(8,128)S(1)} custom-call(bf16[256,8192]{1,0:T(8,128)(2,1)S(1)} %get-tuple-element.19.refs_0_.rows_ref, bf16[3328,1792]{1,0:T(8,128)(2,1)S(1)} %load_rows.3.refs_1_, f32[256,1792]{1,0:T(8,128)S(1)} %mixed_rows.2.refs_2_, bf16[256,64]{1,0:T(8,128)(2,1)S(1)} %add_coefficients.4.refs_3_.refs_0_), custom_call_target="tpu_custom_call" | custom-call | flops 3053453312 | bytes 11927552 | tf_op jit(solution)/shard_map/mixed_rows/pallas_call | solution.py:78
  47.2 2.0 %collective-permute-start.14 = (bf16[256,64]{1,0:T(8,128)(2,1)S(1)}, bf16[256,64]{1,0:T(8,128)(2,1)S(1)}, u32[]{:S(2)}, u32[]{:S(2)}) collective-permute-start(bf16[256,64]{1,0:T(8,128)(2,1)S(1)} %add_coefficients.5.refs_3_.refs_0_), channel_id=1, source_target_pairs={{0,8},{1,9},{2,10},{3,11},{4,12},{5,13},{6,14},{7,15},{8,0},{9,1},... | collective-permute-start | bytes 98312 | tf_op jit(solution)/shard_map/ppermute | solution.py:554
  49.3 4.6 %stream_rows.1.refs_5_ = f32[256,1792]{1,0:T(8,128)S(1)} custom-call(bf16[256,8192]{1,0:T(8,128)(2,1)S(1)} %get-tuple-element.19.refs_0_.rows_ref, bf16[8192,896]{1,0:T(8,128)(2,1)} %refs_0_.7, bf16[8192,896]{1,0:T(8,128)(2,1)} %refs_1_.5, f32[256,1792]{1,0:T(8,128)S(1)} %mixed_rows.3.refs_2_, bf16[256,64]{1,0:T(8,128)(2,1)S(1)} %add_coefficients.5.refs_3_.refs_0_), custom_call_target="tpu_custom_call" | custom-call | flops 1409286144 | bytes 11010048 | tf_op jit(solution)/shard_map/stream_rows/pallas_call | solution.py:395
  53.9 1.0 %hidden_rows.1 = bf16[256,896]{1,0:T(8,128)(2,1)S(1)} custom-call(bf16[256,64]{1,0:T(8,128)(2,1)S(1)} %add_coefficients.5.refs_3_.refs_0_, bf16[256,64]{1,0:T(8,128)(2,1)S(1)} %collective-permute-done.14.refs_1_, bf16[256,256]{1,0:T(8,128)(2,1)S(1)} %get-tuple-element.20.refs_2_, bf16[256,1024]{1,0:T(8,128)(2,1)S(1)} %get-tuple-element.21.refs_3_, ...), custom_call_target="tpu_custom_call" | custom-call | flops 469762048 | bytes 1835008 | tf_op jit(solution)/shard_map/hidden_rows/pallas_call | solution.py:78
  55.0 2.4 %fusion.4.refs_0_.refs_2_.refs_3_ = bf16[256,4096]{1,0:T(8,128)(2,1)S(1)} fusion(bf16[256,896]{1,0:T(8,128)(2,1)S(1)} %hidden_rows.1, bf16[896,8192]{1,0:T(8,128)(2,1)S(1)} %bitcast.17), kind=kOutput, calls=%fused_computation.4 | convolution fusion | flops 1880096768 | bytes 9895936 | tf_op jit(solution)/shard_map/dot_general | solution.py:571
  57.6 2.4 %fusion.7.refs_0_.refs_3_.refs_4_ = bf16[256,4096]{1,0:T(8,128)(2,1)S(1)} fusion(bf16[256,896]{1,0:T(8,128)(2,1)S(1)} %hidden_rows.1, bf16[896,8192]{1,0:T(8,128)(2,1)S(1)} %bitcast.17), kind=kOutput, calls=%fused_computation.5 | convolution fusion | flops 1880096768 | bytes 9895936 | tf_op jit(solution)/shard_map/dot_general | solution.py:571
  60.7 1.1 %collective-permute-start.16 = (bf16[16,4096]{1,0:T(8,128)(2,1)S(1)}, bf16[16,4096]{1,0:T(8,128)(2,1)S(1)}, u32[]{:S(2)}, u32[]{:S(2)}) collective-permute-start(bf16[16,4096]{1,0:T(8,128)(2,1)S(1)} %get-tuple-element.22.refs_2_), channel_id=1, source_target_pairs={{0,4},{1,5},{4,8},{5,9},{8,12},{9,13},{12,14},{13,15},{14,10},{15,... | collective-permute-start | bytes 393224 | tf_op jit(solution)/shard_map/ppermute | solution.py:491
  61.8 1.0 %collective-permute-start.17 = (bf16[16,4096]{1,0:T(8,128)(2,1)S(1)}, bf16[16,4096]{1,0:T(8,128)(2,1)S(1)}, u32[]{:S(2)}, u32[]{:S(2)}) collective-permute-start(bf16[16,4096]{1,0:T(8,128)(2,1)S(1)} %get-tuple-element.23), channel_id=1, source_target_pairs={{0,2},{1,3},{4,0},{5,1},{8,4},{9,5},{12,8},{13,9},{14,12},{15,13},... | collective-permute-start | bytes 393224 | tf_op jit(solution)/shard_map/ppermute | solution.py:491
  63.0 1.1 %collective-permute-start.21 = (bf16[16,4096]{1,0:T(8,128)(2,1)S(1)}, bf16[16,4096]{1,0:T(8,128)(2,1)S(1)}, u32[]{:S(2)}, u32[]{:S(2)}) collective-permute-start(bf16[16,4096]{1,0:T(8,128)(2,1)S(1)} %add_blocks.12.refs_2_), channel_id=1, source_target_pairs={{0,2},{1,3},{4,0},{5,1},{8,4},{9,5},{12,8},{13,9},{14,12},{15,13},... | collective-permute-start | bytes 393224 | tf_op jit(solution)/shard_map/ppermute | solution.py:491
  64.1 1.1 %collective-permute-start.20 = (bf16[16,4096]{1,0:T(8,128)(2,1)S(1)}, bf16[16,4096]{1,0:T(8,128)(2,1)S(1)}, u32[]{:S(2)}, u32[]{:S(2)}) collective-permute-start(bf16[16,4096]{1,0:T(8,128)(2,1)S(1)} %add_blocks.13.refs_6_), channel_id=1, source_target_pairs={{0,4},{1,5},{4,8},{5,9},{8,12},{9,13},{12,14},{13,15},{14,10},{15,... | collective-permute-start | bytes 393224 | tf_op jit(solution)/shard_map/ppermute | solution.py:491
  65.2 1.0 %collective-permute-done.16.refs_2_ = bf16[16,4096]{1,0:T(8,128)(2,1)S(1)} collective-permute-done((bf16[16,4096]{1,0:T(8,128)(2,1)S(1)}, bf16[16,4096]{1,0:T(8,128)(2,1)S(1)}, u32[]{:S(2)}, u32[]{:S(2)}) %collective-permute-start.16) | collective-permute-done | bytes 131104 | tf_op jit(solution)/shard_map/ppermute | solution.py:491
  66.2 1.8 %collective-permute-done.17.refs_5_ = bf16[16,4096]{1,0:T(8,128)(2,1)S(1)} collective-permute-done((bf16[16,4096]{1,0:T(8,128)(2,1)S(1)}, bf16[16,4096]{1,0:T(8,128)(2,1)S(1)}, u32[]{:S(2)}, u32[]{:S(2)}) %collective-permute-start.17) | collective-permute-done | bytes 131104 | tf_op jit(solution)/shard_map/ppermute | solution.py:491
  68.1 1.2 %collective-permute-start.19 = (bf16[16,4096]{1,0:T(8,128)(2,1)S(1)}, bf16[16,4096]{1,0:T(8,128)(2,1)S(1)}, u32[]{:S(2)}, u32[]{:S(2)}) collective-permute-start(bf16[16,4096]{1,0:T(8,128)(2,1)S(1)} %get-tuple-element.24.refs_3_), channel_id=1, source_target_pairs={{0,4},{1,5},{4,8},{5,9},{8,12},{9,13},{12,14},{13,15},{14,10},{15,... | collective-permute-start | bytes 393224 | tf_op jit(solution)/shard_map/ppermute | solution.py:491
  69.8 1.0 %collective-permute-start.23 = (bf16[16,4096]{1,0:T(8,128)(2,1)S(1)}, bf16[16,4096]{1,0:T(8,128)(2,1)S(1)}, u32[]{:S(2)}, u32[]{:S(2)}) collective-permute-start(bf16[16,4096]{1,0:T(8,128)(2,1)S(1)} %add_blocks.15.refs_3_), channel_id=1, source_target_pairs={{0,2},{1,3},{4,0},{5,1},{8,4},{9,5},{12,8},{13,9},{14,12},{15,13},... | collective-permute-start | bytes 393224 | tf_op jit(solution)/shard_map/ppermute | solution.py:491
  70.9 1.1 %collective-permute-start.26 = (bf16[16,4096]{1,0:T(8,128)(2,1)S(1)}, bf16[16,4096]{1,0:T(8,128)(2,1)S(1)}, u32[]{:S(2)}, u32[]{:S(2)}) collective-permute-start(bf16[16,4096]{1,0:T(8,128)(2,1)S(1)} %add_blocks.16.refs_3_), channel_id=1, source_target_pairs={{0,4},{1,5},{4,8},{5,9},{8,12},{9,13},{12,14},{13,15},{14,10},{15,... | collective-permute-start | bytes 393224 | tf_op jit(solution)/shard_map/ppermute | solution.py:491
  72.0 1.0 %collective-permute-start.25 = (bf16[16,4096]{1,0:T(8,128)(2,1)S(1)}, bf16[16,4096]{1,0:T(8,128)(2,1)S(1)}, u32[]{:S(2)}, u32[]{:S(2)}) collective-permute-start(bf16[16,4096]{1,0:T(8,128)(2,1)S(1)} %get-tuple-element.25), channel_id=1, source_target_pairs={{0,2},{1,3},{4,0},{5,1},{8,4},{9,5},{12,8},{13,9},{14,12},{15,13},... | collective-permute-start | bytes 393224 | tf_op jit(solution)/shard_map/ppermute | solution.py:491
  73.0 0.8 collective-permute-done.19.refs_2_
  73.9 2.2 %collective-permute-done.23.refs_2_ = bf16[16,4096]{1,0:T(8,128)(2,1)S(1)} collective-permute-done((bf16[16,4096]{1,0:T(8,128)(2,1)S(1)}, bf16[16,4096]{1,0:T(8,128)(2,1)S(1)}, u32[]{:S(2)}, u32[]{:S(2)}) %collective-permute-start.23) | collective-permute-done | bytes 131104 | tf_op jit(solution)/shard_map/ppermute | solution.py:491
  76.1 1.1 %collective-permute-start.24 = (bf16[16,4096]{1,0:T(8,128)(2,1)S(1)}, bf16[16,4096]{1,0:T(8,128)(2,1)S(1)}, u32[]{:S(2)}, u32[]{:S(2)}) collective-permute-start(bf16[16,4096]{1,0:T(8,128)(2,1)S(1)} %add_blocks.18.refs_3_), channel_id=1, source_target_pairs={{0,2},{1,3},{4,0},{5,1},{8,4},{9,5},{12,8},{13,9},{14,12},{15,13},... | collective-permute-start | bytes 393224 | tf_op jit(solution)/shard_map/ppermute | solution.py:491
  77.2 1.0 %collective-permute-start.22 = (bf16[16,4096]{1,0:T(8,128)(2,1)S(1)}, bf16[16,4096]{1,0:T(8,128)(2,1)S(1)}, u32[]{:S(2)}, u32[]{:S(2)}) collective-permute-start(bf16[16,4096]{1,0:T(8,128)(2,1)S(1)} %add_blocks.17.refs_3_), channel_id=1, source_target_pairs={{0,4},{1,5},{4,8},{5,9},{8,12},{9,13},{12,14},{13,15},{14,10},{15,... | collective-permute-start | bytes 393224 | tf_op jit(solution)/shard_map/ppermute | solution.py:491
  78.2 1.1 %collective-permute-start.29 = (bf16[16,4096]{1,0:T(8,128)(2,1)S(1)}, bf16[16,4096]{1,0:T(8,128)(2,1)S(1)}, u32[]{:S(2)}, u32[]{:S(2)}) collective-permute-start(bf16[16,4096]{1,0:T(8,128)(2,1)S(1)} %add_blocks.19.refs_3_), channel_id=1, source_target_pairs={{0,4},{1,5},{4,8},{5,9},{8,12},{9,13},{12,14},{13,15},{14,10},{15,... | collective-permute-start | bytes 393224 | tf_op jit(solution)/shard_map/ppermute | solution.py:491
  79.5 1.0 %collective-permute-start.28 = (bf16[16,4096]{1,0:T(8,128)(2,1)S(1)}, bf16[16,4096]{1,0:T(8,128)(2,1)S(1)}, u32[]{:S(2)}, u32[]{:S(2)}) collective-permute-start(bf16[16,4096]{1,0:T(8,128)(2,1)S(1)} %add_blocks.20.refs_6_), channel_id=1, source_target_pairs={{0,2},{1,3},{4,0},{5,1},{8,4},{9,5},{12,8},{13,9},{14,12},{15,13},... | collective-permute-start | bytes 393224 | tf_op jit(solution)/shard_map/ppermute | solution.py:491
  80.4 1.1 %collective-permute-done.24.refs_5_ = bf16[16,4096]{1,0:T(8,128)(2,1)S(1)} collective-permute-done((bf16[16,4096]{1,0:T(8,128)(2,1)S(1)}, bf16[16,4096]{1,0:T(8,128)(2,1)S(1)}, u32[]{:S(2)}, u32[]{:S(2)}) %collective-permute-start.24) | collective-permute-done | bytes 131104 | tf_op jit(solution)/shard_map/ppermute | solution.py:491
  81.6 1.2 %collective-permute-done.22.refs_2_ = bf16[16,4096]{1,0:T(8,128)(2,1)S(1)} collective-permute-done((bf16[16,4096]{1,0:T(8,128)(2,1)S(1)}, bf16[16,4096]{1,0:T(8,128)(2,1)S(1)}, u32[]{:S(2)}, u32[]{:S(2)}) %collective-permute-start.22) | collective-permute-done | bytes 131104 | tf_op jit(solution)/shard_map/ppermute | solution.py:491
  82.9 0.9 %collective-permute-start.27 = (bf16[16,4096]{1,0:T(8,128)(2,1)S(1)}, bf16[16,4096]{1,0:T(8,128)(2,1)S(1)}, u32[]{:S(2)}, u32[]{:S(2)}) collective-permute-start(bf16[16,4096]{1,0:T(8,128)(2,1)S(1)} %get-tuple-element.26), channel_id=1, source_target_pairs={{0,4},{1,5},{4,8},{5,9},{8,12},{9,13},{12,14},{13,15},{14,10},{15,... | collective-permute-start | bytes 393224 | tf_op jit(solution)/shard_map/ppermute | solution.py:491
  83.8 1.1 %collective-permute-start.30 = (bf16[16,4096]{1,0:T(8,128)(2,1)S(1)}, bf16[16,4096]{1,0:T(8,128)(2,1)S(1)}, u32[]{:S(2)}, u32[]{:S(2)}) collective-permute-start(bf16[16,4096]{1,0:T(8,128)(2,1)S(1)} %get-tuple-element.27), channel_id=1, source_target_pairs={{0,2},{1,3},{4,0},{5,1},{8,4},{9,5},{12,8},{13,9},{14,12},{15,13},... | collective-permute-start | bytes 393224 | tf_op jit(solution)/shard_map/ppermute | solution.py:491
  85.2 2.8 %collective-permute-done.27.refs_2_ = bf16[16,4096]{1,0:T(8,128)(2,1)S(1)} collective-permute-done((bf16[16,4096]{1,0:T(8,128)(2,1)S(1)}, bf16[16,4096]{1,0:T(8,128)(2,1)S(1)}, u32[]{:S(2)}, u32[]{:S(2)}) %collective-permute-start.27) | collective-permute-done | bytes 131104 | tf_op jit(solution)/shard_map/ppermute | solution.py:491
  87.9 0.9 collective-permute-done.30.refs_7_
  88.8 1.0 %finish_rows.1 = (bf16[16,8192]{1,0:T(8,128)(2,1)}, bf16[16,8192]{1,0:T(8,128)(2,1)}) custom-call(bf16[256,4096]{1,0:T(8,128)(2,1)S(1)} %fusion.4.refs_0_.refs_2_.refs_3_, bf16[128,4096]{1,0:T(8,128)(2,1)S(1)} %collective-permute-done.15.refs_1_.refs_3_.refs_4_, bf16[16,4096]{1,0:T(8,128)(2,1)S(1)} %collective-permute-done.27.refs_2_, ...), custom_call_target="tpu_custom_call" | custom-call | tf_op jit(solution)/shard_map/finish_rows/pallas_call | solution.py:78
  (73 shorter events, 4.7 us)
Async XLA Ops:
  0.6 9.5 %collective-permute-start = (bf16[16,8192]{1,0:T(8,128)(2,1)}, bf16[16,8192]{1,0:T(8,128)(2,1)S(1)}, u32[]{:S(2)}, u32[]{:S(2)}) collective-permute-start(bf16[16,8192]{1,0:T(8,128)(2,1)} %refs_8_.1), channel_id=1, source_target_pairs={{0,4},{1,5},{4,8},{5,9},{8,12},{9,13},{12,14},{13,15},{14,10},{15,... | collective-permute-start | bytes 786440 | tf_op jit(solution)/shard_map/ppermute | solution.py:138
  3.7 8.3 %collective-permute-start.1 = (bf16[16,8192]{1,0:T(8,128)(2,1)}, bf16[16,8192]{1,0:T(8,128)(2,1)S(1)}, u32[]{:S(2)}, u32[]{:S(2)}) collective-permute-start(bf16[16,8192]{1,0:T(8,128)(2,1)} %refs_8_.1), channel_id=1, source_target_pairs={{0,2},{1,3},{4,0},{5,1},{8,4},{9,5},{12,8},{13,9},{14,12},{15,13},... | collective-permute-start | bytes 786440 | tf_op jit(solution)/shard_map/ppermute | solution.py:139
  10.2 7.5 %collective-permute-start.2 = (bf16[16,8192]{1,0:T(8,128)(2,1)S(1)}, bf16[16,8192]{1,0:T(8,128)(2,1)S(1)}, u32[]{:S(2)}, u32[]{:S(2)}) collective-permute-start(bf16[16,8192]{1,0:T(8,128)(2,1)S(1)} %pass_on.2.refs_2_), channel_id=1, source_target_pairs={{0,4},{1,5},{4,8},{5,9},{8,12},{9,13},{12,14},{13,15},{14,10},{15,... | collective-permute-start | bytes 786440 | tf_op jit(solution)/shard_map/ppermute | solution.py:138
  12.0 7.2 %collective-permute-start.3 = (bf16[16,8192]{1,0:T(8,128)(2,1)S(1)}, bf16[16,8192]{1,0:T(8,128)(2,1)S(1)}, u32[]{:S(2)}, u32[]{:S(2)}) collective-permute-start(bf16[16,8192]{1,0:T(8,128)(2,1)S(1)} %collective-permute-done.1.refs_1_), channel_id=1, source_target_pairs={{0,2},{1,3},{4,0},{5,1},{8,4},{9,5},{12,8},{13,9},{14,12},{15,13},... | collective-permute-start | bytes 786440 | tf_op jit(solution)/shard_map/ppermute | solution.py:139
  16.9 3.0 %copy-start.2 = (bf16[1,8192,64]{1,2,0:T(8,128)(2,1)S(1)}, bf16[1,8192,64]{1,2,0:T(8,128)(2,1)}, u32[]{:S(2)}) copy-start(bf16[1,8192,64]{1,2,0:T(8,128)(2,1)} %param.16) | copy-start | bytes 3145732
  16.9 3.0 %copy-start.3 = (s32[32]{0:T(128)S(1)}, s32[32]{0:T(128)}, u32[]{:S(2)}) copy-start(s32[32]{0:T(128)} %param.20) | copy-start | bytes 388
  16.9 2.9 %copy-start.4 = (s32[32]{0:T(128)S(1)}, s32[32]{0:T(128)}, u32[]{:S(2)}) copy-start(s32[32]{0:T(128)} %param.21) | copy-start | bytes 388
  16.9 2.9 %copy-start.5 = (s32[16]{0:T(128)S(1)}, s32[16]{0:T(128)}, u32[]{:S(2)}) copy-start(s32[16]{0:T(128)} %param.18) | copy-start | bytes 196
  16.9 2.9 %copy-start.6 = (s32[16]{0:T(128)S(1)}, s32[16]{0:T(128)}, u32[]{:S(2)}) copy-start(s32[16]{0:T(128)} %param.19) | copy-start | bytes 196
  16.9 11.1 %copy-start.1 = (bf16[16,8192]{1,0:T(8,128)(2,1)S(1)}, bf16[16,8192]{1,0:T(8,128)(2,1)}, u32[]{:S(2)}) copy-start(bf16[16,8192]{1,0:T(8,128)(2,1)} %refs_8_.1) | copy-start | bytes 786436
  17.8 6.6 %collective-permute-start.4 = (bf16[16,8192]{1,0:T(8,128)(2,1)S(1)}, bf16[16,8192]{1,0:T(8,128)(2,1)S(1)}, u32[]{:S(2)}, u32[]{:S(2)}) collective-permute-start(bf16[16,8192]{1,0:T(8,128)(2,1)S(1)} %pass_on.3), channel_id=1, source_target_pairs={{0,4},{1,5},{4,8},{5,9},{8,12},{9,13},{12,14},{13,15},{14,10},{15,... | collective-permute-start | bytes 786440 | tf_op jit(solution)/shard_map/ppermute | solution.py:138
  19.3 6.4 %collective-permute-start.5 = (bf16[16,8192]{1,0:T(8,128)(2,1)S(1)}, bf16[16,8192]{1,0:T(8,128)(2,1)S(1)}, u32[]{:S(2)}, u32[]{:S(2)}) collective-permute-start(bf16[16,8192]{1,0:T(8,128)(2,1)S(1)} %collective-permute-done.3.refs_3_), channel_id=1, source_target_pairs={{0,2},{1,3},{4,0},{5,1},{8,4},{9,5},{12,8},{13,9},{14,12},{15,13},... | collective-permute-start | bytes 786440 | tf_op jit(solution)/shard_map/ppermute | solution.py:139
  25.8 9.0 %collective-permute-start.9 = (bf16[96,8192]{1,0:T(8,128)(2,1)S(1)}, bf16[96,8192]{1,0:T(8,128)(2,1)S(1)}, u32[]{:S(2)}, u32[]{:S(2)}) collective-permute-start(bf16[96,8192]{1,0:T(8,128)(2,1)S(1)} %join_pieces.2.refs_1_), channel_id=1, source_target_pairs={{0,1},{1,0},{2,3},{3,2},{4,5},{5,4},{6,7},{7,6},{8,9},{9,8},{10,11... | collective-permute-start | bytes 4718600 | tf_op jit(solution)/shard_map/ppermute | solution.py:148
  25.9 5.9 %collective-permute-start.6 = (bf16[16,4096]{1,0:T(8,128)(2,1)S(1)}, bf16[16,4096]{1,0:T(8,128)(2,1)S(1)}, u32[]{:S(2)}, u32[]{:S(2)}) collective-permute-start(bf16[16,4096]{1,0:T(8,128)(2,1)S(1)} %column_half.2), channel_id=1, source_target_pairs={{0,4},{1,5},{4,8},{5,9},{8,12},{9,13},{12,14},{13,15},{14,10},{15,... | collective-permute-start | bytes 393224 | tf_op jit(solution)/shard_map/ppermute | solution.py:151
  27.5 5.7 %collective-permute-start.7 = (bf16[16,4096]{1,0:T(8,128)(2,1)S(1)}, bf16[16,4096]{1,0:T(8,128)(2,1)S(1)}, u32[]{:S(2)}, u32[]{:S(2)}) collective-permute-start(bf16[16,4096]{1,0:T(8,128)(2,1)S(1)} %column_half.3), channel_id=1, source_target_pairs={{0,2},{1,3},{4,0},{5,1},{8,4},{9,5},{12,8},{13,9},{14,12},{15,13},... | collective-permute-start | bytes 393224 | tf_op jit(solution)/shard_map/ppermute | solution.py:152
  28.0 5.3 %collective-permute-start.8 = (bf16[16,8192]{1,0:T(8,128)(2,1)S(1)}, bf16[16,8192]{1,0:T(8,128)(2,1)S(1)}, u32[]{:S(2)}, u32[]{:S(2)}) collective-permute-start(bf16[16,8192]{1,0:T(8,128)(2,1)S(1)} %copy-done.1), channel_id=1, source_target_pairs={{0,1},{1,0},{2,3},{3,2},{4,5},{5,4},{6,7},{7,6},{8,9},{9,8},{10,11... | collective-permute-start | bytes 786440 | tf_op jit(solution)/shard_map/ppermute | solution.py:141
  33.2 1.6 %collective-permute-start.10 = (bf16[16,8192]{1,0:T(8,128)(2,1)S(1)}, bf16[16,8192]{1,0:T(8,128)(2,1)S(1)}, u32[]{:S(2)}, u32[]{:S(2)}) collective-permute-start(bf16[16,8192]{1,0:T(8,128)(2,1)S(1)} %join_pieces.3.refs_2_), channel_id=1, source_target_pairs={{0,1},{1,0},{2,3},{3,2},{4,5},{5,4},{6,7},{7,6},{8,9},{9,8},{10,11... | collective-permute-start | bytes 786440 | tf_op jit(solution)/shard_map/ppermute | solution.py:157
  36.6 1.3 %collective-permute-start.11 = (bf16[256,64]{1,0:T(8,128)(2,1)S(1)}, bf16[256,64]{1,0:T(8,128)(2,1)S(1)}, u32[]{:S(2)}, u32[]{:S(2)}) collective-permute-start(bf16[256,64]{1,0:T(8,128)(2,1)S(1)} %get-tuple-element.18.refs_0_), channel_id=1, source_target_pairs={{0,1},{1,0},{2,3},{3,2},{4,5},{5,4},{6,7},{7,6},{8,9},{9,8},{10,11... | collective-permute-start | bytes 98312 | tf_op jit(solution)/shard_map/ppermute | solution.py:554
  37.9 4.3 %collective-permute-start.12 = (bf16[256,64]{1,0:T(8,128)(2,1)S(1)}, bf16[256,64]{1,0:T(8,128)(2,1)S(1)}, u32[]{:S(2)}, u32[]{:S(2)}) collective-permute-start(bf16[256,64]{1,0:T(8,128)(2,1)S(1)} %add_coefficients.3.refs_2_.refs_0_), channel_id=1, source_target_pairs={{0,2},{1,3},{2,0},{3,1},{4,6},{5,7},{6,4},{7,5},{8,10},{9,11},{10,... | collective-permute-start | bytes 98312 | tf_op jit(solution)/shard_map/ppermute | solution.py:554
  42.3 4.9 %collective-permute-start.13 = (bf16[256,64]{1,0:T(8,128)(2,1)S(1)}, bf16[256,64]{1,0:T(8,128)(2,1)S(1)}, u32[]{:S(2)}, u32[]{:S(2)}) collective-permute-start(bf16[256,64]{1,0:T(8,128)(2,1)S(1)} %add_coefficients.4.refs_3_.refs_0_), channel_id=1, source_target_pairs={{0,4},{1,5},{2,6},{3,7},{4,0},{5,1},{6,2},{7,3},{8,12},{9,13},{10,... | collective-permute-start | bytes 98312 | tf_op jit(solution)/shard_map/ppermute | solution.py:554
  47.2 7.8 %slice-start = ((s8[14680064]{0:T(1024)(128)(4,1)}), s8[4194304]{0:T(1024)(128)(4,1)S(1)}, s32[]{:S(2)}) async-start(s8[14680064]{0:T(1024)(128)(4,1)} %bitcast.16), calls=%async_computation | async-start | bytes 8388608
  47.2 6.7 %copy-start = (bf16[16,64,896]{2,1,0:T(8,128)(2,1)S(1)}, bf16[16,64,896]{2,1,0:T(8,128)(2,1)}, u32[]{:S(2)}) copy-start(bf16[16,64,896]{2,1,0:T(8,128)(2,1)} %param.17) | copy-start | bytes 5505028
  47.2 7.7 %slice-start.1 = ((s8[14680064]{0:T(1024)(128)(4,1)}), s8[4194304]{0:T(1024)(128)(4,1)S(1)}, s32[]{:S(2)}) async-start(s8[14680064]{0:T(1024)(128)(4,1)} %bitcast.16), calls=%async_computation.1 | async-start | bytes 8388608
  47.2 7.7 %slice-start.2 = ((s8[14680064]{0:T(1024)(128)(4,1)}), s8[4194304]{0:T(1024)(128)(4,1)S(1)}, s32[]{:S(2)}) async-start(s8[14680064]{0:T(1024)(128)(4,1)} %bitcast.16), calls=%async_computation.2 | async-start | bytes 8388608
  47.2 7.7 %slice-start.3 = ((s8[14680064]{0:T(1024)(128)(4,1)}), s8[2097152]{0:T(1024)(128)(4,1)S(1)}, s32[]{:S(2)}) async-start(s8[14680064]{0:T(1024)(128)(4,1)} %bitcast.16), calls=%async_computation.3 | async-start | bytes 4194304
  47.2 6.7 %collective-permute-start.14 = (bf16[256,64]{1,0:T(8,128)(2,1)S(1)}, bf16[256,64]{1,0:T(8,128)(2,1)S(1)}, u32[]{:S(2)}, u32[]{:S(2)}) collective-permute-start(bf16[256,64]{1,0:T(8,128)(2,1)S(1)} %add_coefficients.5.refs_3_.refs_0_), channel_id=1, source_target_pairs={{0,8},{1,9},{2,10},{3,11},{4,12},{5,13},{6,14},{7,15},{8,0},{9,1},... | collective-permute-start | bytes 98312 | tf_op jit(solution)/shard_map/ppermute | solution.py:554
  57.5 3.2 %collective-permute-start.15 = (bf16[128,4096]{1,0:T(8,128)(2,1)S(1)}, bf16[128,4096]{1,0:T(8,128)(2,1)S(1)}, u32[]{:S(2)}, u32[]{:S(2)}) collective-permute-start(bf16[128,4096]{1,0:T(8,128)(2,1)S(1)} %slice.16), channel_id=1, source_target_pairs={{0,1},{1,0},{2,3},{3,2},{4,5},{5,4},{6,7},{7,6},{8,9},{9,8},{10,11... | collective-permute-start | bytes 3145736 | tf_op jit(solution)/shard_map/ppermute | solution.py:577
  60.1 2.8 %collective-permute-start.18 = (bf16[128,4096]{1,0:T(8,128)(2,1)S(1)}, bf16[128,4096]{1,0:T(8,128)(2,1)S(1)}, u32[]{:S(2)}, u32[]{:S(2)}) collective-permute-start(bf16[128,4096]{1,0:T(8,128)(2,1)S(1)} %slice.17), channel_id=1, source_target_pairs={{0,1},{1,0},{2,3},{3,2},{4,5},{5,4},{6,7},{7,6},{8,9},{9,8},{10,11... | collective-permute-start | bytes 3145736 | tf_op jit(solution)/shard_map/ppermute | solution.py:577
  60.7 5.5 %collective-permute-start.16 = (bf16[16,4096]{1,0:T(8,128)(2,1)S(1)}, bf16[16,4096]{1,0:T(8,128)(2,1)S(1)}, u32[]{:S(2)}, u32[]{:S(2)}) collective-permute-start(bf16[16,4096]{1,0:T(8,128)(2,1)S(1)} %get-tuple-element.22.refs_2_), channel_id=1, source_target_pairs={{0,4},{1,5},{4,8},{5,9},{8,12},{9,13},{12,14},{13,15},{14,10},{15,... | collective-permute-start | bytes 393224 | tf_op jit(solution)/shard_map/ppermute | solution.py:491
  61.8 6.2 %collective-permute-start.17 = (bf16[16,4096]{1,0:T(8,128)(2,1)S(1)}, bf16[16,4096]{1,0:T(8,128)(2,1)S(1)}, u32[]{:S(2)}, u32[]{:S(2)}) collective-permute-start(bf16[16,4096]{1,0:T(8,128)(2,1)S(1)} %get-tuple-element.23), channel_id=1, source_target_pairs={{0,2},{1,3},{4,0},{5,1},{8,4},{9,5},{12,8},{13,9},{14,12},{15,13},... | collective-permute-start | bytes 393224 | tf_op jit(solution)/shard_map/ppermute | solution.py:491
  63.0 6.8 %collective-permute-start.21 = (bf16[16,4096]{1,0:T(8,128)(2,1)S(1)}, bf16[16,4096]{1,0:T(8,128)(2,1)S(1)}, u32[]{:S(2)}, u32[]{:S(2)}) collective-permute-start(bf16[16,4096]{1,0:T(8,128)(2,1)S(1)} %add_blocks.12.refs_2_), channel_id=1, source_target_pairs={{0,2},{1,3},{4,0},{5,1},{8,4},{9,5},{12,8},{13,9},{14,12},{15,13},... | collective-permute-start | bytes 393224 | tf_op jit(solution)/shard_map/ppermute | solution.py:491
  64.1 6.8 %collective-permute-start.20 = (bf16[16,4096]{1,0:T(8,128)(2,1)S(1)}, bf16[16,4096]{1,0:T(8,128)(2,1)S(1)}, u32[]{:S(2)}, u32[]{:S(2)}) collective-permute-start(bf16[16,4096]{1,0:T(8,128)(2,1)S(1)} %add_blocks.13.refs_6_), channel_id=1, source_target_pairs={{0,4},{1,5},{4,8},{5,9},{8,12},{9,13},{12,14},{13,15},{14,10},{15,... | collective-permute-start | bytes 393224 | tf_op jit(solution)/shard_map/ppermute | solution.py:491
  68.1 5.7 %collective-permute-start.19 = (bf16[16,4096]{1,0:T(8,128)(2,1)S(1)}, bf16[16,4096]{1,0:T(8,128)(2,1)S(1)}, u32[]{:S(2)}, u32[]{:S(2)}) collective-permute-start(bf16[16,4096]{1,0:T(8,128)(2,1)S(1)} %get-tuple-element.24.refs_3_), channel_id=1, source_target_pairs={{0,4},{1,5},{4,8},{5,9},{8,12},{9,13},{12,14},{13,15},{14,10},{15,... | collective-permute-start | bytes 393224 | tf_op jit(solution)/shard_map/ppermute | solution.py:491
  69.8 6.2 %collective-permute-start.23 = (bf16[16,4096]{1,0:T(8,128)(2,1)S(1)}, bf16[16,4096]{1,0:T(8,128)(2,1)S(1)}, u32[]{:S(2)}, u32[]{:S(2)}) collective-permute-start(bf16[16,4096]{1,0:T(8,128)(2,1)S(1)} %add_blocks.15.refs_3_), channel_id=1, source_target_pairs={{0,2},{1,3},{4,0},{5,1},{8,4},{9,5},{12,8},{13,9},{14,12},{15,13},... | collective-permute-start | bytes 393224 | tf_op jit(solution)/shard_map/ppermute | solution.py:491
  70.9 7.3 %collective-permute-start.26 = (bf16[16,4096]{1,0:T(8,128)(2,1)S(1)}, bf16[16,4096]{1,0:T(8,128)(2,1)S(1)}, u32[]{:S(2)}, u32[]{:S(2)}) collective-permute-start(bf16[16,4096]{1,0:T(8,128)(2,1)S(1)} %add_blocks.16.refs_3_), channel_id=1, source_target_pairs={{0,4},{1,5},{4,8},{5,9},{8,12},{9,13},{12,14},{13,15},{14,10},{15,... | collective-permute-start | bytes 393224 | tf_op jit(solution)/shard_map/ppermute | solution.py:491
  72.0 7.4 %collective-permute-start.25 = (bf16[16,4096]{1,0:T(8,128)(2,1)S(1)}, bf16[16,4096]{1,0:T(8,128)(2,1)S(1)}, u32[]{:S(2)}, u32[]{:S(2)}) collective-permute-start(bf16[16,4096]{1,0:T(8,128)(2,1)S(1)} %get-tuple-element.25), channel_id=1, source_target_pairs={{0,2},{1,3},{4,0},{5,1},{8,4},{9,5},{12,8},{13,9},{14,12},{15,13},... | collective-permute-start | bytes 393224 | tf_op jit(solution)/shard_map/ppermute | solution.py:491
  76.1 8.9 %copy-start.7 = (bf16[8192]{0:T(1024)(128)(2,1)S(1)}, bf16[8192]{0:T(1024)(128)(2,1)}, u32[]{:S(2)}) copy-start(bf16[8192]{0:T(1024)(128)(2,1)} %param.15) | copy-start | bytes 49156
  76.1 5.5 %collective-permute-start.24 = (bf16[16,4096]{1,0:T(8,128)(2,1)S(1)}, bf16[16,4096]{1,0:T(8,128)(2,1)S(1)}, u32[]{:S(2)}, u32[]{:S(2)}) collective-permute-start(bf16[16,4096]{1,0:T(8,128)(2,1)S(1)} %add_blocks.18.refs_3_), channel_id=1, source_target_pairs={{0,2},{1,3},{4,0},{5,1},{8,4},{9,5},{12,8},{13,9},{14,12},{15,13},... | collective-permute-start | bytes 393224 | tf_op jit(solution)/shard_map/ppermute | solution.py:491
  77.2 5.6 %collective-permute-start.22 = (bf16[16,4096]{1,0:T(8,128)(2,1)S(1)}, bf16[16,4096]{1,0:T(8,128)(2,1)S(1)}, u32[]{:S(2)}, u32[]{:S(2)}) collective-permute-start(bf16[16,4096]{1,0:T(8,128)(2,1)S(1)} %add_blocks.17.refs_3_), channel_id=1, source_target_pairs={{0,4},{1,5},{4,8},{5,9},{8,12},{9,13},{12,14},{13,15},{14,10},{15,... | collective-permute-start | bytes 393224 | tf_op jit(solution)/shard_map/ppermute | solution.py:491
  78.2 6.9 %collective-permute-start.29 = (bf16[16,4096]{1,0:T(8,128)(2,1)S(1)}, bf16[16,4096]{1,0:T(8,128)(2,1)S(1)}, u32[]{:S(2)}, u32[]{:S(2)}) collective-permute-start(bf16[16,4096]{1,0:T(8,128)(2,1)S(1)} %add_blocks.19.refs_3_), channel_id=1, source_target_pairs={{0,4},{1,5},{4,8},{5,9},{8,12},{9,13},{12,14},{13,15},{14,10},{15,... | collective-permute-start | bytes 393224 | tf_op jit(solution)/shard_map/ppermute | solution.py:491
  79.5 5.7 %collective-permute-start.28 = (bf16[16,4096]{1,0:T(8,128)(2,1)S(1)}, bf16[16,4096]{1,0:T(8,128)(2,1)S(1)}, u32[]{:S(2)}, u32[]{:S(2)}) collective-permute-start(bf16[16,4096]{1,0:T(8,128)(2,1)S(1)} %add_blocks.20.refs_6_), channel_id=1, source_target_pairs={{0,2},{1,3},{4,0},{5,1},{8,4},{9,5},{12,8},{13,9},{14,12},{15,13},... | collective-permute-start | bytes 393224 | tf_op jit(solution)/shard_map/ppermute | solution.py:491
  82.9 5.0 %collective-permute-start.27 = (bf16[16,4096]{1,0:T(8,128)(2,1)S(1)}, bf16[16,4096]{1,0:T(8,128)(2,1)S(1)}, u32[]{:S(2)}, u32[]{:S(2)}) collective-permute-start(bf16[16,4096]{1,0:T(8,128)(2,1)S(1)} %get-tuple-element.26), channel_id=1, source_target_pairs={{0,4},{1,5},{4,8},{5,9},{8,12},{9,13},{12,14},{13,15},{14,10},{15,... | collective-permute-start | bytes 393224 | tf_op jit(solution)/shard_map/ppermute | solution.py:491
  83.8 5.0 %collective-permute-start.30 = (bf16[16,4096]{1,0:T(8,128)(2,1)S(1)}, bf16[16,4096]{1,0:T(8,128)(2,1)S(1)}, u32[]{:S(2)}, u32[]{:S(2)}) collective-permute-start(bf16[16,4096]{1,0:T(8,128)(2,1)S(1)} %get-tuple-element.27), channel_id=1, source_target_pairs={{0,2},{1,3},{4,0},{5,1},{8,4},{9,5},{12,8},{13,9},{14,12},{15,13},... | collective-permute-start | bytes 393224 | tf_op jit(solution)/shard_map/ppermute | solution.py:491

commit v13 on v11

--- a/solution.py
+++ b/solution.py
@@ -197,7 +197,7 @@
     model_width = factor.shape[1]
     slots = factor.shape[0] // rank_limit
     batch_rows = to_place.shape[0]
-    width = model_width // 4
+    width = model_width // 2
 
     def kernel(*refs):
         factor_ref, scale_ref, place_ref, rows_out, coeff_out, total = refs[len(parts) :]

time: 89.1 us -> 88.9 us (level)
  no operation moved by 1% of the time
where the time goes in v13:
time: 88.9 us; the launch traced here: 88.7 us
  starting transfers between devices  29.5 us (33%)
  waiting for transfers between devices  27.5 us (31%)
  Pallas kernels  25.6 us (29%)
  matrix products  4.84 us (5%)
  between operations  1.04 us (1%)
    ppermute x14, starting transfers between devices, scatter_rows(): chain[h] = lax.ppermute(value, AXIS, ring(size, by))  15 us
    pallas_call x28, Pallas kernels, call(): pl.pallas_call(run, out_shape=out_shape, in_specs=[whole(pltpu.SMEM if op...  11.7 us
    ppermute x14, waiting for transfers between devices, scatter_rows(): chain[h] = lax.ppermute(value, AXIS, ring(size, by))  10.3 us
    pallas_call x2, Pallas kernels, load_rows(): pl.pallas_call(kernel, out_shape=[jax.ShapeDtypeStruct(shape, weights[0]....  9.2 us
    ppermute x3, waiting for transfers between devices, gather_rows(): right = lax.ppermute(right, AXIS, ring(size, 1))  6.55 us
    ppermute x3, starting transfers between devices, gather_rows(): right = lax.ppermute(right, AXIS, ring(size, 1))  6.45 us
    dot_general x2, matrix products, body(): jnp.dot(hidden, down_weight[:, h * width:(h + 1) * width], preferred_elem...  4.84 us
    pallas_call x1, Pallas kernels, stream_rows(): pl.pallas_call(kernel, out_shape=jax.ShapeDtypeStruct((batch_rows, width)...  4.65 us
  transfers between devices with their start and end apart: 31, of which 19 were waited for; matrix products, arithmetic and copies ran while one was open for 3% of the time, Pallas kernels for 24%

profile of v13, /device:TPU:0, one launch (start us, length us, event | category | flops | bytes accessed | tf_op | source)
XLA Modules:
  0.0 88.7 jit_solution(7553083781548240330)
XLA Ops:
  0.6 3.1 %collective-permute-start = (bf16[16,8192]{1,0:T(8,128)(2,1)}, bf16[16,8192]{1,0:T(8,128)(2,1)S(1)}, u32[]{:S(2)}, u32[]{:S(2)}) collective-permute-start(bf16[16,8192]{1,0:T(8,128)(2,1)} %refs_8_.1), channel_id=1, source_target_pairs={{0,4},{1,5},{4,8},{5,9},{8,12},{9,13},{12,14},{13,15},{14,10},{15,... | collective-permute-start | bytes 786440 | tf_op jit(solution)/shard_map/ppermute | solution.py:138
  3.7 4.6 %load_rows.2.refs_1_ = bf16[3328,1792]{1,0:T(8,128)(2,1)S(1)} custom-call(bf16[8192,896]{1,0:T(8,128)(2,1)} %refs_0_.7, bf16[8192,896]{1,0:T(8,128)(2,1)} %refs_1_.5), custom_call_target="tpu_custom_call" | custom-call | bytes 23855104 | tf_op jit(solution)/shard_map/load_rows/pallas_call | solution.py:292
  8.3 1.8 %collective-permute-done.refs_0_ = bf16[16,8192]{1,0:T(8,128)(2,1)S(1)} collective-permute-done((bf16[16,8192]{1,0:T(8,128)(2,1)}, bf16[16,8192]{1,0:T(8,128)(2,1)S(1)}, u32[]{:S(2)}, u32[]{:S(2)}) %collective-permute-start) | collective-permute-done | bytes 262176 | tf_op jit(solution)/shard_map/ppermute | solution.py:138
  10.2 1.8 %collective-permute-start.2 = (bf16[16,8192]{1,0:T(8,128)(2,1)S(1)}, bf16[16,8192]{1,0:T(8,128)(2,1)S(1)}, u32[]{:S(2)}, u32[]{:S(2)}) collective-permute-start(bf16[16,8192]{1,0:T(8,128)(2,1)S(1)} %pass_on.2.refs_2_), channel_id=1, source_target_pairs={{0,4},{1,5},{4,8},{5,9},{8,12},{9,13},{12,14},{13,15},{14,10},{15,... | collective-permute-start | bytes 786440 | tf_op jit(solution)/shard_map/ppermute | solution.py:138
  12.3 4.6 %load_rows.3.refs_1_ = bf16[3328,1792]{1,0:T(8,128)(2,1)S(1)} custom-call(bf16[8192,896]{1,0:T(8,128)(2,1)} %refs_0_.7, bf16[8192,896]{1,0:T(8,128)(2,1)} %refs_1_.5, bf16[16,8192]{1,0:T(8,128)(2,1)S(1)} %pass_on.2.refs_2_), custom_call_target="tpu_custom_call" | custom-call | bytes 23855104 | tf_op jit(solution)/shard_map/load_rows/pallas_call | solution.py:292
  17.0 0.8 collective-permute-done.2.refs_0_.refs_2_
  17.8 1.5 %collective-permute-start.4 = (bf16[16,8192]{1,0:T(8,128)(2,1)S(1)}, bf16[16,8192]{1,0:T(8,128)(2,1)S(1)}, u32[]{:S(2)}, u32[]{:S(2)}) collective-permute-start(bf16[16,8192]{1,0:T(8,128)(2,1)S(1)} %pass_on.3), channel_id=1, source_target_pairs={{0,4},{1,5},{4,8},{5,9},{8,12},{9,13},{12,14},{13,15},{14,10},{15,... | collective-permute-start | bytes 786440 | tf_op jit(solution)/shard_map/ppermute | solution.py:138
  19.9 0.6 row_masks.1
  20.4 3.9 %collective-permute-done.4.refs_4_.refs_0_ = bf16[16,8192]{1,0:T(8,128)(2,1)S(1)} collective-permute-done((bf16[16,8192]{1,0:T(8,128)(2,1)S(1)}, bf16[16,8192]{1,0:T(8,128)(2,1)S(1)}, u32[]{:S(2)}, u32[]{:S(2)}) %collective-permute-start.4) | collective-permute-done | bytes 262176 | tf_op jit(solution)/shard_map/ppermute | solution.py:138
  24.4 1.3 %collective-permute-done.5.refs_5_.refs_0_ = bf16[16,8192]{1,0:T(8,128)(2,1)S(1)} collective-permute-done((bf16[16,8192]{1,0:T(8,128)(2,1)S(1)}, bf16[16,8192]{1,0:T(8,128)(2,1)S(1)}, u32[]{:S(2)}, u32[]{:S(2)}) %collective-permute-start.5) | collective-permute-done | bytes 262176 | tf_op jit(solution)/shard_map/ppermute | solution.py:139
  25.9 1.6 %collective-permute-start.6 = (bf16[16,4096]{1,0:T(8,128)(2,1)S(1)}, bf16[16,4096]{1,0:T(8,128)(2,1)S(1)}, u32[]{:S(2)}, u32[]{:S(2)}) collective-permute-start(bf16[16,4096]{1,0:T(8,128)(2,1)S(1)} %column_half.2), channel_id=1, source_target_pairs={{0,4},{1,5},{4,8},{5,9},{8,12},{9,13},{12,14},{13,15},{14,10},{15,... | collective-permute-start | bytes 393224 | tf_op jit(solution)/shard_map/ppermute | solution.py:151
  28.0 3.8 %collective-permute-done.6.refs_0_ = bf16[16,4096]{1,0:T(8,128)(2,1)S(1)} collective-permute-done((bf16[16,4096]{1,0:T(8,128)(2,1)S(1)}, bf16[16,4096]{1,0:T(8,128)(2,1)S(1)}, u32[]{:S(2)}, u32[]{:S(2)}) %collective-permute-start.6) | collective-permute-done | bytes 131104 | tf_op jit(solution)/shard_map/ppermute | solution.py:151
  31.8 1.4 %collective-permute-done.7.refs_1_ = bf16[16,4096]{1,0:T(8,128)(2,1)S(1)} collective-permute-done((bf16[16,4096]{1,0:T(8,128)(2,1)S(1)}, bf16[16,4096]{1,0:T(8,128)(2,1)S(1)}, u32[]{:S(2)}, u32[]{:S(2)}) %collective-permute-start.7) | collective-permute-done | bytes 131104 | tf_op jit(solution)/shard_map/ppermute | solution.py:152
  33.3 1.5 %collective-permute-done.10.refs_5_ = bf16[16,8192]{1,0:T(8,128)(2,1)S(1)} collective-permute-done((bf16[16,8192]{1,0:T(8,128)(2,1)S(1)}, bf16[16,8192]{1,0:T(8,128)(2,1)S(1)}, u32[]{:S(2)}, u32[]{:S(2)}) %collective-permute-start.10) | collective-permute-done | bytes 262176 | tf_op jit(solution)/shard_map/ppermute | solution.py:157
  34.8 1.7 %shrink_rows.1 = (bf16[256,8192]{1,0:T(8,128)(2,1)S(1)}, bf16[256,64]{1,0:T(8,128)(2,1)S(1)}) custom-call(bf16[16,8192]{1,0:T(8,128)(2,1)S(1)} %copy-done.1, bf16[96,8192]{1,0:T(8,128)(2,1)S(1)} %join_pieces.2.refs_1_, bf16[16,8192]{1,0:T(8,128)(2,1)S(1)} %join_pieces.3.refs_2_, bf16[16,8192]{1,0:T(8,128)(2,1)S(1)} %collective-permute-done.8.refs_3_, ...), custom_call_target="tpu_custom_call" | custom-call | flops 268435456 | bytes 8388608 | tf_op jit(solution)/shard_map/shrink_rows/pallas_call | solution.py:78
  36.8 1.1 %collective-permute-done.11.refs_1_ = bf16[256,64]{1,0:T(8,128)(2,1)S(1)} collective-permute-done((bf16[256,64]{1,0:T(8,128)(2,1)S(1)}, bf16[256,64]{1,0:T(8,128)(2,1)S(1)}, u32[]{:S(2)}, u32[]{:S(2)}) %collective-permute-start.11) | collective-permute-done | bytes 32800 | tf_op jit(solution)/shard_map/ppermute | solution.py:552
  38.4 3.2 %mixed_rows.2.refs_2_ = f32[256,1792]{1,0:T(8,128)S(1)} custom-call(bf16[256,8192]{1,0:T(8,128)(2,1)S(1)} %get-tuple-element.15.refs_0_.rows_ref, bf16[3328,1792]{1,0:T(8,128)(2,1)S(1)} %load_rows.2.refs_1_, bf16[256,64]{1,0:T(8,128)(2,1)S(1)} %add_coefficients.3.refs_2_.refs_0_), custom_call_target="tpu_custom_call" | custom-call | flops 3053453312 | bytes 11927552 | tf_op jit(solution)/shard_map/mixed_rows/pallas_call | solution.py:78
  41.7 0.6 collective-permute-done.12.refs_1_
  42.3 1.6 %collective-permute-start.13 = (bf16[256,64]{1,0:T(8,128)(2,1)S(1)}, bf16[256,64]{1,0:T(8,128)(2,1)S(1)}, u32[]{:S(2)}, u32[]{:S(2)}) collective-permute-start(bf16[256,64]{1,0:T(8,128)(2,1)S(1)} %add_coefficients.4.refs_3_.refs_0_), channel_id=1, source_target_pairs={{0,4},{1,5},{2,6},{3,7},{4,0},{5,1},{6,2},{7,3},{8,12},{9,13},{10,... | collective-permute-start | bytes 98312 | tf_op jit(solution)/shard_map/ppermute | solution.py:552
  43.9 3.2 %mixed_rows.3.refs_2_ = f32[256,1792]{1,0:T(8,128)S(1)} custom-call(bf16[256,8192]{1,0:T(8,128)(2,1)S(1)} %get-tuple-element.15.refs_0_.rows_ref, bf16[3328,1792]{1,0:T(8,128)(2,1)S(1)} %load_rows.3.refs_1_, f32[256,1792]{1,0:T(8,128)S(1)} %mixed_rows.2.refs_2_, bf16[256,64]{1,0:T(8,128)(2,1)S(1)} %add_coefficients.4.refs_3_.refs_0_), custom_call_target="tpu_custom_call" | custom-call | flops 3053453312 | bytes 11927552 | tf_op jit(solution)/shard_map/mixed_rows/pallas_call | solution.py:78
  47.2 2.0 %collective-permute-start.14 = (bf16[256,64]{1,0:T(8,128)(2,1)S(1)}, bf16[256,64]{1,0:T(8,128)(2,1)S(1)}, u32[]{:S(2)}, u32[]{:S(2)}) collective-permute-start(bf16[256,64]{1,0:T(8,128)(2,1)S(1)} %add_coefficients.5.refs_3_.refs_0_), channel_id=1, source_target_pairs={{0,8},{1,9},{2,10},{3,11},{4,12},{5,13},{6,14},{7,15},{8,0},{9,1},... | collective-permute-start | bytes 98312 | tf_op jit(solution)/shard_map/ppermute | solution.py:552
  49.3 4.6 %stream_rows.1.refs_5_ = f32[256,1792]{1,0:T(8,128)S(1)} custom-call(bf16[256,8192]{1,0:T(8,128)(2,1)S(1)} %get-tuple-element.15.refs_0_.rows_ref, bf16[8192,896]{1,0:T(8,128)(2,1)} %refs_0_.7, bf16[8192,896]{1,0:T(8,128)(2,1)} %refs_1_.5, f32[256,1792]{1,0:T(8,128)S(1)} %mixed_rows.3.refs_2_, bf16[256,64]{1,0:T(8,128)(2,1)S(1)} %add_coefficients.5.refs_3_.refs_0_), custom_call_target="tpu_custom_call" | custom-call | flops 1409286144 | bytes 11010048 | tf_op jit(solution)/shard_map/stream_rows/pallas_call | solution.py:395
  53.9 1.0 %hidden_rows.1 = bf16[256,896]{1,0:T(8,128)(2,1)S(1)} custom-call(bf16[256,64]{1,0:T(8,128)(2,1)S(1)} %add_coefficients.5.refs_3_.refs_0_, bf16[256,64]{1,0:T(8,128)(2,1)S(1)} %collective-permute-done.14.refs_1_, bf16[256,256]{1,0:T(8,128)(2,1)S(1)} %get-tuple-element.16.refs_2_, bf16[256,1024]{1,0:T(8,128)(2,1)S(1)} %get-tuple-element.17.refs_3_, ...), custom_call_target="tpu_custom_call" | custom-call | flops 469762048 | bytes 1835008 | tf_op jit(solution)/shard_map/hidden_rows/pallas_call | solution.py:78
  55.0 2.4 %fusion.4.refs_0_ = bf16[256,4096]{1,0:T(8,128)(2,1)S(1)} fusion(bf16[256,896]{1,0:T(8,128)(2,1)S(1)} %hidden_rows.1, bf16[896,8192]{1,0:T(8,128)(2,1)S(1)} %bitcast.17), kind=kOutput, calls=%fused_computation.4 | convolution fusion | flops 1880096768 | bytes 9895936 | tf_op jit(solution)/shard_map/dot_general | solution.py:569
  57.6 2.4 %fusion.7.refs_0_.refs_3_.refs_4_ = bf16[256,4096]{1,0:T(8,128)(2,1)S(1)} fusion(bf16[256,896]{1,0:T(8,128)(2,1)S(1)} %hidden_rows.1, bf16[896,8192]{1,0:T(8,128)(2,1)S(1)} %bitcast.17), kind=kOutput, calls=%fused_computation.5 | convolution fusion | flops 1880096768 | bytes 9895936 | tf_op jit(solution)/shard_map/dot_general | solution.py:569
  60.1 0.6 collective-permute-start.17
  60.7 1.3 %collective-permute-start.16 = (bf16[16,4096]{1,0:T(8,128)(2,1)S(1)}, bf16[16,4096]{1,0:T(8,128)(2,1)S(1)}, u32[]{:S(2)}, u32[]{:S(2)}) collective-permute-start(bf16[16,4096]{1,0:T(8,128)(2,1)S(1)} %add_blocks.13.refs_2_), channel_id=1, source_target_pairs={{0,4},{1,5},{4,8},{5,9},{8,12},{9,13},{12,14},{13,15},{14,10},{15,... | collective-permute-start | bytes 393224 | tf_op jit(solution)/shard_map/ppermute | solution.py:489
  62.0 0.9 %collective-permute-done.17.refs_1_.refs_4_.refs_5_ = bf16[128,4096]{1,0:T(8,128)(2,1)S(1)} collective-permute-done((bf16[128,4096]{1,0:T(8,128)(2,1)S(1)}, bf16[128,4096]{1,0:T(8,128)(2,1)S(1)}, u32[]{:S(2)}, u32[]{:S(2)}) %collective-permute-start.17) | collective-permute-done | bytes 1048608 | tf_op jit(solution)/shard_map/ppermute | solution.py:575
  63.0 1.1 %collective-permute-start.21 = (bf16[16,4096]{1,0:T(8,128)(2,1)S(1)}, bf16[16,4096]{1,0:T(8,128)(2,1)S(1)}, u32[]{:S(2)}, u32[]{:S(2)}) collective-permute-start(bf16[16,4096]{1,0:T(8,128)(2,1)S(1)} %add_blocks.16.refs_3_), channel_id=1, source_target_pairs={{0,2},{1,3},{4,0},{5,1},{8,4},{9,5},{12,8},{13,9},{14,12},{15,13},... | collective-permute-start | bytes 393224 | tf_op jit(solution)/shard_map/ppermute | solution.py:489
  64.1 1.0 %collective-permute-start.20 = (bf16[16,4096]{1,0:T(8,128)(2,1)S(1)}, bf16[16,4096]{1,0:T(8,128)(2,1)S(1)}, u32[]{:S(2)}, u32[]{:S(2)}) collective-permute-start(bf16[16,4096]{1,0:T(8,128)(2,1)S(1)} %add_blocks.15.refs_2_), channel_id=1, source_target_pairs={{0,4},{1,5},{4,8},{5,9},{8,12},{9,13},{12,14},{13,15},{14,10},{15,... | collective-permute-start | bytes 393224 | tf_op jit(solution)/shard_map/ppermute | solution.py:489
  65.1 1.0 %collective-permute-start.19 = (bf16[16,4096]{1,0:T(8,128)(2,1)S(1)}, bf16[16,4096]{1,0:T(8,128)(2,1)S(1)}, u32[]{:S(2)}, u32[]{:S(2)}) collective-permute-start(bf16[16,4096]{1,0:T(8,128)(2,1)S(1)} %add_blocks.14.refs_2_), channel_id=1, source_target_pairs={{0,2},{1,3},{4,0},{5,1},{8,4},{9,5},{12,8},{13,9},{14,12},{15,13},... | collective-permute-start | bytes 393224 | tf_op jit(solution)/shard_map/ppermute | solution.py:489
  66.4 1.1 %collective-permute-start.18 = (bf16[16,4096]{1,0:T(8,128)(2,1)S(1)}, bf16[16,4096]{1,0:T(8,128)(2,1)S(1)}, u32[]{:S(2)}, u32[]{:S(2)}) collective-permute-start(bf16[16,4096]{1,0:T(8,128)(2,1)S(1)} %add_blocks.17.refs_3_), channel_id=1, source_target_pairs={{0,4},{1,5},{4,8},{5,9},{8,12},{9,13},{12,14},{13,15},{14,10},{15,... | collective-permute-start | bytes 393224 | tf_op jit(solution)/shard_map/ppermute | solution.py:489
  67.5 1.9 %collective-permute-done.21.refs_2_ = bf16[16,4096]{1,0:T(8,128)(2,1)S(1)} collective-permute-done((bf16[16,4096]{1,0:T(8,128)(2,1)S(1)}, bf16[16,4096]{1,0:T(8,128)(2,1)S(1)}, u32[]{:S(2)}, u32[]{:S(2)}) %collective-permute-start.21) | collective-permute-done | bytes 131104 | tf_op jit(solution)/shard_map/ppermute | solution.py:489
  69.5 1.1 %collective-permute-start.23 = (bf16[16,4096]{1,0:T(8,128)(2,1)S(1)}, bf16[16,4096]{1,0:T(8,128)(2,1)S(1)}, u32[]{:S(2)}, u32[]{:S(2)}) collective-permute-start(bf16[16,4096]{1,0:T(8,128)(2,1)S(1)} %add_blocks.18.refs_3_), channel_id=1, source_target_pairs={{0,2},{1,3},{4,0},{5,1},{8,4},{9,5},{12,8},{13,9},{14,12},{15,13},... | collective-permute-start | bytes 393224 | tf_op jit(solution)/shard_map/ppermute | solution.py:489
  70.6 1.1 %collective-permute-start.26 = (bf16[16,4096]{1,0:T(8,128)(2,1)S(1)}, bf16[16,4096]{1,0:T(8,128)(2,1)S(1)}, u32[]{:S(2)}, u32[]{:S(2)}) collective-permute-start(bf16[16,4096]{1,0:T(8,128)(2,1)S(1)} %add_blocks.19.refs_3_), channel_id=1, source_target_pairs={{0,4},{1,5},{4,8},{5,9},{8,12},{9,13},{12,14},{13,15},{14,10},{15,... | collective-permute-start | bytes 393224 | tf_op jit(solution)/shard_map/ppermute | solution.py:489
  72.2 1.1 %collective-permute-start.25 = (bf16[16,4096]{1,0:T(8,128)(2,1)S(1)}, bf16[16,4096]{1,0:T(8,128)(2,1)S(1)}, u32[]{:S(2)}, u32[]{:S(2)}) collective-permute-start(bf16[16,4096]{1,0:T(8,128)(2,1)S(1)} %add_blocks.20.refs_3_), channel_id=1, source_target_pairs={{0,2},{1,3},{4,0},{5,1},{8,4},{9,5},{12,8},{13,9},{14,12},{15,13},... | collective-permute-start | bytes 393224 | tf_op jit(solution)/shard_map/ppermute | solution.py:489
  73.3 1.7 %collective-permute-done.23.refs_2_ = bf16[16,4096]{1,0:T(8,128)(2,1)S(1)} collective-permute-done((bf16[16,4096]{1,0:T(8,128)(2,1)S(1)}, bf16[16,4096]{1,0:T(8,128)(2,1)S(1)}, u32[]{:S(2)}, u32[]{:S(2)}) %collective-permute-start.23) | collective-permute-done | bytes 131104 | tf_op jit(solution)/shard_map/ppermute | solution.py:489
  75.1 1.1 %collective-permute-start.24 = (bf16[16,4096]{1,0:T(8,128)(2,1)S(1)}, bf16[16,4096]{1,0:T(8,128)(2,1)S(1)}, u32[]{:S(2)}, u32[]{:S(2)}) collective-permute-start(bf16[16,4096]{1,0:T(8,128)(2,1)S(1)} %add_blocks.22.refs_3_), channel_id=1, source_target_pairs={{0,2},{1,3},{4,0},{5,1},{8,4},{9,5},{12,8},{13,9},{14,12},{15,13},... | collective-permute-start | bytes 393224 | tf_op jit(solution)/shard_map/ppermute | solution.py:489
  76.2 1.0 %collective-permute-start.22 = (bf16[16,4096]{1,0:T(8,128)(2,1)S(1)}, bf16[16,4096]{1,0:T(8,128)(2,1)S(1)}, u32[]{:S(2)}, u32[]{:S(2)}) collective-permute-start(bf16[16,4096]{1,0:T(8,128)(2,1)S(1)} %add_blocks.21.refs_3_), channel_id=1, source_target_pairs={{0,4},{1,5},{4,8},{5,9},{8,12},{9,13},{12,14},{13,15},{14,10},{15,... | collective-permute-start | bytes 393224 | tf_op jit(solution)/shard_map/ppermute | solution.py:489
  77.3 1.1 %collective-permute-start.29 = (bf16[16,4096]{1,0:T(8,128)(2,1)S(1)}, bf16[16,4096]{1,0:T(8,128)(2,1)S(1)}, u32[]{:S(2)}, u32[]{:S(2)}) collective-permute-start(bf16[16,4096]{1,0:T(8,128)(2,1)S(1)} %add_blocks.23.refs_3_), channel_id=1, source_target_pairs={{0,4},{1,5},{4,8},{5,9},{8,12},{9,13},{12,14},{13,15},{14,10},{15,... | collective-permute-start | bytes 393224 | tf_op jit(solution)/shard_map/ppermute | solution.py:489
  78.7 1.1 %collective-permute-start.28 = (bf16[16,4096]{1,0:T(8,128)(2,1)S(1)}, bf16[16,4096]{1,0:T(8,128)(2,1)S(1)}, u32[]{:S(2)}, u32[]{:S(2)}) collective-permute-start(bf16[16,4096]{1,0:T(8,128)(2,1)S(1)} %add_blocks.24.refs_6_), channel_id=1, source_target_pairs={{0,2},{1,3},{4,0},{5,1},{8,4},{9,5},{12,8},{13,9},{14,12},{15,13},... | collective-permute-start | bytes 393224 | tf_op jit(solution)/shard_map/ppermute | solution.py:489
  79.8 1.7 %collective-permute-done.24.refs_5_ = bf16[16,4096]{1,0:T(8,128)(2,1)S(1)} collective-permute-done((bf16[16,4096]{1,0:T(8,128)(2,1)S(1)}, bf16[16,4096]{1,0:T(8,128)(2,1)S(1)}, u32[]{:S(2)}, u32[]{:S(2)}) %collective-permute-start.24) | collective-permute-done | bytes 131104 | tf_op jit(solution)/shard_map/ppermute | solution.py:489
  81.6 1.1 %collective-permute-start.27 = (bf16[16,4096]{1,0:T(8,128)(2,1)S(1)}, bf16[16,4096]{1,0:T(8,128)(2,1)S(1)}, u32[]{:S(2)}, u32[]{:S(2)}) collective-permute-start(bf16[16,4096]{1,0:T(8,128)(2,1)S(1)} %get-tuple-element.18), channel_id=1, source_target_pairs={{0,4},{1,5},{4,8},{5,9},{8,12},{9,13},{12,14},{13,15},{14,10},{15,... | collective-permute-start | bytes 393224 | tf_op jit(solution)/shard_map/ppermute | solution.py:489
  82.7 1.0 %collective-permute-start.30 = (bf16[16,4096]{1,0:T(8,128)(2,1)S(1)}, bf16[16,4096]{1,0:T(8,128)(2,1)S(1)}, u32[]{:S(2)}, u32[]{:S(2)}) collective-permute-start(bf16[16,4096]{1,0:T(8,128)(2,1)S(1)} %get-tuple-element.19), channel_id=1, source_target_pairs={{0,2},{1,3},{4,0},{5,1},{8,4},{9,5},{12,8},{13,9},{14,12},{15,13},... | collective-permute-start | bytes 393224 | tf_op jit(solution)/shard_map/ppermute | solution.py:489
  83.7 1.4 %collective-permute-done.28.refs_3_ = bf16[16,4096]{1,0:T(8,128)(2,1)S(1)} collective-permute-done((bf16[16,4096]{1,0:T(8,128)(2,1)S(1)}, bf16[16,4096]{1,0:T(8,128)(2,1)S(1)}, u32[]{:S(2)}, u32[]{:S(2)}) %collective-permute-start.28) | collective-permute-done | bytes 131104 | tf_op jit(solution)/shard_map/ppermute | solution.py:489
  85.1 1.5 %collective-permute-done.27.refs_2_ = bf16[16,4096]{1,0:T(8,128)(2,1)S(1)} collective-permute-done((bf16[16,4096]{1,0:T(8,128)(2,1)S(1)}, bf16[16,4096]{1,0:T(8,128)(2,1)S(1)}, u32[]{:S(2)}, u32[]{:S(2)}) %collective-permute-start.27) | collective-permute-done | bytes 131104 | tf_op jit(solution)/shard_map/ppermute | solution.py:489
  86.6 1.0 %collective-permute-done.30.refs_7_ = bf16[16,4096]{1,0:T(8,128)(2,1)S(1)} collective-permute-done((bf16[16,4096]{1,0:T(8,128)(2,1)S(1)}, bf16[16,4096]{1,0:T(8,128)(2,1)S(1)}, u32[]{:S(2)}, u32[]{:S(2)}) %collective-permute-start.30) | collective-permute-done | bytes 131104 | tf_op jit(solution)/shard_map/ppermute | solution.py:489
  87.7 1.0 %finish_rows.1 = (bf16[16,8192]{1,0:T(8,128)(2,1)}, bf16[16,8192]{1,0:T(8,128)(2,1)}) custom-call(bf16[256,4096]{1,0:T(8,128)(2,1)S(1)} %fusion.4.refs_0_, bf16[128,4096]{1,0:T(8,128)(2,1)S(1)} %collective-permute-done.15.refs_1_, bf16[16,4096]{1,0:T(8,128)(2,1)S(1)} %collective-permute-done.27.refs_2_, ...), custom_call_target="tpu_custom_call" | custom-call | tf_op jit(solution)/shard_map/finish_rows/pallas_call | solution.py:78
  (75 shorter events, 4.5 us)
Async XLA Ops:
  0.6 9.5 %collective-permute-start = (bf16[16,8192]{1,0:T(8,128)(2,1)}, bf16[16,8192]{1,0:T(8,128)(2,1)S(1)}, u32[]{:S(2)}, u32[]{:S(2)}) collective-permute-start(bf16[16,8192]{1,0:T(8,128)(2,1)} %refs_8_.1), channel_id=1, source_target_pairs={{0,4},{1,5},{4,8},{5,9},{8,12},{9,13},{12,14},{13,15},{14,10},{15,... | collective-permute-start | bytes 786440 | tf_op jit(solution)/shard_map/ppermute | solution.py:138
  3.7 8.3 %collective-permute-start.1 = (bf16[16,8192]{1,0:T(8,128)(2,1)}, bf16[16,8192]{1,0:T(8,128)(2,1)S(1)}, u32[]{:S(2)}, u32[]{:S(2)}) collective-permute-start(bf16[16,8192]{1,0:T(8,128)(2,1)} %refs_8_.1), channel_id=1, source_target_pairs={{0,2},{1,3},{4,0},{5,1},{8,4},{9,5},{12,8},{13,9},{14,12},{15,13},... | collective-permute-start | bytes 786440 | tf_op jit(solution)/shard_map/ppermute | solution.py:139
  10.2 7.5 %collective-permute-start.2 = (bf16[16,8192]{1,0:T(8,128)(2,1)S(1)}, bf16[16,8192]{1,0:T(8,128)(2,1)S(1)}, u32[]{:S(2)}, u32[]{:S(2)}) collective-permute-start(bf16[16,8192]{1,0:T(8,128)(2,1)S(1)} %pass_on.2.refs_2_), channel_id=1, source_target_pairs={{0,4},{1,5},{4,8},{5,9},{8,12},{9,13},{12,14},{13,15},{14,10},{15,... | collective-permute-start | bytes 786440 | tf_op jit(solution)/shard_map/ppermute | solution.py:138
  12.0 7.2 %collective-permute-start.3 = (bf16[16,8192]{1,0:T(8,128)(2,1)S(1)}, bf16[16,8192]{1,0:T(8,128)(2,1)S(1)}, u32[]{:S(2)}, u32[]{:S(2)}) collective-permute-start(bf16[16,8192]{1,0:T(8,128)(2,1)S(1)} %collective-permute-done.1.refs_1_), channel_id=1, source_target_pairs={{0,2},{1,3},{4,0},{5,1},{8,4},{9,5},{12,8},{13,9},{14,12},{15,13},... | collective-permute-start | bytes 786440 | tf_op jit(solution)/shard_map/ppermute | solution.py:139
  16.9 3.0 %copy-start.2 = (bf16[1,8192,64]{1,2,0:T(8,128)(2,1)S(1)}, bf16[1,8192,64]{1,2,0:T(8,128)(2,1)}, u32[]{:S(2)}) copy-start(bf16[1,8192,64]{1,2,0:T(8,128)(2,1)} %param.16) | copy-start | bytes 3145732
  16.9 3.0 %copy-start.3 = (s32[32]{0:T(128)S(1)}, s32[32]{0:T(128)}, u32[]{:S(2)}) copy-start(s32[32]{0:T(128)} %param.20) | copy-start | bytes 388
  16.9 2.9 %copy-start.4 = (s32[32]{0:T(128)S(1)}, s32[32]{0:T(128)}, u32[]{:S(2)}) copy-start(s32[32]{0:T(128)} %param.21) | copy-start | bytes 388
  16.9 2.9 %copy-start.5 = (s32[16]{0:T(128)S(1)}, s32[16]{0:T(128)}, u32[]{:S(2)}) copy-start(s32[16]{0:T(128)} %param.18) | copy-start | bytes 196
  16.9 2.9 %copy-start.6 = (s32[16]{0:T(128)S(1)}, s32[16]{0:T(128)}, u32[]{:S(2)}) copy-start(s32[16]{0:T(128)} %param.19) | copy-start | bytes 196
  16.9 11.1 %copy-start.1 = (bf16[16,8192]{1,0:T(8,128)(2,1)S(1)}, bf16[16,8192]{1,0:T(8,128)(2,1)}, u32[]{:S(2)}) copy-start(bf16[16,8192]{1,0:T(8,128)(2,1)} %refs_8_.1) | copy-start | bytes 786436
  17.8 6.6 %collective-permute-start.4 = (bf16[16,8192]{1,0:T(8,128)(2,1)S(1)}, bf16[16,8192]{1,0:T(8,128)(2,1)S(1)}, u32[]{:S(2)}, u32[]{:S(2)}) collective-permute-start(bf16[16,8192]{1,0:T(8,128)(2,1)S(1)} %pass_on.3), channel_id=1, source_target_pairs={{0,4},{1,5},{4,8},{5,9},{8,12},{9,13},{12,14},{13,15},{14,10},{15,... | collective-permute-start | bytes 786440 | tf_op jit(solution)/shard_map/ppermute | solution.py:138
  19.3 6.4 %collective-permute-start.5 = (bf16[16,8192]{1,0:T(8,128)(2,1)S(1)}, bf16[16,8192]{1,0:T(8,128)(2,1)S(1)}, u32[]{:S(2)}, u32[]{:S(2)}) collective-permute-start(bf16[16,8192]{1,0:T(8,128)(2,1)S(1)} %collective-permute-done.3.refs_3_), channel_id=1, source_target_pairs={{0,2},{1,3},{4,0},{5,1},{8,4},{9,5},{12,8},{13,9},{14,12},{15,13},... | collective-permute-start | bytes 786440 | tf_op jit(solution)/shard_map/ppermute | solution.py:139
  25.8 9.0 %collective-permute-start.9 = (bf16[96,8192]{1,0:T(8,128)(2,1)S(1)}, bf16[96,8192]{1,0:T(8,128)(2,1)S(1)}, u32[]{:S(2)}, u32[]{:S(2)}) collective-permute-start(bf16[96,8192]{1,0:T(8,128)(2,1)S(1)} %join_pieces.2.refs_1_), channel_id=1, source_target_pairs={{0,1},{1,0},{2,3},{3,2},{4,5},{5,4},{6,7},{7,6},{8,9},{9,8},{10,11... | collective-permute-start | bytes 4718600 | tf_op jit(solution)/shard_map/ppermute | solution.py:148
  25.9 5.9 %collective-permute-start.6 = (bf16[16,4096]{1,0:T(8,128)(2,1)S(1)}, bf16[16,4096]{1,0:T(8,128)(2,1)S(1)}, u32[]{:S(2)}, u32[]{:S(2)}) collective-permute-start(bf16[16,4096]{1,0:T(8,128)(2,1)S(1)} %column_half.2), channel_id=1, source_target_pairs={{0,4},{1,5},{4,8},{5,9},{8,12},{9,13},{12,14},{13,15},{14,10},{15,... | collective-permute-start | bytes 393224 | tf_op jit(solution)/shard_map/ppermute | solution.py:151
  27.5 5.7 %collective-permute-start.7 = (bf16[16,4096]{1,0:T(8,128)(2,1)S(1)}, bf16[16,4096]{1,0:T(8,128)(2,1)S(1)}, u32[]{:S(2)}, u32[]{:S(2)}) collective-permute-start(bf16[16,4096]{1,0:T(8,128)(2,1)S(1)} %column_half.3), channel_id=1, source_target_pairs={{0,2},{1,3},{4,0},{5,1},{8,4},{9,5},{12,8},{13,9},{14,12},{15,13},... | collective-permute-start | bytes 393224 | tf_op jit(solution)/shard_map/ppermute | solution.py:152
  28.0 5.3 %collective-permute-start.8 = (bf16[16,8192]{1,0:T(8,128)(2,1)S(1)}, bf16[16,8192]{1,0:T(8,128)(2,1)S(1)}, u32[]{:S(2)}, u32[]{:S(2)}) collective-permute-start(bf16[16,8192]{1,0:T(8,128)(2,1)S(1)} %copy-done.1), channel_id=1, source_target_pairs={{0,1},{1,0},{2,3},{3,2},{4,5},{5,4},{6,7},{7,6},{8,9},{9,8},{10,11... | collective-permute-start | bytes 786440 | tf_op jit(solution)/shard_map/ppermute | solution.py:141
  33.2 1.6 %collective-permute-start.10 = (bf16[16,8192]{1,0:T(8,128)(2,1)S(1)}, bf16[16,8192]{1,0:T(8,128)(2,1)S(1)}, u32[]{:S(2)}, u32[]{:S(2)}) collective-permute-start(bf16[16,8192]{1,0:T(8,128)(2,1)S(1)} %join_pieces.3.refs_2_), channel_id=1, source_target_pairs={{0,1},{1,0},{2,3},{3,2},{4,5},{5,4},{6,7},{7,6},{8,9},{9,8},{10,11... | collective-permute-start | bytes 786440 | tf_op jit(solution)/shard_map/ppermute | solution.py:157
  36.6 1.3 %collective-permute-start.11 = (bf16[256,64]{1,0:T(8,128)(2,1)S(1)}, bf16[256,64]{1,0:T(8,128)(2,1)S(1)}, u32[]{:S(2)}, u32[]{:S(2)}) collective-permute-start(bf16[256,64]{1,0:T(8,128)(2,1)S(1)} %get-tuple-element.14.refs_0_), channel_id=1, source_target_pairs={{0,1},{1,0},{2,3},{3,2},{4,5},{5,4},{6,7},{7,6},{8,9},{9,8},{10,11... | collective-permute-start | bytes 98312 | tf_op jit(solution)/shard_map/ppermute | solution.py:552
  37.9 4.3 %collective-permute-start.12 = (bf16[256,64]{1,0:T(8,128)(2,1)S(1)}, bf16[256,64]{1,0:T(8,128)(2,1)S(1)}, u32[]{:S(2)}, u32[]{:S(2)}) collective-permute-start(bf16[256,64]{1,0:T(8,128)(2,1)S(1)} %add_coefficients.3.refs_2_.refs_0_), channel_id=1, source_target_pairs={{0,2},{1,3},{2,0},{3,1},{4,6},{5,7},{6,4},{7,5},{8,10},{9,11},{10,... | collective-permute-start | bytes 98312 | tf_op jit(solution)/shard_map/ppermute | solution.py:552
  42.3 4.9 %collective-permute-start.13 = (bf16[256,64]{1,0:T(8,128)(2,1)S(1)}, bf16[256,64]{1,0:T(8,128)(2,1)S(1)}, u32[]{:S(2)}, u32[]{:S(2)}) collective-permute-start(bf16[256,64]{1,0:T(8,128)(2,1)S(1)} %add_coefficients.4.refs_3_.refs_0_), channel_id=1, source_target_pairs={{0,4},{1,5},{2,6},{3,7},{4,0},{5,1},{6,2},{7,3},{8,12},{9,13},{10,... | collective-permute-start | bytes 98312 | tf_op jit(solution)/shard_map/ppermute | solution.py:552
  47.2 7.8 %slice-start = ((s8[14680064]{0:T(1024)(128)(4,1)}), s8[4194304]{0:T(1024)(128)(4,1)S(1)}, s32[]{:S(2)}) async-start(s8[14680064]{0:T(1024)(128)(4,1)} %bitcast.16), calls=%async_computation | async-start | bytes 8388608
  47.2 6.7 %copy-start = (bf16[16,64,896]{2,1,0:T(8,128)(2,1)S(1)}, bf16[16,64,896]{2,1,0:T(8,128)(2,1)}, u32[]{:S(2)}) copy-start(bf16[16,64,896]{2,1,0:T(8,128)(2,1)} %param.17) | copy-start | bytes 5505028
  47.2 7.7 %slice-start.1 = ((s8[14680064]{0:T(1024)(128)(4,1)}), s8[4194304]{0:T(1024)(128)(4,1)S(1)}, s32[]{:S(2)}) async-start(s8[14680064]{0:T(1024)(128)(4,1)} %bitcast.16), calls=%async_computation.1 | async-start | bytes 8388608
  47.2 7.7 %slice-start.2 = ((s8[14680064]{0:T(1024)(128)(4,1)}), s8[4194304]{0:T(1024)(128)(4,1)S(1)}, s32[]{:S(2)}) async-start(s8[14680064]{0:T(1024)(128)(4,1)} %bitcast.16), calls=%async_computation.2 | async-start | bytes 8388608
  47.2 7.7 %slice-start.3 = ((s8[14680064]{0:T(1024)(128)(4,1)}), s8[2097152]{0:T(1024)(128)(4,1)S(1)}, s32[]{:S(2)}) async-start(s8[14680064]{0:T(1024)(128)(4,1)} %bitcast.16), calls=%async_computation.3 | async-start | bytes 4194304
  47.2 6.7 %collective-permute-start.14 = (bf16[256,64]{1,0:T(8,128)(2,1)S(1)}, bf16[256,64]{1,0:T(8,128)(2,1)S(1)}, u32[]{:S(2)}, u32[]{:S(2)}) collective-permute-start(bf16[256,64]{1,0:T(8,128)(2,1)S(1)} %add_coefficients.5.refs_3_.refs_0_), channel_id=1, source_target_pairs={{0,8},{1,9},{2,10},{3,11},{4,12},{5,13},{6,14},{7,15},{8,0},{9,1},... | collective-permute-start | bytes 98312 | tf_op jit(solution)/shard_map/ppermute | solution.py:552
  57.5 3.2 %collective-permute-start.15 = (bf16[128,4096]{1,0:T(8,128)(2,1)S(1)}, bf16[128,4096]{1,0:T(8,128)(2,1)S(1)}, u32[]{:S(2)}, u32[]{:S(2)}) collective-permute-start(bf16[128,4096]{1,0:T(8,128)(2,1)S(1)} %slice.16), channel_id=1, source_target_pairs={{0,1},{1,0},{2,3},{3,2},{4,5},{5,4},{6,7},{7,6},{8,9},{9,8},{10,11... | collective-permute-start | bytes 3145736 | tf_op jit(solution)/shard_map/ppermute | solution.py:575
  60.1 2.8 %collective-permute-start.17 = (bf16[128,4096]{1,0:T(8,128)(2,1)S(1)}, bf16[128,4096]{1,0:T(8,128)(2,1)S(1)}, u32[]{:S(2)}, u32[]{:S(2)}) collective-permute-start(bf16[128,4096]{1,0:T(8,128)(2,1)S(1)} %slice.17), channel_id=1, source_target_pairs={{0,1},{1,0},{2,3},{3,2},{4,5},{5,4},{6,7},{7,6},{8,9},{9,8},{10,11... | collective-permute-start | bytes 3145736 | tf_op jit(solution)/shard_map/ppermute | solution.py:575
  60.7 5.7 %collective-permute-start.16 = (bf16[16,4096]{1,0:T(8,128)(2,1)S(1)}, bf16[16,4096]{1,0:T(8,128)(2,1)S(1)}, u32[]{:S(2)}, u32[]{:S(2)}) collective-permute-start(bf16[16,4096]{1,0:T(8,128)(2,1)S(1)} %add_blocks.13.refs_2_), channel_id=1, source_target_pairs={{0,4},{1,5},{4,8},{5,9},{8,12},{9,13},{12,14},{13,15},{14,10},{15,... | collective-permute-start | bytes 393224 | tf_op jit(solution)/shard_map/ppermute | solution.py:489
  63.0 6.4 %collective-permute-start.21 = (bf16[16,4096]{1,0:T(8,128)(2,1)S(1)}, bf16[16,4096]{1,0:T(8,128)(2,1)S(1)}, u32[]{:S(2)}, u32[]{:S(2)}) collective-permute-start(bf16[16,4096]{1,0:T(8,128)(2,1)S(1)} %add_blocks.16.refs_3_), channel_id=1, source_target_pairs={{0,2},{1,3},{4,0},{5,1},{8,4},{9,5},{12,8},{13,9},{14,12},{15,13},... | collective-permute-start | bytes 393224 | tf_op jit(solution)/shard_map/ppermute | solution.py:489
  64.1 6.4 %collective-permute-start.20 = (bf16[16,4096]{1,0:T(8,128)(2,1)S(1)}, bf16[16,4096]{1,0:T(8,128)(2,1)S(1)}, u32[]{:S(2)}, u32[]{:S(2)}) collective-permute-start(bf16[16,4096]{1,0:T(8,128)(2,1)S(1)} %add_blocks.15.refs_2_), channel_id=1, source_target_pairs={{0,4},{1,5},{4,8},{5,9},{8,12},{9,13},{12,14},{13,15},{14,10},{15,... | collective-permute-start | bytes 393224 | tf_op jit(solution)/shard_map/ppermute | solution.py:489
  65.1 7.0 %collective-permute-start.19 = (bf16[16,4096]{1,0:T(8,128)(2,1)S(1)}, bf16[16,4096]{1,0:T(8,128)(2,1)S(1)}, u32[]{:S(2)}, u32[]{:S(2)}) collective-permute-start(bf16[16,4096]{1,0:T(8,128)(2,1)S(1)} %add_blocks.14.refs_2_), channel_id=1, source_target_pairs={{0,2},{1,3},{4,0},{5,1},{8,4},{9,5},{12,8},{13,9},{14,12},{15,13},... | collective-permute-start | bytes 393224 | tf_op jit(solution)/shard_map/ppermute | solution.py:489
  66.4 6.9 %collective-permute-start.18 = (bf16[16,4096]{1,0:T(8,128)(2,1)S(1)}, bf16[16,4096]{1,0:T(8,128)(2,1)S(1)}, u32[]{:S(2)}, u32[]{:S(2)}) collective-permute-start(bf16[16,4096]{1,0:T(8,128)(2,1)S(1)} %add_blocks.17.refs_3_), channel_id=1, source_target_pairs={{0,4},{1,5},{4,8},{5,9},{8,12},{9,13},{12,14},{13,15},{14,10},{15,... | collective-permute-start | bytes 393224 | tf_op jit(solution)/shard_map/ppermute | solution.py:489
  69.5 5.6 %collective-permute-start.23 = (bf16[16,4096]{1,0:T(8,128)(2,1)S(1)}, bf16[16,4096]{1,0:T(8,128)(2,1)S(1)}, u32[]{:S(2)}, u32[]{:S(2)}) collective-permute-start(bf16[16,4096]{1,0:T(8,128)(2,1)S(1)} %add_blocks.18.refs_3_), channel_id=1, source_target_pairs={{0,2},{1,3},{4,0},{5,1},{8,4},{9,5},{12,8},{13,9},{14,12},{15,13},... | collective-permute-start | bytes 393224 | tf_op jit(solution)/shard_map/ppermute | solution.py:489
  70.6 6.6 %collective-permute-start.26 = (bf16[16,4096]{1,0:T(8,128)(2,1)S(1)}, bf16[16,4096]{1,0:T(8,128)(2,1)S(1)}, u32[]{:S(2)}, u32[]{:S(2)}) collective-permute-start(bf16[16,4096]{1,0:T(8,128)(2,1)S(1)} %add_blocks.19.refs_3_), channel_id=1, source_target_pairs={{0,4},{1,5},{4,8},{5,9},{8,12},{9,13},{12,14},{13,15},{14,10},{15,... | collective-permute-start | bytes 393224 | tf_op jit(solution)/shard_map/ppermute | solution.py:489
  72.2 6.5 %collective-permute-start.25 = (bf16[16,4096]{1,0:T(8,128)(2,1)S(1)}, bf16[16,4096]{1,0:T(8,128)(2,1)S(1)}, u32[]{:S(2)}, u32[]{:S(2)}) collective-permute-start(bf16[16,4096]{1,0:T(8,128)(2,1)S(1)} %add_blocks.20.refs_3_), channel_id=1, source_target_pairs={{0,2},{1,3},{4,0},{5,1},{8,4},{9,5},{12,8},{13,9},{14,12},{15,13},... | collective-permute-start | bytes 393224 | tf_op jit(solution)/shard_map/ppermute | solution.py:489
  75.1 8.6 %copy-start.7 = (bf16[8192]{0:T(1024)(128)(2,1)S(1)}, bf16[8192]{0:T(1024)(128)(2,1)}, u32[]{:S(2)}) copy-start(bf16[8192]{0:T(1024)(128)(2,1)} %param.15) | copy-start | bytes 49156
  75.1 6.4 %collective-permute-start.24 = (bf16[16,4096]{1,0:T(8,128)(2,1)S(1)}, bf16[16,4096]{1,0:T(8,128)(2,1)S(1)}, u32[]{:S(2)}, u32[]{:S(2)}) collective-permute-start(bf16[16,4096]{1,0:T(8,128)(2,1)S(1)} %add_blocks.22.refs_3_), channel_id=1, source_target_pairs={{0,2},{1,3},{4,0},{5,1},{8,4},{9,5},{12,8},{13,9},{14,12},{15,13},... | collective-permute-start | bytes 393224 | tf_op jit(solution)/shard_map/ppermute | solution.py:489
  76.2 5.3 %collective-permute-start.22 = (bf16[16,4096]{1,0:T(8,128)(2,1)S(1)}, bf16[16,4096]{1,0:T(8,128)(2,1)S(1)}, u32[]{:S(2)}, u32[]{:S(2)}) collective-permute-start(bf16[16,4096]{1,0:T(8,128)(2,1)S(1)} %add_blocks.21.refs_3_), channel_id=1, source_target_pairs={{0,4},{1,5},{4,8},{5,9},{8,12},{9,13},{12,14},{13,15},{14,10},{15,... | collective-permute-start | bytes 393224 | tf_op jit(solution)/shard_map/ppermute | solution.py:489
  77.3 7.9 %collective-permute-start.29 = (bf16[16,4096]{1,0:T(8,128)(2,1)S(1)}, bf16[16,4096]{1,0:T(8,128)(2,1)S(1)}, u32[]{:S(2)}, u32[]{:S(2)}) collective-permute-start(bf16[16,4096]{1,0:T(8,128)(2,1)S(1)} %add_blocks.23.refs_3_), channel_id=1, source_target_pairs={{0,4},{1,5},{4,8},{5,9},{8,12},{9,13},{12,14},{13,15},{14,10},{15,... | collective-permute-start | bytes 393224 | tf_op jit(solution)/shard_map/ppermute | solution.py:489
  78.7 6.4 %collective-permute-start.28 = (bf16[16,4096]{1,0:T(8,128)(2,1)S(1)}, bf16[16,4096]{1,0:T(8,128)(2,1)S(1)}, u32[]{:S(2)}, u32[]{:S(2)}) collective-permute-start(bf16[16,4096]{1,0:T(8,128)(2,1)S(1)} %add_blocks.24.refs_6_), channel_id=1, source_target_pairs={{0,2},{1,3},{4,0},{5,1},{8,4},{9,5},{12,8},{13,9},{14,12},{15,13},... | collective-permute-start | bytes 393224 | tf_op jit(solution)/shard_map/ppermute | solution.py:489
  81.6 5.0 %collective-permute-start.27 = (bf16[16,4096]{1,0:T(8,128)(2,1)S(1)}, bf16[16,4096]{1,0:T(8,128)(2,1)S(1)}, u32[]{:S(2)}, u32[]{:S(2)}) collective-permute-start(bf16[16,4096]{1,0:T(8,128)(2,1)S(1)} %get-tuple-element.18), channel_id=1, source_target_pairs={{0,4},{1,5},{4,8},{5,9},{8,12},{9,13},{12,14},{13,15},{14,10},{15,... | collective-permute-start | bytes 393224 | tf_op jit(solution)/shard_map/ppermute | solution.py:489
  82.7 5.0 %collective-permute-start.30 = (bf16[16,4096]{1,0:T(8,128)(2,1)S(1)}, bf16[16,4096]{1,0:T(8,128)(2,1)S(1)}, u32[]{:S(2)}, u32[]{:S(2)}) collective-permute-start(bf16[16,4096]{1,0:T(8,128)(2,1)S(1)} %get-tuple-element.19), channel_id=1, source_target_pairs={{0,2},{1,3},{4,0},{5,1},{8,4},{9,5},{12,8},{13,9},{14,12},{15,13},... | collective-permute-start | bytes 393224 | tf_op jit(solution)/shard_map/ppermute | solution.py:489
